TPU v7x, 32 devices: a whole 2x2x4 slice. The times are simulated.
32 devices in a mesh: seq: 8 (over z, x), tp: 4 (over y, core).
Axes of the slice: x: 2, y: 2, z: 4, core: 2. Of those that a mesh axis runs over, the one named last changes fastest.
Arguments:
- queries: bfloat16 [2048, 4096], P('seq', 'tp'), may hold values from -6 to 6
- vocab_rows: bfloat16 [16384, 1024], P('seq', 'tp'), may hold values from -36 to 36
- neighbour_ids: int32 [32, 2, 128], P('seq'), may hold values from 0 to 16383, as said below
- w_in: bfloat16 [1024, 4096], P(None, 'tp'), may hold values from -0.1875 to 0.1875
- w_out: bfloat16 [4096, 1024], P('tp'), may hold values from -0.09375 to 0.09375
- w_key: bfloat16 [1024, 4096], P(None, 'tp'), may hold values from -0.1875 to 0.1875
- w_value: bfloat16 [1024, 4096], P(None, 'tp'), may hold values from -0.1875 to 0.1875
Outputs:
- cross_out: bfloat16 [2048, 4096], P('seq', 'tp')
Inputs may be any that keep to these rules, and one draw needn't show every extreme that they name: `neighbour_ids`: the owner of id i is i // 2048. Among the neighbour ids of the groups of one index of seq, at most 256 have one owner; some owner has exactly 256 among those of every index.
All inputs are finite; a program needn't handle non-finite values.
Results may differ from a plain program's by a relative error of at most 0.0095.
Values may be sent and summed in bfloat16 or wider, within the bound.
No kernel may reach another device: no remote copies, remote signals or barrier semaphores. Data moves between devices by JAX's collectives and lax.ppermute only.
A program may use at most 64 MiB of HBM per device.

v0:
```python
import jax
import jax.numpy as jnp
from jax import lax
from jax.sharding import PartitionSpec as P

HEAD_WIDTH = 128
GROUP = 64


def shifted(x, axis, by):
    length = lax.axis_size(axis)
    pairs = [(i, i + by) for i in range(length) if 0 <= i + by < length]
    return lax.ppermute(x, axis, pairs)


def attend_blocks(q_blocks, paired):
    blocks, count, width = q_blocks.shape
    heads = width // HEAD_WIDTH
    kcount = paired.shape[2]
    decoder_query = q_blocks.reshape(blocks, count, heads, HEAD_WIDTH)
    neighbour_key_heads = paired[0].reshape(blocks, kcount, heads, HEAD_WIDTH)
    neighbour_value_heads = paired[1].reshape(blocks, kcount, heads, HEAD_WIDTH)
    attention_logits = jnp.einsum(
        "bmhd,bkhd->bhmk", decoder_query, neighbour_key_heads, preferred_element_type=jnp.float32
    ) * HEAD_WIDTH ** (-0.5)
    expo = jnp.exp(attention_logits)
    attention_probs = (expo / jnp.sum(expo, axis=-1, keepdims=True)).astype(jnp.bfloat16)
    attended_values = jnp.einsum(
        "bhmk,bkhd->bmhd",
        attention_probs,
        neighbour_value_heads,
        preferred_element_type=jnp.float32,
    )
    return attended_values.reshape(blocks, count, width).astype(jnp.bfloat16)


def per_device(queries, vocab_rows, neighbour_ids, w_in, w_out, w_key, w_value):
    seq_size = lax.axis_size("seq")
    flat_ids = neighbour_ids.reshape(-1)
    rows = flat_ids.shape[0]
    voc_local = vocab_rows.shape[0]
    capacity = max(2, 2 * rows // seq_size)
    owner = flat_ids // voc_local
    local_row = flat_ids % voc_local
    owner_table = (owner[:, None] == jnp.arange(seq_size, dtype=jnp.int32)[None, :]).astype(
        jnp.int32
    )
    rank = jnp.sum((jnp.cumsum(owner_table, axis=0) - 1) * owner_table, axis=1)
    slot = owner * capacity + rank
    wanted = (
        jnp.zeros((seq_size * capacity,), jnp.int32)
        .at[slot]
        .set(local_row)
        .reshape(seq_size, capacity)
    )
    found = jnp.take(
        vocab_rows, lax.all_to_all(wanted, "seq", split_axis=0, concat_axis=0, tiled=True), axis=0
    )
    answered = lax.all_to_all(found, "seq", split_axis=0, concat_axis=0, tiled=True)
    own_rows = answered[owner, rank]
    gathered = lax.all_gather(own_rows, "tp", axis=1, tiled=True)
    values_f = gathered.astype(jnp.float32)
    normed = (
        values_f * lax.rsqrt(jnp.mean(values_f * values_f, axis=-1, keepdims=True) + 1e-06)
    ).astype(jnp.bfloat16)
    inner = jax.nn.gelu(
        jnp.dot(normed, w_in, preferred_element_type=jnp.float32), approximate=True
    ).astype(jnp.bfloat16)
    total = lax.psum(jnp.dot(inner, w_out, preferred_element_type=jnp.float32), "tp")
    encoded = (values_f + total).astype(jnp.bfloat16)
    keys = jnp.dot(encoded, w_key, preferred_element_type=jnp.float32).astype(jnp.bfloat16)
    values = jnp.dot(encoded, w_value, preferred_element_type=jnp.float32).astype(jnp.bfloat16)
    groups = neighbour_ids.shape[0]
    per_group = neighbour_ids.shape[1] * neighbour_ids.shape[2]
    width = queries.shape[1]
    paired = jnp.stack([keys, values]).reshape(2, groups, per_group, width)
    tok = queries.shape[0]
    edge = GROUP - 1
    behind = shifted(paired[:, groups - 1], "seq", 1)
    local_q = jnp.concatenate([queries[edge:], jnp.zeros((edge, width), queries.dtype)], axis=0)
    windows = attend_blocks(local_q.reshape(groups, GROUP, width), paired)
    head = attend_blocks(queries[:edge][None], behind[:, None])[0]
    flat = windows.reshape(tok, width)[: tok - edge]
    at_start = lax.axis_index("seq") == 0
    head = jnp.where(at_start, jnp.zeros_like(head), head)
    return jnp.concatenate([head, flat], axis=0)


def solution(mesh):
    return jax.shard_map(
        per_device,
        mesh=mesh,
        in_specs=(
            P("seq", "tp"),
            P("seq", "tp"),
            P("seq", None, None),
            P(None, "tp"),
            P("tp", None),
            P(None, "tp"),
            P(None, "tp"),
        ),
        out_specs=P("seq", "tp"),
        check_vma=False,
    )
```

profile of v0, /device:TPU:1, one launch (start us, length us, event | category | flops | bytes accessed | tf_op | source)
XLA Modules:
  0.0 253.3 jit_solution(1917917029585396774)
XLA Ops:
  8.1 2.3 reduce-window.6
  11.7 4.3 %scatter_custom_fusion = s32[2048]{0:T(1024)S(1)} fusion(s32[1024]{0:T(1024)S(1)} %bitcast.102, s32[1024]{0:T(1024)S(1)} %get-tuple-element.9, s32[]{:T(128)} %constant.37.clone.1), kind=kCustom, calls=%fused_computation.92 | custom fusion | bytes 8196 | tf_op jit(solution)/shard_map/scatter | solution.py:53
  16.0 11.5 %all_to_all.20 = s32[8,1,256]{2,1,0:T(1,128)S(1)} all-to-all(s32[8,1,256]{2,1,0:T(1,128)S(1)} %bitcast.99), channel_id=1, replica_groups=mesh['seq'=8,'tp'=4] {'seq'}, dimensions={0} | all-to-all | bytes 16384 | tf_op jit(solution)/shard_map/all_to_all | solution.py:57
  27.5 8.0 %gather_fusion = bf16[2048,256]{1,0:T(8,128)(2,1)S(1)} fusion(bf16[2048,256]{1,0:T(8,128)(2,1)} %param.8, s32[2048]{0:T(1024)S(1)} %broadcast_clamp_fusion), kind=kCustom, calls=%fused_computation | custom fusion | bytes 2105344 | tf_op jit(solution)/shard_map/jit(_take)/gather | solution.py:56
  36.0 27.1 %all_to_all.21 = bf16[8,256,256]{2,1,0:T(8,128)(2,1)S(1)} all-to-all(bf16[8,256,256]{2,1,0:T(8,128)(2,1)S(1)} %broadcast_select_fusion), channel_id=1, replica_groups=mesh['seq'=8,'tp'=4] {'seq'}, dimensions={0} | all-to-all | bytes 2097152 | tf_op jit(solution)/shard_map/all_to_all | solution.py:59
  63.1 10.7 %gather_fusion.1 = bf16[1024,256]{1,0:T(8,128)(2,1)} fusion(bf16[8,256,256]{2,1,0:T(8,128)(2,1)S(1)} %all_to_all.21, s32[1024]{0:T(1024)S(1)} %bitcast.76), kind=kCustom, calls=%fused_computation.1 | custom fusion | bytes 1056768 | tf_op jit(solution)/shard_map/gather | solution.py:60
  73.9 23.7 %all-gather.2.cloned.1.call-done = bf16[1024,1024]{1,0:T(8,128)(2,1)} async-done(((bf16[1024,256]{1,0:T(8,128)(2,1)}), bf16[1024,1024]{1,0:T(8,128)(2,1)}) %all-gather.2.cloned.1.call-update) | async-done | bytes 2097168 | tf_op jit(solution)/shard_map/all_gather | solution.py:61
  97.6 2.1 fusion
  99.7 8.8 %fusion.11 = f32[1024,1024]{1,0:T(8,128)} fusion(bf16[1024,1024]{1,0:T(8,128)(2,1)S(1)} %copy-done, bf16[1024,1024]{1,0:T(8,128)(2,1)} %param.10, bf16[1024,1024]{1,0:T(8,128)(2,1)} %all-gather.2.cloned.1.call-done, f32[1024]{0:T(1024)S(1)} %add_rsqrt_fusion), kind=kOutput, calls=%fused_computation.18 | convolution fusion | flops 4307550208 | bytes 10489856 | tf_op jit(solution)/shard_map/dot_general | solution.py:69
  108.5 85.1 %all-reduce.3.cloned.1.call-done = f32[1024,1024]{1,0:T(8,128)} async-done(((f32[1024,1024]{1,0:T(8,128)}), f32[1024,1024]{1,0:T(8,128)}) %all-reduce.3.cloned.1.call-update) | async-done | bytes 4194320 | tf_op jit(solution)/shard_map/psum | solution.py:69
  193.6 7.1 %convolution_convert_fusion = bf16[1024,1024]{1,0:T(8,128)(2,1)} fusion(bf16[1024,1024]{1,0:T(8,128)(2,1)} %param.13, f32[1024,1024]{1,0:T(8,128)} %all-reduce.3.cloned.1.call-done, bf16[1024,1024]{1,0:T(8,128)(2,1)} %all-gather.2.cloned.1.call-done), kind=kOutput, calls=%fused_computation.31 | convolution fusion | flops 2151677952 | bytes 10485760 | tf_op jit(solution)/shard_map/dot_general | solution.py:72
  200.7 4.0 %copy.21 = bf16[1,4,256,1024]{2,3,0,1:T(8,128)(2,1)} copy(bf16[1,4,256,1024]{3,2,1,0:T(8,128)(2,1)} %bitcast.77) | data formatting | bytes 4194304 | tf_op jit(solution)/shard_map/stack | solution.py:76
  204.7 7.1 %convolution_convert_fusion.1 = bf16[1024,1024]{1,0:T(8,128)(2,1)} fusion(bf16[1024,1024]{1,0:T(8,128)(2,1)} %param.12, f32[1024,1024]{1,0:T(8,128)} %all-reduce.3.cloned.1.call-done, bf16[1024,1024]{1,0:T(8,128)(2,1)} %all-gather.2.cloned.1.call-done), kind=kOutput, calls=%fused_computation.32 | convolution fusion | flops 2151677952 | bytes 10485760 | tf_op jit(solution)/shard_map/dot_general | solution.py:71
  211.8 3.9 %copy.20 = bf16[1,4,256,1024]{2,3,0,1:T(8,128)(2,1)} copy(bf16[1,4,256,1024]{3,2,1,0:T(8,128)(2,1)} %bitcast.79) | data formatting | bytes 4194304 | tf_op jit(solution)/shard_map/stack | solution.py:76
  215.7 1.4 fusion.39
  217.1 4.3 %collective-permute-start = (bf16[2,256,1024]{1,2,0:T(8,128)(2,1)S(1)}, bf16[2,256,1024]{1,2,0:T(8,128)(2,1)}, u32[]{:S(2)}, u32[]{:S(2)}) collective-permute-start(bf16[2,256,1024]{1,2,0:T(8,128)(2,1)S(1)} %fusion.39), channel_id=1, source_target_pairs={{0,4},{4,8},{8,12},{12,16},{16,20},{20,24},{24,28},{1,5},{5,9},{9,... | collective-permute-start | bytes 3145736 | tf_op jit(solution)/shard_map/ppermute | solution.py:13
  222.1 1.1 copy.34
  224.4 1.0 copy-done.2
  226.0 0.9 fusion.24
  228.2 13.8 %collective-permute-done = bf16[2,256,1024]{1,2,0:T(8,128)(2,1)} collective-permute-done((bf16[2,256,1024]{1,2,0:T(8,128)(2,1)S(1)}, bf16[2,256,1024]{1,2,0:T(8,128)(2,1)}, u32[]{:S(2)}, u32[]{:S(2)}) %collective-permute-start) | collective-permute-done | bytes 1048608 | tf_op jit(solution)/shard_map/ppermute | solution.py:13
  242.0 1.3 fusion.68
  243.5 1.0 fusion.34
  244.5 1.0 copy.63
  245.6 0.9 pad_maximum_fusion.1
  (39 shorter events, 7.4 us)
Async XLA Ops:
  6.5 93.2 %copy-start = (bf16[1024,1024]{1,0:T(8,128)(2,1)S(1)}, bf16[1024,1024]{1,0:T(8,128)(2,1)}, u32[]{:S(2)}) copy-start(bf16[1024,1024]{1,0:T(8,128)(2,1)} %param.11) | copy-start | bytes 6291460
  6.5 91.1 %all-gather.2.cloned.1.call-start = ((), (), s32[]{:S(2)}) async-start(), calls=%async_computation.2 | async-start | bytes 2621440 | tf_op jit(solution)/shard_map/all_gather | solution.py:61
  73.8 119.8 %all-reduce.3.cloned.1.call-start = ((), (), s32[]{:S(2)}) async-start(), calls=%async_computation.3 | async-start | bytes 8388608 | tf_op jit(solution)/shard_map/psum | solution.py:69
  215.7 5.6 %copy-start.3 = (bf16[256,1024]{1,0:T(8,128)(2,1)S(1)}, bf16[256,1024]{1,0:T(8,128)(2,1)}, u32[]{:S(2)}) copy-start(bf16[256,1024]{1,0:T(8,128)(2,1)} %param.7) | copy-start | bytes 1572868
  217.1 24.9 %collective-permute-start = (bf16[2,256,1024]{1,2,0:T(8,128)(2,1)S(1)}, bf16[2,256,1024]{1,2,0:T(8,128)(2,1)}, u32[]{:S(2)}, u32[]{:S(2)}) collective-permute-start(bf16[2,256,1024]{1,2,0:T(8,128)(2,1)S(1)} %fusion.39), channel_id=1, source_target_pairs={{0,4},{4,8},{8,12},{12,16},{16,20},{20,24},{24,28},{1,5},{5,9},{9,... | collective-permute-start | bytes 3145736 | tf_op jit(solution)/shard_map/ppermute | solution.py:13
  222.1 1.7 copy-start.1
  223.8 1.6 copy-start.2
Sparse Core Ops, SparseCore 0:
  73.9 23.6 all-gather.1
  108.7 84.9 all-reduce.2
where the time goes:
time: 256 us; the launch traced here: 253 us
  waiting for transfers between devices  123 us (48%)
  blocking collectives  38.6 us (15%)
  local copies, waits for them, and re-layouts  38.5 us (15%)
  matrix products  26 us (10%)
  between operations  13.6 us (5%)
  other arithmetic  9.62 us (4%)
  starting transfers between devices  4.32 us (2%)
    psum x1, waiting for transfers between devices, per_device(): lax.psum(jnp.dot(inner, w_out, preferred_element_type=jnp.float32), 'tp')  85.1 us
    all_to_all x1, blocking collectives, per_device(): lax.all_to_all(found, 'seq', split_axis=0, concat_axis=0, tiled=True)  27.1 us
    all_gather x1, waiting for transfers between devices, per_device(): gathered = lax.all_gather(own_rows, 'tp', axis=1, tiled=True)  23.7 us
    ppermute x1, waiting for transfers between devices, shifted(): return lax.ppermute(x, axis, pairs)  13.8 us
    all_to_all x1, blocking collectives, per_device(): lax.all_to_all(wanted, 'seq', split_axis=0, concat_axis=0, tiled=True)  11.5 us
    gather x1, local copies, waits for them, and re-layouts, per_device(): own_rows = answered[owner, rank]  10.7 us
    dot_general x1, matrix products, per_device(): jnp.dot(inner, w_out, preferred_element_type=jnp.float32)  8.79 us
    gather x1, local copies, waits for them, and re-layouts, per_device(): jnp.take(vocab_rows, lax.all_to_all(wanted, 'seq', split_axis=0, concat_a...  8 us
  transfers between devices with their start and end apart: 3, of which 3 were waited for; matrix products, arithmetic and copies ran while one was open for 2% of the time, Pallas kernels for 0%

commit v1 on v0

v1 whole, which is shorter than its diff:
```python
import functools

import jax
import jax.numpy as jnp
from jax import lax
from jax.experimental import pallas as pl
from jax.experimental.pallas import tpu as pltpu
from jax.sharding import PartitionSpec as P

HEAD_WIDTH = 128
GROUP = 64
LANES = 128
VMEM_LIMIT = 24 * 1024 * 1024
F32 = jnp.float32
BF16 = jnp.bfloat16


def call(body, outs, flops, nbytes, name, unused=None):
    specs = {}
    if unused is not None:
        vmem = pl.BlockSpec(memory_space=pltpu.VMEM)
        specs = dict(in_specs=[vmem] * (unused - 1) + [pl.BlockSpec(memory_space=pl.ANY)])
    return pl.pallas_call(
        body,
        out_shape=outs,
        **specs,
        compiler_params=pltpu.CompilerParams(vmem_limit_bytes=VMEM_LIMIT),
        cost_estimate=pl.CostEstimate(flops=flops, bytes_accessed=nbytes, transcendentals=0),
        name=name,
    )


def exchange(x, bit):
    size = lax.axis_size("tp")
    return lax.ppermute(x, "tp", [(i, i ^ bit) for i in range(size)])


def shifted(x, by):
    length = lax.axis_size("seq")
    pairs = [(i, i + by) for i in range(length) if 0 <= i + by < length]
    return lax.ppermute(x, "seq", pairs)


def columns_of(row):
    return jnp.broadcast_to(row, (LANES, row.shape[1])).T


def one_hot(column, width):
    lane = lax.broadcasted_iota(jnp.int32, column.shape, 1)
    return jnp.concatenate(
        [jnp.where(column == lane + at, 1.0, 0.0).astype(BF16) for at in range(0, width, LANES)],
        axis=1,
    )


def route_body(voc, cap, ids_ref, wanted_ref, slot_ref):
    ids = ids_ref[...]
    count = ids.shape[1]
    owners = wanted_ref.shape[0]
    owner = lax.div(ids, jnp.int32(voc))
    local = ids - owner * voc
    hit = owner == lax.broadcasted_iota(jnp.int32, (owners, count), 0)
    hot = jnp.where(hit, 1.0, 0.0)
    upper = jnp.where(
        lax.broadcasted_iota(jnp.int32, (LANES, LANES), 0)
        <= lax.broadcasted_iota(jnp.int32, (LANES, LANES), 1),
        1.0,
        0.0,
    ).astype(BF16)
    carry = jnp.zeros((owners, 1), F32)
    ranks = []
    for at in range(0, count, LANES):
        part = hot[:, at : at + LANES]
        running = jnp.dot(part.astype(BF16), upper, preferred_element_type=F32) + carry
        ranks.append(jnp.sum(part * running, axis=0, keepdims=True))
        carry = running[:, LANES - 1 :]
    rank = jnp.concatenate(ranks, axis=1).astype(jnp.int32) - 1
    high = jnp.where(hit, lax.div(local, jnp.int32(256)), 0)
    low = jnp.where(hit, lax.rem(local, jnp.int32(256)), 0)
    digits = jnp.concatenate([high, low], axis=0).astype(F32).astype(BF16)
    place = jnp.where(
        rank == lax.broadcasted_iota(jnp.int32, (cap, count), 0), 1.0, 0.0
    ).astype(BF16)
    found = lax.dot_general(
        digits, place, (((1,), (1,)), ((), ())), preferred_element_type=F32
    ).astype(jnp.int32)
    wanted_ref[...] = found[:owners] * 256 + found[owners:]
    slot_ref[...] = columns_of(owner * cap + rank)


def fetch_body(req_ref, vocab_ref, out_ref):
    step = 256
    table = vocab_ref[...]
    for at in range(0, req_ref.shape[1], step):
        picked = one_hot(columns_of(req_ref[:, at : at + step]), table.shape[0])
        out_ref[at : at + step, :] = jnp.dot(
            picked, table, preferred_element_type=F32
        ).astype(BF16)


def order_body(slot_ref, rows_ref, *out_refs):
    rows = rows_ref[...]
    for at, out_ref in enumerate(out_refs):
        count = out_ref.shape[0]
        picked = one_hot(slot_ref[at * count : (at + 1) * count, :], rows.shape[0])
        out_ref[...] = jnp.dot(picked, rows, preferred_element_type=F32).astype(BF16)


def block_rows(ref, index, width):
    return ref[pl.ds(pl.multiple_of(index * width, width), width), :]


def block_cols(ref, index, width):
    return ref[:, pl.ds(pl.multiple_of(index * width, width), width)]


def feed_body(e0_ref, e2_ref, e1_ref, e3_ref, w_in_ref, w_out_ref, _, keep_ref, send_ref):
    me = lax.axis_index("tp")
    width = e0_ref.shape[1]
    index = [me, me ^ 2, me ^ 1, me ^ 3]
    parts = [ref[...].astype(F32) for ref in (e0_ref, e2_ref, e1_ref, e3_ref)]
    square = sum(jnp.sum(part * part, axis=1, keepdims=True) for part in parts)
    scale = lax.rsqrt(square / (4 * width) + 1e-06)
    hidden = sum(
        jnp.dot(
            (part * scale).astype(BF16), block_rows(w_in_ref, at, width), preferred_element_type=F32
        )
        for part, at in zip(parts, index)
    )
    inner = jax.nn.gelu(hidden, approximate=True).astype(BF16)
    for slot in range(2):
        cols = slice(slot * width, (slot + 1) * width)
        keep_ref[:, cols] = jnp.dot(
            inner, block_cols(w_out_ref, index[slot], width), preferred_element_type=F32
        )
        send_ref[:, cols] = jnp.dot(
            inner, block_cols(w_out_ref, index[2 + slot], width), preferred_element_type=F32
        ).astype(BF16)


def add_body(keep_ref, recv_ref, _, chip_ref, send_ref):
    chip = keep_ref[...] + recv_ref[...].astype(F32)
    chip_ref[...] = chip
    send_ref[...] = chip.astype(BF16)


def finish_body(e0_ref, e2_ref, chip_ref, far_ref, _, mine_ref):
    width = e0_ref.shape[1]
    near, past = slice(0, width), slice(width, 2 * width)
    mine_ref[:, near] = (
        e0_ref[...].astype(F32) + (chip_ref[:, near] + far_ref[:, past].astype(F32))
    ).astype(BF16)
    mine_ref[:, past] = (
        e2_ref[...].astype(F32) + (chip_ref[:, past] + far_ref[:, near].astype(F32))
    ).astype(BF16)


def attended(mine_ref, other_ref, w_key_ref, w_value_ref, q_ref):
    me = lax.axis_index("tp")
    width = mine_ref.shape[1] // 2
    parts = [
        (mine_ref[:, :width], me),
        (mine_ref[:, width:], me ^ 2),
        (other_ref[:, :width], me ^ 1),
        (other_ref[:, width:], me ^ 3),
    ]

    def project(w_ref):
        return sum(
            jnp.dot(part, block_rows(w_ref, at, width), preferred_element_type=F32)
            for part, at in parts
        ).astype(BF16)

    heads = [slice(at, at + HEAD_WIDTH) for at in range(0, q_ref.shape[1], HEAD_WIDTH)]
    keys = project(w_key_ref)
    weights = []
    for cols in heads:
        logits = lax.dot_general(
            q_ref[:, cols], keys[:, cols], (((1,), (1,)), ((), ())), preferred_element_type=F32
        ) * HEAD_WIDTH ** (-0.5)
        expo = jnp.exp(logits)
        weights.append((expo * (1.0 / jnp.sum(expo, axis=1, keepdims=True))).astype(BF16))
    values = project(w_value_ref)
    return [
        jnp.dot(weight, values[:, cols], preferred_element_type=F32)
        for weight, cols in zip(weights, heads)
    ]


def attend_body(mine_ref, other_ref, w_key_ref, w_value_ref, q_ref, _, out_ref):
    for at, part in enumerate(attended(mine_ref, other_ref, w_key_ref, w_value_ref, q_ref)):
        out_ref[:, at * HEAD_WIDTH : (at + 1) * HEAD_WIDTH] = part.astype(BF16)


def attend_last_body(
    mine_ref, other_ref, w_key_ref, w_value_ref, q_ref, behind_ref, *refs
):
    before, last_ref, out_ref = refs[:-2], refs[-2], refs[-1]
    parts = attended(mine_ref, other_ref, w_key_ref, w_value_ref, q_ref)
    for at, part in enumerate(parts):
        cols = slice(at * HEAD_WIDTH, (at + 1) * HEAD_WIDTH)
        part = part.astype(BF16).astype(F32)
        stack = [behind_ref[:, cols].astype(F32)]
        stack += [ref[:, cols].astype(F32) for ref in before]
        stack += [part, last_ref[:, cols].astype(F32)]
        tall = jnp.concatenate(stack, axis=0)
        moved = pltpu.roll(tall, tall.shape[0] - 1, 0)
        out_ref[:, cols] = moved[: out_ref.shape[0]].astype(BF16)


def per_device(queries, vocab_rows, neighbour_ids, w_in, w_out, w_key, w_value):
    seq_size = lax.axis_size("seq")
    groups, nbrs, nlen = neighbour_ids.shape
    per_group = nbrs * nlen
    rows = groups * per_group
    voc, width = vocab_rows.shape
    tok, head_cols = queries.shape
    cap = max(2, 2 * rows // seq_size)
    slots = seq_size * cap
    sds = jax.ShapeDtypeStruct

    next_q = shifted(queries[:GROUP], -1)

    wanted, slot = call(
        functools.partial(route_body, voc, cap),
        (sds((seq_size, cap), jnp.int32), sds((rows, LANES), jnp.int32)),
        2 * rows * cap * 16,
        rows * 600,
        "route",
    )(neighbour_ids.reshape(1, rows))
    request = lax.all_to_all(wanted, "seq", split_axis=0, concat_axis=0, tiled=True)
    found = call(
        fetch_body, sds((slots, width), BF16), 2 * slots * voc * width, 3 * slots * width * 2, "fetch"
    )(request.reshape(1, slots), vocab_rows)
    answered = lax.all_to_all(
        found.reshape(seq_size, cap, width), "seq", split_axis=0, concat_axis=0, tiled=True
    ).reshape(slots, width)
    own = call(
        order_body,
        tuple(sds((per_group, width), BF16) for _ in range(groups)),
        2 * slots * rows * width,
        3 * slots * width * 2,
        "order",
    )(slot, answered)

    local_q = jnp.concatenate([queries[GROUP - 1 :], next_q[: GROUP - 1]], axis=0)
    order = [groups - 1] + list(range(groups - 1))
    half = sds((per_group, 2 * width), BF16)
    whole = sds((per_group, 2 * width), F32)
    window = {}
    emb, fed, summed, far = {}, {}, {}, {}
    behind = None
    token = slot

    def embed(g):
        e0 = own[g]
        e2 = exchange(e0, 2)
        emb[g] = (e0, e2, exchange(e0, 1), exchange(e2, 1))

    def feed(g):
        nonlocal token
        keep, send = call(
            feed_body,
            (whole, half),
            16 * per_group * width * w_in.shape[1],
            4 * w_in.shape[0] * w_in.shape[1],
            "feed",
            unused=7,
        )(*emb[g], w_in, w_out, token)
        fed[g] = keep, exchange(send, 1)
        token = send

    def add(g):
        nonlocal token
        chip, send = call(
            add_body, (whole, half), per_group * width, per_group * width * 16, "add", unused=3
        )(*fed[g], token)
        summed[g] = chip
        far[g] = exchange(send, 2)
        token = send

    def finish(g):
        nonlocal token, behind
        mine = call(
            finish_body, half, per_group * width, per_group * width * 16, "finish", unused=5
        )(*emb[g][:2], summed[g], far[g], token)
        other = exchange(mine, 1)
        token = mine
        args = (mine, other, w_key, w_value, local_q[g * GROUP : (g + 1) * GROUP])
        cost = 16 * per_group * width * head_cols, 4 * w_key.shape[0] * w_key.shape[1]
        if g == order[-1]:
            before = [window[at] for at in range(groups - 2)]
            return call(attend_last_body, sds((tok, head_cols), BF16), *cost, "attend_last")(
                *args, behind, *before, window[groups - 1]
            )
        window[g] = call(
            attend_body, sds((GROUP, head_cols), BF16), *cost, "attend", unused=6
        )(*args, token)
        token = window[g]
        if g == groups - 1:
            behind = shifted(window[g], 1)

    for at, g in enumerate(order):
        embed(g)
    for at, g in enumerate(order):
        feed(g)
        if at >= 1:
            add(order[at - 1])
    add(order[-1])
    out = None
    for g in order:
        out = finish(g)
    return out


def solution(mesh):
    return jax.shard_map(
        per_device,
        mesh=mesh,
        in_specs=(
            P("seq", "tp"),
            P("seq", "tp"),
            P("seq", None, None),
            P(None, "tp"),
            P("tp", None),
            P(None, "tp"),
            P(None, "tp"),
        ),
        out_specs=P("seq", "tp"),
        check_vma=False,
    )
```

time: 256 us -> 118 us (0.46)
  waiting for transfers between devices: 123 us -> 30.2 us
  local copies, waits for them, and re-layouts: 38.5 us -> 2.15 us
  matrix products: 26 us -> 0 us
  starting transfers between devices: 4.32 us -> 25.6 us
  Pallas kernels: 0 us -> 19.1 us
  between operations: 13.6 us -> 0.26 us
  other arithmetic: 9.62 us -> 0.04 us
    psum x1 -> x0, waiting for transfers between devices: 85.1 us -> none  [per_device(): lax.psum(jnp.dot(inner, w_out, preferred_element_type=jnp.float32), 'tp')]
    dot_general x7 -> x0, matrix products: 26 us -> none  [the longest x1 8.79 us: per_device(): jnp.dot(inner, w_out, preferred_element_type=jnp.float32)]
    all_gather x1 -> x0, waiting for transfers between devices: 23.7 us -> none  [per_device(): gathered = lax.all_gather(own_rows, 'tp', axis=1, tiled=True)]
    ppermute x1 -> x26, starting transfers between devices: 4.27 us -> 25.6 us  [the longest x24 20.1 us: exchange(): return lax.ppermute(x, 'tp', [(i, i ^ bit) for i in range(size)])]
    pallas_call x0 -> x19, Pallas kernels: none -> 19.1 us  [the longest x4 6.39 us: feed(): call(feed_body, (whole, half), 16 * per_group * width * w_in.shape[1], 4...]
    gather x2 -> x0, local copies, waits for them, and re-layouts: 18.7 us -> none  [the longest x1 10.7 us: per_device(): own_rows = answered[owner, rank]]
    ppermute x1 -> x26, waiting for transfers between devices: 13.8 us -> 30.2 us  [the longest x24 22.3 us: exchange(): return lax.ppermute(x, 'tp', [(i, i ^ bit) for i in range(size)])]
    another operation x3 -> x0, local copies, waits for them, and re-layouts: 7.9 us -> none  [the longest x2 7.89 us: per_device(): paired = jnp.stack([keys, values]).reshape(2, groups, per_group, width)]
  transfers between devices with their start and end apart: 3 -> 26, of which waited for: 3 -> 11; matrix products, arithmetic and copies ran while one was open for 2% -> 0% of each run, Pallas kernels for 0% -> 10%
where the time goes in v1:
time: 118 us; the launch traced here: 116 us
  blocking collectives  38.8 us (33%)
  waiting for transfers between devices  30.2 us (26%)
  starting transfers between devices  25.6 us (22%)
  Pallas kernels  19.1 us (16%)
  local copies, waits for them, and re-layouts  2.15 us (2%)
    all_to_all x1, blocking collectives, per_device(): lax.all_to_all(found.reshape(seq_size, cap, width), 'seq', split_axis=0,...  27.2 us
    ppermute x24, waiting for transfers between devices, exchange(): return lax.ppermute(x, 'tp', [(i, i ^ bit) for i in range(size)])  22.3 us
    ppermute x24, starting transfers between devices, exchange(): return lax.ppermute(x, 'tp', [(i, i ^ bit) for i in range(size)])  20.1 us
    all_to_all x1, blocking collectives, per_device(): lax.all_to_all(wanted, 'seq', split_axis=0, concat_axis=0, tiled=True)  11.5 us
    ppermute x2, waiting for transfers between devices, shifted(): return lax.ppermute(x, 'seq', pairs)  7.82 us
    pallas_call x4, Pallas kernels, feed(): call(feed_body, (whole, half), 16 * per_group * width * w_in.shape[1], 4...  6.39 us
    ppermute x2, starting transfers between devices, shifted(): return lax.ppermute(x, 'seq', pairs)  5.45 us
    pallas_call x3, Pallas kernels, finish(): call(attend_body, sds((GROUP, head_cols), BF16), *cost, 'attend', unused=6)  5.06 us
  transfers between devices with their start and end apart: 26, of which 11 were waited for; matrix products, arithmetic and copies ran while one was open for 0% of the time, Pallas kernels for 10%

profile of v1, /device:TPU:1, one launch (start us, length us, event | category | flops | bytes accessed | tf_op | source)
XLA Modules:
  0.0 116.0 jit_solution(13034878535840381068)
XLA Ops:
  1.5 11.5 %all_to_all.14 = s32[8,1,256]{2,1,0:T(1,128)S(1)} all-to-all(s32[8,1,256]{2,1,0:T(1,128)S(1)} %copy.8), channel_id=1, replica_groups=mesh['seq'=8,'tp'=4] {'seq'}, dimensions={0} | all-to-all | bytes 16384 | tf_op jit(solution)/shard_map/all_to_all | solution.py:231
  14.3 2.4 %fetch.1 = bf16[2048,256]{1,0:T(8,128)(2,1)S(1)} custom-call(s32[1,2048]{1,0:T(1,128)S(1)} %bitcast.9, bf16[2048,256]{1,0:T(8,128)(2,1)S(1)} %copy-done.4), custom_call_target="tpu_custom_call" | custom-call | flops 2147483648 | bytes 3145728 | tf_op jit(solution)/shard_map/fetch/pallas_call | solution.py:232
  16.7 27.2 %all_to_all.15 = bf16[8,256,256]{2,1,0:T(8,128)(2,1)S(1)} all-to-all(bf16[8,256,256]{2,1,0:T(8,128)(2,1)S(1)} %bitcast.7), channel_id=1, replica_groups=mesh['seq'=8,'tp'=4] {'seq'}, dimensions={0} | all-to-all | bytes 2097152 | tf_op jit(solution)/shard_map/all_to_all | solution.py:235
  46.7 2.6 %collective-permute-start.7 = (bf16[256,256]{1,0:T(8,128)(2,1)S(1)}, bf16[256,256]{1,0:T(8,128)(2,1)S(1)}, u32[]{:S(2)}, u32[]{:S(2)}) collective-permute-start(bf16[256,256]{1,0:T(8,128)(2,1)S(1)} %get-tuple-element.31.e0_ref), channel_id=1, source_target_pairs={{0,1},{1,0},{2,3},{3,2},{4,5},{5,4},{6,7},{7,6},{8,9},{9,8},{10,11... | collective-permute-start | bytes 393224 | tf_op jit(solution)/shard_map/ppermute | solution.py:35
  49.3 3.3 %collective-permute-start.8 = (bf16[256,256]{1,0:T(8,128)(2,1)S(1)}, bf16[256,256]{1,0:T(8,128)(2,1)S(1)}, u32[]{:S(2)}, u32[]{:S(2)}) collective-permute-start(bf16[256,256]{1,0:T(8,128)(2,1)S(1)} %collective-permute-done.6.e2_ref), channel_id=1, source_target_pairs={{0,1},{1,0},{2,3},{3,2},{4,5},{5,4},{6,7},{7,6},{8,9},{9,8},{10,11... | collective-permute-start | bytes 393224 | tf_op jit(solution)/shard_map/ppermute | solution.py:35
  52.6 1.4 %collective-permute-start.5 = (bf16[256,256]{1,0:T(8,128)(2,1)S(1)}, bf16[256,256]{1,0:T(8,128)(2,1)S(1)}, u32[]{:S(2)}, u32[]{:S(2)}) collective-permute-start(bf16[256,256]{1,0:T(8,128)(2,1)S(1)} %collective-permute-done.3.e2_ref), channel_id=1, source_target_pairs={{0,1},{1,0},{2,3},{3,2},{4,5},{5,4},{6,7},{7,6},{8,9},{9,8},{10,11... | collective-permute-start | bytes 393224 | tf_op jit(solution)/shard_map/ppermute | solution.py:35
  54.0 1.6 %feed.4 = (f32[256,512]{1,0:T(8,128)S(1)}, bf16[256,512]{1,0:T(8,128)(2,1)S(1)}) custom-call(bf16[256,256]{1,0:T(8,128)(2,1)S(1)} %get-tuple-element.31.e0_ref, bf16[256,256]{1,0:T(8,128)(2,1)S(1)} %collective-permute-done.6.e2_ref, bf16[256,256]{1,0:T(8,128)(2,1)S(1)} %collective-permute-done.7.e1_ref, bf16[256,256]{1,0:T(8,128)(2,1)S(1)} %collective-permute-done.8.e3_ref, ...), custom_call_target="tpu_custom_call" | custom-call | flops 1073741824 | bytes 4194304 | tf_op jit(solution)/shard_map/feed/pallas_call | solution.py:262
  55.7 1.3 %collective-permute-start.10 = (bf16[256,256]{1,0:T(8,128)(2,1)S(1)}, bf16[256,256]{1,0:T(8,128)(2,1)S(1)}, u32[]{:S(2)}, u32[]{:S(2)}) collective-permute-start(bf16[256,256]{1,0:T(8,128)(2,1)S(1)} %get-tuple-element.35.e0_ref), channel_id=1, source_target_pairs={{0,2},{1,3},{2,0},{3,1},{4,6},{5,7},{6,4},{7,5},{8,10},{9,11},{10,... | collective-permute-start | bytes 393224 | tf_op jit(solution)/shard_map/ppermute | solution.py:35
  57.0 1.6 %feed.5 = (f32[256,512]{1,0:T(8,128)S(1)}, bf16[256,512]{1,0:T(8,128)(2,1)S(1)}) custom-call(bf16[256,256]{1,0:T(8,128)(2,1)S(1)} %get-tuple-element.30.e0_ref, bf16[256,256]{1,0:T(8,128)(2,1)S(1)} %collective-permute-done.3.e2_ref, bf16[256,256]{1,0:T(8,128)(2,1)S(1)} %collective-permute-done.4.e1_ref, bf16[256,256]{1,0:T(8,128)(2,1)S(1)} %collective-permute-done.5.e3_ref, ...), custom_call_target="tpu_custom_call" | custom-call | flops 1073741824 | bytes 4194304 | tf_op jit(solution)/shard_map/feed/pallas_call | solution.py:262
  61.7 2.8 %collective-permute-done.e2_ref = bf16[256,256]{1,0:T(8,128)(2,1)S(1)} collective-permute-done((bf16[256,256]{1,0:T(8,128)(2,1)S(1)}, bf16[256,256]{1,0:T(8,128)(2,1)S(1)}, u32[]{:S(2)}, u32[]{:S(2)}) %collective-permute-start) | collective-permute-done | bytes 131104 | tf_op jit(solution)/shard_map/ppermute | solution.py:35
  65.4 1.6 %feed.6 = (f32[256,512]{1,0:T(8,128)S(1)}, bf16[256,512]{1,0:T(8,128)(2,1)S(1)}) custom-call(bf16[256,256]{1,0:T(8,128)(2,1)S(1)} %get-tuple-element.35.e0_ref, bf16[256,256]{1,0:T(8,128)(2,1)S(1)} %collective-permute-done.10.e2_ref, bf16[256,256]{1,0:T(8,128)(2,1)S(1)} %collective-permute-done.11.e1_ref, ...), custom_call_target="tpu_custom_call" | custom-call | flops 1073741824 | bytes 4194304 | tf_op jit(solution)/shard_map/feed/pallas_call | solution.py:262
  67.7 1.6 %feed.7 = (f32[256,512]{1,0:T(8,128)S(1)}, bf16[256,512]{1,0:T(8,128)(2,1)S(1)}) custom-call(bf16[256,256]{1,0:T(8,128)(2,1)S(1)} %get-tuple-element.29.e0_ref, bf16[256,256]{1,0:T(8,128)(2,1)S(1)} %collective-permute-done.e2_ref, bf16[256,256]{1,0:T(8,128)(2,1)S(1)} %collective-permute-done.1.e1_ref, bf16[256,256]{1,0:T(8,128)(2,1)S(1)} %collective-permute-done.2.e3_ref, ...), custom_call_target="tpu_custom_call" | custom-call | flops 1073741824 | bytes 4194304 | tf_op jit(solution)/shard_map/feed/pallas_call | solution.py:262
  71.0 5.9 %collective-permute-done.19.far_ref = bf16[256,512]{1,0:T(8,128)(2,1)S(1)} collective-permute-done((bf16[256,512]{1,0:T(8,128)(2,1)S(1)}, bf16[256,512]{1,0:T(8,128)(2,1)S(1)}, u32[]{:S(2)}, u32[]{:S(2)}) %collective-permute-start.19) | collective-permute-done | bytes 262176 | tf_op jit(solution)/shard_map/ppermute | solution.py:35
  77.0 1.3 %collective-permute-start.20 = (bf16[256,512]{1,0:T(8,128)(2,1)S(1)}, bf16[256,512]{1,0:T(8,128)(2,1)S(1)}, u32[]{:S(2)}, u32[]{:S(2)}) collective-permute-start(bf16[256,512]{1,0:T(8,128)(2,1)S(1)} %finish.4.mine_ref._), channel_id=1, source_target_pairs={{0,1},{1,0},{2,3},{3,2},{4,5},{5,4},{6,7},{7,6},{8,9},{9,8},{10,11... | collective-permute-start | bytes 786440 | tf_op jit(solution)/shard_map/ppermute | solution.py:35
  78.5 1.5 %collective-permute-start.21 = (bf16[64,1024]{1,0:T(8,128)(2,1)S(1)}, bf16[64,1024]{1,0:T(8,128)(2,1)S(1)}, u32[]{:S(2)}, u32[]{:S(2)}) collective-permute-start(bf16[64,1024]{1,0:T(8,128)(2,1)S(1)} %get-tuple-element.51), channel_id=1, source_target_pairs={{4,0},{8,4},{12,8},{16,12},{20,16},{24,20},{28,24},{5,1},{9,5},{13... | collective-permute-start | bytes 393224 | tf_op jit(solution)/shard_map/ppermute | solution.py:41
  80.5 4.9 %collective-permute-done.21 = bf16[64,1024]{1,0:T(8,128)(2,1)S(1)} collective-permute-done((bf16[64,1024]{1,0:T(8,128)(2,1)S(1)}, bf16[64,1024]{1,0:T(8,128)(2,1)S(1)}, u32[]{:S(2)}, u32[]{:S(2)}) %collective-permute-start.21) | collective-permute-done | bytes 131104 | tf_op jit(solution)/shard_map/ppermute | solution.py:41
  85.5 1.7 %attend.3._.refs_2_ = bf16[64,1024]{1,0:T(8,128)(2,1)S(1)} custom-call(bf16[256,512]{1,0:T(8,128)(2,1)S(1)} %finish.4.mine_ref._, bf16[256,512]{1,0:T(8,128)(2,1)S(1)} %collective-permute-done.20.other_ref, bf16[1024,1024]{1,0:T(8,128)(2,1)S(1)} %copy-done, bf16[1024,1024]{1,0:T(8,128)(2,1)S(1)} %copy-done.1, bf16[64,1024]{1,0:T(8,128)(2,1)S(1)} %pad_maximum_fusion.q_ref, ...), custom_call_target="tpu_custom_call" | custom-call | flops 1073741824 | bytes 4194304 | tf_op jit(solution)/shard_map/attend/pallas_call | solution.py:296
  90.0 1.7 %attend.4._.refs_0_ = bf16[64,1024]{1,0:T(8,128)(2,1)S(1)} custom-call(bf16[256,512]{1,0:T(8,128)(2,1)S(1)} %finish.5.mine_ref._, bf16[256,512]{1,0:T(8,128)(2,1)S(1)} %collective-permute-done.22.other_ref, bf16[1024,1024]{1,0:T(8,128)(2,1)S(1)} %copy-done, bf16[1024,1024]{1,0:T(8,128)(2,1)S(1)} %copy-done.1, bf16[64,1024]{1,0:T(8,128)(2,1)S(1)} %get-tuple-element.50.q_ref, ...), custom_call_target="tpu_custom_call" | custom-call | flops 1073741824 | bytes 4194304 | tf_op jit(solution)/shard_map/attend/pallas_call | solution.py:296
  91.7 5.0 %collective-permute-done.17.far_ref = bf16[256,512]{1,0:T(8,128)(2,1)S(1)} collective-permute-done((bf16[256,512]{1,0:T(8,128)(2,1)S(1)}, bf16[256,512]{1,0:T(8,128)(2,1)S(1)}, u32[]{:S(2)}, u32[]{:S(2)}) %collective-permute-start.17) | collective-permute-done | bytes 262176 | tf_op jit(solution)/shard_map/ppermute | solution.py:35
  98.9 1.7 %attend.5._.refs_1_ = bf16[64,1024]{1,0:T(8,128)(2,1)S(1)} custom-call(bf16[256,512]{1,0:T(8,128)(2,1)S(1)} %finish.6.mine_ref._, bf16[256,512]{1,0:T(8,128)(2,1)S(1)} %collective-permute-done.23.other_ref, bf16[1024,1024]{1,0:T(8,128)(2,1)S(1)} %copy-done, bf16[1024,1024]{1,0:T(8,128)(2,1)S(1)} %copy-done.1, bf16[64,1024]{1,0:T(8,128)(2,1)S(1)} %get-tuple-element.52.q_ref, ...), custom_call_target="tpu_custom_call" | custom-call | flops 1073741824 | bytes 4194304 | tf_op jit(solution)/shard_map/attend/pallas_call | solution.py:296
  100.6 5.0 %collective-permute-done.16.far_ref = bf16[256,512]{1,0:T(8,128)(2,1)S(1)} collective-permute-done((bf16[256,512]{1,0:T(8,128)(2,1)S(1)}, bf16[256,512]{1,0:T(8,128)(2,1)S(1)}, u32[]{:S(2)}, u32[]{:S(2)}) %collective-permute-start.16) | collective-permute-done | bytes 262176 | tf_op jit(solution)/shard_map/ppermute | solution.py:35
  106.6 4.0 %collective-permute-start.25 = (bf16[64,1024]{1,0:T(8,128)(2,1)S(1)}, bf16[64,1024]{1,0:T(8,128)(2,1)S(1)}, u32[]{:S(2)}, u32[]{:S(2)}) collective-permute-start(bf16[64,1024]{1,0:T(8,128)(2,1)S(1)} %attend.3._.refs_2_), channel_id=1, source_target_pairs={{0,4},{4,8},{8,12},{12,16},{16,20},{20,24},{24,28},{1,5},{5,9},{9,... | collective-permute-start | bytes 393224 | tf_op jit(solution)/shard_map/ppermute | solution.py:41
  110.6 2.9 %collective-permute-done.25.behind_ref = bf16[64,1024]{1,0:T(8,128)(2,1)S(1)} collective-permute-done((bf16[64,1024]{1,0:T(8,128)(2,1)S(1)}, bf16[64,1024]{1,0:T(8,128)(2,1)S(1)}, u32[]{:S(2)}, u32[]{:S(2)}) %collective-permute-start.25) | collective-permute-done | bytes 131104 | tf_op jit(solution)/shard_map/ppermute | solution.py:41
  113.5 2.5 %attend_last.1 = bf16[256,1024]{1,0:T(8,128)(2,1)} custom-call(bf16[256,512]{1,0:T(8,128)(2,1)S(1)} %finish.7.mine_ref, bf16[256,512]{1,0:T(8,128)(2,1)S(1)} %collective-permute-done.24.other_ref, bf16[1024,1024]{1,0:T(8,128)(2,1)S(1)} %copy-done, bf16[1024,1024]{1,0:T(8,128)(2,1)S(1)} %copy-done.1, bf16[64,1024]{1,0:T(8,128)(2,1)S(1)} %get-tuple-element.49.q_ref, ...), custom_call_target="tpu_custom_call" | custom-call | flops 1073741824 | bytes 4194304 | tf_op jit(solution)/shard_map/attend_last/pallas_call | solution.py:293
  (67 shorter events, 18.7 us)
Async XLA Ops:
  45.2 4.1 %collective-permute-start.6 = (bf16[256,256]{1,0:T(8,128)(2,1)S(1)}, bf16[256,256]{1,0:T(8,128)(2,1)S(1)}, u32[]{:S(2)}, u32[]{:S(2)}) collective-permute-start(bf16[256,256]{1,0:T(8,128)(2,1)S(1)} %get-tuple-element.31.e0_ref), channel_id=1, source_target_pairs={{0,2},{1,3},{2,0},{3,1},{4,6},{5,7},{6,4},{7,5},{8,10},{9,11},{10,... | collective-permute-start | bytes 393224 | tf_op jit(solution)/shard_map/ppermute | solution.py:35
  46.5 6.1 %collective-permute-start.3 = (bf16[256,256]{1,0:T(8,128)(2,1)S(1)}, bf16[256,256]{1,0:T(8,128)(2,1)S(1)}, u32[]{:S(2)}, u32[]{:S(2)}) collective-permute-start(bf16[256,256]{1,0:T(8,128)(2,1)S(1)} %get-tuple-element.30.e0_ref), channel_id=1, source_target_pairs={{0,2},{1,3},{2,0},{3,1},{4,6},{5,7},{6,4},{7,5},{8,10},{9,11},{10,... | collective-permute-start | bytes 393224 | tf_op jit(solution)/shard_map/ppermute | solution.py:35
  46.7 7.3 %collective-permute-start.7 = (bf16[256,256]{1,0:T(8,128)(2,1)S(1)}, bf16[256,256]{1,0:T(8,128)(2,1)S(1)}, u32[]{:S(2)}, u32[]{:S(2)}) collective-permute-start(bf16[256,256]{1,0:T(8,128)(2,1)S(1)} %get-tuple-element.31.e0_ref), channel_id=1, source_target_pairs={{0,1},{1,0},{2,3},{3,2},{4,5},{5,4},{6,7},{7,6},{8,9},{9,8},{10,11... | collective-permute-start | bytes 393224 | tf_op jit(solution)/shard_map/ppermute | solution.py:35
  49.3 4.7 %collective-permute-start.8 = (bf16[256,256]{1,0:T(8,128)(2,1)S(1)}, bf16[256,256]{1,0:T(8,128)(2,1)S(1)}, u32[]{:S(2)}, u32[]{:S(2)}) collective-permute-start(bf16[256,256]{1,0:T(8,128)(2,1)S(1)} %collective-permute-done.6.e2_ref), channel_id=1, source_target_pairs={{0,1},{1,0},{2,3},{3,2},{4,5},{5,4},{6,7},{7,6},{8,9},{9,8},{10,11... | collective-permute-start | bytes 393224 | tf_op jit(solution)/shard_map/ppermute | solution.py:35
  52.6 4.4 %collective-permute-start.4 = (bf16[256,256]{1,0:T(8,128)(2,1)S(1)}, bf16[256,256]{1,0:T(8,128)(2,1)S(1)}, u32[]{:S(2)}, u32[]{:S(2)}) collective-permute-start(bf16[256,256]{1,0:T(8,128)(2,1)S(1)} %get-tuple-element.30.e0_ref), channel_id=1, source_target_pairs={{0,1},{1,0},{2,3},{3,2},{4,5},{5,4},{6,7},{7,6},{8,9},{9,8},{10,11... | collective-permute-start | bytes 393224 | tf_op jit(solution)/shard_map/ppermute | solution.py:35
  52.6 4.4 %collective-permute-start.5 = (bf16[256,256]{1,0:T(8,128)(2,1)S(1)}, bf16[256,256]{1,0:T(8,128)(2,1)S(1)}, u32[]{:S(2)}, u32[]{:S(2)}) collective-permute-start(bf16[256,256]{1,0:T(8,128)(2,1)S(1)} %collective-permute-done.3.e2_ref), channel_id=1, source_target_pairs={{0,1},{1,0},{2,3},{3,2},{4,5},{5,4},{6,7},{7,6},{8,9},{9,8},{10,11... | collective-permute-start | bytes 393224 | tf_op jit(solution)/shard_map/ppermute | solution.py:35
  55.6 9.7 %collective-permute-start.13 = (bf16[256,512]{1,0:T(8,128)(2,1)S(1)}, bf16[256,512]{1,0:T(8,128)(2,1)S(1)}, u32[]{:S(2)}, u32[]{:S(2)}) collective-permute-start(bf16[256,512]{1,0:T(8,128)(2,1)S(1)} %get-tuple-element.32._), channel_id=1, source_target_pairs={{0,1},{1,0},{2,3},{3,2},{4,5},{5,4},{6,7},{7,6},{8,9},{9,8},{10,11... | collective-permute-start | bytes 786440 | tf_op jit(solution)/shard_map/ppermute | solution.py:35
  55.7 4.7 %collective-permute-start.10 = (bf16[256,256]{1,0:T(8,128)(2,1)S(1)}, bf16[256,256]{1,0:T(8,128)(2,1)S(1)}, u32[]{:S(2)}, u32[]{:S(2)}) collective-permute-start(bf16[256,256]{1,0:T(8,128)(2,1)S(1)} %get-tuple-element.35.e0_ref), channel_id=1, source_target_pairs={{0,2},{1,3},{2,0},{3,1},{4,6},{5,7},{6,4},{7,5},{8,10},{9,11},{10,... | collective-permute-start | bytes 393224 | tf_op jit(solution)/shard_map/ppermute | solution.py:35
  58.6 9.0 %collective-permute-start.9 = (bf16[256,512]{1,0:T(8,128)(2,1)S(1)}, bf16[256,512]{1,0:T(8,128)(2,1)S(1)}, u32[]{:S(2)}, u32[]{:S(2)}) collective-permute-start(bf16[256,512]{1,0:T(8,128)(2,1)S(1)} %get-tuple-element.34._), channel_id=1, source_target_pairs={{0,1},{1,0},{2,3},{3,2},{4,5},{5,4},{6,7},{7,6},{8,9},{9,8},{10,11... | collective-permute-start | bytes 786440 | tf_op jit(solution)/shard_map/ppermute | solution.py:35
  59.4 5.1 %collective-permute-start = (bf16[256,256]{1,0:T(8,128)(2,1)S(1)}, bf16[256,256]{1,0:T(8,128)(2,1)S(1)}, u32[]{:S(2)}, u32[]{:S(2)}) collective-permute-start(bf16[256,256]{1,0:T(8,128)(2,1)S(1)} %get-tuple-element.29.e0_ref), channel_id=1, source_target_pairs={{0,2},{1,3},{2,0},{3,1},{4,6},{5,7},{6,4},{7,5},{8,10},{9,11},{10,... | collective-permute-start | bytes 393224 | tf_op jit(solution)/shard_map/ppermute | solution.py:35
  59.6 5.8 %collective-permute-start.11 = (bf16[256,256]{1,0:T(8,128)(2,1)S(1)}, bf16[256,256]{1,0:T(8,128)(2,1)S(1)}, u32[]{:S(2)}, u32[]{:S(2)}) collective-permute-start(bf16[256,256]{1,0:T(8,128)(2,1)S(1)} %get-tuple-element.35.e0_ref), channel_id=1, source_target_pairs={{0,1},{1,0},{2,3},{3,2},{4,5},{5,4},{6,7},{7,6},{8,9},{9,8},{10,11... | collective-permute-start | bytes 393224 | tf_op jit(solution)/shard_map/ppermute | solution.py:35
  60.4 5.0 %collective-permute-start.12 = (bf16[256,256]{1,0:T(8,128)(2,1)S(1)}, bf16[256,256]{1,0:T(8,128)(2,1)S(1)}, u32[]{:S(2)}, u32[]{:S(2)}) collective-permute-start(bf16[256,256]{1,0:T(8,128)(2,1)S(1)} %collective-permute-done.10.e2_ref), channel_id=1, source_target_pairs={{0,1},{1,0},{2,3},{3,2},{4,5},{5,4},{6,7},{7,6},{8,9},{9,8},{10,11... | collective-permute-start | bytes 393224 | tf_op jit(solution)/shard_map/ppermute | solution.py:35
  64.5 3.2 %collective-permute-start.1 = (bf16[256,256]{1,0:T(8,128)(2,1)S(1)}, bf16[256,256]{1,0:T(8,128)(2,1)S(1)}, u32[]{:S(2)}, u32[]{:S(2)}) collective-permute-start(bf16[256,256]{1,0:T(8,128)(2,1)S(1)} %get-tuple-element.29.e0_ref), channel_id=1, source_target_pairs={{0,1},{1,0},{2,3},{3,2},{4,5},{5,4},{6,7},{7,6},{8,9},{9,8},{10,11... | collective-permute-start | bytes 393224 | tf_op jit(solution)/shard_map/ppermute | solution.py:35
  65.3 2.4 %collective-permute-start.2 = (bf16[256,256]{1,0:T(8,128)(2,1)S(1)}, bf16[256,256]{1,0:T(8,128)(2,1)S(1)}, u32[]{:S(2)}, u32[]{:S(2)}) collective-permute-start(bf16[256,256]{1,0:T(8,128)(2,1)S(1)} %collective-permute-done.e2_ref), channel_id=1, source_target_pairs={{0,1},{1,0},{2,3},{3,2},{4,5},{5,4},{6,7},{7,6},{8,9},{9,8},{10,11... | collective-permute-start | bytes 393224 | tf_op jit(solution)/shard_map/ppermute | solution.py:35
  67.0 2.9 %collective-permute-start.15 = (bf16[256,512]{1,0:T(8,128)(2,1)S(1)}, bf16[256,512]{1,0:T(8,128)(2,1)S(1)}, u32[]{:S(2)}, u32[]{:S(2)}) collective-permute-start(bf16[256,512]{1,0:T(8,128)(2,1)S(1)} %get-tuple-element.38._), channel_id=1, source_target_pairs={{0,1},{1,0},{2,3},{3,2},{4,5},{5,4},{6,7},{7,6},{8,9},{9,8},{10,11... | collective-permute-start | bytes 786440 | tf_op jit(solution)/shard_map/ppermute | solution.py:35
  69.4 7.5 %collective-permute-start.19 = (bf16[256,512]{1,0:T(8,128)(2,1)S(1)}, bf16[256,512]{1,0:T(8,128)(2,1)S(1)}, u32[]{:S(2)}, u32[]{:S(2)}) collective-permute-start(bf16[256,512]{1,0:T(8,128)(2,1)S(1)} %get-tuple-element.37._), channel_id=1, source_target_pairs={{0,2},{1,3},{2,0},{3,1},{4,6},{5,7},{6,4},{7,5},{8,10},{9,11},{10,... | collective-permute-start | bytes 786440 | tf_op jit(solution)/shard_map/ppermute | solution.py:35
  77.0 8.5 %collective-permute-start.20 = (bf16[256,512]{1,0:T(8,128)(2,1)S(1)}, bf16[256,512]{1,0:T(8,128)(2,1)S(1)}, u32[]{:S(2)}, u32[]{:S(2)}) collective-permute-start(bf16[256,512]{1,0:T(8,128)(2,1)S(1)} %finish.4.mine_ref._), channel_id=1, source_target_pairs={{0,1},{1,0},{2,3},{3,2},{4,5},{5,4},{6,7},{7,6},{8,9},{9,8},{10,11... | collective-permute-start | bytes 786440 | tf_op jit(solution)/shard_map/ppermute | solution.py:35
  78.5 7.0 %collective-permute-start.21 = (bf16[64,1024]{1,0:T(8,128)(2,1)S(1)}, bf16[64,1024]{1,0:T(8,128)(2,1)S(1)}, u32[]{:S(2)}, u32[]{:S(2)}) collective-permute-start(bf16[64,1024]{1,0:T(8,128)(2,1)S(1)} %get-tuple-element.51), channel_id=1, source_target_pairs={{4,0},{8,4},{12,8},{16,12},{20,16},{24,20},{28,24},{5,1},{9,5},{13... | collective-permute-start | bytes 393224 | tf_op jit(solution)/shard_map/ppermute | solution.py:41
  79.9 8.0 %collective-permute-start.18 = (bf16[256,512]{1,0:T(8,128)(2,1)S(1)}, bf16[256,512]{1,0:T(8,128)(2,1)S(1)}, u32[]{:S(2)}, u32[]{:S(2)}) collective-permute-start(bf16[256,512]{1,0:T(8,128)(2,1)S(1)} %get-tuple-element.39._), channel_id=1, source_target_pairs={{0,2},{1,3},{2,0},{3,1},{4,6},{5,7},{6,4},{7,5},{8,10},{9,11},{10,... | collective-permute-start | bytes 786440 | tf_op jit(solution)/shard_map/ppermute | solution.py:35
  88.9 7.9 %collective-permute-start.17 = (bf16[256,512]{1,0:T(8,128)(2,1)S(1)}, bf16[256,512]{1,0:T(8,128)(2,1)S(1)}, u32[]{:S(2)}, u32[]{:S(2)}) collective-permute-start(bf16[256,512]{1,0:T(8,128)(2,1)S(1)} %get-tuple-element.43._), channel_id=1, source_target_pairs={{0,2},{1,3},{2,0},{3,1},{4,6},{5,7},{6,4},{7,5},{8,10},{9,11},{10,... | collective-permute-start | bytes 786440 | tf_op jit(solution)/shard_map/ppermute | solution.py:35
  96.8 2.1 %collective-permute-start.23 = (bf16[256,512]{1,0:T(8,128)(2,1)S(1)}, bf16[256,512]{1,0:T(8,128)(2,1)S(1)}, u32[]{:S(2)}, u32[]{:S(2)}) collective-permute-start(bf16[256,512]{1,0:T(8,128)(2,1)S(1)} %finish.6.mine_ref._), channel_id=1, source_target_pairs={{0,1},{1,0},{2,3},{3,2},{4,5},{5,4},{6,7},{7,6},{8,9},{9,8},{10,11... | collective-permute-start | bytes 786440 | tf_op jit(solution)/shard_map/ppermute | solution.py:35
  97.8 7.9 %collective-permute-start.16 = (bf16[256,512]{1,0:T(8,128)(2,1)S(1)}, bf16[256,512]{1,0:T(8,128)(2,1)S(1)}, u32[]{:S(2)}, u32[]{:S(2)}) collective-permute-start(bf16[256,512]{1,0:T(8,128)(2,1)S(1)} %get-tuple-element.45._), channel_id=1, source_target_pairs={{0,2},{1,3},{2,0},{3,1},{4,6},{5,7},{6,4},{7,5},{8,10},{9,11},{10,... | collective-permute-start | bytes 786440 | tf_op jit(solution)/shard_map/ppermute | solution.py:35
  105.7 7.8 %collective-permute-start.24 = (bf16[256,512]{1,0:T(8,128)(2,1)S(1)}, bf16[256,512]{1,0:T(8,128)(2,1)S(1)}, u32[]{:S(2)}, u32[]{:S(2)}) collective-permute-start(bf16[256,512]{1,0:T(8,128)(2,1)S(1)} %finish.7.mine_ref), channel_id=1, source_target_pairs={{0,1},{1,0},{2,3},{3,2},{4,5},{5,4},{6,7},{7,6},{8,9},{9,8},{10,11... | collective-permute-start | bytes 786440 | tf_op jit(solution)/shard_map/ppermute | solution.py:35
  106.6 6.9 %collective-permute-start.25 = (bf16[64,1024]{1,0:T(8,128)(2,1)S(1)}, bf16[64,1024]{1,0:T(8,128)(2,1)S(1)}, u32[]{:S(2)}, u32[]{:S(2)}) collective-permute-start(bf16[64,1024]{1,0:T(8,128)(2,1)S(1)} %attend.3._.refs_2_), channel_id=1, source_target_pairs={{0,4},{4,8},{8,12},{12,16},{16,20},{20,24},{24,28},{1,5},{5,9},{9,... | collective-permute-start | bytes 393224 | tf_op jit(solution)/shard_map/ppermute | solution.py:41
  (9 other events, 91.1 us)

commit v2 on v1

--- a/solution.py
+++ b/solution.py
@@ -15,19 +15,21 @@
 BF16 = jnp.bfloat16
 
 
-def call(body, outs, flops, nbytes, name, unused=None):
-    specs = {}
-    if unused is not None:
-        vmem = pl.BlockSpec(memory_space=pltpu.VMEM)
-        specs = dict(in_specs=[vmem] * (unused - 1) + [pl.BlockSpec(memory_space=pl.ANY)])
+def call(body, outs, name, used=None, after=()):
+    vmem = pl.BlockSpec(memory_space=pltpu.VMEM)
+    unread = pl.BlockSpec(memory_space=pl.ANY)
+
+    def without_after(*refs):
+        body(*refs[: len(used)], *refs[len(used) + len(after) :])
+
     return pl.pallas_call(
-        body,
+        without_after,
         out_shape=outs,
-        **specs,
+        in_specs=[vmem] * len(used) + [unread] * len(after),
         compiler_params=pltpu.CompilerParams(vmem_limit_bytes=VMEM_LIMIT),
-        cost_estimate=pl.CostEstimate(flops=flops, bytes_accessed=nbytes, transcendentals=0),
+        cost_estimate=pl.CostEstimate(flops=1024, bytes_accessed=1024, transcendentals=0),
         name=name,
-    )
+    )(*used, *after)
 
 
 def exchange(x, bit):
@@ -98,12 +100,15 @@
         ).astype(BF16)
 
 
-def order_body(slot_ref, rows_ref, *out_refs):
+def order_body(plan, slot_ref, rows_ref, *out_refs):
     rows = rows_ref[...]
-    for at, out_ref in enumerate(out_refs):
-        count = out_ref.shape[0]
-        picked = one_hot(slot_ref[at * count : (at + 1) * count, :], rows.shape[0])
-        out_ref[...] = jnp.dot(picked, rows, preferred_element_type=F32).astype(BF16)
+    for groups, out_ref in zip(plan, out_refs):
+        count = out_ref.shape[0] // len(groups)
+        for at, g in enumerate(groups):
+            picked = one_hot(slot_ref[g * count : (g + 1) * count, :], rows.shape[0])
+            out_ref[at * count : (at + 1) * count, :] = jnp.dot(
+                picked, rows, preferred_element_type=F32
+            ).astype(BF16)
 
 
 def block_rows(ref, index, width):
@@ -114,11 +119,12 @@
     return ref[:, pl.ds(pl.multiple_of(index * width, width), width)]
 
 
-def feed_body(e0_ref, e2_ref, e1_ref, e3_ref, w_in_ref, w_out_ref, _, keep_ref, send_ref):
+def feed_body(first, e0_ref, e2_ref, e1_ref, e3_ref, w_in_ref, w_out_ref, keep_ref, send_ref):
     me = lax.axis_index("tp")
     width = e0_ref.shape[1]
     index = [me, me ^ 2, me ^ 1, me ^ 3]
-    parts = [ref[...].astype(F32) for ref in (e0_ref, e2_ref, e1_ref, e3_ref)]
+    here = slice(first, first + keep_ref.shape[0])
+    parts = [ref[here, :].astype(F32) for ref in (e0_ref, e2_ref, e1_ref, e3_ref)]
     square = sum(jnp.sum(part * part, axis=1, keepdims=True) for part in parts)
     scale = lax.rsqrt(square / (4 * width) + 1e-06)
     hidden = sum(
@@ -138,20 +144,21 @@
         ).astype(BF16)
 
 
-def add_body(keep_ref, recv_ref, _, chip_ref, send_ref):
+def add_body(keep_ref, recv_ref, chip_ref, send_ref):
     chip = keep_ref[...] + recv_ref[...].astype(F32)
     chip_ref[...] = chip
     send_ref[...] = chip.astype(BF16)
 
 
-def finish_body(e0_ref, e2_ref, chip_ref, far_ref, _, mine_ref):
+def finish_body(first, e0_ref, e2_ref, chip_ref, far_ref, mine_ref):
     width = e0_ref.shape[1]
     near, past = slice(0, width), slice(width, 2 * width)
+    here = slice(first, first + mine_ref.shape[0])
     mine_ref[:, near] = (
-        e0_ref[...].astype(F32) + (chip_ref[:, near] + far_ref[:, past].astype(F32))
+        e0_ref[here, :].astype(F32) + (chip_ref[:, near] + far_ref[:, past].astype(F32))
     ).astype(BF16)
     mine_ref[:, past] = (
-        e2_ref[...].astype(F32) + (chip_ref[:, past] + far_ref[:, near].astype(F32))
+        e2_ref[here, :].astype(F32) + (chip_ref[:, past] + far_ref[:, near].astype(F32))
     ).astype(BF16)
 
 
@@ -187,7 +194,7 @@
     ]
 
 
-def attend_body(mine_ref, other_ref, w_key_ref, w_value_ref, q_ref, _, out_ref):
+def attend_body(mine_ref, other_ref, w_key_ref, w_value_ref, q_ref, out_ref):
     for at, part in enumerate(attended(mine_ref, other_ref, w_key_ref, w_value_ref, q_ref)):
         out_ref[:, at * HEAD_WIDTH : (at + 1) * HEAD_WIDTH] = part.astype(BF16)
 
@@ -224,92 +231,93 @@
     wanted, slot = call(
         functools.partial(route_body, voc, cap),
         (sds((seq_size, cap), jnp.int32), sds((rows, LANES), jnp.int32)),
-        2 * rows * cap * 16,
-        rows * 600,
         "route",
-    )(neighbour_ids.reshape(1, rows))
+        (neighbour_ids.reshape(1, rows),),
+    )
     request = lax.all_to_all(wanted, "seq", split_axis=0, concat_axis=0, tiled=True)
     found = call(
-        fetch_body, sds((slots, width), BF16), 2 * slots * voc * width, 3 * slots * width * 2, "fetch"
-    )(request.reshape(1, slots), vocab_rows)
+        fetch_body,
+        sds((slots, width), BF16),
+        "fetch",
+        (request.reshape(1, slots), vocab_rows),
+        (next_q,),
+    )
     answered = lax.all_to_all(
         found.reshape(seq_size, cap, width), "seq", split_axis=0, concat_axis=0, tiled=True
     ).reshape(slots, width)
+    order = [groups - 1] + list(range(groups - 1))
+    plan = [order[at : at + 2] for at in range(0, groups, 2)]
     own = call(
-        order_body,
-        tuple(sds((per_group, width), BF16) for _ in range(groups)),
-        2 * slots * rows * width,
-        3 * slots * width * 2,
+        functools.partial(order_body, plan),
+        tuple(sds((len(part) * per_group, width), BF16) for part in plan),
         "order",
-    )(slot, answered)
+        (slot, answered),
+    )
 
     local_q = jnp.concatenate([queries[GROUP - 1 :], next_q[: GROUP - 1]], axis=0)
-    order = [groups - 1] + list(range(groups - 1))
     half = sds((per_group, 2 * width), BF16)
     whole = sds((per_group, 2 * width), F32)
-    window = {}
-    emb, fed, summed, far = {}, {}, {}, {}
+    emb, first, window = {}, {}, {}
+    fed, summed, far, encoded = {}, {}, {}, {}
     behind = None
     token = slot
 
-    def embed(g):
-        e0 = own[g]
+    for part, e0 in zip(plan, own):
         e2 = exchange(e0, 2)
-        emb[g] = (e0, e2, exchange(e0, 1), exchange(e2, 1))
+        pieces = e0, e2, exchange(e0, 1), exchange(e2, 1)
+        for at, g in enumerate(part):
+            emb[g], first[g] = pieces, at * per_group
 
     def feed(g):
         nonlocal token
-        keep, send = call(
-            feed_body,
+        keep, token = call(
+            functools.partial(feed_body, first[g]),
             (whole, half),
-            16 * per_group * width * w_in.shape[1],
-            4 * w_in.shape[0] * w_in.shape[1],
             "feed",
-            unused=7,
-        )(*emb[g], w_in, w_out, token)
-        fed[g] = keep, exchange(send, 1)
-        token = send
+            (*emb[g], w_in, w_out),
+            (token,),
+        )
+        fed[g] = keep, exchange(token, 1)
 
     def add(g):
         nonlocal token
-        chip, send = call(
-            add_body, (whole, half), per_group * width, per_group * width * 16, "add", unused=3
-        )(*fed[g], token)
-        summed[g] = chip
-        far[g] = exchange(send, 2)
-        token = send
+        summed[g], token = call(add_body, (whole, half), "add", fed[g], (token,))
+        far[g] = exchange(token, 2)
 
     def finish(g):
+        nonlocal token
+        token = call(
+            functools.partial(finish_body, first[g]),
+            half,
+            "finish",
+            (*emb[g][:2], summed[g], far[g]),
+            (token, behind) if g == order[-1] else (token,),
+        )
+        encoded[g] = token, exchange(token, 1)
+
+    def attend(g):
         nonlocal token, behind
-        mine = call(
-            finish_body, half, per_group * width, per_group * width * 16, "finish", unused=5
-        )(*emb[g][:2], summed[g], far[g], token)
-        other = exchange(mine, 1)
-        token = mine
-        args = (mine, other, w_key, w_value, local_q[g * GROUP : (g + 1) * GROUP])
-        cost = 16 * per_group * width * head_cols, 4 * w_key.shape[0] * w_key.shape[1]
+        args = (*encoded[g], w_key, w_value, local_q[g * GROUP : (g + 1) * GROUP])
         if g == order[-1]:
-            before = [window[at] for at in range(groups - 2)]
-            return call(attend_last_body, sds((tok, head_cols), BF16), *cost, "attend_last")(
-                *args, behind, *before, window[groups - 1]
+            before = [window[at] for at in order[1:-1]]
+            return call(
+                attend_last_body,
+                sds((tok, head_cols), BF16),
+                "attend_last",
+                (*args, behind, *before, window[groups - 1]),
             )
-        window[g] = call(
-            attend_body, sds((GROUP, head_cols), BF16), *cost, "attend", unused=6
-        )(*args, token)
-        token = window[g]
+        window[g] = token = call(
+            attend_body, sds((GROUP, head_cols), BF16), "attend", args, (token,)
+        )
         if g == groups - 1:
-            behind = shifted(window[g], 1)
-
-    for at, g in enumerate(order):
-        embed(g)
-    for at, g in enumerate(order):
-        feed(g)
-        if at >= 1:
-            add(order[at - 1])
-    add(order[-1])
+            behind = shifted(token, 1)
+        return None
+
     out = None
-    for g in order:
-        out = finish(g)
+    for stage in range(groups + 4):
+        for step, lag in ((finish, 3), (attend, 4), (feed, 0), (add, 1)):
+            if 0 <= stage - lag < groups:
+                out = step(order[stage - lag])
     return out
 
 

time: 118 us -> 98.8 us (0.84); the launches traced: 116 us -> 98.5 us
  waiting for transfers between devices: 30.2 us -> 11.6 us
    ppermute x24 -> x18, waiting for transfers between devices: 22.3 us -> 11.6 us  [exchange(): return lax.ppermute(x, 'tp', [(i, i ^ bit) for i in range(size)])]
    ppermute x2, waiting for transfers between devices: 7.82 us -> 0.03 us  [shifted(): return lax.ppermute(x, 'seq', pairs)]
    ppermute x24 -> x18, starting transfers between devices: 20.1 us -> 20.1 us  [exchange(): return lax.ppermute(x, 'tp', [(i, i ^ bit) for i in range(size)])]
  transfers between devices with their start and end apart: 26 -> 20, of which waited for: 11 -> 4; matrix products, arithmetic and copies ran while one was open for 0% -> 0% of each run, Pallas kernels for 10% -> 13%
where the time goes in v2:
time: 98.8 us; the launch traced here: 98.5 us
  blocking collectives  39.6 us (40%)
  starting transfers between devices  24.6 us (25%)
  Pallas kernels  19.1 us (19%)
  waiting for transfers between devices  11.6 us (12%)
  local copies, waits for them, and re-layouts  3.26 us (3%)
    all_to_all x1, blocking collectives, per_device(): lax.all_to_all(found.reshape(seq_size, cap, width), 'seq', split_axis=0,...  27.2 us
    ppermute x18, starting transfers between devices, exchange(): return lax.ppermute(x, 'tp', [(i, i ^ bit) for i in range(size)])  20.1 us
    pallas_call x19, Pallas kernels, call(): pl.pallas_call(without_after, out_shape=outs, in_specs=[vmem] * len(used)...  19.1 us
    all_to_all x1, blocking collectives, per_device(): lax.all_to_all(wanted, 'seq', split_axis=0, concat_axis=0, tiled=True)  12.4 us
    ppermute x18, waiting for transfers between devices, exchange(): return lax.ppermute(x, 'tp', [(i, i ^ bit) for i in range(size)])  11.6 us
    ppermute x2, starting transfers between devices, shifted(): return lax.ppermute(x, 'seq', pairs)  4.49 us
  transfers between devices with their start and end apart: 20, of which 4 were waited for; matrix products, arithmetic and copies ran while one was open for 0% of the time, Pallas kernels for 13%

profile of v2, /device:TPU:1, one launch (start us, length us, event | category | flops | bytes accessed | tf_op | source)
XLA Modules:
  0.0 98.5 jit_solution(4565502531624905966)
XLA Ops:
  4.1 12.4 %all_to_all.14 = s32[8,1,256]{2,1,0:T(1,128)S(1)} all-to-all(s32[8,1,256]{2,1,0:T(1,128)S(1)} %copy.8), channel_id=1, replica_groups=mesh['seq'=8,'tp'=4] {'seq'}, dimensions={0} | all-to-all | bytes 16384 | tf_op jit(solution)/shard_map/all_to_all | solution.py:237
  17.7 2.4 %fetch.1 = bf16[2048,256]{1,0:T(8,128)(2,1)S(1)} custom-call(s32[1,2048]{1,0:T(1,128)S(1)} %bitcast.9, bf16[2048,256]{1,0:T(8,128)(2,1)S(1)} %copy-done.4, bf16[64,1024]{1,0:T(8,128)(2,1)S(1)} %collective-permute-done.refs_2_), custom_call_target="tpu_custom_call" | custom-call | flops 1024 | bytes 1024 | tf_op jit(solution)/shard_map/fetch/pallas_call | solution.py:25
  20.1 27.2 %all_to_all.15 = bf16[8,256,256]{2,1,0:T(8,128)(2,1)S(1)} all-to-all(bf16[8,256,256]{2,1,0:T(8,128)(2,1)S(1)} %bitcast.7), channel_id=1, replica_groups=mesh['seq'=8,'tp'=4] {'seq'}, dimensions={0} | all-to-all | bytes 2097152 | tf_op jit(solution)/shard_map/all_to_all | solution.py:245
  48.6 1.3 %collective-permute-start.4 = (bf16[512,256]{1,0:T(8,128)(2,1)S(1)}, bf16[512,256]{1,0:T(8,128)(2,1)S(1)}, u32[]{:S(2)}, u32[]{:S(2)}) collective-permute-start(bf16[512,256]{1,0:T(8,128)(2,1)S(1)} %get-tuple-element.28.refs_0_), channel_id=1, source_target_pairs={{0,2},{1,3},{2,0},{3,1},{4,6},{5,7},{6,4},{7,5},{8,10},{9,11},{10,... | collective-permute-start | bytes 786440 | tf_op jit(solution)/shard_map/ppermute | solution.py:37
  49.9 2.3 %collective-permute-start.5 = (bf16[512,256]{1,0:T(8,128)(2,1)S(1)}, bf16[512,256]{1,0:T(8,128)(2,1)S(1)}, u32[]{:S(2)}, u32[]{:S(2)}) collective-permute-start(bf16[512,256]{1,0:T(8,128)(2,1)S(1)} %get-tuple-element.28.refs_0_), channel_id=1, source_target_pairs={{0,1},{1,0},{2,3},{3,2},{4,5},{5,4},{6,7},{7,6},{8,9},{9,8},{10,11... | collective-permute-start | bytes 786440 | tf_op jit(solution)/shard_map/ppermute | solution.py:37
  52.2 2.2 %collective-permute-done.4.refs_1_ = bf16[512,256]{1,0:T(8,128)(2,1)S(1)} collective-permute-done((bf16[512,256]{1,0:T(8,128)(2,1)S(1)}, bf16[512,256]{1,0:T(8,128)(2,1)S(1)}, u32[]{:S(2)}, u32[]{:S(2)}) %collective-permute-start.4) | collective-permute-done | bytes 262176 | tf_op jit(solution)/shard_map/ppermute | solution.py:37
  54.4 2.9 %collective-permute-start.6 = (bf16[512,256]{1,0:T(8,128)(2,1)S(1)}, bf16[512,256]{1,0:T(8,128)(2,1)S(1)}, u32[]{:S(2)}, u32[]{:S(2)}) collective-permute-start(bf16[512,256]{1,0:T(8,128)(2,1)S(1)} %collective-permute-done.4.refs_1_), channel_id=1, source_target_pairs={{0,1},{1,0},{2,3},{3,2},{4,5},{5,4},{6,7},{7,6},{8,9},{9,8},{10,11... | collective-permute-start | bytes 786440 | tf_op jit(solution)/shard_map/ppermute | solution.py:37
  58.6 1.6 %feed.4 = (f32[256,512]{1,0:T(8,128)S(1)}, bf16[256,512]{1,0:T(8,128)(2,1)S(1)}) custom-call(bf16[512,256]{1,0:T(8,128)(2,1)S(1)} %get-tuple-element.28.refs_0_, bf16[512,256]{1,0:T(8,128)(2,1)S(1)} %collective-permute-done.4.refs_1_, bf16[512,256]{1,0:T(8,128)(2,1)S(1)} %collective-permute-done.5.refs_2_, ...), custom_call_target="tpu_custom_call" | custom-call | flops 1024 | bytes 1024 | tf_op jit(solution)/shard_map/feed/pallas_call | solution.py:25
  60.8 4.5 %collective-permute-done.1.refs_1_ = bf16[512,256]{1,0:T(8,128)(2,1)S(1)} collective-permute-done((bf16[512,256]{1,0:T(8,128)(2,1)S(1)}, bf16[512,256]{1,0:T(8,128)(2,1)S(1)}, u32[]{:S(2)}, u32[]{:S(2)}) %collective-permute-start.1) | collective-permute-done | bytes 262176 | tf_op jit(solution)/shard_map/ppermute | solution.py:37
  66.1 1.6 %feed.5 = (f32[256,512]{1,0:T(8,128)S(1)}, bf16[256,512]{1,0:T(8,128)(2,1)S(1)}) custom-call(bf16[512,256]{1,0:T(8,128)(2,1)S(1)} %get-tuple-element.28.refs_0_, bf16[512,256]{1,0:T(8,128)(2,1)S(1)} %collective-permute-done.4.refs_1_, bf16[512,256]{1,0:T(8,128)(2,1)S(1)} %collective-permute-done.5.refs_2_, ...), custom_call_target="tpu_custom_call" | custom-call | flops 1024 | bytes 1024 | tf_op jit(solution)/shard_map/feed/pallas_call | solution.py:25
  67.9 1.3 %collective-permute-start.8 = (bf16[256,512]{1,0:T(8,128)(2,1)S(1)}, bf16[256,512]{1,0:T(8,128)(2,1)S(1)}, u32[]{:S(2)}, u32[]{:S(2)}) collective-permute-start(bf16[256,512]{1,0:T(8,128)(2,1)S(1)} %get-tuple-element.33.refs_6_), channel_id=1, source_target_pairs={{0,2},{1,3},{2,0},{3,1},{4,6},{5,7},{6,4},{7,5},{8,10},{9,11},{10,... | collective-permute-start | bytes 786440 | tf_op jit(solution)/shard_map/ppermute | solution.py:37
  69.2 1.6 %feed.6 = (f32[256,512]{1,0:T(8,128)S(1)}, bf16[256,512]{1,0:T(8,128)(2,1)S(1)}) custom-call(bf16[512,256]{1,0:T(8,128)(2,1)S(1)} %get-tuple-element.27.refs_0_, bf16[512,256]{1,0:T(8,128)(2,1)S(1)} %collective-permute-done.1.refs_1_, bf16[512,256]{1,0:T(8,128)(2,1)S(1)} %collective-permute-done.2.refs_2_, ...), custom_call_target="tpu_custom_call" | custom-call | flops 1024 | bytes 1024 | tf_op jit(solution)/shard_map/feed/pallas_call | solution.py:25
  72.0 3.3 %collective-permute-done.8.refs_3_ = bf16[256,512]{1,0:T(8,128)(2,1)S(1)} collective-permute-done((bf16[256,512]{1,0:T(8,128)(2,1)S(1)}, bf16[256,512]{1,0:T(8,128)(2,1)S(1)}, u32[]{:S(2)}, u32[]{:S(2)}) %collective-permute-start.8) | collective-permute-done | bytes 262176 | tf_op jit(solution)/shard_map/ppermute | solution.py:37
  75.4 2.3 %collective-permute-start.11 = (bf16[256,512]{1,0:T(8,128)(2,1)S(1)}, bf16[256,512]{1,0:T(8,128)(2,1)S(1)}, u32[]{:S(2)}, u32[]{:S(2)}) collective-permute-start(bf16[256,512]{1,0:T(8,128)(2,1)S(1)} %finish.4.refs_6_.refs_0_), channel_id=1, source_target_pairs={{0,1},{1,0},{2,3},{3,2},{4,5},{5,4},{6,7},{7,6},{8,9},{9,8},{10,11... | collective-permute-start | bytes 786440 | tf_op jit(solution)/shard_map/ppermute | solution.py:37
  77.8 1.6 %feed.7 = (f32[256,512]{1,0:T(8,128)S(1)}, bf16[256,512]{1,0:T(8,128)(2,1)S(1)}) custom-call(bf16[512,256]{1,0:T(8,128)(2,1)S(1)} %get-tuple-element.27.refs_0_, bf16[512,256]{1,0:T(8,128)(2,1)S(1)} %collective-permute-done.1.refs_1_, bf16[512,256]{1,0:T(8,128)(2,1)S(1)} %collective-permute-done.2.refs_2_, ...), custom_call_target="tpu_custom_call" | custom-call | flops 1024 | bytes 1024 | tf_op jit(solution)/shard_map/feed/pallas_call | solution.py:25
  79.7 1.3 %collective-permute-start.16 = (bf16[256,512]{1,0:T(8,128)(2,1)S(1)}, bf16[256,512]{1,0:T(8,128)(2,1)S(1)}, u32[]{:S(2)}, u32[]{:S(2)}) collective-permute-start(bf16[256,512]{1,0:T(8,128)(2,1)S(1)} %get-tuple-element.41.refs_4_), channel_id=1, source_target_pairs={{0,2},{1,3},{2,0},{3,1},{4,6},{5,7},{6,4},{7,5},{8,10},{9,11},{10,... | collective-permute-start | bytes 786440 | tf_op jit(solution)/shard_map/ppermute | solution.py:37
  82.4 1.7 %attend.3.refs_2_.refs_8_ = bf16[64,1024]{1,0:T(8,128)(2,1)S(1)} custom-call(bf16[256,512]{1,0:T(8,128)(2,1)S(1)} %finish.4.refs_6_.refs_0_, bf16[256,512]{1,0:T(8,128)(2,1)S(1)} %collective-permute-done.11.refs_1_, bf16[1024,1024]{1,0:T(8,128)(2,1)S(1)} %copy-done, bf16[1024,1024]{1,0:T(8,128)(2,1)S(1)} %copy-done.1, ...), custom_call_target="tpu_custom_call" | custom-call | flops 1024 | bytes 1024 | tf_op jit(solution)/shard_map/attend/pallas_call | solution.py:25
  84.2 1.3 %collective-permute-start.14 = (bf16[256,512]{1,0:T(8,128)(2,1)S(1)}, bf16[256,512]{1,0:T(8,128)(2,1)S(1)}, u32[]{:S(2)}, u32[]{:S(2)}) collective-permute-start(bf16[256,512]{1,0:T(8,128)(2,1)S(1)} %get-tuple-element.43.refs_4_), channel_id=1, source_target_pairs={{0,2},{1,3},{2,0},{3,1},{4,6},{5,7},{6,4},{7,5},{8,10},{9,11},{10,... | collective-permute-start | bytes 786440 | tf_op jit(solution)/shard_map/ppermute | solution.py:37
  85.6 3.2 %collective-permute-start.17 = (bf16[64,1024]{1,0:T(8,128)(2,1)S(1)}, bf16[64,1024]{1,0:T(8,128)(2,1)S(1)}, u32[]{:S(2)}, u32[]{:S(2)}) collective-permute-start(bf16[64,1024]{1,0:T(8,128)(2,1)S(1)} %attend.3.refs_2_.refs_8_), channel_id=1, source_target_pairs={{0,4},{4,8},{8,12},{12,16},{16,20},{20,24},{24,28},{1,5},{5,9},{9,... | collective-permute-start | bytes 393224 | tf_op jit(solution)/shard_map/ppermute | solution.py:43
  89.6 1.7 %attend.4.refs_4_.refs_6_ = bf16[64,1024]{1,0:T(8,128)(2,1)S(1)} custom-call(bf16[256,512]{1,0:T(8,128)(2,1)S(1)} %finish.5.refs_5_.refs_0_, bf16[256,512]{1,0:T(8,128)(2,1)S(1)} %collective-permute-done.15.refs_1_, bf16[1024,1024]{1,0:T(8,128)(2,1)S(1)} %copy-done, bf16[1024,1024]{1,0:T(8,128)(2,1)S(1)} %copy-done.1, ...), custom_call_target="tpu_custom_call" | custom-call | flops 1024 | bytes 1024 | tf_op jit(solution)/shard_map/attend/pallas_call | solution.py:25
  91.3 1.5 %collective-permute-done.14.refs_3_ = bf16[256,512]{1,0:T(8,128)(2,1)S(1)} collective-permute-done((bf16[256,512]{1,0:T(8,128)(2,1)S(1)}, bf16[256,512]{1,0:T(8,128)(2,1)S(1)}, u32[]{:S(2)}, u32[]{:S(2)}) %collective-permute-start.14) | collective-permute-done | bytes 262176 | tf_op jit(solution)/shard_map/ppermute | solution.py:37
  92.9 1.4 %collective-permute-start.18 = (bf16[256,512]{1,0:T(8,128)(2,1)S(1)}, bf16[256,512]{1,0:T(8,128)(2,1)S(1)}, u32[]{:S(2)}, u32[]{:S(2)}) collective-permute-start(bf16[256,512]{1,0:T(8,128)(2,1)S(1)} %finish.7.refs_5_.refs_0_), channel_id=1, source_target_pairs={{0,1},{1,0},{2,3},{3,2},{4,5},{5,4},{6,7},{7,6},{8,9},{9,8},{10,11... | collective-permute-start | bytes 786440 | tf_op jit(solution)/shard_map/ppermute | solution.py:37
  94.3 1.7 %attend.5.refs_7_ = bf16[64,1024]{1,0:T(8,128)(2,1)S(1)} custom-call(bf16[256,512]{1,0:T(8,128)(2,1)S(1)} %finish.6.refs_5_.refs_0_, bf16[256,512]{1,0:T(8,128)(2,1)S(1)} %collective-permute-done.19.refs_1_, bf16[1024,1024]{1,0:T(8,128)(2,1)S(1)} %copy-done, bf16[1024,1024]{1,0:T(8,128)(2,1)S(1)} %copy-done.1, ...), custom_call_target="tpu_custom_call" | custom-call | flops 1024 | bytes 1024 | tf_op jit(solution)/shard_map/attend/pallas_call | solution.py:25
  96.0 2.5 %attend_last.1 = bf16[256,1024]{1,0:T(8,128)(2,1)} custom-call(bf16[256,512]{1,0:T(8,128)(2,1)S(1)} %finish.7.refs_5_.refs_0_, bf16[256,512]{1,0:T(8,128)(2,1)S(1)} %collective-permute-done.18.refs_1_, bf16[1024,1024]{1,0:T(8,128)(2,1)S(1)} %copy-done, bf16[1024,1024]{1,0:T(8,128)(2,1)S(1)} %copy-done.1, bf16[64,1024]{1,0:T(8,128)(2,1)S(1)} %get-tuple-element.48.refs_4_, ...), custom_call_target="tpu_custom_call" | custom-call | flops 1024 | bytes 1024 | tf_op jit(solution)/shard_map/attend_last/pallas_call | solution.py:25
  (55 shorter events, 13.2 us)
Async XLA Ops:
  1.2 15.2 %collective-permute-start = (bf16[64,1024]{1,0:T(8,128)(2,1)S(1)}, bf16[64,1024]{1,0:T(8,128)(2,1)S(1)}, u32[]{:S(2)}, u32[]{:S(2)}) collective-permute-start(bf16[64,1024]{1,0:T(8,128)(2,1)S(1)} %get-tuple-element.47), channel_id=1, source_target_pairs={{4,0},{8,4},{12,8},{16,12},{20,16},{24,20},{28,24},{5,1},{9,5},{13... | collective-permute-start | bytes 393224 | tf_op jit(solution)/shard_map/ppermute | solution.py:43
  17.7 40.9 %copy-start.3 = (bf16[1024,1024]{1,0:T(8,128)(2,1)S(1)}, bf16[1024,1024]{1,0:T(8,128)(2,1)}, u32[]{:S(2)}) copy-start(bf16[1024,1024]{1,0:T(8,128)(2,1)} %refs_5_.7) | copy-start | bytes 6291460
  20.1 38.6 %copy-start.2 = (bf16[1024,1024]{1,0:T(8,128)(2,1)S(1)}, bf16[1024,1024]{1,0:T(8,128)(2,1)}, u32[]{:S(2)}) copy-start(bf16[1024,1024]{1,0:T(8,128)(2,1)} %refs_4_.7) | copy-start | bytes 6291460
  48.6 5.8 %collective-permute-start.4 = (bf16[512,256]{1,0:T(8,128)(2,1)S(1)}, bf16[512,256]{1,0:T(8,128)(2,1)S(1)}, u32[]{:S(2)}, u32[]{:S(2)}) collective-permute-start(bf16[512,256]{1,0:T(8,128)(2,1)S(1)} %get-tuple-element.28.refs_0_), channel_id=1, source_target_pairs={{0,2},{1,3},{2,0},{3,1},{4,6},{5,7},{6,4},{7,5},{8,10},{9,11},{10,... | collective-permute-start | bytes 786440 | tf_op jit(solution)/shard_map/ppermute | solution.py:37
  49.9 8.7 %collective-permute-start.5 = (bf16[512,256]{1,0:T(8,128)(2,1)S(1)}, bf16[512,256]{1,0:T(8,128)(2,1)S(1)}, u32[]{:S(2)}, u32[]{:S(2)}) collective-permute-start(bf16[512,256]{1,0:T(8,128)(2,1)S(1)} %get-tuple-element.28.refs_0_), channel_id=1, source_target_pairs={{0,1},{1,0},{2,3},{3,2},{4,5},{5,4},{6,7},{7,6},{8,9},{9,8},{10,11... | collective-permute-start | bytes 786440 | tf_op jit(solution)/shard_map/ppermute | solution.py:37
  54.4 4.2 %collective-permute-start.6 = (bf16[512,256]{1,0:T(8,128)(2,1)S(1)}, bf16[512,256]{1,0:T(8,128)(2,1)S(1)}, u32[]{:S(2)}, u32[]{:S(2)}) collective-permute-start(bf16[512,256]{1,0:T(8,128)(2,1)S(1)} %collective-permute-done.4.refs_1_), channel_id=1, source_target_pairs={{0,1},{1,0},{2,3},{3,2},{4,5},{5,4},{6,7},{7,6},{8,9},{9,8},{10,11... | collective-permute-start | bytes 786440 | tf_op jit(solution)/shard_map/ppermute | solution.py:37
  57.4 7.9 %collective-permute-start.1 = (bf16[512,256]{1,0:T(8,128)(2,1)S(1)}, bf16[512,256]{1,0:T(8,128)(2,1)S(1)}, u32[]{:S(2)}, u32[]{:S(2)}) collective-permute-start(bf16[512,256]{1,0:T(8,128)(2,1)S(1)} %get-tuple-element.27.refs_0_), channel_id=1, source_target_pairs={{0,2},{1,3},{2,0},{3,1},{4,6},{5,7},{6,4},{7,5},{8,10},{9,11},{10,... | collective-permute-start | bytes 786440 | tf_op jit(solution)/shard_map/ppermute | solution.py:37
  60.3 7.5 %collective-permute-start.7 = (bf16[256,512]{1,0:T(8,128)(2,1)S(1)}, bf16[256,512]{1,0:T(8,128)(2,1)S(1)}, u32[]{:S(2)}, u32[]{:S(2)}) collective-permute-start(bf16[256,512]{1,0:T(8,128)(2,1)S(1)} %get-tuple-element.30.refs_6_), channel_id=1, source_target_pairs={{0,1},{1,0},{2,3},{3,2},{4,5},{5,4},{6,7},{7,6},{8,9},{9,8},{10,11... | collective-permute-start | bytes 786440 | tf_op jit(solution)/shard_map/ppermute | solution.py:37
  60.6 8.6 %collective-permute-start.2 = (bf16[512,256]{1,0:T(8,128)(2,1)S(1)}, bf16[512,256]{1,0:T(8,128)(2,1)S(1)}, u32[]{:S(2)}, u32[]{:S(2)}) collective-permute-start(bf16[512,256]{1,0:T(8,128)(2,1)S(1)} %get-tuple-element.27.refs_0_), channel_id=1, source_target_pairs={{0,1},{1,0},{2,3},{3,2},{4,5},{5,4},{6,7},{7,6},{8,9},{9,8},{10,11... | collective-permute-start | bytes 786440 | tf_op jit(solution)/shard_map/ppermute | solution.py:37
  65.3 3.9 %collective-permute-start.3 = (bf16[512,256]{1,0:T(8,128)(2,1)S(1)}, bf16[512,256]{1,0:T(8,128)(2,1)S(1)}, u32[]{:S(2)}, u32[]{:S(2)}) collective-permute-start(bf16[512,256]{1,0:T(8,128)(2,1)S(1)} %collective-permute-done.1.refs_1_), channel_id=1, source_target_pairs={{0,1},{1,0},{2,3},{3,2},{4,5},{5,4},{6,7},{7,6},{8,9},{9,8},{10,11... | collective-permute-start | bytes 786440 | tf_op jit(solution)/shard_map/ppermute | solution.py:37
  67.7 3.9 %collective-permute-start.9 = (bf16[256,512]{1,0:T(8,128)(2,1)S(1)}, bf16[256,512]{1,0:T(8,128)(2,1)S(1)}, u32[]{:S(2)}, u32[]{:S(2)}) collective-permute-start(bf16[256,512]{1,0:T(8,128)(2,1)S(1)} %get-tuple-element.31.refs_2_), channel_id=1, source_target_pairs={{0,1},{1,0},{2,3},{3,2},{4,5},{5,4},{6,7},{7,6},{8,9},{9,8},{10,11... | collective-permute-start | bytes 786440 | tf_op jit(solution)/shard_map/ppermute | solution.py:37
  67.9 7.5 %collective-permute-start.8 = (bf16[256,512]{1,0:T(8,128)(2,1)S(1)}, bf16[256,512]{1,0:T(8,128)(2,1)S(1)}, u32[]{:S(2)}, u32[]{:S(2)}) collective-permute-start(bf16[256,512]{1,0:T(8,128)(2,1)S(1)} %get-tuple-element.33.refs_6_), channel_id=1, source_target_pairs={{0,2},{1,3},{2,0},{3,1},{4,6},{5,7},{6,4},{7,5},{8,10},{9,11},{10,... | collective-permute-start | bytes 786440 | tf_op jit(solution)/shard_map/ppermute | solution.py:37
  70.8 8.8 %collective-permute-start.13 = (bf16[256,512]{1,0:T(8,128)(2,1)S(1)}, bf16[256,512]{1,0:T(8,128)(2,1)S(1)}, u32[]{:S(2)}, u32[]{:S(2)}) collective-permute-start(bf16[256,512]{1,0:T(8,128)(2,1)S(1)} %get-tuple-element.35.refs_2_), channel_id=1, source_target_pairs={{0,1},{1,0},{2,3},{3,2},{4,5},{5,4},{6,7},{7,6},{8,9},{9,8},{10,11... | collective-permute-start | bytes 786440 | tf_op jit(solution)/shard_map/ppermute | solution.py:37
  71.7 9.3 %collective-permute-start.12 = (bf16[256,512]{1,0:T(8,128)(2,1)S(1)}, bf16[256,512]{1,0:T(8,128)(2,1)S(1)}, u32[]{:S(2)}, u32[]{:S(2)}) collective-permute-start(bf16[256,512]{1,0:T(8,128)(2,1)S(1)} %get-tuple-element.36.refs_4_), channel_id=1, source_target_pairs={{0,2},{1,3},{2,0},{3,1},{4,6},{5,7},{6,4},{7,5},{8,10},{9,11},{10,... | collective-permute-start | bytes 786440 | tf_op jit(solution)/shard_map/ppermute | solution.py:37
  75.4 4.1 %copy-start.6 = (bf16[256,1024]{1,0:T(8,128)(2,1)S(1)}, bf16[256,1024]{1,0:T(8,128)(2,1)}, u32[]{:S(2)}) copy-start(bf16[256,1024]{1,0:T(8,128)(2,1)} %param.7) | copy-start | bytes 1572868
  75.4 7.0 %collective-permute-start.11 = (bf16[256,512]{1,0:T(8,128)(2,1)S(1)}, bf16[256,512]{1,0:T(8,128)(2,1)S(1)}, u32[]{:S(2)}, u32[]{:S(2)}) collective-permute-start(bf16[256,512]{1,0:T(8,128)(2,1)S(1)} %finish.4.refs_6_.refs_0_), channel_id=1, source_target_pairs={{0,1},{1,0},{2,3},{3,2},{4,5},{5,4},{6,7},{7,6},{8,9},{9,8},{10,11... | collective-permute-start | bytes 786440 | tf_op jit(solution)/shard_map/ppermute | solution.py:37
  79.4 3.1 %copy-start = (bf16[1024,1024]{1,0:T(8,128)(2,1)S(1)}, bf16[1024,1024]{1,0:T(8,128)(2,1)}, u32[]{:S(2)}) copy-start(bf16[1024,1024]{1,0:T(8,128)(2,1)} %refs_2_.7) | copy-start | bytes 6291460
  79.4 4.8 %collective-permute-start.10 = (bf16[256,512]{1,0:T(8,128)(2,1)S(1)}, bf16[256,512]{1,0:T(8,128)(2,1)S(1)}, u32[]{:S(2)}, u32[]{:S(2)}) collective-permute-start(bf16[256,512]{1,0:T(8,128)(2,1)S(1)} %get-tuple-element.38.refs_2_), channel_id=1, source_target_pairs={{0,1},{1,0},{2,3},{3,2},{4,5},{5,4},{6,7},{7,6},{8,9},{9,8},{10,11... | collective-permute-start | bytes 786440 | tf_op jit(solution)/shard_map/ppermute | solution.py:37
  79.7 9.0 %collective-permute-start.16 = (bf16[256,512]{1,0:T(8,128)(2,1)S(1)}, bf16[256,512]{1,0:T(8,128)(2,1)S(1)}, u32[]{:S(2)}, u32[]{:S(2)}) collective-permute-start(bf16[256,512]{1,0:T(8,128)(2,1)S(1)} %get-tuple-element.41.refs_4_), channel_id=1, source_target_pairs={{0,2},{1,3},{2,0},{3,1},{4,6},{5,7},{6,4},{7,5},{8,10},{9,11},{10,... | collective-permute-start | bytes 786440 | tf_op jit(solution)/shard_map/ppermute | solution.py:37
  81.1 8.5 %collective-permute-start.15 = (bf16[256,512]{1,0:T(8,128)(2,1)S(1)}, bf16[256,512]{1,0:T(8,128)(2,1)S(1)}, u32[]{:S(2)}, u32[]{:S(2)}) collective-permute-start(bf16[256,512]{1,0:T(8,128)(2,1)S(1)} %finish.5.refs_5_.refs_0_), channel_id=1, source_target_pairs={{0,1},{1,0},{2,3},{3,2},{4,5},{5,4},{6,7},{7,6},{8,9},{9,8},{10,11... | collective-permute-start | bytes 786440 | tf_op jit(solution)/shard_map/ppermute | solution.py:37
  84.2 8.6 %collective-permute-start.14 = (bf16[256,512]{1,0:T(8,128)(2,1)S(1)}, bf16[256,512]{1,0:T(8,128)(2,1)S(1)}, u32[]{:S(2)}, u32[]{:S(2)}) collective-permute-start(bf16[256,512]{1,0:T(8,128)(2,1)S(1)} %get-tuple-element.43.refs_4_), channel_id=1, source_target_pairs={{0,2},{1,3},{2,0},{3,1},{4,6},{5,7},{6,4},{7,5},{8,10},{9,11},{10,... | collective-permute-start | bytes 786440 | tf_op jit(solution)/shard_map/ppermute | solution.py:37
  85.6 5.8 %collective-permute-start.17 = (bf16[64,1024]{1,0:T(8,128)(2,1)S(1)}, bf16[64,1024]{1,0:T(8,128)(2,1)S(1)}, u32[]{:S(2)}, u32[]{:S(2)}) collective-permute-start(bf16[64,1024]{1,0:T(8,128)(2,1)S(1)} %attend.3.refs_2_.refs_8_), channel_id=1, source_target_pairs={{0,4},{4,8},{8,12},{12,16},{16,20},{20,24},{24,28},{1,5},{5,9},{9,... | collective-permute-start | bytes 393224 | tf_op jit(solution)/shard_map/ppermute | solution.py:43
  88.9 5.4 %collective-permute-start.19 = (bf16[256,512]{1,0:T(8,128)(2,1)S(1)}, bf16[256,512]{1,0:T(8,128)(2,1)S(1)}, u32[]{:S(2)}, u32[]{:S(2)}) collective-permute-start(bf16[256,512]{1,0:T(8,128)(2,1)S(1)} %finish.6.refs_5_.refs_0_), channel_id=1, source_target_pairs={{0,1},{1,0},{2,3},{3,2},{4,5},{5,4},{6,7},{7,6},{8,9},{9,8},{10,11... | collective-permute-start | bytes 786440 | tf_op jit(solution)/shard_map/ppermute | solution.py:37
  92.9 3.1 %collective-permute-start.18 = (bf16[256,512]{1,0:T(8,128)(2,1)S(1)}, bf16[256,512]{1,0:T(8,128)(2,1)S(1)}, u32[]{:S(2)}, u32[]{:S(2)}) collective-permute-start(bf16[256,512]{1,0:T(8,128)(2,1)S(1)} %finish.7.refs_5_.refs_0_), channel_id=1, source_target_pairs={{0,1},{1,0},{2,3},{3,2},{4,5},{5,4},{6,7},{7,6},{8,9},{9,8},{10,11... | collective-permute-start | bytes 786440 | tf_op jit(solution)/shard_map/ppermute | solution.py:37
  (3 other events, 5.0 us)

commit v3 on v2

--- a/solution.py
+++ b/solution.py
@@ -55,7 +55,7 @@
     )
 
 
-def route_body(voc, cap, ids_ref, wanted_ref, slot_ref):
+def route_body(voc, cap, mirrored, ids_ref, wanted_ref, slot_ref):
     ids = ids_ref[...]
     count = ids.shape[1]
     owners = wanted_ref.shape[0]
@@ -87,6 +87,8 @@
         digits, place, (((1,), (1,)), ((), ())), preferred_element_type=F32
     ).astype(jnp.int32)
     wanted_ref[...] = found[:owners] * 256 + found[owners:]
+    if mirrored:
+        owner = owner ^ lax.axis_index("seq")
     slot_ref[...] = columns_of(owner * cap + rank)
 
 
@@ -100,15 +102,27 @@
         ).astype(BF16)
 
 
-def order_body(plan, slot_ref, rows_ref, *out_refs):
-    rows = rows_ref[...]
-    for groups, out_ref in zip(plan, out_refs):
-        count = out_ref.shape[0] // len(groups)
-        for at, g in enumerate(groups):
-            picked = one_hot(slot_ref[g * count : (g + 1) * count, :], rows.shape[0])
-            out_ref[at * count : (at + 1) * count, :] = jnp.dot(
-                picked, rows, preferred_element_type=F32
-            ).astype(BF16)
+def fetch_for_body(partners, req_ref, vocab_ref, *out_refs):
+    me = lax.axis_index("seq")
+    table = vocab_ref[...]
+    for at, k in enumerate(partners):
+        picked = one_hot(columns_of(req_ref[me ^ k]), table.shape[0])
+        rows = jnp.dot(picked, table, preferred_element_type=F32).astype(BF16)
+        for half in range(2):
+            out_refs[2 * at + half][...] = rows[:, half * LANES : (half + 1) * LANES]
+
+
+def order_body(slot_ref, *refs):
+    rows_refs, out_ref = refs[:-1], refs[-1]
+    step = 256
+    for at in range(0, out_ref.shape[0], step):
+        total, base = None, 0
+        for rows_ref in rows_refs:
+            count = rows_ref.shape[0]
+            picked = one_hot(slot_ref[at : at + step, :] - base, count)
+            part = jnp.dot(picked, rows_ref[...], preferred_element_type=F32)
+            total, base = part if total is None else total + part, base + count
+        out_ref[at : at + step, :] = total.astype(BF16)
 
 
 def block_rows(ref, index, width):
@@ -119,12 +133,17 @@
     return ref[:, pl.ds(pl.multiple_of(index * width, width), width)]
 
 
-def feed_body(first, e0_ref, e2_ref, e1_ref, e3_ref, w_in_ref, w_out_ref, keep_ref, send_ref):
+def piece(refs, here):
+    return jnp.concatenate([ref[here, :] for ref in refs], axis=1)
+
+
+def feed_body(first, *refs):
+    emb_refs, (w_in_ref, w_out_ref, keep_ref, send_ref) = refs[:-4], refs[-4:]
     me = lax.axis_index("tp")
-    width = e0_ref.shape[1]
     index = [me, me ^ 2, me ^ 1, me ^ 3]
     here = slice(first, first + keep_ref.shape[0])
-    parts = [ref[here, :].astype(F32) for ref in (e0_ref, e2_ref, e1_ref, e3_ref)]
+    parts = [piece(emb_refs[2 * at : 2 * at + 2], here).astype(F32) for at in range(4)]
+    width = parts[0].shape[1]
     square = sum(jnp.sum(part * part, axis=1, keepdims=True) for part in parts)
     scale = lax.rsqrt(square / (4 * width) + 1e-06)
     hidden = sum(
@@ -150,15 +169,16 @@
     send_ref[...] = chip.astype(BF16)
 
 
-def finish_body(first, e0_ref, e2_ref, chip_ref, far_ref, mine_ref):
-    width = e0_ref.shape[1]
+def finish_body(first, *refs):
+    emb_refs, (chip_ref, far_ref, mine_ref) = refs[:-3], refs[-3:]
+    width = mine_ref.shape[1] // 2
     near, past = slice(0, width), slice(width, 2 * width)
     here = slice(first, first + mine_ref.shape[0])
     mine_ref[:, near] = (
-        e0_ref[here, :].astype(F32) + (chip_ref[:, near] + far_ref[:, past].astype(F32))
+        piece(emb_refs[:2], here).astype(F32) + (chip_ref[:, near] + far_ref[:, past].astype(F32))
     ).astype(BF16)
     mine_ref[:, past] = (
-        e2_ref[here, :].astype(F32) + (chip_ref[:, past] + far_ref[:, near].astype(F32))
+        piece(emb_refs[2:], here).astype(F32) + (chip_ref[:, past] + far_ref[:, near].astype(F32))
     ).astype(BF16)
 
 
@@ -228,53 +248,73 @@
 
     next_q = shifted(queries[:GROUP], -1)
 
+    mirrored = seq_size <= 8 and seq_size & (seq_size - 1) == 0
     wanted, slot = call(
-        functools.partial(route_body, voc, cap),
+        functools.partial(route_body, voc, cap, mirrored),
         (sds((seq_size, cap), jnp.int32), sds((rows, LANES), jnp.int32)),
         "route",
         (neighbour_ids.reshape(1, rows),),
     )
     request = lax.all_to_all(wanted, "seq", split_axis=0, concat_axis=0, tiled=True)
-    found = call(
-        fetch_body,
-        sds((slots, width), BF16),
-        "fetch",
-        (request.reshape(1, slots), vocab_rows),
-        (next_q,),
-    )
-    answered = lax.all_to_all(
-        found.reshape(seq_size, cap, width), "seq", split_axis=0, concat_axis=0, tiled=True
-    ).reshape(slots, width)
+    if mirrored:
+        request = request.reshape(seq_size, 1, cap)
+        part = sds((cap, LANES), BF16)
+        found = {}
+        token = None
+        for partners in (range(seq_size // 2, seq_size), range(seq_size // 2)):
+            got = call(
+                functools.partial(fetch_for_body, partners),
+                (part,) * (2 * len(partners)),
+                "fetch",
+                (request, vocab_rows),
+                () if token is None else (token,),
+            )
+            token = got[0]
+            for at, k in enumerate(partners):
+                found[k] = got[2 * at : 2 * at + 2]
+        answered = [
+            [found[k][half] if k == 0 else lax.ppermute(
+                found[k][half], "seq", [(i, i ^ k) for i in range(seq_size)]
+            ) for k in range(seq_size)]
+            for half in range(2)
+        ]
+    else:
+        found = call(
+            fetch_body,
+            sds((slots, width), BF16),
+            "fetch",
+            (request.reshape(1, slots), vocab_rows),
+        )
+        answered = lax.all_to_all(
+            found.reshape(seq_size, cap, width), "seq", split_axis=0, concat_axis=0, tiled=True
+        ).reshape(slots, width)
+        answered = [[answered[:, :LANES]], [answered[:, LANES:]]]
     order = [groups - 1] + list(range(groups - 1))
-    plan = [order[at : at + 2] for at in range(0, groups, 2)]
-    own = call(
-        functools.partial(order_body, plan),
-        tuple(sds((len(part) * per_group, width), BF16) for part in plan),
-        "order",
-        (slot, answered),
-    )
+    emb = [[], [], [], []]
+    token = slot
+    for half in range(2):
+        e0 = call(
+            order_body, sds((rows, LANES), BF16), "order", (slot, *answered[half]), (token,)
+        )
+        e2 = exchange(e0, 2)
+        for at, part in enumerate((e0, e2, exchange(e0, 1), exchange(e2, 1))):
+            emb[at].append(part)
+        token = e2
+    emb = [part for pair in emb for part in pair]
 
     local_q = jnp.concatenate([queries[GROUP - 1 :], next_q[: GROUP - 1]], axis=0)
     half = sds((per_group, 2 * width), BF16)
     whole = sds((per_group, 2 * width), F32)
-    emb, first, window = {}, {}, {}
-    fed, summed, far, encoded = {}, {}, {}, {}
+    window, fed, summed, far, encoded = {}, {}, {}, {}, {}
     behind = None
-    token = slot
-
-    for part, e0 in zip(plan, own):
-        e2 = exchange(e0, 2)
-        pieces = e0, e2, exchange(e0, 1), exchange(e2, 1)
-        for at, g in enumerate(part):
-            emb[g], first[g] = pieces, at * per_group
 
     def feed(g):
         nonlocal token
         keep, token = call(
-            functools.partial(feed_body, first[g]),
+            functools.partial(feed_body, g * per_group),
             (whole, half),
             "feed",
-            (*emb[g], w_in, w_out),
+            (*emb, w_in, w_out),
             (token,),
         )
         fed[g] = keep, exchange(token, 1)
@@ -287,10 +327,10 @@
     def finish(g):
         nonlocal token
         token = call(
-            functools.partial(finish_body, first[g]),
+            functools.partial(finish_body, g * per_group),
             half,
             "finish",
-            (*emb[g][:2], summed[g], far[g]),
+            (*emb[:4], summed[g], far[g]),
             (token, behind) if g == order[-1] else (token,),
         )
         encoded[g] = token, exchange(token, 1)

time: 98.8 us -> 104 us (1.053)
  blocking collectives: 39.6 us -> 11.5 us
  starting transfers between devices: 24.6 us -> 51.8 us
  waiting for transfers between devices: 11.6 us -> 16.9 us
  Pallas kernels: 19.1 us -> 20.7 us
  local copies, waits for them, and re-layouts: 3.26 us -> 2.14 us
    all_to_all x1 -> x0, blocking collectives: 27.2 us -> none  [per_device(): lax.all_to_all(found.reshape(seq_size, cap, width), 'seq', split_axis=0,...]
    ppermute x0 -> x14, starting transfers between devices: none -> 20.4 us  [per_device(): lax.ppermute(found[k][half], 'seq', [(i, i ^ k) for i in range(seq_size)])]
    ppermute x0 -> x14, waiting for transfers between devices: none -> 6.99 us  [per_device(): lax.ppermute(found[k][half], 'seq', [(i, i ^ k) for i in range(seq_size)])]
    ppermute x18, starting transfers between devices: 20.1 us -> 26.9 us  [exchange(): return lax.ppermute(x, 'tp', [(i, i ^ bit) for i in range(size)])]
    ppermute x18, waiting for transfers between devices: 11.6 us -> 4.82 us  [exchange(): return lax.ppermute(x, 'tp', [(i, i ^ bit) for i in range(size)])]
    ppermute x2, waiting for transfers between devices: 0.03 us -> 5.05 us  [shifted(): return lax.ppermute(x, 'seq', pairs)]
    pallas_call x19 -> x21, Pallas kernels: 19.1 us -> 20.7 us  [call(): pl.pallas_call(without_after, out_shape=outs, in_specs=[vmem] * len(used)...]
    slice x1, local copies, waits for them, and re-layouts: 1.21 us -> 0.1 us  [attend(): args = (*encoded[g], w_key, w_value, local_q[g * GROUP:(g + 1) * GROUP])]
  transfers between devices with their start and end apart: 20 -> 34, of which waited for: 4 -> 8; matrix products, arithmetic and copies ran while one was open for 0% -> 0% of each run, Pallas kernels for 13% -> 10%
where the time goes in v3:
time: 104 us; the launch traced here: 103 us
  starting transfers between devices  51.8 us (50%)
  Pallas kernels  20.7 us (20%)
  waiting for transfers between devices  16.9 us (16%)
  blocking collectives  11.5 us (11%)
  local copies, waits for them, and re-layouts  2.14 us (2%)
    ppermute x18, starting transfers between devices, exchange(): return lax.ppermute(x, 'tp', [(i, i ^ bit) for i in range(size)])  26.9 us
    pallas_call x21, Pallas kernels, call(): pl.pallas_call(without_after, out_shape=outs, in_specs=[vmem] * len(used)...  20.7 us
    ppermute x14, starting transfers between devices, per_device(): lax.ppermute(found[k][half], 'seq', [(i, i ^ k) for i in range(seq_size)])  20.4 us
    all_to_all x1, blocking collectives, per_device(): lax.all_to_all(wanted, 'seq', split_axis=0, concat_axis=0, tiled=True)  11.5 us
    ppermute x14, waiting for transfers between devices, per_device(): lax.ppermute(found[k][half], 'seq', [(i, i ^ k) for i in range(seq_size)])  6.99 us
    ppermute x2, waiting for transfers between devices, shifted(): return lax.ppermute(x, 'seq', pairs)  5.05 us
    ppermute x18, waiting for transfers between devices, exchange(): return lax.ppermute(x, 'tp', [(i, i ^ bit) for i in range(size)])  4.82 us
    ppermute x2, starting transfers between devices, shifted(): return lax.ppermute(x, 'seq', pairs)  4.46 us
  transfers between devices with their start and end apart: 34, of which 8 were waited for; matrix products, arithmetic and copies ran while one was open for 0% of the time, Pallas kernels for 10%

profile of v3, /device:TPU:1, one launch (start us, length us, event | category | flops | bytes accessed | tf_op | source)
XLA Modules:
  0.0 103.3 jit_solution(11029276786455988444)
XLA Ops:
  1.5 11.5 %all_to_all.9.refs_0_ = s32[8,1,256]{2,1,0:T(1,128)S(1)} all-to-all(s32[8,1,256]{2,1,0:T(1,128)S(1)} %all_to_all.6), channel_id=1, replica_groups=mesh['seq'=8,'tp'=4] {'seq'}, dimensions={0} | all-to-all | bytes 16384 | tf_op jit(solution)/shard_map/all_to_all | solution.py:258
  18.2 1.8 %collective-permute-start.2 = (bf16[256,128]{1,0:T(8,128)(2,1)S(1)}, bf16[256,128]{1,0:T(8,128)(2,1)S(1)}, u32[]{:S(2)}, u32[]{:S(2)}) collective-permute-start(bf16[256,128]{1,0:T(8,128)(2,1)S(1)} %get-tuple-element.45), channel_id=1, source_target_pairs={{0,12},{4,8},{8,4},{12,0},{16,28},{20,24},{24,20},{28,16},{1,13},{... | collective-permute-start | bytes 196616 | tf_op jit(solution)/shard_map/ppermute | solution.py:276
  19.9 2.1 %collective-permute-start.4 = (bf16[256,128]{1,0:T(8,128)(2,1)S(1)}, bf16[256,128]{1,0:T(8,128)(2,1)S(1)}, u32[]{:S(2)}, u32[]{:S(2)}) collective-permute-start(bf16[256,128]{1,0:T(8,128)(2,1)S(1)} %get-tuple-element.46), channel_id=1, source_target_pairs={{0,20},{4,16},{8,28},{12,24},{16,4},{20,0},{24,12},{28,8},{1,21},{... | collective-permute-start | bytes 196616 | tf_op jit(solution)/shard_map/ppermute | solution.py:276
  22.6 3.6 %collective-permute-start.6 = (bf16[256,128]{1,0:T(8,128)(2,1)S(1)}, bf16[256,128]{1,0:T(8,128)(2,1)S(1)}, u32[]{:S(2)}, u32[]{:S(2)}) collective-permute-start(bf16[256,128]{1,0:T(8,128)(2,1)S(1)} %get-tuple-element.48), channel_id=1, source_target_pairs={{0,28},{4,24},{8,20},{12,16},{16,12},{20,8},{24,4},{28,0},{1,29},{... | collective-permute-start | bytes 196616 | tf_op jit(solution)/shard_map/ppermute | solution.py:276
  27.5 1.9 %collective-permute-done.6.refs_8_ = bf16[256,128]{1,0:T(8,128)(2,1)S(1)} collective-permute-done((bf16[256,128]{1,0:T(8,128)(2,1)S(1)}, bf16[256,128]{1,0:T(8,128)(2,1)S(1)}, u32[]{:S(2)}, u32[]{:S(2)}) %collective-permute-start.6) | collective-permute-done | bytes 65568 | tf_op jit(solution)/shard_map/ppermute | solution.py:276
  32.8 2.7 %collective-permute-start.8 = (bf16[256,128]{1,0:T(8,128)(2,1)S(1)}, bf16[256,128]{1,0:T(8,128)(2,1)S(1)}, u32[]{:S(2)}, u32[]{:S(2)}) collective-permute-start(bf16[256,128]{1,0:T(8,128)(2,1)S(1)} %get-tuple-element.51), channel_id=1, source_target_pairs={{0,8},{4,12},{8,0},{12,4},{16,24},{20,28},{24,16},{28,20},{1,9},{5... | collective-permute-start | bytes 196616 | tf_op jit(solution)/shard_map/ppermute | solution.py:276
  36.6 1.8 %collective-permute-start.10 = (bf16[256,128]{1,0:T(8,128)(2,1)S(1)}, bf16[256,128]{1,0:T(8,128)(2,1)S(1)}, u32[]{:S(2)}, u32[]{:S(2)}) collective-permute-start(bf16[256,128]{1,0:T(8,128)(2,1)S(1)} %get-tuple-element.53), channel_id=1, source_target_pairs={{0,16},{4,20},{8,24},{12,28},{16,0},{20,4},{24,8},{28,12},{1,17},{... | collective-permute-start | bytes 196616 | tf_op jit(solution)/shard_map/ppermute | solution.py:276
  40.6 2.6 %collective-permute-start.13 = (bf16[256,128]{1,0:T(8,128)(2,1)S(1)}, bf16[256,128]{1,0:T(8,128)(2,1)S(1)}, u32[]{:S(2)}, u32[]{:S(2)}) collective-permute-start(bf16[256,128]{1,0:T(8,128)(2,1)S(1)} %get-tuple-element.56), channel_id=1, source_target_pairs={{0,28},{4,24},{8,20},{12,16},{16,12},{20,8},{24,4},{28,0},{1,29},{... | collective-permute-start | bytes 196616 | tf_op jit(solution)/shard_map/ppermute | solution.py:276
  44.2 2.7 %collective-permute-done.13.refs_8_ = bf16[256,128]{1,0:T(8,128)(2,1)S(1)} collective-permute-done((bf16[256,128]{1,0:T(8,128)(2,1)S(1)}, bf16[256,128]{1,0:T(8,128)(2,1)S(1)}, u32[]{:S(2)}, u32[]{:S(2)}) %collective-permute-start.13) | collective-permute-done | bytes 65568 | tf_op jit(solution)/shard_map/ppermute | solution.py:276
  48.4 6.9 %collective-permute-start.16 = (bf16[1024,128]{1,0:T(8,128)(2,1)S(1)}, bf16[1024,128]{1,0:T(8,128)(2,1)S(1)}, u32[]{:S(2)}, u32[]{:S(2)}) collective-permute-start(bf16[1024,128]{1,0:T(8,128)(2,1)S(1)} %order.2.refs_0_), channel_id=1, source_target_pairs={{0,1},{1,0},{2,3},{3,2},{4,5},{5,4},{6,7},{7,6},{8,9},{9,8},{10,11... | collective-permute-start | bytes 786440 | tf_op jit(solution)/shard_map/ppermute | solution.py:37
  55.8 5.3 %collective-permute-start.19 = (bf16[1024,128]{1,0:T(8,128)(2,1)S(1)}, bf16[1024,128]{1,0:T(8,128)(2,1)S(1)}, u32[]{:S(2)}, u32[]{:S(2)}) collective-permute-start(bf16[1024,128]{1,0:T(8,128)(2,1)S(1)} %collective-permute-done.15.refs_3_.refs_10_), channel_id=1, source_target_pairs={{0,1},{1,0},{2,3},{3,2},{4,5},{5,4},{6,7},{7,6},{8,9},{9,8},{10,11... | collective-permute-start | bytes 786440 | tf_op jit(solution)/shard_map/ppermute | solution.py:37
  62.3 1.6 %feed.4 = (f32[256,512]{1,0:T(8,128)S(1)}, bf16[256,512]{1,0:T(8,128)(2,1)S(1)}) custom-call(bf16[1024,128]{1,0:T(8,128)(2,1)S(1)} %order.2.refs_0_, bf16[1024,128]{1,0:T(8,128)(2,1)S(1)} %order.3.refs_1_, bf16[1024,128]{1,0:T(8,128)(2,1)S(1)} %collective-permute-done.14.refs_9_.refs_2_, bf16[1024,128]{1,0:T(8,128)(2,1)S(1)} %collective-permute-done.15.refs_3_.refs_10_, ...), custom_call_target="tpu_custom_call" | custom-call | flops 1024 | bytes 1024 | tf_op jit(solution)/shard_map/feed/pallas_call | solution.py:25
  70.2 3.6 %collective-permute-done.21.refs_5_ = bf16[256,512]{1,0:T(8,128)(2,1)S(1)} collective-permute-done((bf16[256,512]{1,0:T(8,128)(2,1)S(1)}, bf16[256,512]{1,0:T(8,128)(2,1)S(1)}, u32[]{:S(2)}, u32[]{:S(2)}) %collective-permute-start.21) | collective-permute-done | bytes 262176 | tf_op jit(solution)/shard_map/ppermute | solution.py:37
  73.9 2.1 %collective-permute-start.24 = (bf16[256,512]{1,0:T(8,128)(2,1)S(1)}, bf16[256,512]{1,0:T(8,128)(2,1)S(1)}, u32[]{:S(2)}, u32[]{:S(2)}) collective-permute-start(bf16[256,512]{1,0:T(8,128)(2,1)S(1)} %finish.4.refs_10_.refs_0_), channel_id=1, source_target_pairs={{0,1},{1,0},{2,3},{3,2},{4,5},{5,4},{6,7},{7,6},{8,9},{9,8},{10,11... | collective-permute-start | bytes 786440 | tf_op jit(solution)/shard_map/ppermute | solution.py:37
  76.0 1.8 %feed.7 = (f32[256,512]{1,0:T(8,128)S(1)}, bf16[256,512]{1,0:T(8,128)(2,1)S(1)}) custom-call(bf16[1024,128]{1,0:T(8,128)(2,1)S(1)} %order.2.refs_0_, bf16[1024,128]{1,0:T(8,128)(2,1)S(1)} %order.3.refs_1_, bf16[1024,128]{1,0:T(8,128)(2,1)S(1)} %collective-permute-done.14.refs_9_.refs_2_, bf16[1024,128]{1,0:T(8,128)(2,1)S(1)} %collective-permute-done.15.refs_3_.refs_10_, ...), custom_call_target="tpu_custom_call" | custom-call | flops 1024 | bytes 1024 | tf_op jit(solution)/shard_map/feed/pallas_call | solution.py:25
  79.4 5.0 %collective-permute-done.25 = bf16[64,1024]{1,0:T(8,128)(2,1)S(1)} collective-permute-done((bf16[64,1024]{1,0:T(8,128)(2,1)S(1)}, bf16[64,1024]{1,0:T(8,128)(2,1)S(1)}, u32[]{:S(2)}, u32[]{:S(2)}) %collective-permute-start.25) | collective-permute-done | bytes 131104 | tf_op jit(solution)/shard_map/ppermute | solution.py:43
  84.9 1.7 %collective-permute-start.29 = (bf16[256,512]{1,0:T(8,128)(2,1)S(1)}, bf16[256,512]{1,0:T(8,128)(2,1)S(1)}, u32[]{:S(2)}, u32[]{:S(2)}) collective-permute-start(bf16[256,512]{1,0:T(8,128)(2,1)S(1)} %finish.5.refs_5_.refs_0_), channel_id=1, source_target_pairs={{0,1},{1,0},{2,3},{3,2},{4,5},{5,4},{6,7},{7,6},{8,9},{9,8},{10,11... | collective-permute-start | bytes 786440 | tf_op jit(solution)/shard_map/ppermute | solution.py:37
  86.6 1.7 %attend.3.refs_2_.refs_8_ = bf16[64,1024]{1,0:T(8,128)(2,1)S(1)} custom-call(bf16[256,512]{1,0:T(8,128)(2,1)S(1)} %finish.4.refs_10_.refs_0_, bf16[256,512]{1,0:T(8,128)(2,1)S(1)} %collective-permute-done.24.refs_1_, bf16[1024,1024]{1,0:T(8,128)(2,1)S(1)} %copy-done.2, bf16[1024,1024]{1,0:T(8,128)(2,1)S(1)} %copy-done.3, ...), custom_call_target="tpu_custom_call" | custom-call | flops 1024 | bytes 1024 | tf_op jit(solution)/shard_map/attend/pallas_call | solution.py:25
  89.7 3.2 %collective-permute-start.31 = (bf16[64,1024]{1,0:T(8,128)(2,1)S(1)}, bf16[64,1024]{1,0:T(8,128)(2,1)S(1)}, u32[]{:S(2)}, u32[]{:S(2)}) collective-permute-start(bf16[64,1024]{1,0:T(8,128)(2,1)S(1)} %attend.3.refs_2_.refs_8_), channel_id=1, source_target_pairs={{0,4},{4,8},{8,12},{12,16},{16,20},{20,24},{24,28},{1,5},{5,9},{9,... | collective-permute-start | bytes 393224 | tf_op jit(solution)/shard_map/ppermute | solution.py:43
  93.0 2.1 %collective-permute-start.33 = (bf16[256,512]{1,0:T(8,128)(2,1)S(1)}, bf16[256,512]{1,0:T(8,128)(2,1)S(1)}, u32[]{:S(2)}, u32[]{:S(2)}) collective-permute-start(bf16[256,512]{1,0:T(8,128)(2,1)S(1)} %finish.6.refs_5_.refs_0_), channel_id=1, source_target_pairs={{0,1},{1,0},{2,3},{3,2},{4,5},{5,4},{6,7},{7,6},{8,9},{9,8},{10,11... | collective-permute-start | bytes 786440 | tf_op jit(solution)/shard_map/ppermute | solution.py:37
  95.1 1.7 %attend.4.refs_6_ = bf16[64,1024]{1,0:T(8,128)(2,1)S(1)} custom-call(bf16[256,512]{1,0:T(8,128)(2,1)S(1)} %finish.5.refs_5_.refs_0_, bf16[256,512]{1,0:T(8,128)(2,1)S(1)} %collective-permute-done.29.refs_1_, bf16[1024,1024]{1,0:T(8,128)(2,1)S(1)} %copy-done.2, bf16[1024,1024]{1,0:T(8,128)(2,1)S(1)} %copy-done.3, ...), custom_call_target="tpu_custom_call" | custom-call | flops 1024 | bytes 1024 | tf_op jit(solution)/shard_map/attend/pallas_call | solution.py:25
  97.0 2.1 %collective-permute-start.32 = (bf16[256,512]{1,0:T(8,128)(2,1)S(1)}, bf16[256,512]{1,0:T(8,128)(2,1)S(1)}, u32[]{:S(2)}, u32[]{:S(2)}) collective-permute-start(bf16[256,512]{1,0:T(8,128)(2,1)S(1)} %finish.7.refs_5_.refs_0_), channel_id=1, source_target_pairs={{0,1},{1,0},{2,3},{3,2},{4,5},{5,4},{6,7},{7,6},{8,9},{9,8},{10,11... | collective-permute-start | bytes 786440 | tf_op jit(solution)/shard_map/ppermute | solution.py:37
  99.1 1.7 %attend.5.refs_7_ = bf16[64,1024]{1,0:T(8,128)(2,1)S(1)} custom-call(bf16[256,512]{1,0:T(8,128)(2,1)S(1)} %finish.6.refs_5_.refs_0_, bf16[256,512]{1,0:T(8,128)(2,1)S(1)} %collective-permute-done.33.refs_1_, bf16[1024,1024]{1,0:T(8,128)(2,1)S(1)} %copy-done.2, bf16[1024,1024]{1,0:T(8,128)(2,1)S(1)} %copy-done.3, ...), custom_call_target="tpu_custom_call" | custom-call | flops 1024 | bytes 1024 | tf_op jit(solution)/shard_map/attend/pallas_call | solution.py:25
  100.8 2.5 %attend_last.1 = bf16[256,1024]{1,0:T(8,128)(2,1)} custom-call(bf16[256,512]{1,0:T(8,128)(2,1)S(1)} %finish.7.refs_5_.refs_0_, bf16[256,512]{1,0:T(8,128)(2,1)S(1)} %collective-permute-done.32.refs_1_, bf16[1024,1024]{1,0:T(8,128)(2,1)S(1)} %copy-done.2, bf16[1024,1024]{1,0:T(8,128)(2,1)S(1)} %copy-done.3, bf16[64,1024]{1,0:T(8,128)(2,1)S(1)} %get-tuple-element.76.refs_4_, ...), custom_call_target="tpu_custom_call" | custom-call | flops 1024 | bytes 1024 | tf_op jit(solution)/shard_map/attend_last/pallas_call | solution.py:25
  (84 shorter events, 29.4 us)
Async XLA Ops:
  17.6 8.6 %collective-permute-start.3 = (bf16[256,128]{1,0:T(8,128)(2,1)S(1)}, bf16[256,128]{1,0:T(8,128)(2,1)S(1)}, u32[]{:S(2)}, u32[]{:S(2)}) collective-permute-start(bf16[256,128]{1,0:T(8,128)(2,1)S(1)} %get-tuple-element.41.refs_2_), channel_id=1, source_target_pairs={{0,16},{4,20},{8,24},{12,28},{16,0},{20,4},{24,8},{28,12},{1,17},{... | collective-permute-start | bytes 196616 | tf_op jit(solution)/shard_map/ppermute | solution.py:276
  18.2 8.0 %collective-permute-start.2 = (bf16[256,128]{1,0:T(8,128)(2,1)S(1)}, bf16[256,128]{1,0:T(8,128)(2,1)S(1)}, u32[]{:S(2)}, u32[]{:S(2)}) collective-permute-start(bf16[256,128]{1,0:T(8,128)(2,1)S(1)} %get-tuple-element.45), channel_id=1, source_target_pairs={{0,12},{4,8},{8,4},{12,0},{16,28},{20,24},{24,20},{28,16},{1,13},{... | collective-permute-start | bytes 196616 | tf_op jit(solution)/shard_map/ppermute | solution.py:276
  19.9 6.3 %collective-permute-start.4 = (bf16[256,128]{1,0:T(8,128)(2,1)S(1)}, bf16[256,128]{1,0:T(8,128)(2,1)S(1)}, u32[]{:S(2)}, u32[]{:S(2)}) collective-permute-start(bf16[256,128]{1,0:T(8,128)(2,1)S(1)} %get-tuple-element.46), channel_id=1, source_target_pairs={{0,20},{4,16},{8,28},{12,24},{16,4},{20,0},{24,12},{28,8},{1,21},{... | collective-permute-start | bytes 196616 | tf_op jit(solution)/shard_map/ppermute | solution.py:276
  22.6 6.8 %collective-permute-start.6 = (bf16[256,128]{1,0:T(8,128)(2,1)S(1)}, bf16[256,128]{1,0:T(8,128)(2,1)S(1)}, u32[]{:S(2)}, u32[]{:S(2)}) collective-permute-start(bf16[256,128]{1,0:T(8,128)(2,1)S(1)} %get-tuple-element.48), channel_id=1, source_target_pairs={{0,28},{4,24},{8,20},{12,16},{16,12},{20,8},{24,4},{28,0},{1,29},{... | collective-permute-start | bytes 196616 | tf_op jit(solution)/shard_map/ppermute | solution.py:276
  30.7 16.3 %collective-permute-start.14 = (bf16[1024,128]{1,0:T(8,128)(2,1)S(1)}, bf16[1024,128]{1,0:T(8,128)(2,1)S(1)}, u32[]{:S(2)}, u32[]{:S(2)}) collective-permute-start(bf16[1024,128]{1,0:T(8,128)(2,1)S(1)} %order.2.refs_0_), channel_id=1, source_target_pairs={{0,2},{1,3},{2,0},{3,1},{4,6},{5,7},{6,4},{7,5},{8,10},{9,11},{10,... | collective-permute-start | bytes 786440 | tf_op jit(solution)/shard_map/ppermute | solution.py:37
  32.0 6.5 %collective-permute-start.7 = (bf16[256,128]{1,0:T(8,128)(2,1)S(1)}, bf16[256,128]{1,0:T(8,128)(2,1)S(1)}, u32[]{:S(2)}, u32[]{:S(2)}) collective-permute-start(bf16[256,128]{1,0:T(8,128)(2,1)S(1)} %get-tuple-element.50), channel_id=1, source_target_pairs={{0,4},{4,0},{8,12},{12,8},{16,20},{20,16},{24,28},{28,24},{1,5},{5... | collective-permute-start | bytes 196616 | tf_op jit(solution)/shard_map/ppermute | solution.py:276
  32.8 6.2 %collective-permute-start.8 = (bf16[256,128]{1,0:T(8,128)(2,1)S(1)}, bf16[256,128]{1,0:T(8,128)(2,1)S(1)}, u32[]{:S(2)}, u32[]{:S(2)}) collective-permute-start(bf16[256,128]{1,0:T(8,128)(2,1)S(1)} %get-tuple-element.51), channel_id=1, source_target_pairs={{0,8},{4,12},{8,0},{12,4},{16,24},{20,28},{24,16},{28,20},{1,9},{5... | collective-permute-start | bytes 196616 | tf_op jit(solution)/shard_map/ppermute | solution.py:276
  36.6 6.5 %collective-permute-start.10 = (bf16[256,128]{1,0:T(8,128)(2,1)S(1)}, bf16[256,128]{1,0:T(8,128)(2,1)S(1)}, u32[]{:S(2)}, u32[]{:S(2)}) collective-permute-start(bf16[256,128]{1,0:T(8,128)(2,1)S(1)} %get-tuple-element.53), channel_id=1, source_target_pairs={{0,16},{4,20},{8,24},{12,28},{16,0},{20,4},{24,8},{28,12},{1,17},{... | collective-permute-start | bytes 196616 | tf_op jit(solution)/shard_map/ppermute | solution.py:276
  40.6 6.4 %collective-permute-start.13 = (bf16[256,128]{1,0:T(8,128)(2,1)S(1)}, bf16[256,128]{1,0:T(8,128)(2,1)S(1)}, u32[]{:S(2)}, u32[]{:S(2)}) collective-permute-start(bf16[256,128]{1,0:T(8,128)(2,1)S(1)} %get-tuple-element.56), channel_id=1, source_target_pairs={{0,28},{4,24},{8,20},{12,16},{16,12},{20,8},{24,4},{28,0},{1,29},{... | collective-permute-start | bytes 196616 | tf_op jit(solution)/shard_map/ppermute | solution.py:276
  48.2 7.6 %collective-permute-start.15 = (bf16[1024,128]{1,0:T(8,128)(2,1)S(1)}, bf16[1024,128]{1,0:T(8,128)(2,1)S(1)}, u32[]{:S(2)}, u32[]{:S(2)}) collective-permute-start(bf16[1024,128]{1,0:T(8,128)(2,1)S(1)} %order.3.refs_1_), channel_id=1, source_target_pairs={{0,2},{1,3},{2,0},{3,1},{4,6},{5,7},{6,4},{7,5},{8,10},{9,11},{10,... | collective-permute-start | bytes 786440 | tf_op jit(solution)/shard_map/ppermute | solution.py:37
  48.4 12.7 %collective-permute-start.16 = (bf16[1024,128]{1,0:T(8,128)(2,1)S(1)}, bf16[1024,128]{1,0:T(8,128)(2,1)S(1)}, u32[]{:S(2)}, u32[]{:S(2)}) collective-permute-start(bf16[1024,128]{1,0:T(8,128)(2,1)S(1)} %order.2.refs_0_), channel_id=1, source_target_pairs={{0,1},{1,0},{2,3},{3,2},{4,5},{5,4},{6,7},{7,6},{8,9},{9,8},{10,11... | collective-permute-start | bytes 786440 | tf_op jit(solution)/shard_map/ppermute | solution.py:37
  55.3 5.9 %collective-permute-start.17 = (bf16[1024,128]{1,0:T(8,128)(2,1)S(1)}, bf16[1024,128]{1,0:T(8,128)(2,1)S(1)}, u32[]{:S(2)}, u32[]{:S(2)}) collective-permute-start(bf16[1024,128]{1,0:T(8,128)(2,1)S(1)} %order.3.refs_1_), channel_id=1, source_target_pairs={{0,1},{1,0},{2,3},{3,2},{4,5},{5,4},{6,7},{7,6},{8,9},{9,8},{10,11... | collective-permute-start | bytes 786440 | tf_op jit(solution)/shard_map/ppermute | solution.py:37
  55.8 6.5 %collective-permute-start.19 = (bf16[1024,128]{1,0:T(8,128)(2,1)S(1)}, bf16[1024,128]{1,0:T(8,128)(2,1)S(1)}, u32[]{:S(2)}, u32[]{:S(2)}) collective-permute-start(bf16[1024,128]{1,0:T(8,128)(2,1)S(1)} %collective-permute-done.15.refs_3_.refs_10_), channel_id=1, source_target_pairs={{0,1},{1,0},{2,3},{3,2},{4,5},{5,4},{6,7},{7,6},{8,9},{9,8},{10,11... | collective-permute-start | bytes 786440 | tf_op jit(solution)/shard_map/ppermute | solution.py:37
  66.2 7.6 %collective-permute-start.21 = (bf16[256,512]{1,0:T(8,128)(2,1)S(1)}, bf16[256,512]{1,0:T(8,128)(2,1)S(1)}, u32[]{:S(2)}, u32[]{:S(2)}) collective-permute-start(bf16[256,512]{1,0:T(8,128)(2,1)S(1)} %get-tuple-element.61.refs_10_), channel_id=1, source_target_pairs={{0,2},{1,3},{2,0},{3,1},{4,6},{5,7},{6,4},{7,5},{8,10},{9,11},{10,... | collective-permute-start | bytes 786440 | tf_op jit(solution)/shard_map/ppermute | solution.py:37
  68.1 16.3 %collective-permute-start.27 = (bf16[256,512]{1,0:T(8,128)(2,1)S(1)}, bf16[256,512]{1,0:T(8,128)(2,1)S(1)}, u32[]{:S(2)}, u32[]{:S(2)}) collective-permute-start(bf16[256,512]{1,0:T(8,128)(2,1)S(1)} %get-tuple-element.63.refs_2_), channel_id=1, source_target_pairs={{0,1},{1,0},{2,3},{3,2},{4,5},{5,4},{6,7},{7,6},{8,9},{9,8},{10,11... | collective-permute-start | bytes 786440 | tf_op jit(solution)/shard_map/ppermute | solution.py:37
  68.9 15.9 %collective-permute-start.26 = (bf16[256,512]{1,0:T(8,128)(2,1)S(1)}, bf16[256,512]{1,0:T(8,128)(2,1)S(1)}, u32[]{:S(2)}, u32[]{:S(2)}) collective-permute-start(bf16[256,512]{1,0:T(8,128)(2,1)S(1)} %get-tuple-element.64.refs_6_), channel_id=1, source_target_pairs={{0,2},{1,3},{2,0},{3,1},{4,6},{5,7},{6,4},{7,5},{8,10},{9,11},{10,... | collective-permute-start | bytes 786440 | tf_op jit(solution)/shard_map/ppermute | solution.py:37
  73.9 12.7 %collective-permute-start.24 = (bf16[256,512]{1,0:T(8,128)(2,1)S(1)}, bf16[256,512]{1,0:T(8,128)(2,1)S(1)}, u32[]{:S(2)}, u32[]{:S(2)}) collective-permute-start(bf16[256,512]{1,0:T(8,128)(2,1)S(1)} %finish.4.refs_10_.refs_0_), channel_id=1, source_target_pairs={{0,1},{1,0},{2,3},{3,2},{4,5},{5,4},{6,7},{7,6},{8,9},{9,8},{10,11... | collective-permute-start | bytes 786440 | tf_op jit(solution)/shard_map/ppermute | solution.py:37
  77.7 10.6 %collective-permute-start.23 = (bf16[256,512]{1,0:T(8,128)(2,1)S(1)}, bf16[256,512]{1,0:T(8,128)(2,1)S(1)}, u32[]{:S(2)}, u32[]{:S(2)}) collective-permute-start(bf16[256,512]{1,0:T(8,128)(2,1)S(1)} %get-tuple-element.66.refs_2_), channel_id=1, source_target_pairs={{0,1},{1,0},{2,3},{3,2},{4,5},{5,4},{6,7},{7,6},{8,9},{9,8},{10,11... | collective-permute-start | bytes 786440 | tf_op jit(solution)/shard_map/ppermute | solution.py:37
  77.9 6.5 %collective-permute-start.25 = (bf16[64,1024]{1,0:T(8,128)(2,1)S(1)}, bf16[64,1024]{1,0:T(8,128)(2,1)S(1)}, u32[]{:S(2)}, u32[]{:S(2)}) collective-permute-start(bf16[64,1024]{1,0:T(8,128)(2,1)S(1)} %get-tuple-element.75), channel_id=1, source_target_pairs={{4,0},{8,4},{12,8},{16,12},{20,16},{24,20},{28,24},{5,1},{9,5},{13... | collective-permute-start | bytes 393224 | tf_op jit(solution)/shard_map/ppermute | solution.py:43
  84.5 8.3 %collective-permute-start.30 = (bf16[256,512]{1,0:T(8,128)(2,1)S(1)}, bf16[256,512]{1,0:T(8,128)(2,1)S(1)}, u32[]{:S(2)}, u32[]{:S(2)}) collective-permute-start(bf16[256,512]{1,0:T(8,128)(2,1)S(1)} %get-tuple-element.69.refs_6_), channel_id=1, source_target_pairs={{0,2},{1,3},{2,0},{3,1},{4,6},{5,7},{6,4},{7,5},{8,10},{9,11},{10,... | collective-permute-start | bytes 786440 | tf_op jit(solution)/shard_map/ppermute | solution.py:37
  84.9 10.2 %collective-permute-start.29 = (bf16[256,512]{1,0:T(8,128)(2,1)S(1)}, bf16[256,512]{1,0:T(8,128)(2,1)S(1)}, u32[]{:S(2)}, u32[]{:S(2)}) collective-permute-start(bf16[256,512]{1,0:T(8,128)(2,1)S(1)} %finish.5.refs_5_.refs_0_), channel_id=1, source_target_pairs={{0,1},{1,0},{2,3},{3,2},{4,5},{5,4},{6,7},{7,6},{8,9},{9,8},{10,11... | collective-permute-start | bytes 786440 | tf_op jit(solution)/shard_map/ppermute | solution.py:37
  88.4 8.5 %collective-permute-start.28 = (bf16[256,512]{1,0:T(8,128)(2,1)S(1)}, bf16[256,512]{1,0:T(8,128)(2,1)S(1)}, u32[]{:S(2)}, u32[]{:S(2)}) collective-permute-start(bf16[256,512]{1,0:T(8,128)(2,1)S(1)} %get-tuple-element.71.refs_6_), channel_id=1, source_target_pairs={{0,2},{1,3},{2,0},{3,1},{4,6},{5,7},{6,4},{7,5},{8,10},{9,11},{10,... | collective-permute-start | bytes 786440 | tf_op jit(solution)/shard_map/ppermute | solution.py:37
  89.7 7.1 %collective-permute-start.31 = (bf16[64,1024]{1,0:T(8,128)(2,1)S(1)}, bf16[64,1024]{1,0:T(8,128)(2,1)S(1)}, u32[]{:S(2)}, u32[]{:S(2)}) collective-permute-start(bf16[64,1024]{1,0:T(8,128)(2,1)S(1)} %attend.3.refs_2_.refs_8_), channel_id=1, source_target_pairs={{0,4},{4,8},{8,12},{12,16},{16,20},{20,24},{24,28},{1,5},{5,9},{9,... | collective-permute-start | bytes 393224 | tf_op jit(solution)/shard_map/ppermute | solution.py:43
  93.0 6.1 %collective-permute-start.33 = (bf16[256,512]{1,0:T(8,128)(2,1)S(1)}, bf16[256,512]{1,0:T(8,128)(2,1)S(1)}, u32[]{:S(2)}, u32[]{:S(2)}) collective-permute-start(bf16[256,512]{1,0:T(8,128)(2,1)S(1)} %finish.6.refs_5_.refs_0_), channel_id=1, source_target_pairs={{0,1},{1,0},{2,3},{3,2},{4,5},{5,4},{6,7},{7,6},{8,9},{9,8},{10,11... | collective-permute-start | bytes 786440 | tf_op jit(solution)/shard_map/ppermute | solution.py:37
  (17 other events, 160.5 us)

commit v4 on v2

--- a/solution.py
+++ b/solution.py
@@ -15,9 +15,10 @@
 BF16 = jnp.bfloat16
 
 
-def call(body, outs, name, used=None, after=()):
+def call(body, outs, name, used, after=(), flops=1024, **extra):
     vmem = pl.BlockSpec(memory_space=pltpu.VMEM)
     unread = pl.BlockSpec(memory_space=pl.ANY)
+    in_specs = extra.pop("in_specs", [vmem] * len(used))
 
     def without_after(*refs):
         body(*refs[: len(used)], *refs[len(used) + len(after) :])
@@ -25,10 +26,11 @@
     return pl.pallas_call(
         without_after,
         out_shape=outs,
-        in_specs=[vmem] * len(used) + [unread] * len(after),
+        in_specs=in_specs + [unread] * len(after),
         compiler_params=pltpu.CompilerParams(vmem_limit_bytes=VMEM_LIMIT),
-        cost_estimate=pl.CostEstimate(flops=1024, bytes_accessed=1024, transcendentals=0),
+        cost_estimate=pl.CostEstimate(flops=flops, bytes_accessed=1024, transcendentals=0),
         name=name,
+        **extra,
     )(*used, *after)
 
 
@@ -100,15 +102,22 @@
         ).astype(BF16)
 
 
-def order_body(plan, slot_ref, rows_ref, *out_refs):
+def mark_body(out_ref):
+    out_ref[...] = jnp.zeros_like(out_ref)
+
+
+def head_body(queries_ref, out_ref):
+    out_ref[...] = queries_ref[: out_ref.shape[0], :]
+
+
+def order_body(groups, slot_ref, rows_ref, out_ref):
     rows = rows_ref[...]
-    for groups, out_ref in zip(plan, out_refs):
-        count = out_ref.shape[0] // len(groups)
-        for at, g in enumerate(groups):
-            picked = one_hot(slot_ref[g * count : (g + 1) * count, :], rows.shape[0])
-            out_ref[at * count : (at + 1) * count, :] = jnp.dot(
-                picked, rows, preferred_element_type=F32
-            ).astype(BF16)
+    count = out_ref.shape[0] // len(groups)
+    for at, g in enumerate(groups):
+        picked = one_hot(slot_ref[g * count : (g + 1) * count, :], rows.shape[0])
+        out_ref[at * count : (at + 1) * count, :] = jnp.dot(
+            picked, rows, preferred_element_type=F32
+        ).astype(BF16)
 
 
 def block_rows(ref, index, width):
@@ -199,20 +208,39 @@
         out_ref[:, at * HEAD_WIDTH : (at + 1) * HEAD_WIDTH] = part.astype(BF16)
 
 
+def one_up(refs, cols, rows):
+    tall = jnp.concatenate([ref[:, cols].astype(F32) for ref in refs], axis=0)
+    return pltpu.roll(tall, tall.shape[0] - 1, 0)[:rows].astype(BF16)
+
+
+def attend_before_body(
+    mine_ref, other_ref, w_key_ref, w_value_ref, q_ref, *refs
+):
+    earlier, (window_ref, out_hbm, rows_ref, sem) = refs[:-4], refs[-4:]
+    for at, part in enumerate(attended(mine_ref, other_ref, w_key_ref, w_value_ref, q_ref)):
+        cols = slice(at * HEAD_WIDTH, (at + 1) * HEAD_WIDTH)
+        window_ref[:, cols] = part.astype(BF16)
+        rows_ref[:, cols] = one_up((*earlier, window_ref), cols, rows_ref.shape[0])
+    copy = pltpu.make_async_copy(rows_ref, out_hbm.at[pl.ds(0, rows_ref.shape[0]), :], sem)
+    copy.start()
+    copy.wait()
+
+
 def attend_last_body(
-    mine_ref, other_ref, w_key_ref, w_value_ref, q_ref, behind_ref, *refs
+    mine_ref, other_ref, w_key_ref, w_value_ref, q_ref, before_ref, after_ref, _, out_hbm, window_ref, rows_ref, sem
 ):
-    before, last_ref, out_ref = refs[:-2], refs[-2], refs[-1]
-    parts = attended(mine_ref, other_ref, w_key_ref, w_value_ref, q_ref)
-    for at, part in enumerate(parts):
+    count = rows_ref.shape[0]
+    edge = (count - window_ref.shape[0])
+    for at, part in enumerate(attended(mine_ref, other_ref, w_key_ref, w_value_ref, q_ref)):
         cols = slice(at * HEAD_WIDTH, (at + 1) * HEAD_WIDTH)
-        part = part.astype(BF16).astype(F32)
-        stack = [behind_ref[:, cols].astype(F32)]
-        stack += [ref[:, cols].astype(F32) for ref in before]
-        stack += [part, last_ref[:, cols].astype(F32)]
-        tall = jnp.concatenate(stack, axis=0)
-        moved = pltpu.roll(tall, tall.shape[0] - 1, 0)
-        out_ref[:, cols] = moved[: out_ref.shape[0]].astype(BF16)
+        window_ref[:, cols] = part.astype(BF16)
+        pieces = (before_ref.at[pl.ds(GROUP - edge, edge), :], window_ref, after_ref.at[pl.ds(0, edge), :])
+        rows_ref[:, cols] = one_up(pieces, cols, count)
+    copy = pltpu.make_async_copy(
+        rows_ref, out_hbm.at[pl.ds(out_hbm.shape[0] - count, count), :], sem
+    )
+    copy.start()
+    copy.wait()
 
 
 def per_device(queries, vocab_rows, neighbour_ids, w_in, w_out, w_key, w_value):
@@ -226,13 +254,12 @@
     slots = seq_size * cap
     sds = jax.ShapeDtypeStruct
 
-    next_q = shifted(queries[:GROUP], -1)
-
     wanted, slot = call(
         functools.partial(route_body, voc, cap),
         (sds((seq_size, cap), jnp.int32), sds((rows, LANES), jnp.int32)),
         "route",
         (neighbour_ids.reshape(1, rows),),
+        flops=8 * 10**9,
     )
     request = lax.all_to_all(wanted, "seq", split_axis=0, concat_axis=0, tiled=True)
     found = call(
@@ -240,33 +267,36 @@
         sds((slots, width), BF16),
         "fetch",
         (request.reshape(1, slots), vocab_rows),
-        (next_q,),
     )
     answered = lax.all_to_all(
         found.reshape(seq_size, cap, width), "seq", split_axis=0, concat_axis=0, tiled=True
     ).reshape(slots, width)
     order = [groups - 1] + list(range(groups - 1))
-    plan = [order[at : at + 2] for at in range(0, groups, 2)]
-    own = call(
-        functools.partial(order_body, plan),
-        tuple(sds((len(part) * per_group, width), BF16) for part in plan),
-        "order",
-        (slot, answered),
-    )
-
+    plan = [order[:1], order[1:2], order[2:]]
+    emb, first, window = {}, {}, {}
+    token = slot
+    ahead = []
+    for part in plan:
+        e0 = token = call(
+            functools.partial(order_body, part),
+            sds((len(part) * per_group, width), BF16),
+            "order",
+            (slot, answered),
+            (token,),
+        )
+        e2 = exchange(e0, 2)
+        pieces = e0, e2, exchange(e0, 1), exchange(e2, 1)
+        ahead.append(e2)
+        for at, g in enumerate(part):
+            emb[g], first[g] = pieces, at * per_group
+
+    head = call(head_body, sds((GROUP, head_cols), BF16), "head", (queries,), (token,))
+    next_q = shifted(head, -1)
     local_q = jnp.concatenate([queries[GROUP - 1 :], next_q[: GROUP - 1]], axis=0)
     half = sds((per_group, 2 * width), BF16)
     whole = sds((per_group, 2 * width), F32)
-    emb, first, window = {}, {}, {}
     fed, summed, far, encoded = {}, {}, {}, {}
-    behind = None
-    token = slot
-
-    for part, e0 in zip(plan, own):
-        e2 = exchange(e0, 2)
-        pieces = e0, e2, exchange(e0, 1), exchange(e2, 1)
-        for at, g in enumerate(part):
-            emb[g], first[g] = pieces, at * per_group
+    behind = out = None
 
     def feed(g):
         nonlocal token
@@ -279,6 +309,11 @@
         )
         fed[g] = keep, exchange(token, 1)
 
+    def pause(g):
+        nonlocal token
+        if g == order[0]:
+            token = call(mark_body, sds((8, LANES), F32), "mark", (), (token, ahead[-1]))
+
     def add(g):
         nonlocal token
         summed[g], token = call(add_body, (whole, half), "add", fed[g], (token,))
@@ -291,33 +326,52 @@
             half,
             "finish",
             (*emb[g][:2], summed[g], far[g]),
-            (token, behind) if g == order[-1] else (token,),
+            (token, *{order[0]: (next_q,), order[-1]: (behind,)}.get(g, ())),
         )
         encoded[g] = token, exchange(token, 1)
 
     def attend(g):
-        nonlocal token, behind
+        nonlocal token, behind, out
         args = (*encoded[g], w_key, w_value, local_q[g * GROUP : (g + 1) * GROUP])
+        piece = sds((GROUP, head_cols), BF16)
+        edge = 16
+        last_rows = GROUP + edge
+        vmem, hbm = pl.BlockSpec(memory_space=pltpu.VMEM), pl.BlockSpec(memory_space=pl.ANY)
+
+        def scratch(count):
+            return [pltpu.VMEM((count, head_cols), BF16), pltpu.SemaphoreType.DMA]
+
         if g == order[-1]:
-            before = [window[at] for at in order[1:-1]]
-            return call(
+            out = call(
                 attend_last_body,
                 sds((tok, head_cols), BF16),
                 "attend_last",
-                (*args, behind, *before, window[groups - 1]),
+                (*args, window[order[-2]], window[order[0]], out),
+                in_specs=[vmem] * (len(args) + 2) + [hbm],
+                out_specs=hbm,
+                scratch_shapes=[pltpu.VMEM((GROUP, head_cols), BF16), *scratch(last_rows)],
+                input_output_aliases={len(args) + 2: 0},
             )
-        window[g] = token = call(
-            attend_body, sds((GROUP, head_cols), BF16), "attend", args, (token,)
-        )
-        if g == groups - 1:
-            behind = shifted(token, 1)
-        return None
-
-    out = None
+        elif g == order[-2]:
+            window[g], out = call(
+                attend_before_body,
+                (piece, sds((tok, head_cols), BF16)),
+                "attend_before",
+                (*args, behind, *[window[at] for at in order[1:-2]]),
+                (token,),
+                out_specs=(vmem, hbm),
+                scratch_shapes=scratch(tok - last_rows),
+            )
+            token = window[g]
+        else:
+            window[g] = token = call(attend_body, piece, "attend", args, (token,))
+            if g == order[0]:
+                behind = shifted(token, 1)
+
     for stage in range(groups + 4):
-        for step, lag in ((finish, 3), (attend, 4), (feed, 0), (add, 1)):
+        for step, lag in ((finish, 3), (attend, 4), (feed, 0), (pause, 1), (add, 1)):
             if 0 <= stage - lag < groups:
-                out = step(order[stage - lag])
+                step(order[stage - lag])
     return out
 
 

time: 98.8 us -> 97.7 us (0.989)
  local copies, waits for them, and re-layouts: 3.26 us -> 0.92 us
  blocking collectives: 39.6 us -> 38.6 us
    ppermute x2, waiting for transfers between devices: 0.03 us -> 2.53 us  [shifted(): return lax.ppermute(x, 'seq', pairs)]
    ppermute x18 -> x21, waiting for transfers between devices: 11.6 us -> 9.91 us  [exchange(): return lax.ppermute(x, 'tp', [(i, i ^ bit) for i in range(size)])]
    unnamed x14, local copies, waits for them, and re-layouts: 1.94 us -> 0.72 us
    slice x1, local copies, waits for them, and re-layouts: 1.21 us -> 0.1 us  [attend(): args = (*encoded[g], w_key, w_value, local_q[g * GROUP:(g + 1) * GROUP])]
    pallas_call x19 -> x23, Pallas kernels: 19.1 us -> 20 us  [call(): pl.pallas_call(without_after, out_shape=outs, in_specs=in_specs + [unread...]
    ppermute x18 -> x21, starting transfers between devices: 20.1 us -> 19.9 us  [exchange(): return lax.ppermute(x, 'tp', [(i, i ^ bit) for i in range(size)])]
  transfers between devices with their start and end apart: 20 -> 23, of which waited for: 4 -> 6; matrix products, arithmetic and copies ran while one was open for 0% -> 0% of each run, Pallas kernels for 13% -> 14%
where the time goes in v4:
time: 97.7 us; the launch traced here: 97 us
  blocking collectives  38.6 us (40%)
  starting transfers between devices  24.5 us (25%)
  Pallas kernels  20 us (20%)
  waiting for transfers between devices  12.4 us (13%)
    all_to_all x1, blocking collectives, per_device(): lax.all_to_all(found.reshape(seq_size, cap, width), 'seq', split_axis=0,...  27.1 us
    pallas_call x23, Pallas kernels, call(): pl.pallas_call(without_after, out_shape=outs, in_specs=in_specs + [unread...  20 us
    ppermute x21, starting transfers between devices, exchange(): return lax.ppermute(x, 'tp', [(i, i ^ bit) for i in range(size)])  19.9 us
    all_to_all x1, blocking collectives, per_device(): lax.all_to_all(wanted, 'seq', split_axis=0, concat_axis=0, tiled=True)  11.5 us
    ppermute x21, waiting for transfers between devices, exchange(): return lax.ppermute(x, 'tp', [(i, i ^ bit) for i in range(size)])  9.91 us
    ppermute x2, starting transfers between devices, shifted(): return lax.ppermute(x, 'seq', pairs)  4.54 us
    ppermute x2, waiting for transfers between devices, shifted(): return lax.ppermute(x, 'seq', pairs)  2.53 us
  transfers between devices with their start and end apart: 23, of which 6 were waited for; matrix products, arithmetic and copies ran while one was open for 0% of the time, Pallas kernels for 14%

profile of v4, /device:TPU:1, one launch (start us, length us, event | category | flops | bytes accessed | tf_op | source)
XLA Modules:
  0.0 97.0 jit_solution(5264474443838741964)
XLA Ops:
  1.5 11.5 %all_to_all.14 = s32[8,1,256]{2,1,0:T(1,128)S(1)} all-to-all(s32[8,1,256]{2,1,0:T(1,128)S(1)} %copy.9), channel_id=1, replica_groups=mesh['seq'=8,'tp'=4] {'seq'}, dimensions={0} | all-to-all | bytes 16384 | tf_op jit(solution)/shard_map/all_to_all | solution.py:264
  13.1 2.4 %fetch.1 = bf16[2048,256]{1,0:T(8,128)(2,1)S(1)} custom-call(s32[1,2048]{1,0:T(1,128)S(1)} %bitcast.11, bf16[2048,256]{1,0:T(8,128)(2,1)S(1)} %copy-done.5), custom_call_target="tpu_custom_call" | custom-call | flops 1024 | bytes 1024 | tf_op jit(solution)/shard_map/fetch/pallas_call | solution.py:26
  15.4 27.1 %all_to_all.15 = bf16[8,256,256]{2,1,0:T(8,128)(2,1)S(1)} all-to-all(bf16[8,256,256]{2,1,0:T(8,128)(2,1)S(1)} %bitcast.9), channel_id=1, replica_groups=mesh['seq'=8,'tp'=4] {'seq'}, dimensions={0} | all-to-all | bytes 2097152 | tf_op jit(solution)/shard_map/all_to_all | solution.py:271
  43.0 1.3 %collective-permute-start.3 = (bf16[256,256]{1,0:T(8,128)(2,1)S(1)}, bf16[256,256]{1,0:T(8,128)(2,1)S(1)}, u32[]{:S(2)}, u32[]{:S(2)}) collective-permute-start(bf16[256,256]{1,0:T(8,128)(2,1)S(1)} %order.3.refs_2_.refs_0_), channel_id=1, source_target_pairs={{0,2},{1,3},{2,0},{3,1},{4,6},{5,7},{6,4},{7,5},{8,10},{9,11},{10,... | collective-permute-start | bytes 393224 | tf_op jit(solution)/shard_map/ppermute | solution.py:39
  44.3 2.3 %collective-permute-start.4 = (bf16[256,256]{1,0:T(8,128)(2,1)S(1)}, bf16[256,256]{1,0:T(8,128)(2,1)S(1)}, u32[]{:S(2)}, u32[]{:S(2)}) collective-permute-start(bf16[256,256]{1,0:T(8,128)(2,1)S(1)} %order.3.refs_2_.refs_0_), channel_id=1, source_target_pairs={{0,1},{1,0},{2,3},{3,2},{4,5},{5,4},{6,7},{7,6},{8,9},{9,8},{10,11... | collective-permute-start | bytes 393224 | tf_op jit(solution)/shard_map/ppermute | solution.py:39
  46.9 3.2 %collective-permute-start.5 = (bf16[256,256]{1,0:T(8,128)(2,1)S(1)}, bf16[256,256]{1,0:T(8,128)(2,1)S(1)}, u32[]{:S(2)}, u32[]{:S(2)}) collective-permute-start(bf16[256,256]{1,0:T(8,128)(2,1)S(1)} %collective-permute-done.3.refs_1_), channel_id=1, source_target_pairs={{0,1},{1,0},{2,3},{3,2},{4,5},{5,4},{6,7},{7,6},{8,9},{9,8},{10,11... | collective-permute-start | bytes 393224 | tf_op jit(solution)/shard_map/ppermute | solution.py:39
  51.2 1.3 %collective-permute-start = (bf16[512,256]{1,0:T(8,128)(2,1)S(1)}, bf16[512,256]{1,0:T(8,128)(2,1)S(1)}, u32[]{:S(2)}, u32[]{:S(2)}) collective-permute-start(bf16[512,256]{1,0:T(8,128)(2,1)S(1)} %order.5.refs_6_.refs_0_.refs_1_), channel_id=1, source_target_pairs={{0,2},{1,3},{2,0},{3,1},{4,6},{5,7},{6,4},{7,5},{8,10},{9,11},{10,... | collective-permute-start | bytes 786440 | tf_op jit(solution)/shard_map/ppermute | solution.py:39
  52.8 1.6 %feed.4 = (f32[256,512]{1,0:T(8,128)S(1)}, bf16[256,512]{1,0:T(8,128)(2,1)S(1)}) custom-call(bf16[256,256]{1,0:T(8,128)(2,1)S(1)} %order.3.refs_2_.refs_0_, bf16[256,256]{1,0:T(8,128)(2,1)S(1)} %collective-permute-done.3.refs_1_, bf16[256,256]{1,0:T(8,128)(2,1)S(1)} %collective-permute-done.4.refs_2_, bf16[256,256]{1,0:T(8,128)(2,1)S(1)} %collective-permute-done.5.refs_3_, ...), custom_call_target="tpu_custom_call" | custom-call | flops 1024 | bytes 1024 | tf_op jit(solution)/shard_map/feed/pallas_call | solution.py:26
  55.1 7.0 %collective-permute-done.7.refs_1_ = bf16[256,256]{1,0:T(8,128)(2,1)S(1)} collective-permute-done((bf16[256,256]{1,0:T(8,128)(2,1)S(1)}, bf16[256,256]{1,0:T(8,128)(2,1)S(1)}, u32[]{:S(2)}, u32[]{:S(2)}) %collective-permute-start.7) | collective-permute-done | bytes 131104 | tf_op jit(solution)/shard_map/ppermute | solution.py:39
  63.8 1.6 %feed.5 = (f32[256,512]{1,0:T(8,128)S(1)}, bf16[256,512]{1,0:T(8,128)(2,1)S(1)}) custom-call(bf16[256,256]{1,0:T(8,128)(2,1)S(1)} %order.4.refs_2_.refs_0_, bf16[256,256]{1,0:T(8,128)(2,1)S(1)} %collective-permute-done.7.refs_1_, bf16[256,256]{1,0:T(8,128)(2,1)S(1)} %collective-permute-done.8.refs_2_, bf16[256,256]{1,0:T(8,128)(2,1)S(1)} %collective-permute-done.9.refs_3_, ...), custom_call_target="tpu_custom_call" | custom-call | flops 1024 | bytes 1024 | tf_op jit(solution)/shard_map/feed/pallas_call | solution.py:26
  65.9 1.3 %collective-permute-start.10 = (bf16[256,512]{1,0:T(8,128)(2,1)S(1)}, bf16[256,512]{1,0:T(8,128)(2,1)S(1)}, u32[]{:S(2)}, u32[]{:S(2)}) collective-permute-start(bf16[256,512]{1,0:T(8,128)(2,1)S(1)} %get-tuple-element.31.refs_6_), channel_id=1, source_target_pairs={{0,2},{1,3},{2,0},{3,1},{4,6},{5,7},{6,4},{7,5},{8,10},{9,11},{10,... | collective-permute-start | bytes 786440 | tf_op jit(solution)/shard_map/ppermute | solution.py:39
  67.3 1.5 %collective-permute-start.12 = (bf16[64,1024]{1,0:T(8,128)(2,1)S(1)}, bf16[64,1024]{1,0:T(8,128)(2,1)S(1)}, u32[]{:S(2)}, u32[]{:S(2)}) collective-permute-start(bf16[64,1024]{1,0:T(8,128)(2,1)S(1)} %head.1), channel_id=1, source_target_pairs={{4,0},{8,4},{12,8},{16,12},{20,16},{24,20},{28,24},{5,1},{9,5},{13... | collective-permute-start | bytes 393224 | tf_op jit(solution)/shard_map/ppermute | solution.py:45
  68.8 1.6 %feed.6 = (f32[256,512]{1,0:T(8,128)S(1)}, bf16[256,512]{1,0:T(8,128)(2,1)S(1)}) custom-call(bf16[512,256]{1,0:T(8,128)(2,1)S(1)} %order.5.refs_6_.refs_0_.refs_1_, bf16[512,256]{1,0:T(8,128)(2,1)S(1)} %collective-permute-done.refs_1_, bf16[512,256]{1,0:T(8,128)(2,1)S(1)} %collective-permute-done.1.refs_2_, ...), custom_call_target="tpu_custom_call" | custom-call | flops 1024 | bytes 1024 | tf_op jit(solution)/shard_map/feed/pallas_call | solution.py:26
  71.3 2.5 %collective-permute-done.12.refs_5_ = bf16[64,1024]{1,0:T(8,128)(2,1)S(1)} collective-permute-done((bf16[64,1024]{1,0:T(8,128)(2,1)S(1)}, bf16[64,1024]{1,0:T(8,128)(2,1)S(1)}, u32[]{:S(2)}, u32[]{:S(2)}) %collective-permute-start.12) | collective-permute-done | bytes 131104 | tf_op jit(solution)/shard_map/ppermute | solution.py:45
  73.9 1.6 %collective-permute-start.14 = (bf16[256,512]{1,0:T(8,128)(2,1)S(1)}, bf16[256,512]{1,0:T(8,128)(2,1)S(1)}, u32[]{:S(2)}, u32[]{:S(2)}) collective-permute-start(bf16[256,512]{1,0:T(8,128)(2,1)S(1)} %finish.4.refs_6_.refs_0_), channel_id=1, source_target_pairs={{0,1},{1,0},{2,3},{3,2},{4,5},{5,4},{6,7},{7,6},{8,9},{9,8},{10,11... | collective-permute-start | bytes 786440 | tf_op jit(solution)/shard_map/ppermute | solution.py:39
  75.4 1.6 %feed.7 = (f32[256,512]{1,0:T(8,128)S(1)}, bf16[256,512]{1,0:T(8,128)(2,1)S(1)}) custom-call(bf16[512,256]{1,0:T(8,128)(2,1)S(1)} %order.5.refs_6_.refs_0_.refs_1_, bf16[512,256]{1,0:T(8,128)(2,1)S(1)} %collective-permute-done.refs_1_, bf16[512,256]{1,0:T(8,128)(2,1)S(1)} %collective-permute-done.1.refs_2_, ...), custom_call_target="tpu_custom_call" | custom-call | flops 1024 | bytes 1024 | tf_op jit(solution)/shard_map/feed/pallas_call | solution.py:26
  77.4 1.3 %collective-permute-start.19 = (bf16[256,512]{1,0:T(8,128)(2,1)S(1)}, bf16[256,512]{1,0:T(8,128)(2,1)S(1)}, u32[]{:S(2)}, u32[]{:S(2)}) collective-permute-start(bf16[256,512]{1,0:T(8,128)(2,1)S(1)} %get-tuple-element.39.refs_4_), channel_id=1, source_target_pairs={{0,2},{1,3},{2,0},{3,1},{4,6},{5,7},{6,4},{7,5},{8,10},{9,11},{10,... | collective-permute-start | bytes 786440 | tf_op jit(solution)/shard_map/ppermute | solution.py:39
  80.5 1.7 %attend.2.refs_2_.refs_6_ = bf16[64,1024]{1,0:T(8,128)(2,1)S(1)} custom-call(bf16[256,512]{1,0:T(8,128)(2,1)S(1)} %finish.4.refs_6_.refs_0_, bf16[256,512]{1,0:T(8,128)(2,1)S(1)} %collective-permute-done.14.refs_1_, bf16[1024,1024]{1,0:T(8,128)(2,1)S(1)} %copy-done.2, bf16[1024,1024]{1,0:T(8,128)(2,1)S(1)} %copy-done.3, ...), custom_call_target="tpu_custom_call" | custom-call | flops 1024 | bytes 1024 | tf_op jit(solution)/shard_map/attend/pallas_call | solution.py:26
  82.3 1.3 %collective-permute-start.17 = (bf16[256,512]{1,0:T(8,128)(2,1)S(1)}, bf16[256,512]{1,0:T(8,128)(2,1)S(1)}, u32[]{:S(2)}, u32[]{:S(2)}) collective-permute-start(bf16[256,512]{1,0:T(8,128)(2,1)S(1)} %get-tuple-element.41.refs_4_), channel_id=1, source_target_pairs={{0,2},{1,3},{2,0},{3,1},{4,6},{5,7},{6,4},{7,5},{8,10},{9,11},{10,... | collective-permute-start | bytes 786440 | tf_op jit(solution)/shard_map/ppermute | solution.py:39
  83.6 3.1 %collective-permute-start.20 = (bf16[64,1024]{1,0:T(8,128)(2,1)S(1)}, bf16[64,1024]{1,0:T(8,128)(2,1)S(1)}, u32[]{:S(2)}, u32[]{:S(2)}) collective-permute-start(bf16[64,1024]{1,0:T(8,128)(2,1)S(1)} %attend.2.refs_2_.refs_6_), channel_id=1, source_target_pairs={{0,4},{4,8},{8,12},{12,16},{16,20},{20,24},{24,28},{1,5},{5,9},{9,... | collective-permute-start | bytes 393224 | tf_op jit(solution)/shard_map/ppermute | solution.py:45
  87.5 1.7 %attend.3.refs_4_.refs_6_ = bf16[64,1024]{1,0:T(8,128)(2,1)S(1)} custom-call(bf16[256,512]{1,0:T(8,128)(2,1)S(1)} %finish.5.refs_5_.refs_0_, bf16[256,512]{1,0:T(8,128)(2,1)S(1)} %collective-permute-done.18.refs_1_, bf16[1024,1024]{1,0:T(8,128)(2,1)S(1)} %copy-done.2, bf16[1024,1024]{1,0:T(8,128)(2,1)S(1)} %copy-done.3, ...), custom_call_target="tpu_custom_call" | custom-call | flops 1024 | bytes 1024 | tf_op jit(solution)/shard_map/attend/pallas_call | solution.py:26
  89.3 1.5 %collective-permute-done.17.refs_3_ = bf16[256,512]{1,0:T(8,128)(2,1)S(1)} collective-permute-done((bf16[256,512]{1,0:T(8,128)(2,1)S(1)}, bf16[256,512]{1,0:T(8,128)(2,1)S(1)}, u32[]{:S(2)}, u32[]{:S(2)}) %collective-permute-start.17) | collective-permute-done | bytes 262176 | tf_op jit(solution)/shard_map/ppermute | solution.py:39
  92.0 2.5 %attend_before.1 = (bf16[64,1024]{1,0:T(8,128)(2,1)S(1)}, bf16[256,1024]{1,0:T(8,128)(2,1)}) custom-call(bf16[256,512]{1,0:T(8,128)(2,1)S(1)} %finish.6.refs_5_.refs_0_, bf16[256,512]{1,0:T(8,128)(2,1)S(1)} %collective-permute-done.22.refs_1_, bf16[1024,1024]{1,0:T(8,128)(2,1)S(1)} %copy-done.2, bf16[1024,1024]{1,0:T(8,128)(2,1)S(1)} %copy-done.3, ...), custom_call_target="tpu_custom_call" | custom-call | flops 1024 | bytes 1024 | tf_op jit(solution)/shard_map/attend_before/pallas_call | solution.py:26
  94.5 2.4 %attend_last.1 = bf16[256,1024]{1,0:T(8,128)(2,1)} custom-call(bf16[256,512]{1,0:T(8,128)(2,1)S(1)} %finish.7.refs_7_.refs_0_, bf16[256,512]{1,0:T(8,128)(2,1)S(1)} %collective-permute-done.21.refs_1_, bf16[1024,1024]{1,0:T(8,128)(2,1)S(1)} %copy-done.2, bf16[1024,1024]{1,0:T(8,128)(2,1)S(1)} %copy-done.3, ...), custom_call_target="tpu_custom_call", output_to_operand_aliasing={{}: (7, {})} | custom-call | flops 1024 | bytes 1024 | tf_op jit(solution)/shard_map/attend_last/pallas_call | solution.py:26
  (65 shorter events, 11.8 us)
Async XLA Ops:
  43.0 3.9 %collective-permute-start.3 = (bf16[256,256]{1,0:T(8,128)(2,1)S(1)}, bf16[256,256]{1,0:T(8,128)(2,1)S(1)}, u32[]{:S(2)}, u32[]{:S(2)}) collective-permute-start(bf16[256,256]{1,0:T(8,128)(2,1)S(1)} %order.3.refs_2_.refs_0_), channel_id=1, source_target_pairs={{0,2},{1,3},{2,0},{3,1},{4,6},{5,7},{6,4},{7,5},{8,10},{9,11},{10,... | collective-permute-start | bytes 393224 | tf_op jit(solution)/shard_map/ppermute | solution.py:39
  44.3 8.5 %collective-permute-start.4 = (bf16[256,256]{1,0:T(8,128)(2,1)S(1)}, bf16[256,256]{1,0:T(8,128)(2,1)S(1)}, u32[]{:S(2)}, u32[]{:S(2)}) collective-permute-start(bf16[256,256]{1,0:T(8,128)(2,1)S(1)} %order.3.refs_2_.refs_0_), channel_id=1, source_target_pairs={{0,1},{1,0},{2,3},{3,2},{4,5},{5,4},{6,7},{7,6},{8,9},{9,8},{10,11... | collective-permute-start | bytes 393224 | tf_op jit(solution)/shard_map/ppermute | solution.py:39
  46.9 5.9 %collective-permute-start.5 = (bf16[256,256]{1,0:T(8,128)(2,1)S(1)}, bf16[256,256]{1,0:T(8,128)(2,1)S(1)}, u32[]{:S(2)}, u32[]{:S(2)}) collective-permute-start(bf16[256,256]{1,0:T(8,128)(2,1)S(1)} %collective-permute-done.3.refs_1_), channel_id=1, source_target_pairs={{0,1},{1,0},{2,3},{3,2},{4,5},{5,4},{6,7},{7,6},{8,9},{9,8},{10,11... | collective-permute-start | bytes 393224 | tf_op jit(solution)/shard_map/ppermute | solution.py:39
  51.2 11.6 %collective-permute-start = (bf16[512,256]{1,0:T(8,128)(2,1)S(1)}, bf16[512,256]{1,0:T(8,128)(2,1)S(1)}, u32[]{:S(2)}, u32[]{:S(2)}) collective-permute-start(bf16[512,256]{1,0:T(8,128)(2,1)S(1)} %order.5.refs_6_.refs_0_.refs_1_), channel_id=1, source_target_pairs={{0,2},{1,3},{2,0},{3,1},{4,6},{5,7},{6,4},{7,5},{8,10},{9,11},{10,... | collective-permute-start | bytes 786440 | tf_op jit(solution)/shard_map/ppermute | solution.py:39
  52.5 9.5 %collective-permute-start.7 = (bf16[256,256]{1,0:T(8,128)(2,1)S(1)}, bf16[256,256]{1,0:T(8,128)(2,1)S(1)}, u32[]{:S(2)}, u32[]{:S(2)}) collective-permute-start(bf16[256,256]{1,0:T(8,128)(2,1)S(1)} %order.4.refs_2_.refs_0_), channel_id=1, source_target_pairs={{0,2},{1,3},{2,0},{3,1},{4,6},{5,7},{6,4},{7,5},{8,10},{9,11},{10,... | collective-permute-start | bytes 393224 | tf_op jit(solution)/shard_map/ppermute | solution.py:39
  54.4 12.8 %copy-start.4 = (bf16[256,1024]{1,0:T(8,128)(2,1)S(1)}, bf16[256,1024]{1,0:T(8,128)(2,1)}, u32[]{:S(2)}) copy-start(bf16[256,1024]{1,0:T(8,128)(2,1)} %refs_0_.1) | copy-start | bytes 1572868
  54.4 11.4 %collective-permute-start.6 = (bf16[256,512]{1,0:T(8,128)(2,1)S(1)}, bf16[256,512]{1,0:T(8,128)(2,1)S(1)}, u32[]{:S(2)}, u32[]{:S(2)}) collective-permute-start(bf16[256,512]{1,0:T(8,128)(2,1)S(1)} %get-tuple-element.28.refs_6_), channel_id=1, source_target_pairs={{0,1},{1,0},{2,3},{3,2},{4,5},{5,4},{6,7},{7,6},{8,9},{9,8},{10,11... | collective-permute-start | bytes 786440 | tf_op jit(solution)/shard_map/ppermute | solution.py:39
  55.0 8.3 %collective-permute-start.8 = (bf16[256,256]{1,0:T(8,128)(2,1)S(1)}, bf16[256,256]{1,0:T(8,128)(2,1)S(1)}, u32[]{:S(2)}, u32[]{:S(2)}) collective-permute-start(bf16[256,256]{1,0:T(8,128)(2,1)S(1)} %order.4.refs_2_.refs_0_), channel_id=1, source_target_pairs={{0,1},{1,0},{2,3},{3,2},{4,5},{5,4},{6,7},{7,6},{8,9},{9,8},{10,11... | collective-permute-start | bytes 393224 | tf_op jit(solution)/shard_map/ppermute | solution.py:39
  62.1 1.8 %collective-permute-start.9 = (bf16[256,256]{1,0:T(8,128)(2,1)S(1)}, bf16[256,256]{1,0:T(8,128)(2,1)S(1)}, u32[]{:S(2)}, u32[]{:S(2)}) collective-permute-start(bf16[256,256]{1,0:T(8,128)(2,1)S(1)} %collective-permute-done.7.refs_1_), channel_id=1, source_target_pairs={{0,1},{1,0},{2,3},{3,2},{4,5},{5,4},{6,7},{7,6},{8,9},{9,8},{10,11... | collective-permute-start | bytes 393224 | tf_op jit(solution)/shard_map/ppermute | solution.py:39
  62.8 5.9 %collective-permute-start.1 = (bf16[512,256]{1,0:T(8,128)(2,1)S(1)}, bf16[512,256]{1,0:T(8,128)(2,1)S(1)}, u32[]{:S(2)}, u32[]{:S(2)}) collective-permute-start(bf16[512,256]{1,0:T(8,128)(2,1)S(1)} %order.5.refs_6_.refs_0_.refs_1_), channel_id=1, source_target_pairs={{0,1},{1,0},{2,3},{3,2},{4,5},{5,4},{6,7},{7,6},{8,9},{9,8},{10,11... | collective-permute-start | bytes 786440 | tf_op jit(solution)/shard_map/ppermute | solution.py:39
  62.8 5.9 %collective-permute-start.2 = (bf16[512,256]{1,0:T(8,128)(2,1)S(1)}, bf16[512,256]{1,0:T(8,128)(2,1)S(1)}, u32[]{:S(2)}, u32[]{:S(2)}) collective-permute-start(bf16[512,256]{1,0:T(8,128)(2,1)S(1)} %collective-permute-done.refs_1_), channel_id=1, source_target_pairs={{0,1},{1,0},{2,3},{3,2},{4,5},{5,4},{6,7},{7,6},{8,9},{9,8},{10,11... | collective-permute-start | bytes 786440 | tf_op jit(solution)/shard_map/ppermute | solution.py:39
  65.4 5.5 %collective-permute-start.11 = (bf16[256,512]{1,0:T(8,128)(2,1)S(1)}, bf16[256,512]{1,0:T(8,128)(2,1)S(1)}, u32[]{:S(2)}, u32[]{:S(2)}) collective-permute-start(bf16[256,512]{1,0:T(8,128)(2,1)S(1)} %get-tuple-element.29.refs_0_), channel_id=1, source_target_pairs={{0,1},{1,0},{2,3},{3,2},{4,5},{5,4},{6,7},{7,6},{8,9},{9,8},{10,11... | collective-permute-start | bytes 786440 | tf_op jit(solution)/shard_map/ppermute | solution.py:39
  65.9 7.9 %collective-permute-start.10 = (bf16[256,512]{1,0:T(8,128)(2,1)S(1)}, bf16[256,512]{1,0:T(8,128)(2,1)S(1)}, u32[]{:S(2)}, u32[]{:S(2)}) collective-permute-start(bf16[256,512]{1,0:T(8,128)(2,1)S(1)} %get-tuple-element.31.refs_6_), channel_id=1, source_target_pairs={{0,2},{1,3},{2,0},{3,1},{4,6},{5,7},{6,4},{7,5},{8,10},{9,11},{10,... | collective-permute-start | bytes 786440 | tf_op jit(solution)/shard_map/ppermute | solution.py:39
  67.3 6.5 %collective-permute-start.12 = (bf16[64,1024]{1,0:T(8,128)(2,1)S(1)}, bf16[64,1024]{1,0:T(8,128)(2,1)S(1)}, u32[]{:S(2)}, u32[]{:S(2)}) collective-permute-start(bf16[64,1024]{1,0:T(8,128)(2,1)S(1)} %head.1), channel_id=1, source_target_pairs={{4,0},{8,4},{12,8},{16,12},{20,16},{24,20},{28,24},{5,1},{9,5},{13... | collective-permute-start | bytes 393224 | tf_op jit(solution)/shard_map/ppermute | solution.py:45
  70.4 6.9 %collective-permute-start.16 = (bf16[256,512]{1,0:T(8,128)(2,1)S(1)}, bf16[256,512]{1,0:T(8,128)(2,1)S(1)}, u32[]{:S(2)}, u32[]{:S(2)}) collective-permute-start(bf16[256,512]{1,0:T(8,128)(2,1)S(1)} %get-tuple-element.33.refs_2_), channel_id=1, source_target_pairs={{0,1},{1,0},{2,3},{3,2},{4,5},{5,4},{6,7},{7,6},{8,9},{9,8},{10,11... | collective-permute-start | bytes 786440 | tf_op jit(solution)/shard_map/ppermute | solution.py:39
  71.0 8.4 %collective-permute-start.15 = (bf16[256,512]{1,0:T(8,128)(2,1)S(1)}, bf16[256,512]{1,0:T(8,128)(2,1)S(1)}, u32[]{:S(2)}, u32[]{:S(2)}) collective-permute-start(bf16[256,512]{1,0:T(8,128)(2,1)S(1)} %get-tuple-element.34.refs_4_), channel_id=1, source_target_pairs={{0,2},{1,3},{2,0},{3,1},{4,6},{5,7},{6,4},{7,5},{8,10},{9,11},{10,... | collective-permute-start | bytes 786440 | tf_op jit(solution)/shard_map/ppermute | solution.py:39
  73.9 6.6 %collective-permute-start.14 = (bf16[256,512]{1,0:T(8,128)(2,1)S(1)}, bf16[256,512]{1,0:T(8,128)(2,1)S(1)}, u32[]{:S(2)}, u32[]{:S(2)}) collective-permute-start(bf16[256,512]{1,0:T(8,128)(2,1)S(1)} %finish.4.refs_6_.refs_0_), channel_id=1, source_target_pairs={{0,1},{1,0},{2,3},{3,2},{4,5},{5,4},{6,7},{7,6},{8,9},{9,8},{10,11... | collective-permute-start | bytes 786440 | tf_op jit(solution)/shard_map/ppermute | solution.py:39
  77.1 5.1 %collective-permute-start.13 = (bf16[256,512]{1,0:T(8,128)(2,1)S(1)}, bf16[256,512]{1,0:T(8,128)(2,1)S(1)}, u32[]{:S(2)}, u32[]{:S(2)}) collective-permute-start(bf16[256,512]{1,0:T(8,128)(2,1)S(1)} %get-tuple-element.36.refs_2_), channel_id=1, source_target_pairs={{0,1},{1,0},{2,3},{3,2},{4,5},{5,4},{6,7},{7,6},{8,9},{9,8},{10,11... | collective-permute-start | bytes 786440 | tf_op jit(solution)/shard_map/ppermute | solution.py:39
  77.4 9.4 %collective-permute-start.19 = (bf16[256,512]{1,0:T(8,128)(2,1)S(1)}, bf16[256,512]{1,0:T(8,128)(2,1)S(1)}, u32[]{:S(2)}, u32[]{:S(2)}) collective-permute-start(bf16[256,512]{1,0:T(8,128)(2,1)S(1)} %get-tuple-element.39.refs_4_), channel_id=1, source_target_pairs={{0,2},{1,3},{2,0},{3,1},{4,6},{5,7},{6,4},{7,5},{8,10},{9,11},{10,... | collective-permute-start | bytes 786440 | tf_op jit(solution)/shard_map/ppermute | solution.py:39
  79.5 8.1 %collective-permute-start.18 = (bf16[256,512]{1,0:T(8,128)(2,1)S(1)}, bf16[256,512]{1,0:T(8,128)(2,1)S(1)}, u32[]{:S(2)}, u32[]{:S(2)}) collective-permute-start(bf16[256,512]{1,0:T(8,128)(2,1)S(1)} %finish.5.refs_5_.refs_0_), channel_id=1, source_target_pairs={{0,1},{1,0},{2,3},{3,2},{4,5},{5,4},{6,7},{7,6},{8,9},{9,8},{10,11... | collective-permute-start | bytes 786440 | tf_op jit(solution)/shard_map/ppermute | solution.py:39
  82.3 8.5 %collective-permute-start.17 = (bf16[256,512]{1,0:T(8,128)(2,1)S(1)}, bf16[256,512]{1,0:T(8,128)(2,1)S(1)}, u32[]{:S(2)}, u32[]{:S(2)}) collective-permute-start(bf16[256,512]{1,0:T(8,128)(2,1)S(1)} %get-tuple-element.41.refs_4_), channel_id=1, source_target_pairs={{0,2},{1,3},{2,0},{3,1},{4,6},{5,7},{6,4},{7,5},{8,10},{9,11},{10,... | collective-permute-start | bytes 786440 | tf_op jit(solution)/shard_map/ppermute | solution.py:39
  83.6 5.6 %collective-permute-start.20 = (bf16[64,1024]{1,0:T(8,128)(2,1)S(1)}, bf16[64,1024]{1,0:T(8,128)(2,1)S(1)}, u32[]{:S(2)}, u32[]{:S(2)}) collective-permute-start(bf16[64,1024]{1,0:T(8,128)(2,1)S(1)} %attend.2.refs_2_.refs_6_), channel_id=1, source_target_pairs={{0,4},{4,8},{8,12},{12,16},{16,20},{20,24},{24,28},{1,5},{5,9},{9,... | collective-permute-start | bytes 393224 | tf_op jit(solution)/shard_map/ppermute | solution.py:45
  86.9 5.1 %collective-permute-start.22 = (bf16[256,512]{1,0:T(8,128)(2,1)S(1)}, bf16[256,512]{1,0:T(8,128)(2,1)S(1)}, u32[]{:S(2)}, u32[]{:S(2)}) collective-permute-start(bf16[256,512]{1,0:T(8,128)(2,1)S(1)} %finish.6.refs_5_.refs_0_), channel_id=1, source_target_pairs={{0,1},{1,0},{2,3},{3,2},{4,5},{5,4},{6,7},{7,6},{8,9},{9,8},{10,11... | collective-permute-start | bytes 786440 | tf_op jit(solution)/shard_map/ppermute | solution.py:39
  90.8 3.6 %collective-permute-start.21 = (bf16[256,512]{1,0:T(8,128)(2,1)S(1)}, bf16[256,512]{1,0:T(8,128)(2,1)S(1)}, u32[]{:S(2)}, u32[]{:S(2)}) collective-permute-start(bf16[256,512]{1,0:T(8,128)(2,1)S(1)} %finish.7.refs_7_.refs_0_), channel_id=1, source_target_pairs={{0,1},{1,0},{2,3},{3,2},{4,5},{5,4},{6,7},{7,6},{8,9},{9,8},{10,11... | collective-permute-start | bytes 786440 | tf_op jit(solution)/shard_map/ppermute | solution.py:39
  (6 other events, 41.6 us)

commit v5 on v4

--- a/solution.py
+++ b/solution.py
@@ -102,8 +102,10 @@
         ).astype(BF16)
 
 
-def mark_body(out_ref):
-    out_ref[...] = jnp.zeros_like(out_ref)
+def pair_body(left_ref, right_ref, out_ref):
+    width = left_ref.shape[1]
+    out_ref[:, :width] = left_ref[...]
+    out_ref[:, width:] = right_ref[...]
 
 
 def head_body(queries_ref, out_ref):
@@ -128,12 +130,13 @@
     return ref[:, pl.ds(pl.multiple_of(index * width, width), width)]
 
 
-def feed_body(first, e0_ref, e2_ref, e1_ref, e3_ref, w_in_ref, w_out_ref, keep_ref, send_ref):
+def feed_body(first, e0_ref, e2_ref, other_ref, w_in_ref, w_out_ref, keep_ref, send_ref):
     me = lax.axis_index("tp")
     width = e0_ref.shape[1]
     index = [me, me ^ 2, me ^ 1, me ^ 3]
     here = slice(first, first + keep_ref.shape[0])
-    parts = [ref[here, :].astype(F32) for ref in (e0_ref, e2_ref, e1_ref, e3_ref)]
+    parts = [e0_ref[here, :], e2_ref[here, :], other_ref[here, :width], other_ref[here, width:]]
+    parts = [part.astype(F32) for part in parts]
     square = sum(jnp.sum(part * part, axis=1, keepdims=True) for part in parts)
     scale = lax.rsqrt(square / (4 * width) + 1e-06)
     hidden = sum(
@@ -272,10 +275,10 @@
         found.reshape(seq_size, cap, width), "seq", split_axis=0, concat_axis=0, tiled=True
     ).reshape(slots, width)
     order = [groups - 1] + list(range(groups - 1))
-    plan = [order[:1], order[1:2], order[2:]]
-    emb, first, window = {}, {}, {}
+    plan = [order[:1], order[1:]]
+    first, window = {}, {}
     token = slot
-    ahead = []
+    pieces = []
     for part in plan:
         e0 = token = call(
             functools.partial(order_body, part),
@@ -284,12 +287,16 @@
             (slot, answered),
             (token,),
         )
-        e2 = exchange(e0, 2)
-        pieces = e0, e2, exchange(e0, 1), exchange(e2, 1)
-        ahead.append(e2)
+        pieces.append([e0, exchange(e0, 2), None])
         for at, g in enumerate(part):
-            emb[g], first[g] = pieces, at * per_group
-
+            first[g] = at * per_group
+
+    def across(piece, after=()):
+        count = piece[0].shape[0]
+        both = call(pair_body, sds((count, 2 * width), BF16), "pair", piece[:2], after)
+        piece[2] = exchange(both, 1)
+
+    across(pieces[0])
     head = call(head_body, sds((GROUP, head_cols), BF16), "head", (queries,), (token,))
     next_q = shifted(head, -1)
     local_q = jnp.concatenate([queries[GROUP - 1 :], next_q[: GROUP - 1]], axis=0)
@@ -298,21 +305,22 @@
     fed, summed, far, encoded = {}, {}, {}, {}
     behind = out = None
 
+    def emb(g):
+        return pieces[0 if g in plan[0] else 1]
+
+    def rest(_):
+        across(pieces[1], (token,))
+
     def feed(g):
         nonlocal token
         keep, token = call(
             functools.partial(feed_body, first[g]),
             (whole, half),
             "feed",
-            (*emb[g], w_in, w_out),
-            (token,),
+            (*emb(g), w_in, w_out),
+            (token, pieces[1][1]),
         )
         fed[g] = keep, exchange(token, 1)
-
-    def pause(g):
-        nonlocal token
-        if g == order[0]:
-            token = call(mark_body, sds((8, LANES), F32), "mark", (), (token, ahead[-1]))
 
     def add(g):
         nonlocal token
@@ -325,7 +333,7 @@
             functools.partial(finish_body, first[g]),
             half,
             "finish",
-            (*emb[g][:2], summed[g], far[g]),
+            (*emb(g)[:2], summed[g], far[g]),
             (token, *{order[0]: (next_q,), order[-1]: (behind,)}.get(g, ())),
         )
         encoded[g] = token, exchange(token, 1)
@@ -368,10 +376,15 @@
             if g == order[0]:
                 behind = shifted(token, 1)
 
-    for stage in range(groups + 4):
-        for step, lag in ((finish, 3), (attend, 4), (feed, 0), (pause, 1), (add, 1)):
-            if 0 <= stage - lag < groups:
-                step(order[stage - lag])
+    a, b, c, d = order
+    for step, g in (
+        (feed, a), (rest, b), (add, a), (feed, b), (feed, c),
+        (finish, a), (add, b), (add, c), (feed, d),
+        (finish, b), (add, d), (attend, a),
+        (finish, c), (attend, b),
+        (finish, d), (attend, c), (attend, d),
+    ):
+        step(g)
     return out
 
 

time: 97.7 us -> 100 us (1.024)
  waiting for transfers between devices: 12.4 us -> 14.8 us
    ppermute x2, waiting for transfers between devices: 2.53 us -> 5.18 us  [shifted(): return lax.ppermute(x, 'seq', pairs)]
    ppermute x21 -> x16, waiting for transfers between devices: 9.91 us -> 9.65 us  [exchange(): return lax.ppermute(x, 'tp', [(i, i ^ bit) for i in range(size)])]
    ppermute x21 -> x16, starting transfers between devices: 19.9 us -> 19.7 us  [exchange(): return lax.ppermute(x, 'tp', [(i, i ^ bit) for i in range(size)])]
  transfers between devices with their start and end apart: 23 -> 18, of which waited for: 6 -> 5; matrix products, arithmetic and copies ran while one was open for 0% -> 0% of each run, Pallas kernels for 14% -> 12%
where the time goes in v5:
time: 100 us; the launch traced here: 99.9 us
  blocking collectives  38.6 us (39%)
  starting transfers between devices  25.1 us (25%)
  Pallas kernels  19.9 us (20%)
  waiting for transfers between devices  14.8 us (15%)
    all_to_all x1, blocking collectives, per_device(): lax.all_to_all(found.reshape(seq_size, cap, width), 'seq', split_axis=0,...  27.1 us
    pallas_call x23, Pallas kernels, call(): pl.pallas_call(without_after, out_shape=outs, in_specs=in_specs + [unread...  19.9 us
    ppermute x16, starting transfers between devices, exchange(): return lax.ppermute(x, 'tp', [(i, i ^ bit) for i in range(size)])  19.7 us
    all_to_all x1, blocking collectives, per_device(): lax.all_to_all(wanted, 'seq', split_axis=0, concat_axis=0, tiled=True)  11.5 us
    ppermute x16, waiting for transfers between devices, exchange(): return lax.ppermute(x, 'tp', [(i, i ^ bit) for i in range(size)])  9.65 us
    ppermute x2, starting transfers between devices, shifted(): return lax.ppermute(x, 'seq', pairs)  5.42 us
    ppermute x2, waiting for transfers between devices, shifted(): return lax.ppermute(x, 'seq', pairs)  5.18 us
  transfers between devices with their start and end apart: 18, of which 5 were waited for; matrix products, arithmetic and copies ran while one was open for 0% of the time, Pallas kernels for 12%

profile of v5, /device:TPU:1, one launch (start us, length us, event | category | flops | bytes accessed | tf_op | source)
XLA Modules:
  0.0 99.9 jit_solution(4627902959765709257)
XLA Ops:
  1.5 11.5 %all_to_all.14 = s32[8,1,256]{2,1,0:T(1,128)S(1)} all-to-all(s32[8,1,256]{2,1,0:T(1,128)S(1)} %copy.9), channel_id=1, replica_groups=mesh['seq'=8,'tp'=4] {'seq'}, dimensions={0} | all-to-all | bytes 16384 | tf_op jit(solution)/shard_map/all_to_all | solution.py:267
  13.1 2.4 %fetch.1 = bf16[2048,256]{1,0:T(8,128)(2,1)S(1)} custom-call(s32[1,2048]{1,0:T(1,128)S(1)} %bitcast.10, bf16[2048,256]{1,0:T(8,128)(2,1)S(1)} %copy-done.5), custom_call_target="tpu_custom_call" | custom-call | flops 1024 | bytes 1024 | tf_op jit(solution)/shard_map/fetch/pallas_call | solution.py:26
  15.4 27.1 %all_to_all.15 = bf16[8,256,256]{2,1,0:T(8,128)(2,1)S(1)} all-to-all(bf16[8,256,256]{2,1,0:T(8,128)(2,1)S(1)} %bitcast.8), channel_id=1, replica_groups=mesh['seq'=8,'tp'=4] {'seq'}, dimensions={0} | all-to-all | bytes 2097152 | tf_op jit(solution)/shard_map/all_to_all | solution.py:274
  43.0 1.3 %collective-permute-start.1 = (bf16[256,256]{1,0:T(8,128)(2,1)S(1)}, bf16[256,256]{1,0:T(8,128)(2,1)S(1)}, u32[]{:S(2)}, u32[]{:S(2)}) collective-permute-start(bf16[256,256]{1,0:T(8,128)(2,1)S(1)} %order.2.refs_2_.refs_0_), channel_id=1, source_target_pairs={{0,2},{1,3},{2,0},{3,1},{4,6},{5,7},{6,4},{7,5},{8,10},{9,11},{10,... | collective-permute-start | bytes 393224 | tf_op jit(solution)/shard_map/ppermute | solution.py:39
  45.6 1.3 %collective-permute-done.1.refs_1_ = bf16[256,256]{1,0:T(8,128)(2,1)S(1)} collective-permute-done((bf16[256,256]{1,0:T(8,128)(2,1)S(1)}, bf16[256,256]{1,0:T(8,128)(2,1)S(1)}, u32[]{:S(2)}, u32[]{:S(2)}) %collective-permute-start.1) | collective-permute-done | bytes 131104 | tf_op jit(solution)/shard_map/ppermute | solution.py:39
  46.9 4.6 %collective-permute-start.2 = (bf16[256,512]{1,0:T(8,128)(2,1)S(1)}, bf16[256,512]{1,0:T(8,128)(2,1)S(1)}, u32[]{:S(2)}, u32[]{:S(2)}) collective-permute-start(bf16[256,512]{1,0:T(8,128)(2,1)S(1)} %pair.2), channel_id=1, source_target_pairs={{0,1},{1,0},{2,3},{3,2},{4,5},{5,4},{6,7},{7,6},{8,9},{9,8},{10,11... | collective-permute-start | bytes 786440 | tf_op jit(solution)/shard_map/ppermute | solution.py:39
  51.5 4.7 %collective-permute-done.refs_6_.refs_1_ = bf16[768,256]{1,0:T(8,128)(2,1)S(1)} collective-permute-done((bf16[768,256]{1,0:T(8,128)(2,1)S(1)}, bf16[768,256]{1,0:T(8,128)(2,1)S(1)}, u32[]{:S(2)}, u32[]{:S(2)}) %collective-permute-start) | collective-permute-done | bytes 393248 | tf_op jit(solution)/shard_map/ppermute | solution.py:39
  56.3 1.6 %feed.4 = (f32[256,512]{1,0:T(8,128)S(1)}, bf16[256,512]{1,0:T(8,128)(2,1)S(1)}) custom-call(bf16[256,256]{1,0:T(8,128)(2,1)S(1)} %order.2.refs_2_.refs_0_, bf16[256,256]{1,0:T(8,128)(2,1)S(1)} %collective-permute-done.1.refs_1_, bf16[256,512]{1,0:T(8,128)(2,1)S(1)} %collective-permute-done.2.refs_2_, bf16[1024,1024]{1,0:T(8,128)(2,1)S(1)} %copy-done, ...), custom_call_target="tpu_custom_call" | custom-call | flops 1024 | bytes 1024 | tf_op jit(solution)/shard_map/feed/pallas_call | solution.py:26
  58.0 2.1 %collective-permute-start.3 = (bf16[768,512]{1,0:T(8,128)(2,1)S(1)}, bf16[768,512]{1,0:T(8,128)(2,1)S(1)}, u32[]{:S(2)}, u32[]{:S(2)}) collective-permute-start(bf16[768,512]{1,0:T(8,128)(2,1)S(1)} %pair.3), channel_id=1, source_target_pairs={{0,1},{1,0},{2,3},{3,2},{4,5},{5,4},{6,7},{7,6},{8,9},{9,8},{10,11... | collective-permute-start | bytes 2359304 | tf_op jit(solution)/shard_map/ppermute | solution.py:39
  60.1 2.2 %collective-permute-done.4.refs_1_ = bf16[256,512]{1,0:T(8,128)(2,1)S(1)} collective-permute-done((bf16[256,512]{1,0:T(8,128)(2,1)S(1)}, bf16[256,512]{1,0:T(8,128)(2,1)S(1)}, u32[]{:S(2)}, u32[]{:S(2)}) %collective-permute-start.4) | collective-permute-done | bytes 262176 | tf_op jit(solution)/shard_map/ppermute | solution.py:39
  62.8 1.6 %feed.5 = (f32[256,512]{1,0:T(8,128)S(1)}, bf16[256,512]{1,0:T(8,128)(2,1)S(1)}) custom-call(bf16[768,256]{1,0:T(8,128)(2,1)S(1)} %order.3.refs_5_.refs_0_.refs_1_, bf16[768,256]{1,0:T(8,128)(2,1)S(1)} %collective-permute-done.refs_6_.refs_1_, bf16[768,512]{1,0:T(8,128)(2,1)S(1)} %collective-permute-done.3.refs_2_, bf16[1024,1024]{1,0:T(8,128)(2,1)S(1)} %copy-done, ...), custom_call_target="tpu_custom_call" | custom-call | flops 1024 | bytes 1024 | tf_op jit(solution)/shard_map/feed/pallas_call | solution.py:26
  65.2 1.6 %feed.6 = (f32[256,512]{1,0:T(8,128)S(1)}, bf16[256,512]{1,0:T(8,128)(2,1)S(1)}) custom-call(bf16[768,256]{1,0:T(8,128)(2,1)S(1)} %order.3.refs_5_.refs_0_.refs_1_, bf16[768,256]{1,0:T(8,128)(2,1)S(1)} %collective-permute-done.refs_6_.refs_1_, bf16[768,512]{1,0:T(8,128)(2,1)S(1)} %collective-permute-done.3.refs_2_, bf16[1024,1024]{1,0:T(8,128)(2,1)S(1)} %copy-done, ...), custom_call_target="tpu_custom_call" | custom-call | flops 1024 | bytes 1024 | tf_op jit(solution)/shard_map/feed/pallas_call | solution.py:26
  66.9 1.3 %collective-permute-start.8 = (bf16[64,1024]{1,0:T(8,128)(2,1)S(1)}, bf16[64,1024]{1,0:T(8,128)(2,1)S(1)}, u32[]{:S(2)}, u32[]{:S(2)}) collective-permute-start(bf16[64,1024]{1,0:T(8,128)(2,1)S(1)} %head.1), channel_id=1, source_target_pairs={{4,0},{8,4},{12,8},{16,12},{20,16},{24,20},{28,24},{5,1},{9,5},{13... | collective-permute-start | bytes 393224 | tf_op jit(solution)/shard_map/ppermute | solution.py:45
  68.2 5.2 %collective-permute-done.8.refs_5_ = bf16[64,1024]{1,0:T(8,128)(2,1)S(1)} collective-permute-done((bf16[64,1024]{1,0:T(8,128)(2,1)S(1)}, bf16[64,1024]{1,0:T(8,128)(2,1)S(1)}, u32[]{:S(2)}, u32[]{:S(2)}) %collective-permute-start.8) | collective-permute-done | bytes 131104 | tf_op jit(solution)/shard_map/ppermute | solution.py:45
  74.8 1.6 %feed.7 = (f32[256,512]{1,0:T(8,128)S(1)}, bf16[256,512]{1,0:T(8,128)(2,1)S(1)}) custom-call(bf16[768,256]{1,0:T(8,128)(2,1)S(1)} %order.3.refs_5_.refs_0_.refs_1_, bf16[768,256]{1,0:T(8,128)(2,1)S(1)} %collective-permute-done.refs_6_.refs_1_, bf16[768,512]{1,0:T(8,128)(2,1)S(1)} %collective-permute-done.3.refs_2_, bf16[1024,1024]{1,0:T(8,128)(2,1)S(1)} %copy-done, ...), custom_call_target="tpu_custom_call" | custom-call | flops 1024 | bytes 1024 | tf_op jit(solution)/shard_map/feed/pallas_call | solution.py:26
  76.4 1.7 %collective-permute-start.9 = (bf16[256,512]{1,0:T(8,128)(2,1)S(1)}, bf16[256,512]{1,0:T(8,128)(2,1)S(1)}, u32[]{:S(2)}, u32[]{:S(2)}) collective-permute-start(bf16[256,512]{1,0:T(8,128)(2,1)S(1)} %get-tuple-element.38.refs_4_), channel_id=1, source_target_pairs={{0,1},{1,0},{2,3},{3,2},{4,5},{5,4},{6,7},{7,6},{8,9},{9,8},{10,11... | collective-permute-start | bytes 786440 | tf_op jit(solution)/shard_map/ppermute | solution.py:39
  78.7 1.4 %collective-permute-done.10.refs_3_ = bf16[256,512]{1,0:T(8,128)(2,1)S(1)} collective-permute-done((bf16[256,512]{1,0:T(8,128)(2,1)S(1)}, bf16[256,512]{1,0:T(8,128)(2,1)S(1)}, u32[]{:S(2)}, u32[]{:S(2)}) %collective-permute-start.10) | collective-permute-done | bytes 262176 | tf_op jit(solution)/shard_map/ppermute | solution.py:39
  80.1 3.1 %collective-permute-start.12 = (bf16[256,512]{1,0:T(8,128)(2,1)S(1)}, bf16[256,512]{1,0:T(8,128)(2,1)S(1)}, u32[]{:S(2)}, u32[]{:S(2)}) collective-permute-start(bf16[256,512]{1,0:T(8,128)(2,1)S(1)} %finish.5.refs_2_.refs_0_), channel_id=1, source_target_pairs={{0,1},{1,0},{2,3},{3,2},{4,5},{5,4},{6,7},{7,6},{8,9},{9,8},{10,11... | collective-permute-start | bytes 786440 | tf_op jit(solution)/shard_map/ppermute | solution.py:39
  83.3 2.0 %collective-permute-start.11 = (bf16[256,512]{1,0:T(8,128)(2,1)S(1)}, bf16[256,512]{1,0:T(8,128)(2,1)S(1)}, u32[]{:S(2)}, u32[]{:S(2)}) collective-permute-start(bf16[256,512]{1,0:T(8,128)(2,1)S(1)} %get-tuple-element.41.refs_5_), channel_id=1, source_target_pairs={{0,2},{1,3},{2,0},{3,1},{4,6},{5,7},{6,4},{7,5},{8,10},{9,11},{10,... | collective-permute-start | bytes 786440 | tf_op jit(solution)/shard_map/ppermute | solution.py:39
  85.4 1.7 %attend.2.refs_4_.refs_6_ = bf16[64,1024]{1,0:T(8,128)(2,1)S(1)} custom-call(bf16[256,512]{1,0:T(8,128)(2,1)S(1)} %finish.4.refs_2_.refs_0_, bf16[256,512]{1,0:T(8,128)(2,1)S(1)} %collective-permute-done.14.refs_1_, bf16[1024,1024]{1,0:T(8,128)(2,1)S(1)} %copy-done.2, bf16[1024,1024]{1,0:T(8,128)(2,1)S(1)} %copy-done.3, ...), custom_call_target="tpu_custom_call" | custom-call | flops 1024 | bytes 1024 | tf_op jit(solution)/shard_map/attend/pallas_call | solution.py:26
  87.1 4.1 %collective-permute-start.15 = (bf16[64,1024]{1,0:T(8,128)(2,1)S(1)}, bf16[64,1024]{1,0:T(8,128)(2,1)S(1)}, u32[]{:S(2)}, u32[]{:S(2)}) collective-permute-start(bf16[64,1024]{1,0:T(8,128)(2,1)S(1)} %attend.2.refs_4_.refs_6_), channel_id=1, source_target_pairs={{0,4},{4,8},{8,12},{12,16},{16,20},{20,24},{24,28},{1,5},{5,9},{9,... | collective-permute-start | bytes 393224 | tf_op jit(solution)/shard_map/ppermute | solution.py:45
  92.1 1.7 %attend.3.refs_4_.refs_6_ = bf16[64,1024]{1,0:T(8,128)(2,1)S(1)} custom-call(bf16[256,512]{1,0:T(8,128)(2,1)S(1)} %finish.5.refs_2_.refs_0_, bf16[256,512]{1,0:T(8,128)(2,1)S(1)} %collective-permute-done.12.refs_1_, bf16[1024,1024]{1,0:T(8,128)(2,1)S(1)} %copy-done.2, bf16[1024,1024]{1,0:T(8,128)(2,1)S(1)} %copy-done.3, ...), custom_call_target="tpu_custom_call" | custom-call | flops 1024 | bytes 1024 | tf_op jit(solution)/shard_map/attend/pallas_call | solution.py:26
  94.9 2.5 %attend_before.1 = (bf16[64,1024]{1,0:T(8,128)(2,1)S(1)}, bf16[256,1024]{1,0:T(8,128)(2,1)}) custom-call(bf16[256,512]{1,0:T(8,128)(2,1)S(1)} %finish.6.refs_5_.refs_0_, bf16[256,512]{1,0:T(8,128)(2,1)S(1)} %collective-permute-done.17.refs_1_, bf16[1024,1024]{1,0:T(8,128)(2,1)S(1)} %copy-done.2, bf16[1024,1024]{1,0:T(8,128)(2,1)S(1)} %copy-done.3, ...), custom_call_target="tpu_custom_call" | custom-call | flops 1024 | bytes 1024 | tf_op jit(solution)/shard_map/attend_before/pallas_call | solution.py:26
  97.4 2.4 %attend_last.1 = bf16[256,1024]{1,0:T(8,128)(2,1)} custom-call(bf16[256,512]{1,0:T(8,128)(2,1)S(1)} %finish.7.refs_7_.refs_0_, bf16[256,512]{1,0:T(8,128)(2,1)S(1)} %collective-permute-done.16.refs_1_, bf16[1024,1024]{1,0:T(8,128)(2,1)S(1)} %copy-done.2, bf16[1024,1024]{1,0:T(8,128)(2,1)S(1)} %copy-done.3, ...), custom_call_target="tpu_custom_call", output_to_operand_aliasing={{}: (7, {})} | custom-call | flops 1024 | bytes 1024 | tf_op jit(solution)/shard_map/attend_last/pallas_call | solution.py:26
  (55 shorter events, 8.9 us)
Async XLA Ops:
  0.7 12.4 %copy-start.5 = (bf16[2048,256]{1,0:T(8,128)(2,1)S(1)}, bf16[2048,256]{1,0:T(8,128)(2,1)}, u32[]{:S(2)}) copy-start(bf16[2048,256]{1,0:T(8,128)(2,1)} %refs_1_.1) | copy-start | bytes 3145732
  42.6 13.7 %copy-start = (bf16[1024,1024]{1,0:T(8,128)(2,1)S(1)}, bf16[1024,1024]{1,0:T(8,128)(2,1)}, u32[]{:S(2)}) copy-start(bf16[1024,1024]{1,0:T(8,128)(2,1)} %refs_3_.11) | copy-start | bytes 6291460
  42.6 13.7 %copy-start.1 = (bf16[1024,1024]{1,0:T(8,128)(2,1)S(1)}, bf16[1024,1024]{1,0:T(8,128)(2,1)}, u32[]{:S(2)}) copy-start(bf16[1024,1024]{1,0:T(8,128)(2,1)} %refs_4_.7) | copy-start | bytes 6291460
  43.0 3.9 %collective-permute-start.1 = (bf16[256,256]{1,0:T(8,128)(2,1)S(1)}, bf16[256,256]{1,0:T(8,128)(2,1)S(1)}, u32[]{:S(2)}, u32[]{:S(2)}) collective-permute-start(bf16[256,256]{1,0:T(8,128)(2,1)S(1)} %order.2.refs_2_.refs_0_), channel_id=1, source_target_pairs={{0,2},{1,3},{2,0},{3,1},{4,6},{5,7},{6,4},{7,5},{8,10},{9,11},{10,... | collective-permute-start | bytes 393224 | tf_op jit(solution)/shard_map/ppermute | solution.py:39
  45.3 11.0 %collective-permute-start = (bf16[768,256]{1,0:T(8,128)(2,1)S(1)}, bf16[768,256]{1,0:T(8,128)(2,1)S(1)}, u32[]{:S(2)}, u32[]{:S(2)}) collective-permute-start(bf16[768,256]{1,0:T(8,128)(2,1)S(1)} %order.3.refs_5_.refs_0_.refs_1_), channel_id=1, source_target_pairs={{0,2},{1,3},{2,0},{3,1},{4,6},{5,7},{6,4},{7,5},{8,10},{9,11},{10,... | collective-permute-start | bytes 1179656 | tf_op jit(solution)/shard_map/ppermute | solution.py:39
  46.9 9.4 %collective-permute-start.2 = (bf16[256,512]{1,0:T(8,128)(2,1)S(1)}, bf16[256,512]{1,0:T(8,128)(2,1)S(1)}, u32[]{:S(2)}, u32[]{:S(2)}) collective-permute-start(bf16[256,512]{1,0:T(8,128)(2,1)S(1)} %pair.2), channel_id=1, source_target_pairs={{0,1},{1,0},{2,3},{3,2},{4,5},{5,4},{6,7},{7,6},{8,9},{9,8},{10,11... | collective-permute-start | bytes 786440 | tf_op jit(solution)/shard_map/ppermute | solution.py:39
  58.0 4.9 %collective-permute-start.3 = (bf16[768,512]{1,0:T(8,128)(2,1)S(1)}, bf16[768,512]{1,0:T(8,128)(2,1)S(1)}, u32[]{:S(2)}, u32[]{:S(2)}) collective-permute-start(bf16[768,512]{1,0:T(8,128)(2,1)S(1)} %pair.3), channel_id=1, source_target_pairs={{0,1},{1,0},{2,3},{3,2},{4,5},{5,4},{6,7},{7,6},{8,9},{9,8},{10,11... | collective-permute-start | bytes 2359304 | tf_op jit(solution)/shard_map/ppermute | solution.py:39
  60.0 2.3 %collective-permute-start.4 = (bf16[256,512]{1,0:T(8,128)(2,1)S(1)}, bf16[256,512]{1,0:T(8,128)(2,1)S(1)}, u32[]{:S(2)}, u32[]{:S(2)}) collective-permute-start(bf16[256,512]{1,0:T(8,128)(2,1)S(1)} %get-tuple-element.27.refs_2_), channel_id=1, source_target_pairs={{0,1},{1,0},{2,3},{3,2},{4,5},{5,4},{6,7},{7,6},{8,9},{9,8},{10,11... | collective-permute-start | bytes 786440 | tf_op jit(solution)/shard_map/ppermute | solution.py:39
  62.4 10.9 %collective-permute-start.7 = (bf16[256,512]{1,0:T(8,128)(2,1)S(1)}, bf16[256,512]{1,0:T(8,128)(2,1)S(1)}, u32[]{:S(2)}, u32[]{:S(2)}) collective-permute-start(bf16[256,512]{1,0:T(8,128)(2,1)S(1)} %get-tuple-element.29.refs_5_), channel_id=1, source_target_pairs={{0,2},{1,3},{2,0},{3,1},{4,6},{5,7},{6,4},{7,5},{8,10},{9,11},{10,... | collective-permute-start | bytes 786440 | tf_op jit(solution)/shard_map/ppermute | solution.py:39
  64.4 2.4 %copy-start.4 = (bf16[256,1024]{1,0:T(8,128)(2,1)S(1)}, bf16[256,1024]{1,0:T(8,128)(2,1)}, u32[]{:S(2)}) copy-start(bf16[256,1024]{1,0:T(8,128)(2,1)} %refs_0_.1) | copy-start | bytes 1572868
  64.4 9.0 %collective-permute-start.6 = (bf16[256,512]{1,0:T(8,128)(2,1)S(1)}, bf16[256,512]{1,0:T(8,128)(2,1)S(1)}, u32[]{:S(2)}, u32[]{:S(2)}) collective-permute-start(bf16[256,512]{1,0:T(8,128)(2,1)S(1)} %get-tuple-element.30.refs_5_), channel_id=1, source_target_pairs={{0,1},{1,0},{2,3},{3,2},{4,5},{5,4},{6,7},{7,6},{8,9},{9,8},{10,11... | collective-permute-start | bytes 786440 | tf_op jit(solution)/shard_map/ppermute | solution.py:39
  66.8 8.0 %collective-permute-start.5 = (bf16[256,512]{1,0:T(8,128)(2,1)S(1)}, bf16[256,512]{1,0:T(8,128)(2,1)S(1)}, u32[]{:S(2)}, u32[]{:S(2)}) collective-permute-start(bf16[256,512]{1,0:T(8,128)(2,1)S(1)} %get-tuple-element.32.refs_4_), channel_id=1, source_target_pairs={{0,1},{1,0},{2,3},{3,2},{4,5},{5,4},{6,7},{7,6},{8,9},{9,8},{10,11... | collective-permute-start | bytes 786440 | tf_op jit(solution)/shard_map/ppermute | solution.py:39
  66.9 6.5 %collective-permute-start.8 = (bf16[64,1024]{1,0:T(8,128)(2,1)S(1)}, bf16[64,1024]{1,0:T(8,128)(2,1)S(1)}, u32[]{:S(2)}, u32[]{:S(2)}) collective-permute-start(bf16[64,1024]{1,0:T(8,128)(2,1)S(1)} %head.1), channel_id=1, source_target_pairs={{4,0},{8,4},{12,8},{16,12},{20,16},{24,20},{28,24},{5,1},{9,5},{13... | collective-permute-start | bytes 393224 | tf_op jit(solution)/shard_map/ppermute | solution.py:45
  73.5 6.5 %collective-permute-start.10 = (bf16[256,512]{1,0:T(8,128)(2,1)S(1)}, bf16[256,512]{1,0:T(8,128)(2,1)S(1)}, u32[]{:S(2)}, u32[]{:S(2)}) collective-permute-start(bf16[256,512]{1,0:T(8,128)(2,1)S(1)} %get-tuple-element.35.refs_2_), channel_id=1, source_target_pairs={{0,2},{1,3},{2,0},{3,1},{4,6},{5,7},{6,4},{7,5},{8,10},{9,11},{10,... | collective-permute-start | bytes 786440 | tf_op jit(solution)/shard_map/ppermute | solution.py:39
  76.4 6.8 %collective-permute-start.9 = (bf16[256,512]{1,0:T(8,128)(2,1)S(1)}, bf16[256,512]{1,0:T(8,128)(2,1)S(1)}, u32[]{:S(2)}, u32[]{:S(2)}) collective-permute-start(bf16[256,512]{1,0:T(8,128)(2,1)S(1)} %get-tuple-element.38.refs_4_), channel_id=1, source_target_pairs={{0,1},{1,0},{2,3},{3,2},{4,5},{5,4},{6,7},{7,6},{8,9},{9,8},{10,11... | collective-permute-start | bytes 786440 | tf_op jit(solution)/shard_map/ppermute | solution.py:39
  78.1 7.3 %collective-permute-start.14 = (bf16[256,512]{1,0:T(8,128)(2,1)S(1)}, bf16[256,512]{1,0:T(8,128)(2,1)S(1)}, u32[]{:S(2)}, u32[]{:S(2)}) collective-permute-start(bf16[256,512]{1,0:T(8,128)(2,1)S(1)} %finish.4.refs_2_.refs_0_), channel_id=1, source_target_pairs={{0,1},{1,0},{2,3},{3,2},{4,5},{5,4},{6,7},{7,6},{8,9},{9,8},{10,11... | collective-permute-start | bytes 786440 | tf_op jit(solution)/shard_map/ppermute | solution.py:39
  78.2 7.2 %copy-start.3 = (bf16[1024,1024]{1,0:T(8,128)(2,1)S(1)}, bf16[1024,1024]{1,0:T(8,128)(2,1)}, u32[]{:S(2)}) copy-start(bf16[1024,1024]{1,0:T(8,128)(2,1)} %refs_3_.15) | copy-start | bytes 6291460
  78.3 7.1 %copy-start.2 = (bf16[1024,1024]{1,0:T(8,128)(2,1)S(1)}, bf16[1024,1024]{1,0:T(8,128)(2,1)}, u32[]{:S(2)}) copy-start(bf16[1024,1024]{1,0:T(8,128)(2,1)} %refs_2_.7) | copy-start | bytes 6291460
  78.3 13.0 %collective-permute-start.13 = (bf16[256,512]{1,0:T(8,128)(2,1)S(1)}, bf16[256,512]{1,0:T(8,128)(2,1)S(1)}, u32[]{:S(2)}, u32[]{:S(2)}) collective-permute-start(bf16[256,512]{1,0:T(8,128)(2,1)S(1)} %get-tuple-element.36.refs_5_), channel_id=1, source_target_pairs={{0,2},{1,3},{2,0},{3,1},{4,6},{5,7},{6,4},{7,5},{8,10},{9,11},{10,... | collective-permute-start | bytes 786440 | tf_op jit(solution)/shard_map/ppermute | solution.py:39
  80.1 11.9 %collective-permute-start.12 = (bf16[256,512]{1,0:T(8,128)(2,1)S(1)}, bf16[256,512]{1,0:T(8,128)(2,1)S(1)}, u32[]{:S(2)}, u32[]{:S(2)}) collective-permute-start(bf16[256,512]{1,0:T(8,128)(2,1)S(1)} %finish.5.refs_2_.refs_0_), channel_id=1, source_target_pairs={{0,1},{1,0},{2,3},{3,2},{4,5},{5,4},{6,7},{7,6},{8,9},{9,8},{10,11... | collective-permute-start | bytes 786440 | tf_op jit(solution)/shard_map/ppermute | solution.py:39
  83.3 10.4 %collective-permute-start.11 = (bf16[256,512]{1,0:T(8,128)(2,1)S(1)}, bf16[256,512]{1,0:T(8,128)(2,1)S(1)}, u32[]{:S(2)}, u32[]{:S(2)}) collective-permute-start(bf16[256,512]{1,0:T(8,128)(2,1)S(1)} %get-tuple-element.41.refs_5_), channel_id=1, source_target_pairs={{0,2},{1,3},{2,0},{3,1},{4,6},{5,7},{6,4},{7,5},{8,10},{9,11},{10,... | collective-permute-start | bytes 786440 | tf_op jit(solution)/shard_map/ppermute | solution.py:39
  87.1 6.7 %collective-permute-start.15 = (bf16[64,1024]{1,0:T(8,128)(2,1)S(1)}, bf16[64,1024]{1,0:T(8,128)(2,1)S(1)}, u32[]{:S(2)}, u32[]{:S(2)}) collective-permute-start(bf16[64,1024]{1,0:T(8,128)(2,1)S(1)} %attend.2.refs_4_.refs_6_), channel_id=1, source_target_pairs={{0,4},{4,8},{8,12},{12,16},{16,20},{20,24},{24,28},{1,5},{5,9},{9,... | collective-permute-start | bytes 393224 | tf_op jit(solution)/shard_map/ppermute | solution.py:45
  91.4 3.5 %collective-permute-start.17 = (bf16[256,512]{1,0:T(8,128)(2,1)S(1)}, bf16[256,512]{1,0:T(8,128)(2,1)S(1)}, u32[]{:S(2)}, u32[]{:S(2)}) collective-permute-start(bf16[256,512]{1,0:T(8,128)(2,1)S(1)} %finish.6.refs_5_.refs_0_), channel_id=1, source_target_pairs={{0,1},{1,0},{2,3},{3,2},{4,5},{5,4},{6,7},{7,6},{8,9},{9,8},{10,11... | collective-permute-start | bytes 786440 | tf_op jit(solution)/shard_map/ppermute | solution.py:39
  93.9 3.5 %collective-permute-start.16 = (bf16[256,512]{1,0:T(8,128)(2,1)S(1)}, bf16[256,512]{1,0:T(8,128)(2,1)S(1)}, u32[]{:S(2)}, u32[]{:S(2)}) collective-permute-start(bf16[256,512]{1,0:T(8,128)(2,1)S(1)} %finish.7.refs_7_.refs_0_), channel_id=1, source_target_pairs={{0,1},{1,0},{2,3},{3,2},{4,5},{5,4},{6,7},{7,6},{8,9},{9,8},{10,11... | collective-permute-start | bytes 786440 | tf_op jit(solution)/shard_map/ppermute | solution.py:39
  (1 other events, 0.7 us)

commit v6 on v5

--- a/solution.py
+++ b/solution.py
@@ -92,7 +92,9 @@
     slot_ref[...] = columns_of(owner * cap + rank)
 
 
-def fetch_body(req_ref, vocab_ref, out_ref):
+def fetch_body(req_ref, vocab_ref, queries_hbm, out_ref, head_ref, sem):
+    copy = pltpu.make_async_copy(queries_hbm.at[pl.ds(0, head_ref.shape[0]), :], head_ref, sem)
+    copy.start()
     step = 256
     table = vocab_ref[...]
     for at in range(0, req_ref.shape[1], step):
@@ -100,16 +102,26 @@
         out_ref[at : at + step, :] = jnp.dot(
             picked, table, preferred_element_type=F32
         ).astype(BF16)
+    copy.wait()
+
+
+def relay(x, after):
+    unread = pl.BlockSpec(memory_space=pl.ANY)
+    return pl.pallas_call(
+        lambda *refs: None,
+        out_shape=jax.ShapeDtypeStruct(x.shape, x.dtype),
+        in_specs=[unread] * 2,
+        out_specs=unread,
+        input_output_aliases={0: 0},
+        cost_estimate=pl.CostEstimate(flops=1024, bytes_accessed=1024, transcendentals=0),
+        name="relay",
+    )(x, after)
 
 
 def pair_body(left_ref, right_ref, out_ref):
     width = left_ref.shape[1]
     out_ref[:, :width] = left_ref[...]
     out_ref[:, width:] = right_ref[...]
-
-
-def head_body(queries_ref, out_ref):
-    out_ref[...] = queries_ref[: out_ref.shape[0], :]
 
 
 def order_body(groups, slot_ref, rows_ref, out_ref):
@@ -211,39 +223,20 @@
         out_ref[:, at * HEAD_WIDTH : (at + 1) * HEAD_WIDTH] = part.astype(BF16)
 
 
-def one_up(refs, cols, rows):
-    tall = jnp.concatenate([ref[:, cols].astype(F32) for ref in refs], axis=0)
-    return pltpu.roll(tall, tall.shape[0] - 1, 0)[:rows].astype(BF16)
-
-
-def attend_before_body(
-    mine_ref, other_ref, w_key_ref, w_value_ref, q_ref, *refs
+def attend_last_body(
+    mine_ref, other_ref, w_key_ref, w_value_ref, q_ref, behind_ref, *refs
 ):
-    earlier, (window_ref, out_hbm, rows_ref, sem) = refs[:-4], refs[-4:]
-    for at, part in enumerate(attended(mine_ref, other_ref, w_key_ref, w_value_ref, q_ref)):
+    before, last_ref, out_ref = refs[:-2], refs[-2], refs[-1]
+    parts = attended(mine_ref, other_ref, w_key_ref, w_value_ref, q_ref)
+    for at, part in enumerate(parts):
         cols = slice(at * HEAD_WIDTH, (at + 1) * HEAD_WIDTH)
-        window_ref[:, cols] = part.astype(BF16)
-        rows_ref[:, cols] = one_up((*earlier, window_ref), cols, rows_ref.shape[0])
-    copy = pltpu.make_async_copy(rows_ref, out_hbm.at[pl.ds(0, rows_ref.shape[0]), :], sem)
-    copy.start()
-    copy.wait()
-
-
-def attend_last_body(
-    mine_ref, other_ref, w_key_ref, w_value_ref, q_ref, before_ref, after_ref, _, out_hbm, window_ref, rows_ref, sem
-):
-    count = rows_ref.shape[0]
-    edge = (count - window_ref.shape[0])
-    for at, part in enumerate(attended(mine_ref, other_ref, w_key_ref, w_value_ref, q_ref)):
-        cols = slice(at * HEAD_WIDTH, (at + 1) * HEAD_WIDTH)
-        window_ref[:, cols] = part.astype(BF16)
-        pieces = (before_ref.at[pl.ds(GROUP - edge, edge), :], window_ref, after_ref.at[pl.ds(0, edge), :])
-        rows_ref[:, cols] = one_up(pieces, cols, count)
-    copy = pltpu.make_async_copy(
-        rows_ref, out_hbm.at[pl.ds(out_hbm.shape[0] - count, count), :], sem
-    )
-    copy.start()
-    copy.wait()
+        part = part.astype(BF16).astype(F32)
+        stack = [behind_ref[:, cols].astype(F32)]
+        stack += [ref[:, cols].astype(F32) for ref in before]
+        stack += [part, last_ref[:, cols].astype(F32)]
+        tall = jnp.concatenate(stack, axis=0)
+        moved = pltpu.roll(tall, tall.shape[0] - 1, 0)
+        out_ref[:, cols] = moved[: out_ref.shape[0]].astype(BF16)
 
 
 def per_device(queries, vocab_rows, neighbour_ids, w_in, w_out, w_key, w_value):
@@ -265,19 +258,23 @@
         flops=8 * 10**9,
     )
     request = lax.all_to_all(wanted, "seq", split_axis=0, concat_axis=0, tiled=True)
-    found = call(
+    vmem = pl.BlockSpec(memory_space=pltpu.VMEM)
+    found, head = call(
         fetch_body,
-        sds((slots, width), BF16),
+        (sds((slots, width), BF16), sds((GROUP, head_cols), BF16)),
         "fetch",
-        (request.reshape(1, slots), vocab_rows),
-    )
+        (request.reshape(1, slots), vocab_rows, queries),
+        in_specs=[vmem, vmem, pl.BlockSpec(memory_space=pl.ANY)],
+        scratch_shapes=[pltpu.SemaphoreType.DMA],
+    )
+    next_q = shifted(head, -1)
     answered = lax.all_to_all(
         found.reshape(seq_size, cap, width), "seq", split_axis=0, concat_axis=0, tiled=True
     ).reshape(slots, width)
     order = [groups - 1] + list(range(groups - 1))
     plan = [order[:1], order[1:]]
     first, window = {}, {}
-    token = slot
+    token = next_q
     pieces = []
     for part in plan:
         e0 = token = call(
@@ -297,8 +294,6 @@
         piece[2] = exchange(both, 1)
 
     across(pieces[0])
-    head = call(head_body, sds((GROUP, head_cols), BF16), "head", (queries,), (token,))
-    next_q = shifted(head, -1)
     local_q = jnp.concatenate([queries[GROUP - 1 :], next_q[: GROUP - 1]], axis=0)
     half = sds((per_group, 2 * width), BF16)
     whole = sds((per_group, 2 * width), F32)
@@ -334,53 +329,37 @@
             half,
             "finish",
             (*emb(g)[:2], summed[g], far[g]),
-            (token, *{order[0]: (next_q,), order[-1]: (behind,)}.get(g, ())),
-        )
-        encoded[g] = token, exchange(token, 1)
+            (token, behind) if g == order[-1] else (token,),
+        )
+        encoded[g] = token, None if g == order[0] else exchange(token, 1)
+
+    def hand(g):
+        mine = relay(encoded[g][0], token)
+        encoded[g] = mine, exchange(mine, 1)
 
     def attend(g):
         nonlocal token, behind, out
         args = (*encoded[g], w_key, w_value, local_q[g * GROUP : (g + 1) * GROUP])
-        piece = sds((GROUP, head_cols), BF16)
-        edge = 16
-        last_rows = GROUP + edge
-        vmem, hbm = pl.BlockSpec(memory_space=pltpu.VMEM), pl.BlockSpec(memory_space=pl.ANY)
-
-        def scratch(count):
-            return [pltpu.VMEM((count, head_cols), BF16), pltpu.SemaphoreType.DMA]
-
         if g == order[-1]:
+            before = [window[at] for at in order[1:-1]]
             out = call(
                 attend_last_body,
                 sds((tok, head_cols), BF16),
                 "attend_last",
-                (*args, window[order[-2]], window[order[0]], out),
-                in_specs=[vmem] * (len(args) + 2) + [hbm],
-                out_specs=hbm,
-                scratch_shapes=[pltpu.VMEM((GROUP, head_cols), BF16), *scratch(last_rows)],
-                input_output_aliases={len(args) + 2: 0},
+                (*args, behind, *before, window[order[0]]),
             )
-        elif g == order[-2]:
-            window[g], out = call(
-                attend_before_body,
-                (piece, sds((tok, head_cols), BF16)),
-                "attend_before",
-                (*args, behind, *[window[at] for at in order[1:-2]]),
-                (token,),
-                out_specs=(vmem, hbm),
-                scratch_shapes=scratch(tok - last_rows),
-            )
-            token = window[g]
-        else:
-            window[g] = token = call(attend_body, piece, "attend", args, (token,))
-            if g == order[0]:
-                behind = shifted(token, 1)
+            return
+        window[g] = token = call(
+            attend_body, sds((GROUP, head_cols), BF16), "attend", args, (token,)
+        )
+        if g == order[0]:
+            behind = shifted(token, 1)
 
     a, b, c, d = order
     for step, g in (
         (feed, a), (rest, b), (add, a), (feed, b), (feed, c),
-        (finish, a), (add, b), (add, c), (feed, d),
-        (finish, b), (add, d), (attend, a),
+        (finish, a), (add, b), (hand, a), (add, c), (feed, d), (attend, a),
+        (finish, b), (add, d),
         (finish, c), (attend, b),
         (finish, d), (attend, c), (attend, d),
     ):

time: 100 us -> 106 us (1.060); the launches traced: 99.9 us -> 104 us
  blocking collectives: 38.6 us -> 11.5 us
  waiting for transfers between devices: 14.8 us -> 30 us
  local copies, waits for them, and re-layouts: 0.92 us -> 10.6 us
  starting transfers between devices: 25.1 us -> 30.4 us
  Pallas kernels: 19.9 us -> 21.2 us
    all_to_all x1 -> x0, blocking collectives: 27.1 us -> none  [per_device(): lax.all_to_all(found.reshape(seq_size, cap, width), 'seq', split_axis=0,...]
    all_to_all x0 -> x1, waiting for transfers between devices: none -> 13.1 us  [per_device(): lax.all_to_all(found.reshape(seq_size, cap, width), 'seq', split_axis=0,...]
    unnamed x14 -> x50, local copies, waits for them, and re-layouts: 0.71 us -> 10.4 us
    ppermute x2, waiting for transfers between devices: 5.18 us -> 9.14 us  [shifted(): return lax.ppermute(x, 'seq', pairs)]
    all_to_all x0 -> x1, starting transfers between devices: none -> 3.57 us  [per_device(): lax.all_to_all(found.reshape(seq_size, cap, width), 'seq', split_axis=0,...]
    ppermute x16, starting transfers between devices: 19.7 us -> 21.6 us  [exchange(): return lax.ppermute(x, 'tp', [(i, i ^ bit) for i in range(size)])]
    ppermute x16, waiting for transfers between devices: 9.65 us -> 7.75 us  [exchange(): return lax.ppermute(x, 'tp', [(i, i ^ bit) for i in range(size)])]
    pallas_call x23 -> x22, Pallas kernels: 19.9 us -> 21.2 us  [call(): pl.pallas_call(without_after, out_shape=outs, in_specs=in_specs + [unread...]
  transfers between devices with their start and end apart: 18 -> 19, of which waited for: 5 -> 6; matrix products, arithmetic and copies ran while one was open for 0% -> 0% of each run, Pallas kernels for 12% -> 12%
where the time goes in v6:
time: 106 us; the launch traced here: 104 us
  starting transfers between devices  30.4 us (29%)
  waiting for transfers between devices  30 us (28%)
  Pallas kernels  21.2 us (20%)
  blocking collectives  11.5 us (11%)
  local copies, waits for them, and re-layouts  10.6 us (10%)
    ppermute x16, starting transfers between devices, exchange(): return lax.ppermute(x, 'tp', [(i, i ^ bit) for i in range(size)])  21.6 us
    pallas_call x22, Pallas kernels, call(): pl.pallas_call(without_after, out_shape=outs, in_specs=in_specs + [unread...  21.2 us
    all_to_all x1, waiting for transfers between devices, per_device(): lax.all_to_all(found.reshape(seq_size, cap, width), 'seq', split_axis=0,...  13.1 us
    all_to_all x1, blocking collectives, per_device(): lax.all_to_all(wanted, 'seq', split_axis=0, concat_axis=0, tiled=True)  11.5 us
    unnamed x50, local copies, waits for them, and re-layouts  10.4 us
    ppermute x2, waiting for transfers between devices, shifted(): return lax.ppermute(x, 'seq', pairs)  9.14 us
    ppermute x16, waiting for transfers between devices, exchange(): return lax.ppermute(x, 'tp', [(i, i ^ bit) for i in range(size)])  7.75 us
    ppermute x2, starting transfers between devices, shifted(): return lax.ppermute(x, 'seq', pairs)  5.21 us
  transfers between devices with their start and end apart: 19, of which 6 were waited for; matrix products, arithmetic and copies ran while one was open for 0% of the time, Pallas kernels for 12%

profile of v6, /device:TPU:1, one launch (start us, length us, event | category | flops | bytes accessed | tf_op | source)
XLA Modules:
  0.0 104.1 jit_solution(15518388970889430243)
XLA Ops:
  2.3 11.5 %all_to_all.14 = s32[8,1,256]{2,1,0:T(1,128)S(1)} all-to-all(s32[8,1,256]{2,1,0:T(1,128)S(1)} %copy.9), channel_id=1, replica_groups=mesh['seq'=8,'tp'=4] {'seq'}, dimensions={0} | all-to-all | bytes 16384 | tf_op jit(solution)/shard_map/all_to_all | solution.py:260
  13.9 3.6 %fetch.1 = (bf16[2048,256]{1,0:T(8,128)(2,1)}, bf16[64,1024]{1,0:T(8,128)(2,1)S(1)}) custom-call(s32[1,2048]{1,0:T(1,128)S(1)} %bitcast.9, bf16[2048,256]{1,0:T(8,128)(2,1)S(1)} %copy-done.15, bf16[256,1024]{1,0:T(8,128)(2,1)S(1)} %copy-done.11), custom_call_target="tpu_custom_call" | custom-call | flops 1024 | bytes 1024 | tf_op jit(solution)/shard_map/fetch/pallas_call | solution.py:26
  17.4 3.6 %all-to-all-start.1 = ((bf16[8,256,256]{2,1,0:T(8,128)(2,1)}), bf16[8,256,256]{2,1,0:T(8,128)(2,1)S(1)}, u32[]{:S(2)}, u32[]{:S(2)}) async-start(bf16[8,256,256]{2,1,0:T(8,128)(2,1)} %bitcast.3), calls=%async_computation.1 | async-start | bytes 2097152 | tf_op jit(solution)/shard_map/all_to_all | solution.py:271
  21.0 1.5 %collective-permute-start = (bf16[64,1024]{1,0:T(8,128)(2,1)S(1)}, bf16[64,1024]{1,0:T(8,128)(2,1)S(1)}, u32[]{:S(2)}, u32[]{:S(2)}) collective-permute-start(bf16[64,1024]{1,0:T(8,128)(2,1)S(1)} %get-tuple-element.28), channel_id=1, source_target_pairs={{4,0},{8,4},{12,8},{16,12},{20,16},{24,20},{28,24},{5,1},{9,5},{13... | collective-permute-start | bytes 393224 | tf_op jit(solution)/shard_map/ppermute | solution.py:45
  22.5 9.1 %collective-permute-done.refs_2_ = bf16[64,1024]{1,0:T(8,128)(2,1)S(1)} collective-permute-done((bf16[64,1024]{1,0:T(8,128)(2,1)S(1)}, bf16[64,1024]{1,0:T(8,128)(2,1)S(1)}, u32[]{:S(2)}, u32[]{:S(2)}) %collective-permute-start) | collective-permute-done | bytes 131104 | tf_op jit(solution)/shard_map/ppermute | solution.py:45
  31.6 13.1 %all-to-all-done.1 = bf16[8,256,256]{2,1,0:T(8,128)(2,1)S(1)} async-done(((bf16[8,256,256]{2,1,0:T(8,128)(2,1)}), bf16[8,256,256]{2,1,0:T(8,128)(2,1)S(1)}, u32[]{:S(2)}, u32[]{:S(2)}) %all-to-all-start.1) | async-done | bytes 1048608 | tf_op jit(solution)/shard_map/all_to_all | solution.py:271
  44.8 1.4 %copy-done.14 = s32[1024,128]{1,0:T(8,128)S(1)} copy-done((s32[1024,128]{1,0:T(8,128)S(1)}, s32[1024,128]{1,0:T(8,128)}, u32[]{:S(2)}) %copy-start.14) | copy-done | bytes 524312
  46.6 1.3 %collective-permute-start.2 = (bf16[256,256]{1,0:T(8,128)(2,1)S(1)}, bf16[256,256]{1,0:T(8,128)(2,1)S(1)}, u32[]{:S(2)}, u32[]{:S(2)}) collective-permute-start(bf16[256,256]{1,0:T(8,128)(2,1)S(1)} %order.2.refs_2_.refs_0_), channel_id=1, source_target_pairs={{0,2},{1,3},{2,0},{3,1},{4,6},{5,7},{6,4},{7,5},{8,10},{9,11},{10,... | collective-permute-start | bytes 393224 | tf_op jit(solution)/shard_map/ppermute | solution.py:39
  50.8 6.9 %collective-permute-start.3 = (bf16[256,512]{1,0:T(8,128)(2,1)S(1)}, bf16[256,512]{1,0:T(8,128)(2,1)S(1)}, u32[]{:S(2)}, u32[]{:S(2)}) collective-permute-start(bf16[256,512]{1,0:T(8,128)(2,1)S(1)} %pair.2), channel_id=1, source_target_pairs={{0,1},{1,0},{2,3},{3,2},{4,5},{5,4},{6,7},{7,6},{8,9},{9,8},{10,11... | collective-permute-start | bytes 786440 | tf_op jit(solution)/shard_map/ppermute | solution.py:39
  58.9 1.6 %feed.4 = (f32[256,512]{1,0:T(8,128)S(1)}, bf16[256,512]{1,0:T(8,128)(2,1)S(1)}) custom-call(bf16[256,256]{1,0:T(8,128)(2,1)S(1)} %order.2.refs_2_.refs_0_, bf16[256,256]{1,0:T(8,128)(2,1)S(1)} %collective-permute-done.2.refs_1_, bf16[256,512]{1,0:T(8,128)(2,1)S(1)} %collective-permute-done.3.refs_2_, bf16[1024,1024]{1,0:T(8,128)(2,1)S(1)} %copy-done, ...), custom_call_target="tpu_custom_call" | custom-call | flops 1024 | bytes 1024 | tf_op jit(solution)/shard_map/feed/pallas_call | solution.py:26
  60.5 4.3 %collective-permute-start.4 = (bf16[768,512]{1,0:T(8,128)(2,1)S(1)}, bf16[768,512]{1,0:T(8,128)(2,1)S(1)}, u32[]{:S(2)}, u32[]{:S(2)}) collective-permute-start(bf16[768,512]{1,0:T(8,128)(2,1)S(1)} %pair.3), channel_id=1, source_target_pairs={{0,1},{1,0},{2,3},{3,2},{4,5},{5,4},{6,7},{7,6},{8,9},{9,8},{10,11... | collective-permute-start | bytes 2359304 | tf_op jit(solution)/shard_map/ppermute | solution.py:39
  65.0 2.2 %collective-permute-done.5.refs_1_ = bf16[256,512]{1,0:T(8,128)(2,1)S(1)} collective-permute-done((bf16[256,512]{1,0:T(8,128)(2,1)S(1)}, bf16[256,512]{1,0:T(8,128)(2,1)S(1)}, u32[]{:S(2)}, u32[]{:S(2)}) %collective-permute-start.5) | collective-permute-done | bytes 262176 | tf_op jit(solution)/shard_map/ppermute | solution.py:39
  67.9 1.6 %feed.5 = (f32[256,512]{1,0:T(8,128)S(1)}, bf16[256,512]{1,0:T(8,128)(2,1)S(1)}) custom-call(bf16[768,256]{1,0:T(8,128)(2,1)S(1)} %order.3.refs_5_.refs_0_, bf16[768,256]{1,0:T(8,128)(2,1)S(1)} %collective-permute-done.1.refs_6_.refs_1_, bf16[768,512]{1,0:T(8,128)(2,1)S(1)} %collective-permute-done.4.refs_2_, bf16[1024,1024]{1,0:T(8,128)(2,1)S(1)} %copy-done, ...), custom_call_target="tpu_custom_call" | custom-call | flops 1024 | bytes 1024 | tf_op jit(solution)/shard_map/feed/pallas_call | solution.py:26
  70.2 2.3 %feed.6 = (f32[256,512]{1,0:T(8,128)S(1)}, bf16[256,512]{1,0:T(8,128)(2,1)}) custom-call(bf16[768,256]{1,0:T(8,128)(2,1)S(1)} %order.3.refs_5_.refs_0_, bf16[768,256]{1,0:T(8,128)(2,1)S(1)} %collective-permute-done.1.refs_6_.refs_1_, bf16[768,512]{1,0:T(8,128)(2,1)S(1)} %collective-permute-done.4.refs_2_, bf16[1024,1024]{1,0:T(8,128)(2,1)S(1)} %copy-done, ...), custom_call_target="tpu_custom_call" | custom-call | flops 1024 | bytes 1024 | tf_op jit(solution)/shard_map/feed/pallas_call | solution.py:26
  72.6 2.2 %collective-permute-done.8.refs_3_ = bf16[256,512]{1,0:T(8,128)(2,1)S(1)} collective-permute-done((bf16[256,512]{1,0:T(8,128)(2,1)S(1)}, bf16[256,512]{1,0:T(8,128)(2,1)S(1)}, u32[]{:S(2)}, u32[]{:S(2)}) %collective-permute-start.8) | collective-permute-done | bytes 262176 | tf_op jit(solution)/shard_map/ppermute | solution.py:39
  80.4 1.6 %copy-done.2 = bf16[1024,1024]{1,0:T(8,128)(2,1)S(1)} copy-done((bf16[1024,1024]{1,0:T(8,128)(2,1)S(1)}, bf16[1024,1024]{1,0:T(8,128)(2,1)}, u32[]{:S(2)}) %copy-start.2) | copy-done | bytes 2097176
  83.2 1.6 %feed.7 = (f32[256,512]{1,0:T(8,128)S(1)}, bf16[256,512]{1,0:T(8,128)(2,1)S(1)}) custom-call(bf16[768,256]{1,0:T(8,128)(2,1)S(1)} %order.3.refs_5_.refs_0_, bf16[768,256]{1,0:T(8,128)(2,1)S(1)} %collective-permute-done.1.refs_6_.refs_1_, bf16[768,512]{1,0:T(8,128)(2,1)S(1)} %copy-done.8, bf16[1024,1024]{1,0:T(8,128)(2,1)S(1)} %copy-done, ...), custom_call_target="tpu_custom_call" | custom-call | flops 1024 | bytes 1024 | tf_op jit(solution)/shard_map/feed/pallas_call | solution.py:26
  86.3 1.7 %attend.3.refs_4_.refs_8_ = bf16[64,1024]{1,0:T(8,128)(2,1)S(1)} custom-call(bf16[256,512]{1,0:T(8,128)(2,1)S(1)} %copy-done.10, bf16[256,512]{1,0:T(8,128)(2,1)S(1)} %collective-permute-done.11.refs_1_, bf16[1024,1024]{1,0:T(8,128)(2,1)S(1)} %copy-done.3, bf16[1024,1024]{1,0:T(8,128)(2,1)S(1)} %copy-done.4, bf16[64,1024]{1,0:T(8,128)(2,1)S(1)} %pad_maximum_fusion.refs_4_, ...), custom_call_target="tpu_custom_call" | custom-call | flops 1024 | bytes 1024 | tf_op jit(solution)/shard_map/attend/pallas_call | solution.py:26
  89.4 3.7 %collective-permute-start.15 = (bf16[64,1024]{1,0:T(8,128)(2,1)S(1)}, bf16[64,1024]{1,0:T(8,128)(2,1)S(1)}, u32[]{:S(2)}, u32[]{:S(2)}) collective-permute-start(bf16[64,1024]{1,0:T(8,128)(2,1)S(1)} %attend.3.refs_4_.refs_8_), channel_id=1, source_target_pairs={{0,4},{4,8},{8,12},{12,16},{16,20},{20,24},{24,28},{1,5},{5,9},{9,... | collective-permute-start | bytes 393224 | tf_op jit(solution)/shard_map/ppermute | solution.py:45
  93.3 1.5 %collective-permute-start.17 = (bf16[256,512]{1,0:T(8,128)(2,1)S(1)}, bf16[256,512]{1,0:T(8,128)(2,1)S(1)}, u32[]{:S(2)}, u32[]{:S(2)}) collective-permute-start(bf16[256,512]{1,0:T(8,128)(2,1)S(1)} %finish.6.refs_5_.refs_0_), channel_id=1, source_target_pairs={{0,1},{1,0},{2,3},{3,2},{4,5},{5,4},{6,7},{7,6},{8,9},{9,8},{10,11... | collective-permute-start | bytes 786440 | tf_op jit(solution)/shard_map/ppermute | solution.py:39
  94.9 1.7 %attend.4.refs_4_.refs_6_ = bf16[64,1024]{1,0:T(8,128)(2,1)S(1)} custom-call(bf16[256,512]{1,0:T(8,128)(2,1)S(1)} %finish.5.refs_2_.refs_0_, bf16[256,512]{1,0:T(8,128)(2,1)S(1)} %collective-permute-done.13.refs_1_, bf16[1024,1024]{1,0:T(8,128)(2,1)S(1)} %copy-done.3, bf16[1024,1024]{1,0:T(8,128)(2,1)S(1)} %copy-done.4, ...), custom_call_target="tpu_custom_call" | custom-call | flops 1024 | bytes 1024 | tf_op jit(solution)/shard_map/attend/pallas_call | solution.py:26
  96.6 2.1 %collective-permute-done.12.refs_3_ = bf16[256,512]{1,0:T(8,128)(2,1)S(1)} collective-permute-done((bf16[256,512]{1,0:T(8,128)(2,1)S(1)}, bf16[256,512]{1,0:T(8,128)(2,1)S(1)}, u32[]{:S(2)}, u32[]{:S(2)}) %collective-permute-start.12) | collective-permute-done | bytes 262176 | tf_op jit(solution)/shard_map/ppermute | solution.py:39
  99.9 1.7 %attend.5.refs_7_ = bf16[64,1024]{1,0:T(8,128)(2,1)S(1)} custom-call(bf16[256,512]{1,0:T(8,128)(2,1)S(1)} %finish.6.refs_5_.refs_0_, bf16[256,512]{1,0:T(8,128)(2,1)S(1)} %collective-permute-done.17.refs_1_, bf16[1024,1024]{1,0:T(8,128)(2,1)S(1)} %copy-done.3, bf16[1024,1024]{1,0:T(8,128)(2,1)S(1)} %copy-done.4, ...), custom_call_target="tpu_custom_call" | custom-call | flops 1024 | bytes 1024 | tf_op jit(solution)/shard_map/attend/pallas_call | solution.py:26
  101.6 2.6 %attend_last.1 = bf16[256,1024]{1,0:T(8,128)(2,1)} custom-call(bf16[256,512]{1,0:T(8,128)(2,1)S(1)} %finish.7.refs_5_.refs_0_, bf16[256,512]{1,0:T(8,128)(2,1)S(1)} %collective-permute-done.16.refs_1_, bf16[1024,1024]{1,0:T(8,128)(2,1)S(1)} %copy-done.3, bf16[1024,1024]{1,0:T(8,128)(2,1)S(1)} %copy-done.4, bf16[64,1024]{1,0:T(8,128)(2,1)S(1)} %get-tuple-element.47.refs_4_, ...), custom_call_target="tpu_custom_call" | custom-call | flops 1024 | bytes 1024 | tf_op jit(solution)/shard_map/attend_last/pallas_call | solution.py:26
  (92 shorter events, 19.4 us)
Async XLA Ops:
  0.7 13.2 %copy-start.11 = (bf16[256,1024]{1,0:T(8,128)(2,1)S(1)}, bf16[256,1024]{1,0:T(8,128)(2,1)}, u32[]{:S(2)}) copy-start(bf16[256,1024]{1,0:T(8,128)(2,1)} %refs_2_.5) | copy-start | bytes 1572868
  0.7 13.2 %copy-start.15 = (bf16[2048,256]{1,0:T(8,128)(2,1)S(1)}, bf16[2048,256]{1,0:T(8,128)(2,1)}, u32[]{:S(2)}) copy-start(bf16[2048,256]{1,0:T(8,128)(2,1)} %refs_1_.1) | copy-start | bytes 3145732
  17.4 27.3 %all-to-all-start.1 = ((bf16[8,256,256]{2,1,0:T(8,128)(2,1)}), bf16[8,256,256]{2,1,0:T(8,128)(2,1)S(1)}, u32[]{:S(2)}, u32[]{:S(2)}) async-start(bf16[8,256,256]{2,1,0:T(8,128)(2,1)} %bitcast.3), calls=%async_computation.1 | async-start | bytes 2097152 | tf_op jit(solution)/shard_map/all_to_all | solution.py:271
  21.0 10.6 %collective-permute-start = (bf16[64,1024]{1,0:T(8,128)(2,1)S(1)}, bf16[64,1024]{1,0:T(8,128)(2,1)S(1)}, u32[]{:S(2)}, u32[]{:S(2)}) collective-permute-start(bf16[64,1024]{1,0:T(8,128)(2,1)S(1)} %get-tuple-element.28), channel_id=1, source_target_pairs={{4,0},{8,4},{12,8},{16,12},{20,16},{24,20},{28,24},{5,1},{9,5},{13... | collective-permute-start | bytes 393224 | tf_op jit(solution)/shard_map/ppermute | solution.py:45
  31.6 16.3 %copy-start.18 = (bf16[64,1024]{1,0:T(8,128)(2,1)}, bf16[64,1024]{1,0:T(8,128)(2,1)S(1)}, u32[]{:S(2)}) copy-start(bf16[64,1024]{1,0:T(8,128)(2,1)S(1)} %collective-permute-done.refs_2_) | copy-start | bytes 393220
  46.2 12.7 %copy-start = (bf16[1024,1024]{1,0:T(8,128)(2,1)S(1)}, bf16[1024,1024]{1,0:T(8,128)(2,1)}, u32[]{:S(2)}) copy-start(bf16[1024,1024]{1,0:T(8,128)(2,1)} %refs_3_.11) | copy-start | bytes 6291460
  46.2 12.7 %copy-start.1 = (bf16[1024,1024]{1,0:T(8,128)(2,1)S(1)}, bf16[1024,1024]{1,0:T(8,128)(2,1)}, u32[]{:S(2)}) copy-start(bf16[1024,1024]{1,0:T(8,128)(2,1)} %refs_4_.7) | copy-start | bytes 6291460
  46.6 4.2 %collective-permute-start.2 = (bf16[256,256]{1,0:T(8,128)(2,1)S(1)}, bf16[256,256]{1,0:T(8,128)(2,1)S(1)}, u32[]{:S(2)}, u32[]{:S(2)}) collective-permute-start(bf16[256,256]{1,0:T(8,128)(2,1)S(1)} %order.2.refs_2_.refs_0_), channel_id=1, source_target_pairs={{0,2},{1,3},{2,0},{3,1},{4,6},{5,7},{6,4},{7,5},{8,10},{9,11},{10,... | collective-permute-start | bytes 393224 | tf_op jit(solution)/shard_map/ppermute | solution.py:39
  50.1 8.7 %collective-permute-start.1 = (bf16[768,256]{1,0:T(8,128)(2,1)S(1)}, bf16[768,256]{1,0:T(8,128)(2,1)S(1)}, u32[]{:S(2)}, u32[]{:S(2)}) collective-permute-start(bf16[768,256]{1,0:T(8,128)(2,1)S(1)} %order.3.refs_5_.refs_0_), channel_id=1, source_target_pairs={{0,2},{1,3},{2,0},{3,1},{4,6},{5,7},{6,4},{7,5},{8,10},{9,11},{10,... | collective-permute-start | bytes 1179656 | tf_op jit(solution)/shard_map/ppermute | solution.py:39
  50.8 8.0 %collective-permute-start.3 = (bf16[256,512]{1,0:T(8,128)(2,1)S(1)}, bf16[256,512]{1,0:T(8,128)(2,1)S(1)}, u32[]{:S(2)}, u32[]{:S(2)}) collective-permute-start(bf16[256,512]{1,0:T(8,128)(2,1)S(1)} %pair.2), channel_id=1, source_target_pairs={{0,1},{1,0},{2,3},{3,2},{4,5},{5,4},{6,7},{7,6},{8,9},{9,8},{10,11... | collective-permute-start | bytes 786440 | tf_op jit(solution)/shard_map/ppermute | solution.py:39
  60.5 7.4 %collective-permute-start.4 = (bf16[768,512]{1,0:T(8,128)(2,1)S(1)}, bf16[768,512]{1,0:T(8,128)(2,1)S(1)}, u32[]{:S(2)}, u32[]{:S(2)}) collective-permute-start(bf16[768,512]{1,0:T(8,128)(2,1)S(1)} %pair.3), channel_id=1, source_target_pairs={{0,1},{1,0},{2,3},{3,2},{4,5},{5,4},{6,7},{7,6},{8,9},{9,8},{10,11... | collective-permute-start | bytes 2359304 | tf_op jit(solution)/shard_map/ppermute | solution.py:39
  64.9 2.3 %collective-permute-start.5 = (bf16[256,512]{1,0:T(8,128)(2,1)S(1)}, bf16[256,512]{1,0:T(8,128)(2,1)S(1)}, u32[]{:S(2)}, u32[]{:S(2)}) collective-permute-start(bf16[256,512]{1,0:T(8,128)(2,1)S(1)} %get-tuple-element.29.refs_2_), channel_id=1, source_target_pairs={{0,1},{1,0},{2,3},{3,2},{4,5},{5,4},{6,7},{7,6},{8,9},{9,8},{10,11... | collective-permute-start | bytes 786440 | tf_op jit(solution)/shard_map/ppermute | solution.py:39
  67.2 7.6 %collective-permute-start.8 = (bf16[256,512]{1,0:T(8,128)(2,1)S(1)}, bf16[256,512]{1,0:T(8,128)(2,1)S(1)}, u32[]{:S(2)}, u32[]{:S(2)}) collective-permute-start(bf16[256,512]{1,0:T(8,128)(2,1)S(1)} %get-tuple-element.31.refs_5_), channel_id=1, source_target_pairs={{0,2},{1,3},{2,0},{3,1},{4,6},{5,7},{6,4},{7,5},{8,10},{9,11},{10,... | collective-permute-start | bytes 786440 | tf_op jit(solution)/shard_map/ppermute | solution.py:39
  69.5 5.4 %collective-permute-start.7 = (bf16[256,512]{1,0:T(8,128)(2,1)S(1)}, bf16[256,512]{1,0:T(8,128)(2,1)S(1)}, u32[]{:S(2)}, u32[]{:S(2)}) collective-permute-start(bf16[256,512]{1,0:T(8,128)(2,1)S(1)} %get-tuple-element.32.refs_5_), channel_id=1, source_target_pairs={{0,1},{1,0},{2,3},{3,2},{4,5},{5,4},{6,7},{7,6},{8,9},{9,8},{10,11... | collective-permute-start | bytes 786440 | tf_op jit(solution)/shard_map/ppermute | solution.py:39
  72.6 5.8 %collective-permute-start.6 = (bf16[256,512]{1,0:T(8,128)(2,1)}, bf16[256,512]{1,0:T(8,128)(2,1)S(1)}, u32[]{:S(2)}, u32[]{:S(2)}) collective-permute-start(bf16[256,512]{1,0:T(8,128)(2,1)} %get-tuple-element.34.refs_4_), channel_id=1, source_target_pairs={{0,1},{1,0},{2,3},{3,2},{4,5},{5,4},{6,7},{7,6},{8,9},{9,8},{10,11... | collective-permute-start | bytes 786440 | tf_op jit(solution)/shard_map/ppermute | solution.py:39
  76.5 9.7 %collective-permute-start.11 = (bf16[256,512]{1,0:T(8,128)(2,1)}, bf16[256,512]{1,0:T(8,128)(2,1)S(1)}, u32[]{:S(2)}, u32[]{:S(2)}) collective-permute-start(bf16[256,512]{1,0:T(8,128)(2,1)} %relay.1.refs_0_), channel_id=1, source_target_pairs={{0,1},{1,0},{2,3},{3,2},{4,5},{5,4},{6,7},{7,6},{8,9},{9,8},{10,11... | collective-permute-start | bytes 786440 | tf_op jit(solution)/shard_map/ppermute | solution.py:39
  77.7 10.2 %collective-permute-start.10 = (bf16[256,512]{1,0:T(8,128)(2,1)}, bf16[256,512]{1,0:T(8,128)(2,1)S(1)}, u32[]{:S(2)}, u32[]{:S(2)}) collective-permute-start(bf16[256,512]{1,0:T(8,128)(2,1)} %copy-done.16), channel_id=1, source_target_pairs={{0,2},{1,3},{2,0},{3,1},{4,6},{5,7},{6,4},{7,5},{8,10},{9,11},{10,... | collective-permute-start | bytes 786440 | tf_op jit(solution)/shard_map/ppermute | solution.py:39
  84.8 3.9 %collective-permute-start.9 = (bf16[256,512]{1,0:T(8,128)(2,1)S(1)}, bf16[256,512]{1,0:T(8,128)(2,1)S(1)}, u32[]{:S(2)}, u32[]{:S(2)}) collective-permute-start(bf16[256,512]{1,0:T(8,128)(2,1)S(1)} %get-tuple-element.40.refs_5_), channel_id=1, source_target_pairs={{0,1},{1,0},{2,3},{3,2},{4,5},{5,4},{6,7},{7,6},{8,9},{9,8},{10,11... | collective-permute-start | bytes 786440 | tf_op jit(solution)/shard_map/ppermute | solution.py:39
  85.3 7.9 %collective-permute-start.14 = (bf16[256,512]{1,0:T(8,128)(2,1)S(1)}, bf16[256,512]{1,0:T(8,128)(2,1)S(1)}, u32[]{:S(2)}, u32[]{:S(2)}) collective-permute-start(bf16[256,512]{1,0:T(8,128)(2,1)S(1)} %get-tuple-element.38.refs_5_), channel_id=1, source_target_pairs={{0,2},{1,3},{2,0},{3,1},{4,6},{5,7},{6,4},{7,5},{8,10},{9,11},{10,... | collective-permute-start | bytes 786440 | tf_op jit(solution)/shard_map/ppermute | solution.py:39
  88.1 6.8 %collective-permute-start.13 = (bf16[256,512]{1,0:T(8,128)(2,1)S(1)}, bf16[256,512]{1,0:T(8,128)(2,1)S(1)}, u32[]{:S(2)}, u32[]{:S(2)}) collective-permute-start(bf16[256,512]{1,0:T(8,128)(2,1)S(1)} %finish.5.refs_2_.refs_0_), channel_id=1, source_target_pairs={{0,1},{1,0},{2,3},{3,2},{4,5},{5,4},{6,7},{7,6},{8,9},{9,8},{10,11... | collective-permute-start | bytes 786440 | tf_op jit(solution)/shard_map/ppermute | solution.py:39
  88.7 9.9 %collective-permute-start.12 = (bf16[256,512]{1,0:T(8,128)(2,1)S(1)}, bf16[256,512]{1,0:T(8,128)(2,1)S(1)}, u32[]{:S(2)}, u32[]{:S(2)}) collective-permute-start(bf16[256,512]{1,0:T(8,128)(2,1)S(1)} %get-tuple-element.43.refs_4_), channel_id=1, source_target_pairs={{0,2},{1,3},{2,0},{3,1},{4,6},{5,7},{6,4},{7,5},{8,10},{9,11},{10,... | collective-permute-start | bytes 786440 | tf_op jit(solution)/shard_map/ppermute | solution.py:39
  89.4 7.2 %collective-permute-start.15 = (bf16[64,1024]{1,0:T(8,128)(2,1)S(1)}, bf16[64,1024]{1,0:T(8,128)(2,1)S(1)}, u32[]{:S(2)}, u32[]{:S(2)}) collective-permute-start(bf16[64,1024]{1,0:T(8,128)(2,1)S(1)} %attend.3.refs_4_.refs_8_), channel_id=1, source_target_pairs={{0,4},{4,8},{8,12},{12,16},{16,20},{20,24},{24,28},{1,5},{5,9},{9,... | collective-permute-start | bytes 393224 | tf_op jit(solution)/shard_map/ppermute | solution.py:45
  93.3 6.5 %collective-permute-start.17 = (bf16[256,512]{1,0:T(8,128)(2,1)S(1)}, bf16[256,512]{1,0:T(8,128)(2,1)S(1)}, u32[]{:S(2)}, u32[]{:S(2)}) collective-permute-start(bf16[256,512]{1,0:T(8,128)(2,1)S(1)} %finish.6.refs_5_.refs_0_), channel_id=1, source_target_pairs={{0,1},{1,0},{2,3},{3,2},{4,5},{5,4},{6,7},{7,6},{8,9},{9,8},{10,11... | collective-permute-start | bytes 786440 | tf_op jit(solution)/shard_map/ppermute | solution.py:39
  98.8 2.8 %collective-permute-start.16 = (bf16[256,512]{1,0:T(8,128)(2,1)S(1)}, bf16[256,512]{1,0:T(8,128)(2,1)S(1)}, u32[]{:S(2)}, u32[]{:S(2)}) collective-permute-start(bf16[256,512]{1,0:T(8,128)(2,1)S(1)} %finish.7.refs_5_.refs_0_), channel_id=1, source_target_pairs={{0,1},{1,0},{2,3},{3,2},{4,5},{5,4},{6,7},{7,6},{8,9},{9,8},{10,11... | collective-permute-start | bytes 786440 | tf_op jit(solution)/shard_map/ppermute | solution.py:39
  (20 other events, 34.6 us)

commit v7 on v6

--- a/solution.py
+++ b/solution.py
@@ -92,9 +92,7 @@
     slot_ref[...] = columns_of(owner * cap + rank)
 
 
-def fetch_body(req_ref, vocab_ref, queries_hbm, out_ref, head_ref, sem):
-    copy = pltpu.make_async_copy(queries_hbm.at[pl.ds(0, head_ref.shape[0]), :], head_ref, sem)
-    copy.start()
+def fetch_body(req_ref, vocab_ref, out_ref):
     step = 256
     table = vocab_ref[...]
     for at in range(0, req_ref.shape[1], step):
@@ -102,26 +100,16 @@
         out_ref[at : at + step, :] = jnp.dot(
             picked, table, preferred_element_type=F32
         ).astype(BF16)
-    copy.wait()
-
-
-def relay(x, after):
-    unread = pl.BlockSpec(memory_space=pl.ANY)
-    return pl.pallas_call(
-        lambda *refs: None,
-        out_shape=jax.ShapeDtypeStruct(x.shape, x.dtype),
-        in_specs=[unread] * 2,
-        out_specs=unread,
-        input_output_aliases={0: 0},
-        cost_estimate=pl.CostEstimate(flops=1024, bytes_accessed=1024, transcendentals=0),
-        name="relay",
-    )(x, after)
 
 
 def pair_body(left_ref, right_ref, out_ref):
     width = left_ref.shape[1]
     out_ref[:, :width] = left_ref[...]
     out_ref[:, width:] = right_ref[...]
+
+
+def head_body(queries_ref, out_ref):
+    out_ref[...] = queries_ref[: out_ref.shape[0], :]
 
 
 def order_body(groups, slot_ref, rows_ref, out_ref):
@@ -258,23 +246,19 @@
         flops=8 * 10**9,
     )
     request = lax.all_to_all(wanted, "seq", split_axis=0, concat_axis=0, tiled=True)
-    vmem = pl.BlockSpec(memory_space=pltpu.VMEM)
-    found, head = call(
+    found = call(
         fetch_body,
-        (sds((slots, width), BF16), sds((GROUP, head_cols), BF16)),
+        sds((slots, width), BF16),
         "fetch",
-        (request.reshape(1, slots), vocab_rows, queries),
-        in_specs=[vmem, vmem, pl.BlockSpec(memory_space=pl.ANY)],
-        scratch_shapes=[pltpu.SemaphoreType.DMA],
-    )
-    next_q = shifted(head, -1)
+        (request.reshape(1, slots), vocab_rows),
+    )
     answered = lax.all_to_all(
         found.reshape(seq_size, cap, width), "seq", split_axis=0, concat_axis=0, tiled=True
     ).reshape(slots, width)
     order = [groups - 1] + list(range(groups - 1))
     plan = [order[:1], order[1:]]
     first, window = {}, {}
-    token = next_q
+    token = slot
     pieces = []
     for part in plan:
         e0 = token = call(
@@ -294,6 +278,8 @@
         piece[2] = exchange(both, 1)
 
     across(pieces[0])
+    head = call(head_body, sds((GROUP, head_cols), BF16), "head", (queries,), (token,))
+    next_q = shifted(head, -1)
     local_q = jnp.concatenate([queries[GROUP - 1 :], next_q[: GROUP - 1]], axis=0)
     half = sds((per_group, 2 * width), BF16)
     whole = sds((per_group, 2 * width), F32)
@@ -313,7 +299,7 @@
             (whole, half),
             "feed",
             (*emb(g), w_in, w_out),
-            (token, pieces[1][1]),
+            (token, pieces[1][1], next_q),
         )
         fed[g] = keep, exchange(token, 1)
 
@@ -331,11 +317,7 @@
             (*emb(g)[:2], summed[g], far[g]),
             (token, behind) if g == order[-1] else (token,),
         )
-        encoded[g] = token, None if g == order[0] else exchange(token, 1)
-
-    def hand(g):
-        mine = relay(encoded[g][0], token)
-        encoded[g] = mine, exchange(mine, 1)
+        encoded[g] = token, exchange(token, 1)
 
     def attend(g):
         nonlocal token, behind, out
@@ -357,9 +339,9 @@
 
     a, b, c, d = order
     for step, g in (
-        (feed, a), (rest, b), (add, a), (feed, b), (feed, c),
-        (finish, a), (add, b), (hand, a), (add, c), (feed, d), (attend, a),
-        (finish, b), (add, d),
+        (feed, a), (rest, b), (feed, b), (add, a), (feed, c), (add, b),
+        (finish, a), (feed, d), (add, c),
+        (finish, b), (attend, a), (add, d),
         (finish, c), (attend, b),
         (finish, d), (attend, c), (attend, d),
     ):

time: 106 us -> 95.8 us (0.904); the launches traced: 104 us -> 95.4 us
  blocking collectives: 11.5 us -> 38.6 us
  waiting for transfers between devices: 30 us -> 13.9 us
  local copies, waits for them, and re-layouts: 10.6 us -> 0.92 us
  starting transfers between devices: 30.4 us -> 22.4 us
  Pallas kernels: 21.2 us -> 19.3 us
    all_to_all x0 -> x1, blocking collectives: none -> 27.1 us  [per_device(): lax.all_to_all(found.reshape(seq_size, cap, width), 'seq', split_axis=0,...]
    all_to_all x1 -> x0, waiting for transfers between devices: 13.1 us -> none  [per_device(): lax.all_to_all(found.reshape(seq_size, cap, width), 'seq', split_axis=0,...]
    unnamed x50 -> x14, local copies, waits for them, and re-layouts: 10.4 us -> 0.71 us
    ppermute x16, starting transfers between devices: 21.6 us -> 16.9 us  [exchange(): return lax.ppermute(x, 'tp', [(i, i ^ bit) for i in range(size)])]
    all_to_all x1 -> x0, starting transfers between devices: 3.57 us -> none  [per_device(): lax.all_to_all(found.reshape(seq_size, cap, width), 'seq', split_axis=0,...]
    ppermute x2, waiting for transfers between devices: 9.14 us -> 5.7 us  [shifted(): return lax.ppermute(x, 'seq', pairs)]
    pallas_call x22 -> x23, Pallas kernels: 21.2 us -> 19.3 us  [call(): pl.pallas_call(without_after, out_shape=outs, in_specs=in_specs + [unread...]
  transfers between devices with their start and end apart: 19 -> 18, of which waited for: 6 -> 6; matrix products, arithmetic and copies ran while one was open for 0% -> 0% of each run, Pallas kernels for 12% -> 12%
where the time goes in v7:
time: 95.8 us; the launch traced here: 95.4 us
  blocking collectives  38.6 us (40%)
  starting transfers between devices  22.4 us (23%)
  Pallas kernels  19.3 us (20%)
  waiting for transfers between devices  13.9 us (15%)
    all_to_all x1, blocking collectives, per_device(): lax.all_to_all(found.reshape(seq_size, cap, width), 'seq', split_axis=0,...  27.1 us
    pallas_call x23, Pallas kernels, call(): pl.pallas_call(without_after, out_shape=outs, in_specs=in_specs + [unread...  19.3 us
    ppermute x16, starting transfers between devices, exchange(): return lax.ppermute(x, 'tp', [(i, i ^ bit) for i in range(size)])  16.9 us
    all_to_all x1, blocking collectives, per_device(): lax.all_to_all(wanted, 'seq', split_axis=0, concat_axis=0, tiled=True)  11.5 us
    ppermute x16, waiting for transfers between devices, exchange(): return lax.ppermute(x, 'tp', [(i, i ^ bit) for i in range(size)])  8.18 us
    ppermute x2, waiting for transfers between devices, shifted(): return lax.ppermute(x, 'seq', pairs)  5.7 us
    ppermute x2, starting transfers between devices, shifted(): return lax.ppermute(x, 'seq', pairs)  5.46 us
  transfers between devices with their start and end apart: 18, of which 6 were waited for; matrix products, arithmetic and copies ran while one was open for 0% of the time, Pallas kernels for 12%

profile of v7, /device:TPU:1, one launch (start us, length us, event | category | flops | bytes accessed | tf_op | source)
XLA Modules:
  0.0 95.4 jit_solution(17550492375969739351)
XLA Ops:
  1.5 11.5 %all_to_all.14 = s32[8,1,256]{2,1,0:T(1,128)S(1)} all-to-all(s32[8,1,256]{2,1,0:T(1,128)S(1)} %copy.8), channel_id=1, replica_groups=mesh['seq'=8,'tp'=4] {'seq'}, dimensions={0} | all-to-all | bytes 16384 | tf_op jit(solution)/shard_map/all_to_all | solution.py:248
  13.1 2.4 %fetch.1 = bf16[2048,256]{1,0:T(8,128)(2,1)S(1)} custom-call(s32[1,2048]{1,0:T(1,128)S(1)} %bitcast.10, bf16[2048,256]{1,0:T(8,128)(2,1)S(1)} %copy-done.5), custom_call_target="tpu_custom_call" | custom-call | flops 1024 | bytes 1024 | tf_op jit(solution)/shard_map/fetch/pallas_call | solution.py:26
  15.4 27.1 %all_to_all.15 = bf16[8,256,256]{2,1,0:T(8,128)(2,1)S(1)} all-to-all(bf16[8,256,256]{2,1,0:T(8,128)(2,1)S(1)} %bitcast.8), channel_id=1, replica_groups=mesh['seq'=8,'tp'=4] {'seq'}, dimensions={0} | all-to-all | bytes 2097152 | tf_op jit(solution)/shard_map/all_to_all | solution.py:255
  43.0 1.3 %collective-permute-start.1 = (bf16[256,256]{1,0:T(8,128)(2,1)S(1)}, bf16[256,256]{1,0:T(8,128)(2,1)S(1)}, u32[]{:S(2)}, u32[]{:S(2)}) collective-permute-start(bf16[256,256]{1,0:T(8,128)(2,1)S(1)} %order.2.refs_2_.refs_0_), channel_id=1, source_target_pairs={{0,2},{1,3},{2,0},{3,1},{4,6},{5,7},{6,4},{7,5},{8,10},{9,11},{10,... | collective-permute-start | bytes 393224 | tf_op jit(solution)/shard_map/ppermute | solution.py:39
  45.6 1.3 %collective-permute-done.1.refs_1_ = bf16[256,256]{1,0:T(8,128)(2,1)S(1)} collective-permute-done((bf16[256,256]{1,0:T(8,128)(2,1)S(1)}, bf16[256,256]{1,0:T(8,128)(2,1)S(1)}, u32[]{:S(2)}, u32[]{:S(2)}) %collective-permute-start.1) | collective-permute-done | bytes 131104 | tf_op jit(solution)/shard_map/ppermute | solution.py:39
  46.9 4.6 %collective-permute-start.2 = (bf16[256,512]{1,0:T(8,128)(2,1)S(1)}, bf16[256,512]{1,0:T(8,128)(2,1)S(1)}, u32[]{:S(2)}, u32[]{:S(2)}) collective-permute-start(bf16[256,512]{1,0:T(8,128)(2,1)S(1)} %pair.2), channel_id=1, source_target_pairs={{0,1},{1,0},{2,3},{3,2},{4,5},{5,4},{6,7},{7,6},{8,9},{9,8},{10,11... | collective-permute-start | bytes 786440 | tf_op jit(solution)/shard_map/ppermute | solution.py:39
  51.6 1.3 %collective-permute-start.3 = (bf16[64,1024]{1,0:T(8,128)(2,1)S(1)}, bf16[64,1024]{1,0:T(8,128)(2,1)S(1)}, u32[]{:S(2)}, u32[]{:S(2)}) collective-permute-start(bf16[64,1024]{1,0:T(8,128)(2,1)S(1)} %head.1), channel_id=1, source_target_pairs={{4,0},{8,4},{12,8},{16,12},{20,16},{24,20},{28,24},{5,1},{9,5},{13... | collective-permute-start | bytes 393224 | tf_op jit(solution)/shard_map/ppermute | solution.py:45
  52.9 5.7 %collective-permute-done.3.refs_7_ = bf16[64,1024]{1,0:T(8,128)(2,1)S(1)} collective-permute-done((bf16[64,1024]{1,0:T(8,128)(2,1)S(1)}, bf16[64,1024]{1,0:T(8,128)(2,1)S(1)}, u32[]{:S(2)}, u32[]{:S(2)}) %collective-permute-start.3) | collective-permute-done | bytes 131104 | tf_op jit(solution)/shard_map/ppermute | solution.py:45
  58.6 1.6 %feed.4 = (f32[256,512]{1,0:T(8,128)S(1)}, bf16[256,512]{1,0:T(8,128)(2,1)S(1)}) custom-call(bf16[256,256]{1,0:T(8,128)(2,1)S(1)} %order.2.refs_2_.refs_0_, bf16[256,256]{1,0:T(8,128)(2,1)S(1)} %collective-permute-done.1.refs_1_, bf16[256,512]{1,0:T(8,128)(2,1)S(1)} %collective-permute-done.2.refs_2_, bf16[1024,1024]{1,0:T(8,128)(2,1)S(1)} %copy-done, ...), custom_call_target="tpu_custom_call" | custom-call | flops 1024 | bytes 1024 | tf_op jit(solution)/shard_map/feed/pallas_call | solution.py:26
  61.2 1.8 %collective-permute-done.4.refs_2_ = bf16[768,512]{1,0:T(8,128)(2,1)S(1)} collective-permute-done((bf16[768,512]{1,0:T(8,128)(2,1)S(1)}, bf16[768,512]{1,0:T(8,128)(2,1)S(1)}, u32[]{:S(2)}, u32[]{:S(2)}) %collective-permute-start.4) | collective-permute-done | bytes 786464 | tf_op jit(solution)/shard_map/ppermute | solution.py:39
  63.1 1.6 %feed.5 = (f32[256,512]{1,0:T(8,128)S(1)}, bf16[256,512]{1,0:T(8,128)(2,1)S(1)}) custom-call(bf16[768,256]{1,0:T(8,128)(2,1)S(1)} %order.3.refs_1_.refs_5_.refs_0_, bf16[768,256]{1,0:T(8,128)(2,1)S(1)} %collective-permute-done.refs_6_.refs_1_, bf16[768,512]{1,0:T(8,128)(2,1)S(1)} %collective-permute-done.4.refs_2_, bf16[1024,1024]{1,0:T(8,128)(2,1)S(1)} %copy-done, ...), custom_call_target="tpu_custom_call" | custom-call | flops 1024 | bytes 1024 | tf_op jit(solution)/shard_map/feed/pallas_call | solution.py:26
  65.2 1.4 %collective-permute-start.6 = (bf16[256,512]{1,0:T(8,128)(2,1)S(1)}, bf16[256,512]{1,0:T(8,128)(2,1)S(1)}, u32[]{:S(2)}, u32[]{:S(2)}) collective-permute-start(bf16[256,512]{1,0:T(8,128)(2,1)S(1)} %get-tuple-element.29.refs_5_), channel_id=1, source_target_pairs={{0,2},{1,3},{2,0},{3,1},{4,6},{5,7},{6,4},{7,5},{8,10},{9,11},{10,... | collective-permute-start | bytes 786440 | tf_op jit(solution)/shard_map/ppermute | solution.py:39
  66.6 1.6 %feed.6 = (f32[256,512]{1,0:T(8,128)S(1)}, bf16[256,512]{1,0:T(8,128)(2,1)S(1)}) custom-call(bf16[768,256]{1,0:T(8,128)(2,1)S(1)} %order.3.refs_1_.refs_5_.refs_0_, bf16[768,256]{1,0:T(8,128)(2,1)S(1)} %collective-permute-done.refs_6_.refs_1_, bf16[768,512]{1,0:T(8,128)(2,1)S(1)} %collective-permute-done.4.refs_2_, bf16[1024,1024]{1,0:T(8,128)(2,1)S(1)} %copy-done, ...), custom_call_target="tpu_custom_call" | custom-call | flops 1024 | bytes 1024 | tf_op jit(solution)/shard_map/feed/pallas_call | solution.py:26
  69.0 4.0 %collective-permute-done.6.refs_3_ = bf16[256,512]{1,0:T(8,128)(2,1)S(1)} collective-permute-done((bf16[256,512]{1,0:T(8,128)(2,1)S(1)}, bf16[256,512]{1,0:T(8,128)(2,1)S(1)}, u32[]{:S(2)}, u32[]{:S(2)}) %collective-permute-start.6) | collective-permute-done | bytes 262176 | tf_op jit(solution)/shard_map/ppermute | solution.py:39
  73.1 1.6 %collective-permute-start.9 = (bf16[256,512]{1,0:T(8,128)(2,1)S(1)}, bf16[256,512]{1,0:T(8,128)(2,1)S(1)}, u32[]{:S(2)}, u32[]{:S(2)}) collective-permute-start(bf16[256,512]{1,0:T(8,128)(2,1)S(1)} %finish.4.refs_5_.refs_0_), channel_id=1, source_target_pairs={{0,1},{1,0},{2,3},{3,2},{4,5},{5,4},{6,7},{7,6},{8,9},{9,8},{10,11... | collective-permute-start | bytes 786440 | tf_op jit(solution)/shard_map/ppermute | solution.py:39
  74.7 1.6 %feed.7 = (f32[256,512]{1,0:T(8,128)S(1)}, bf16[256,512]{1,0:T(8,128)(2,1)S(1)}) custom-call(bf16[768,256]{1,0:T(8,128)(2,1)S(1)} %order.3.refs_1_.refs_5_.refs_0_, bf16[768,256]{1,0:T(8,128)(2,1)S(1)} %collective-permute-done.refs_6_.refs_1_, bf16[768,512]{1,0:T(8,128)(2,1)S(1)} %collective-permute-done.4.refs_2_, bf16[1024,1024]{1,0:T(8,128)(2,1)S(1)} %copy-done, ...), custom_call_target="tpu_custom_call" | custom-call | flops 1024 | bytes 1024 | tf_op jit(solution)/shard_map/feed/pallas_call | solution.py:26
  76.6 1.4 %collective-permute-start.14 = (bf16[256,512]{1,0:T(8,128)(2,1)S(1)}, bf16[256,512]{1,0:T(8,128)(2,1)S(1)}, u32[]{:S(2)}, u32[]{:S(2)}) collective-permute-start(bf16[256,512]{1,0:T(8,128)(2,1)S(1)} %get-tuple-element.37.refs_4_), channel_id=1, source_target_pairs={{0,2},{1,3},{2,0},{3,1},{4,6},{5,7},{6,4},{7,5},{8,10},{9,11},{10,... | collective-permute-start | bytes 786440 | tf_op jit(solution)/shard_map/ppermute | solution.py:39
  79.7 1.7 %attend.3.refs_2_.refs_8_ = bf16[64,1024]{1,0:T(8,128)(2,1)S(1)} custom-call(bf16[256,512]{1,0:T(8,128)(2,1)S(1)} %finish.4.refs_5_.refs_0_, bf16[256,512]{1,0:T(8,128)(2,1)S(1)} %collective-permute-done.9.refs_1_, bf16[1024,1024]{1,0:T(8,128)(2,1)S(1)} %copy-done.2, bf16[1024,1024]{1,0:T(8,128)(2,1)S(1)} %copy-done.3, ...), custom_call_target="tpu_custom_call" | custom-call | flops 1024 | bytes 1024 | tf_op jit(solution)/shard_map/attend/pallas_call | solution.py:26
  81.5 1.4 %collective-permute-start.12 = (bf16[256,512]{1,0:T(8,128)(2,1)S(1)}, bf16[256,512]{1,0:T(8,128)(2,1)S(1)}, u32[]{:S(2)}, u32[]{:S(2)}) collective-permute-start(bf16[256,512]{1,0:T(8,128)(2,1)S(1)} %get-tuple-element.39.refs_4_), channel_id=1, source_target_pairs={{0,2},{1,3},{2,0},{3,1},{4,6},{5,7},{6,4},{7,5},{8,10},{9,11},{10,... | collective-permute-start | bytes 786440 | tf_op jit(solution)/shard_map/ppermute | solution.py:39
  82.9 4.2 %collective-permute-start.15 = (bf16[64,1024]{1,0:T(8,128)(2,1)S(1)}, bf16[64,1024]{1,0:T(8,128)(2,1)S(1)}, u32[]{:S(2)}, u32[]{:S(2)}) collective-permute-start(bf16[64,1024]{1,0:T(8,128)(2,1)S(1)} %attend.3.refs_2_.refs_8_), channel_id=1, source_target_pairs={{0,4},{4,8},{8,12},{12,16},{16,20},{20,24},{24,28},{1,5},{5,9},{9,... | collective-permute-start | bytes 393224 | tf_op jit(solution)/shard_map/ppermute | solution.py:45
  87.9 1.7 %attend.4.refs_4_.refs_6_ = bf16[64,1024]{1,0:T(8,128)(2,1)S(1)} custom-call(bf16[256,512]{1,0:T(8,128)(2,1)S(1)} %finish.5.refs_5_.refs_0_, bf16[256,512]{1,0:T(8,128)(2,1)S(1)} %collective-permute-done.13.refs_1_, bf16[1024,1024]{1,0:T(8,128)(2,1)S(1)} %copy-done.2, bf16[1024,1024]{1,0:T(8,128)(2,1)S(1)} %copy-done.3, ...), custom_call_target="tpu_custom_call" | custom-call | flops 1024 | bytes 1024 | tf_op jit(solution)/shard_map/attend/pallas_call | solution.py:26
  90.1 1.1 %collective-permute-start.16 = (bf16[256,512]{1,0:T(8,128)(2,1)S(1)}, bf16[256,512]{1,0:T(8,128)(2,1)S(1)}, u32[]{:S(2)}, u32[]{:S(2)}) collective-permute-start(bf16[256,512]{1,0:T(8,128)(2,1)S(1)} %finish.7.refs_5_.refs_0_), channel_id=1, source_target_pairs={{0,1},{1,0},{2,3},{3,2},{4,5},{5,4},{6,7},{7,6},{8,9},{9,8},{10,11... | collective-permute-start | bytes 786440 | tf_op jit(solution)/shard_map/ppermute | solution.py:39
  91.2 1.7 %attend.5.refs_7_ = bf16[64,1024]{1,0:T(8,128)(2,1)S(1)} custom-call(bf16[256,512]{1,0:T(8,128)(2,1)S(1)} %finish.6.refs_5_.refs_0_, bf16[256,512]{1,0:T(8,128)(2,1)S(1)} %collective-permute-done.17.refs_1_, bf16[1024,1024]{1,0:T(8,128)(2,1)S(1)} %copy-done.2, bf16[1024,1024]{1,0:T(8,128)(2,1)S(1)} %copy-done.3, ...), custom_call_target="tpu_custom_call" | custom-call | flops 1024 | bytes 1024 | tf_op jit(solution)/shard_map/attend/pallas_call | solution.py:26
  92.9 2.5 %attend_last.1 = bf16[256,1024]{1,0:T(8,128)(2,1)} custom-call(bf16[256,512]{1,0:T(8,128)(2,1)S(1)} %finish.7.refs_5_.refs_0_, bf16[256,512]{1,0:T(8,128)(2,1)S(1)} %collective-permute-done.16.refs_1_, bf16[1024,1024]{1,0:T(8,128)(2,1)S(1)} %copy-done.2, bf16[1024,1024]{1,0:T(8,128)(2,1)S(1)} %copy-done.3, bf16[64,1024]{1,0:T(8,128)(2,1)S(1)} %get-tuple-element.43.refs_4_, ...), custom_call_target="tpu_custom_call" | custom-call | flops 1024 | bytes 1024 | tf_op jit(solution)/shard_map/attend_last/pallas_call | solution.py:26
  (55 shorter events, 9.1 us)
Async XLA Ops:
  0.7 12.4 %copy-start.5 = (bf16[2048,256]{1,0:T(8,128)(2,1)S(1)}, bf16[2048,256]{1,0:T(8,128)(2,1)}, u32[]{:S(2)}) copy-start(bf16[2048,256]{1,0:T(8,128)(2,1)} %refs_1_.1) | copy-start | bytes 3145732
  42.6 9.0 %copy-start.4 = (bf16[256,1024]{1,0:T(8,128)(2,1)S(1)}, bf16[256,1024]{1,0:T(8,128)(2,1)}, u32[]{:S(2)}) copy-start(bf16[256,1024]{1,0:T(8,128)(2,1)} %refs_0_.1) | copy-start | bytes 1572868
  42.6 16.0 %copy-start.1 = (bf16[1024,1024]{1,0:T(8,128)(2,1)S(1)}, bf16[1024,1024]{1,0:T(8,128)(2,1)}, u32[]{:S(2)}) copy-start(bf16[1024,1024]{1,0:T(8,128)(2,1)} %refs_4_.7) | copy-start | bytes 6291460
  43.0 15.6 %copy-start = (bf16[1024,1024]{1,0:T(8,128)(2,1)S(1)}, bf16[1024,1024]{1,0:T(8,128)(2,1)}, u32[]{:S(2)}) copy-start(bf16[1024,1024]{1,0:T(8,128)(2,1)} %refs_3_.11) | copy-start | bytes 6291460
  43.0 3.9 %collective-permute-start.1 = (bf16[256,256]{1,0:T(8,128)(2,1)S(1)}, bf16[256,256]{1,0:T(8,128)(2,1)S(1)}, u32[]{:S(2)}, u32[]{:S(2)}) collective-permute-start(bf16[256,256]{1,0:T(8,128)(2,1)S(1)} %order.2.refs_2_.refs_0_), channel_id=1, source_target_pairs={{0,2},{1,3},{2,0},{3,1},{4,6},{5,7},{6,4},{7,5},{8,10},{9,11},{10,... | collective-permute-start | bytes 393224 | tf_op jit(solution)/shard_map/ppermute | solution.py:39
  45.3 13.3 %collective-permute-start = (bf16[768,256]{1,0:T(8,128)(2,1)S(1)}, bf16[768,256]{1,0:T(8,128)(2,1)S(1)}, u32[]{:S(2)}, u32[]{:S(2)}) collective-permute-start(bf16[768,256]{1,0:T(8,128)(2,1)S(1)} %order.3.refs_1_.refs_5_.refs_0_), channel_id=1, source_target_pairs={{0,2},{1,3},{2,0},{3,1},{4,6},{5,7},{6,4},{7,5},{8,10},{9,11},{10,... | collective-permute-start | bytes 1179656 | tf_op jit(solution)/shard_map/ppermute | solution.py:39
  46.9 11.7 %collective-permute-start.2 = (bf16[256,512]{1,0:T(8,128)(2,1)S(1)}, bf16[256,512]{1,0:T(8,128)(2,1)S(1)}, u32[]{:S(2)}, u32[]{:S(2)}) collective-permute-start(bf16[256,512]{1,0:T(8,128)(2,1)S(1)} %pair.2), channel_id=1, source_target_pairs={{0,1},{1,0},{2,3},{3,2},{4,5},{5,4},{6,7},{7,6},{8,9},{9,8},{10,11... | collective-permute-start | bytes 786440 | tf_op jit(solution)/shard_map/ppermute | solution.py:39
  51.6 7.0 %collective-permute-start.3 = (bf16[64,1024]{1,0:T(8,128)(2,1)S(1)}, bf16[64,1024]{1,0:T(8,128)(2,1)S(1)}, u32[]{:S(2)}, u32[]{:S(2)}) collective-permute-start(bf16[64,1024]{1,0:T(8,128)(2,1)S(1)} %head.1), channel_id=1, source_target_pairs={{4,0},{8,4},{12,8},{16,12},{20,16},{24,20},{28,24},{5,1},{9,5},{13... | collective-permute-start | bytes 393224 | tf_op jit(solution)/shard_map/ppermute | solution.py:45
  60.3 2.8 %collective-permute-start.4 = (bf16[768,512]{1,0:T(8,128)(2,1)S(1)}, bf16[768,512]{1,0:T(8,128)(2,1)S(1)}, u32[]{:S(2)}, u32[]{:S(2)}) collective-permute-start(bf16[768,512]{1,0:T(8,128)(2,1)S(1)} %pair.3), channel_id=1, source_target_pairs={{0,1},{1,0},{2,3},{3,2},{4,5},{5,4},{6,7},{7,6},{8,9},{9,8},{10,11... | collective-permute-start | bytes 2359304 | tf_op jit(solution)/shard_map/ppermute | solution.py:39
  61.1 4.0 %collective-permute-start.5 = (bf16[256,512]{1,0:T(8,128)(2,1)S(1)}, bf16[256,512]{1,0:T(8,128)(2,1)S(1)}, u32[]{:S(2)}, u32[]{:S(2)}) collective-permute-start(bf16[256,512]{1,0:T(8,128)(2,1)S(1)} %get-tuple-element.25.refs_2_.refs_5_), channel_id=1, source_target_pairs={{0,1},{1,0},{2,3},{3,2},{4,5},{5,4},{6,7},{7,6},{8,9},{9,8},{10,11... | collective-permute-start | bytes 786440 | tf_op jit(solution)/shard_map/ppermute | solution.py:39
  64.7 4.0 %collective-permute-start.7 = (bf16[256,512]{1,0:T(8,128)(2,1)S(1)}, bf16[256,512]{1,0:T(8,128)(2,1)S(1)}, u32[]{:S(2)}, u32[]{:S(2)}) collective-permute-start(bf16[256,512]{1,0:T(8,128)(2,1)S(1)} %get-tuple-element.27.refs_2_), channel_id=1, source_target_pairs={{0,1},{1,0},{2,3},{3,2},{4,5},{5,4},{6,7},{7,6},{8,9},{9,8},{10,11... | collective-permute-start | bytes 786440 | tf_op jit(solution)/shard_map/ppermute | solution.py:39
  65.2 7.8 %collective-permute-start.6 = (bf16[256,512]{1,0:T(8,128)(2,1)S(1)}, bf16[256,512]{1,0:T(8,128)(2,1)S(1)}, u32[]{:S(2)}, u32[]{:S(2)}) collective-permute-start(bf16[256,512]{1,0:T(8,128)(2,1)S(1)} %get-tuple-element.29.refs_5_), channel_id=1, source_target_pairs={{0,2},{1,3},{2,0},{3,1},{4,6},{5,7},{6,4},{7,5},{8,10},{9,11},{10,... | collective-permute-start | bytes 786440 | tf_op jit(solution)/shard_map/ppermute | solution.py:39
  68.2 8.4 %collective-permute-start.11 = (bf16[256,512]{1,0:T(8,128)(2,1)S(1)}, bf16[256,512]{1,0:T(8,128)(2,1)S(1)}, u32[]{:S(2)}, u32[]{:S(2)}) collective-permute-start(bf16[256,512]{1,0:T(8,128)(2,1)S(1)} %get-tuple-element.31.refs_2_), channel_id=1, source_target_pairs={{0,1},{1,0},{2,3},{3,2},{4,5},{5,4},{6,7},{7,6},{8,9},{9,8},{10,11... | collective-permute-start | bytes 786440 | tf_op jit(solution)/shard_map/ppermute | solution.py:39
  68.7 9.9 %collective-permute-start.10 = (bf16[256,512]{1,0:T(8,128)(2,1)S(1)}, bf16[256,512]{1,0:T(8,128)(2,1)S(1)}, u32[]{:S(2)}, u32[]{:S(2)}) collective-permute-start(bf16[256,512]{1,0:T(8,128)(2,1)S(1)} %get-tuple-element.32.refs_4_), channel_id=1, source_target_pairs={{0,2},{1,3},{2,0},{3,1},{4,6},{5,7},{6,4},{7,5},{8,10},{9,11},{10,... | collective-permute-start | bytes 786440 | tf_op jit(solution)/shard_map/ppermute | solution.py:39
  73.1 6.6 %collective-permute-start.9 = (bf16[256,512]{1,0:T(8,128)(2,1)S(1)}, bf16[256,512]{1,0:T(8,128)(2,1)S(1)}, u32[]{:S(2)}, u32[]{:S(2)}) collective-permute-start(bf16[256,512]{1,0:T(8,128)(2,1)S(1)} %finish.4.refs_5_.refs_0_), channel_id=1, source_target_pairs={{0,1},{1,0},{2,3},{3,2},{4,5},{5,4},{6,7},{7,6},{8,9},{9,8},{10,11... | collective-permute-start | bytes 786440 | tf_op jit(solution)/shard_map/ppermute | solution.py:39
  76.3 5.2 %collective-permute-start.8 = (bf16[256,512]{1,0:T(8,128)(2,1)S(1)}, bf16[256,512]{1,0:T(8,128)(2,1)S(1)}, u32[]{:S(2)}, u32[]{:S(2)}) collective-permute-start(bf16[256,512]{1,0:T(8,128)(2,1)S(1)} %get-tuple-element.34.refs_2_), channel_id=1, source_target_pairs={{0,1},{1,0},{2,3},{3,2},{4,5},{5,4},{6,7},{7,6},{8,9},{9,8},{10,11... | collective-permute-start | bytes 786440 | tf_op jit(solution)/shard_map/ppermute | solution.py:39
  76.4 3.4 %copy-start.3 = (bf16[1024,1024]{1,0:T(8,128)(2,1)S(1)}, bf16[1024,1024]{1,0:T(8,128)(2,1)}, u32[]{:S(2)}) copy-start(bf16[1024,1024]{1,0:T(8,128)(2,1)} %refs_3_.15) | copy-start | bytes 6291460
  76.5 3.3 %copy-start.2 = (bf16[1024,1024]{1,0:T(8,128)(2,1)S(1)}, bf16[1024,1024]{1,0:T(8,128)(2,1)}, u32[]{:S(2)}) copy-start(bf16[1024,1024]{1,0:T(8,128)(2,1)} %refs_2_.7) | copy-start | bytes 6291460
  76.6 10.6 %collective-permute-start.14 = (bf16[256,512]{1,0:T(8,128)(2,1)S(1)}, bf16[256,512]{1,0:T(8,128)(2,1)S(1)}, u32[]{:S(2)}, u32[]{:S(2)}) collective-permute-start(bf16[256,512]{1,0:T(8,128)(2,1)S(1)} %get-tuple-element.37.refs_4_), channel_id=1, source_target_pairs={{0,2},{1,3},{2,0},{3,1},{4,6},{5,7},{6,4},{7,5},{8,10},{9,11},{10,... | collective-permute-start | bytes 786440 | tf_op jit(solution)/shard_map/ppermute | solution.py:39
  78.7 9.2 %collective-permute-start.13 = (bf16[256,512]{1,0:T(8,128)(2,1)S(1)}, bf16[256,512]{1,0:T(8,128)(2,1)S(1)}, u32[]{:S(2)}, u32[]{:S(2)}) collective-permute-start(bf16[256,512]{1,0:T(8,128)(2,1)S(1)} %finish.5.refs_5_.refs_0_), channel_id=1, source_target_pairs={{0,1},{1,0},{2,3},{3,2},{4,5},{5,4},{6,7},{7,6},{8,9},{9,8},{10,11... | collective-permute-start | bytes 786440 | tf_op jit(solution)/shard_map/ppermute | solution.py:39
  81.5 8.5 %collective-permute-start.12 = (bf16[256,512]{1,0:T(8,128)(2,1)S(1)}, bf16[256,512]{1,0:T(8,128)(2,1)S(1)}, u32[]{:S(2)}, u32[]{:S(2)}) collective-permute-start(bf16[256,512]{1,0:T(8,128)(2,1)S(1)} %get-tuple-element.39.refs_4_), channel_id=1, source_target_pairs={{0,2},{1,3},{2,0},{3,1},{4,6},{5,7},{6,4},{7,5},{8,10},{9,11},{10,... | collective-permute-start | bytes 786440 | tf_op jit(solution)/shard_map/ppermute | solution.py:39
  82.9 6.7 %collective-permute-start.15 = (bf16[64,1024]{1,0:T(8,128)(2,1)S(1)}, bf16[64,1024]{1,0:T(8,128)(2,1)S(1)}, u32[]{:S(2)}, u32[]{:S(2)}) collective-permute-start(bf16[64,1024]{1,0:T(8,128)(2,1)S(1)} %attend.3.refs_2_.refs_8_), channel_id=1, source_target_pairs={{0,4},{4,8},{8,12},{12,16},{16,20},{20,24},{24,28},{1,5},{5,9},{9,... | collective-permute-start | bytes 393224 | tf_op jit(solution)/shard_map/ppermute | solution.py:45
  87.3 3.9 %collective-permute-start.17 = (bf16[256,512]{1,0:T(8,128)(2,1)S(1)}, bf16[256,512]{1,0:T(8,128)(2,1)S(1)}, u32[]{:S(2)}, u32[]{:S(2)}) collective-permute-start(bf16[256,512]{1,0:T(8,128)(2,1)S(1)} %finish.6.refs_5_.refs_0_), channel_id=1, source_target_pairs={{0,1},{1,0},{2,3},{3,2},{4,5},{5,4},{6,7},{7,6},{8,9},{9,8},{10,11... | collective-permute-start | bytes 786440 | tf_op jit(solution)/shard_map/ppermute | solution.py:39
  90.1 2.8 %collective-permute-start.16 = (bf16[256,512]{1,0:T(8,128)(2,1)S(1)}, bf16[256,512]{1,0:T(8,128)(2,1)S(1)}, u32[]{:S(2)}, u32[]{:S(2)}) collective-permute-start(bf16[256,512]{1,0:T(8,128)(2,1)S(1)} %finish.7.refs_5_.refs_0_), channel_id=1, source_target_pairs={{0,1},{1,0},{2,3},{3,2},{4,5},{5,4},{6,7},{7,6},{8,9},{9,8},{10,11... | collective-permute-start | bytes 786440 | tf_op jit(solution)/shard_map/ppermute | solution.py:39
  (1 other events, 0.7 us)

commit v8 on v7

--- a/solution.py
+++ b/solution.py
@@ -276,8 +276,9 @@
         count = piece[0].shape[0]
         both = call(pair_body, sds((count, 2 * width), BF16), "pair", piece[:2], after)
         piece[2] = exchange(both, 1)
-
-    across(pieces[0])
+        return both
+
+    across(pieces[0], (token,))
     head = call(head_body, sds((GROUP, head_cols), BF16), "head", (queries,), (token,))
     next_q = shifted(head, -1)
     local_q = jnp.concatenate([queries[GROUP - 1 :], next_q[: GROUP - 1]], axis=0)
@@ -290,7 +291,8 @@
         return pieces[0 if g in plan[0] else 1]
 
     def rest(_):
-        across(pieces[1], (token,))
+        nonlocal token
+        token = across(pieces[1], (token, next_q))
 
     def feed(g):
         nonlocal token
@@ -299,7 +301,7 @@
             (whole, half),
             "feed",
             (*emb(g), w_in, w_out),
-            (token, pieces[1][1], next_q),
+            (token,),
         )
         fed[g] = keep, exchange(token, 1)
 
@@ -339,9 +341,9 @@
 
     a, b, c, d = order
     for step, g in (
-        (feed, a), (rest, b), (feed, b), (add, a), (feed, c), (add, b),
-        (finish, a), (feed, d), (add, c),
-        (finish, b), (attend, a), (add, d),
+        (feed, a), (add, a), (rest, b), (feed, b), (feed, c),
+        (finish, a), (add, b), (add, c), (feed, d),
+        (finish, b), (add, d), (attend, a),
         (finish, c), (attend, b),
         (finish, d), (attend, c), (attend, d),
     ):

time: 95.8 us -> 95.4 us (level)
  waiting for transfers between devices: 13.9 us -> 12.8 us
    ppermute x16, starting transfers between devices: 16.9 us -> 18 us  [exchange(): return lax.ppermute(x, 'tp', [(i, i ^ bit) for i in range(size)])]
  transfers between devices with their start and end apart: 18 -> 18, of which waited for: 6 -> 6; matrix products, arithmetic and copies ran while one was open for 0% -> 0% of each run, Pallas kernels for 12% -> 14%
where the time goes in v8:
time: 95.4 us; the launch traced here: 94.9 us
  blocking collectives  38.6 us (40%)
  starting transfers between devices  23 us (24%)
  Pallas kernels  19.3 us (20%)
  waiting for transfers between devices  12.8 us (13%)
    all_to_all x1, blocking collectives, per_device(): lax.all_to_all(found.reshape(seq_size, cap, width), 'seq', split_axis=0,...  27.1 us
    pallas_call x23, Pallas kernels, call(): pl.pallas_call(without_after, out_shape=outs, in_specs=in_specs + [unread...  19.3 us
    ppermute x16, starting transfers between devices, exchange(): return lax.ppermute(x, 'tp', [(i, i ^ bit) for i in range(size)])  18 us
    all_to_all x1, blocking collectives, per_device(): lax.all_to_all(wanted, 'seq', split_axis=0, concat_axis=0, tiled=True)  11.5 us
    ppermute x16, waiting for transfers between devices, exchange(): return lax.ppermute(x, 'tp', [(i, i ^ bit) for i in range(size)])  7.32 us
    ppermute x2, waiting for transfers between devices, shifted(): return lax.ppermute(x, 'seq', pairs)  5.45 us
    ppermute x2, starting transfers between devices, shifted(): return lax.ppermute(x, 'seq', pairs)  4.96 us
  transfers between devices with their start and end apart: 18, of which 6 were waited for; matrix products, arithmetic and copies ran while one was open for 0% of the time, Pallas kernels for 14%

profile of v8, /device:TPU:1, one launch (start us, length us, event | category | flops | bytes accessed | tf_op | source)
XLA Modules:
  0.0 94.9 jit_solution(12063647160204469294)
XLA Ops:
  1.5 11.5 %all_to_all.14 = s32[8,1,256]{2,1,0:T(1,128)S(1)} all-to-all(s32[8,1,256]{2,1,0:T(1,128)S(1)} %copy.8), channel_id=1, replica_groups=mesh['seq'=8,'tp'=4] {'seq'}, dimensions={0} | all-to-all | bytes 16384 | tf_op jit(solution)/shard_map/all_to_all | solution.py:248
  13.1 2.4 %fetch.1 = bf16[2048,256]{1,0:T(8,128)(2,1)S(1)} custom-call(s32[1,2048]{1,0:T(1,128)S(1)} %bitcast.10, bf16[2048,256]{1,0:T(8,128)(2,1)S(1)} %copy-done.5), custom_call_target="tpu_custom_call" | custom-call | flops 1024 | bytes 1024 | tf_op jit(solution)/shard_map/fetch/pallas_call | solution.py:26
  15.4 27.1 %all_to_all.15 = bf16[8,256,256]{2,1,0:T(8,128)(2,1)S(1)} all-to-all(bf16[8,256,256]{2,1,0:T(8,128)(2,1)S(1)} %bitcast.8), channel_id=1, replica_groups=mesh['seq'=8,'tp'=4] {'seq'}, dimensions={0} | all-to-all | bytes 2097152 | tf_op jit(solution)/shard_map/all_to_all | solution.py:255
  43.0 1.3 %collective-permute-start.1 = (bf16[256,256]{1,0:T(8,128)(2,1)S(1)}, bf16[256,256]{1,0:T(8,128)(2,1)S(1)}, u32[]{:S(2)}, u32[]{:S(2)}) collective-permute-start(bf16[256,256]{1,0:T(8,128)(2,1)S(1)} %order.2.refs_2_.refs_0_), channel_id=1, source_target_pairs={{0,2},{1,3},{2,0},{3,1},{4,6},{5,7},{6,4},{7,5},{8,10},{9,11},{10,... | collective-permute-start | bytes 393224 | tf_op jit(solution)/shard_map/ppermute | solution.py:39
  45.3 1.6 %collective-permute-done.1.refs_1_ = bf16[256,256]{1,0:T(8,128)(2,1)S(1)} collective-permute-done((bf16[256,256]{1,0:T(8,128)(2,1)S(1)}, bf16[256,256]{1,0:T(8,128)(2,1)S(1)}, u32[]{:S(2)}, u32[]{:S(2)}) %collective-permute-start.1) | collective-permute-done | bytes 131104 | tf_op jit(solution)/shard_map/ppermute | solution.py:39
  46.9 3.2 %collective-permute-start.2 = (bf16[256,512]{1,0:T(8,128)(2,1)S(1)}, bf16[256,512]{1,0:T(8,128)(2,1)S(1)}, u32[]{:S(2)}, u32[]{:S(2)}) collective-permute-start(bf16[256,512]{1,0:T(8,128)(2,1)S(1)} %pair.2), channel_id=1, source_target_pairs={{0,1},{1,0},{2,3},{3,2},{4,5},{5,4},{6,7},{7,6},{8,9},{9,8},{10,11... | collective-permute-start | bytes 786440 | tf_op jit(solution)/shard_map/ppermute | solution.py:39
  50.2 1.3 %collective-permute-start = (bf16[768,256]{1,0:T(8,128)(2,1)S(1)}, bf16[768,256]{1,0:T(8,128)(2,1)S(1)}, u32[]{:S(2)}, u32[]{:S(2)}) collective-permute-start(bf16[768,256]{1,0:T(8,128)(2,1)S(1)} %order.3.refs_2_.refs_5_.refs_1_.refs_0_), channel_id=1, source_target_pairs={{0,2},{1,3},{2,0},{3,1},{4,6},{5,7},{6,4},{7,5},{8,10},{9,11},{10,... | collective-permute-start | bytes 1179656 | tf_op jit(solution)/shard_map/ppermute | solution.py:39
  51.4 1.6 %feed.4 = (f32[256,512]{1,0:T(8,128)S(1)}, bf16[256,512]{1,0:T(8,128)(2,1)S(1)}) custom-call(bf16[256,256]{1,0:T(8,128)(2,1)S(1)} %order.2.refs_2_.refs_0_, bf16[256,256]{1,0:T(8,128)(2,1)S(1)} %collective-permute-done.1.refs_1_, bf16[256,512]{1,0:T(8,128)(2,1)S(1)} %collective-permute-done.2.refs_2_, bf16[1024,1024]{1,0:T(8,128)(2,1)S(1)} %copy-done, ...), custom_call_target="tpu_custom_call" | custom-call | flops 1024 | bytes 1024 | tf_op jit(solution)/shard_map/feed/pallas_call | solution.py:26
  53.5 1.3 %collective-permute-start.4 = (bf16[64,1024]{1,0:T(8,128)(2,1)S(1)}, bf16[64,1024]{1,0:T(8,128)(2,1)S(1)}, u32[]{:S(2)}, u32[]{:S(2)}) collective-permute-start(bf16[64,1024]{1,0:T(8,128)(2,1)S(1)} %head.1), channel_id=1, source_target_pairs={{4,0},{8,4},{12,8},{16,12},{20,16},{24,20},{28,24},{5,1},{9,5},{13... | collective-permute-start | bytes 393224 | tf_op jit(solution)/shard_map/ppermute | solution.py:45
  54.9 5.4 %collective-permute-done.4.refs_3_ = bf16[64,1024]{1,0:T(8,128)(2,1)S(1)} collective-permute-done((bf16[64,1024]{1,0:T(8,128)(2,1)S(1)}, bf16[64,1024]{1,0:T(8,128)(2,1)S(1)}, u32[]{:S(2)}, u32[]{:S(2)}) %collective-permute-start.4) | collective-permute-done | bytes 131104 | tf_op jit(solution)/shard_map/ppermute | solution.py:45
  61.8 1.3 %collective-permute-start.8 = (bf16[256,512]{1,0:T(8,128)(2,1)S(1)}, bf16[256,512]{1,0:T(8,128)(2,1)S(1)}, u32[]{:S(2)}, u32[]{:S(2)}) collective-permute-start(bf16[256,512]{1,0:T(8,128)(2,1)S(1)} %get-tuple-element.27.refs_2_), channel_id=1, source_target_pairs={{0,2},{1,3},{2,0},{3,1},{4,6},{5,7},{6,4},{7,5},{8,10},{9,11},{10,... | collective-permute-start | bytes 786440 | tf_op jit(solution)/shard_map/ppermute | solution.py:39
  63.7 1.6 %feed.5 = (f32[256,512]{1,0:T(8,128)S(1)}, bf16[256,512]{1,0:T(8,128)(2,1)S(1)}) custom-call(bf16[768,256]{1,0:T(8,128)(2,1)S(1)} %order.3.refs_2_.refs_5_.refs_1_.refs_0_, bf16[768,256]{1,0:T(8,128)(2,1)S(1)} %collective-permute-done.refs_1_, bf16[768,512]{1,0:T(8,128)(2,1)S(1)} %collective-permute-done.5.refs_2_, bf16[1024,1024]{1,0:T(8,128)(2,1)S(1)} %copy-done, ...), custom_call_target="tpu_custom_call" | custom-call | flops 1024 | bytes 1024 | tf_op jit(solution)/shard_map/feed/pallas_call | solution.py:26
  65.8 1.6 %feed.6 = (f32[256,512]{1,0:T(8,128)S(1)}, bf16[256,512]{1,0:T(8,128)(2,1)S(1)}) custom-call(bf16[768,256]{1,0:T(8,128)(2,1)S(1)} %order.3.refs_2_.refs_5_.refs_1_.refs_0_, bf16[768,256]{1,0:T(8,128)(2,1)S(1)} %collective-permute-done.refs_1_, bf16[768,512]{1,0:T(8,128)(2,1)S(1)} %collective-permute-done.5.refs_2_, bf16[1024,1024]{1,0:T(8,128)(2,1)S(1)} %copy-done, ...), custom_call_target="tpu_custom_call" | custom-call | flops 1024 | bytes 1024 | tf_op jit(solution)/shard_map/feed/pallas_call | solution.py:26
  67.6 2.1 %collective-permute-done.8.refs_3_ = bf16[256,512]{1,0:T(8,128)(2,1)S(1)} collective-permute-done((bf16[256,512]{1,0:T(8,128)(2,1)S(1)}, bf16[256,512]{1,0:T(8,128)(2,1)S(1)}, u32[]{:S(2)}, u32[]{:S(2)}) %collective-permute-start.8) | collective-permute-done | bytes 262176 | tf_op jit(solution)/shard_map/ppermute | solution.py:39
  69.9 1.3 %collective-permute-start.10 = (bf16[256,512]{1,0:T(8,128)(2,1)S(1)}, bf16[256,512]{1,0:T(8,128)(2,1)S(1)}, u32[]{:S(2)}, u32[]{:S(2)}) collective-permute-start(bf16[256,512]{1,0:T(8,128)(2,1)S(1)} %get-tuple-element.33.refs_2_), channel_id=1, source_target_pairs={{0,2},{1,3},{2,0},{3,1},{4,6},{5,7},{6,4},{7,5},{8,10},{9,11},{10,... | collective-permute-start | bytes 786440 | tf_op jit(solution)/shard_map/ppermute | solution.py:39
  71.3 1.6 %feed.7 = (f32[256,512]{1,0:T(8,128)S(1)}, bf16[256,512]{1,0:T(8,128)(2,1)S(1)}) custom-call(bf16[768,256]{1,0:T(8,128)(2,1)S(1)} %order.3.refs_2_.refs_5_.refs_1_.refs_0_, bf16[768,256]{1,0:T(8,128)(2,1)S(1)} %collective-permute-done.refs_1_, bf16[768,512]{1,0:T(8,128)(2,1)S(1)} %collective-permute-done.5.refs_2_, bf16[1024,1024]{1,0:T(8,128)(2,1)S(1)} %copy-done, ...), custom_call_target="tpu_custom_call" | custom-call | flops 1024 | bytes 1024 | tf_op jit(solution)/shard_map/feed/pallas_call | solution.py:26
  74.6 2.4 %collective-permute-done.10.refs_3_ = bf16[256,512]{1,0:T(8,128)(2,1)S(1)} collective-permute-done((bf16[256,512]{1,0:T(8,128)(2,1)S(1)}, bf16[256,512]{1,0:T(8,128)(2,1)S(1)}, u32[]{:S(2)}, u32[]{:S(2)}) %collective-permute-start.10) | collective-permute-done | bytes 262176 | tf_op jit(solution)/shard_map/ppermute | solution.py:39
  77.0 3.0 %collective-permute-start.12 = (bf16[256,512]{1,0:T(8,128)(2,1)S(1)}, bf16[256,512]{1,0:T(8,128)(2,1)S(1)}, u32[]{:S(2)}, u32[]{:S(2)}) collective-permute-start(bf16[256,512]{1,0:T(8,128)(2,1)S(1)} %finish.5.refs_2_.refs_0_), channel_id=1, source_target_pairs={{0,1},{1,0},{2,3},{3,2},{4,5},{5,4},{6,7},{7,6},{8,9},{9,8},{10,11... | collective-permute-start | bytes 786440 | tf_op jit(solution)/shard_map/ppermute | solution.py:39
  80.1 1.5 %collective-permute-start.11 = (bf16[256,512]{1,0:T(8,128)(2,1)S(1)}, bf16[256,512]{1,0:T(8,128)(2,1)S(1)}, u32[]{:S(2)}, u32[]{:S(2)}) collective-permute-start(bf16[256,512]{1,0:T(8,128)(2,1)S(1)} %get-tuple-element.39.refs_5_), channel_id=1, source_target_pairs={{0,2},{1,3},{2,0},{3,1},{4,6},{5,7},{6,4},{7,5},{8,10},{9,11},{10,... | collective-permute-start | bytes 786440 | tf_op jit(solution)/shard_map/ppermute | solution.py:39
  81.6 1.7 %attend.3.refs_4_.refs_8_ = bf16[64,1024]{1,0:T(8,128)(2,1)S(1)} custom-call(bf16[256,512]{1,0:T(8,128)(2,1)S(1)} %finish.4.refs_2_.refs_0_, bf16[256,512]{1,0:T(8,128)(2,1)S(1)} %collective-permute-done.14.refs_1_, bf16[1024,1024]{1,0:T(8,128)(2,1)S(1)} %copy-done.2, bf16[1024,1024]{1,0:T(8,128)(2,1)S(1)} %copy-done.3, ...), custom_call_target="tpu_custom_call" | custom-call | flops 1024 | bytes 1024 | tf_op jit(solution)/shard_map/attend/pallas_call | solution.py:26
  83.3 3.7 %collective-permute-start.15 = (bf16[64,1024]{1,0:T(8,128)(2,1)S(1)}, bf16[64,1024]{1,0:T(8,128)(2,1)S(1)}, u32[]{:S(2)}, u32[]{:S(2)}) collective-permute-start(bf16[64,1024]{1,0:T(8,128)(2,1)S(1)} %attend.3.refs_4_.refs_8_), channel_id=1, source_target_pairs={{0,4},{4,8},{8,12},{12,16},{16,20},{20,24},{24,28},{1,5},{5,9},{9,... | collective-permute-start | bytes 393224 | tf_op jit(solution)/shard_map/ppermute | solution.py:45
  87.9 1.7 %attend.4.refs_4_.refs_6_ = bf16[64,1024]{1,0:T(8,128)(2,1)S(1)} custom-call(bf16[256,512]{1,0:T(8,128)(2,1)S(1)} %finish.5.refs_2_.refs_0_, bf16[256,512]{1,0:T(8,128)(2,1)S(1)} %collective-permute-done.12.refs_1_, bf16[1024,1024]{1,0:T(8,128)(2,1)S(1)} %copy-done.2, bf16[1024,1024]{1,0:T(8,128)(2,1)S(1)} %copy-done.3, ...), custom_call_target="tpu_custom_call" | custom-call | flops 1024 | bytes 1024 | tf_op jit(solution)/shard_map/attend/pallas_call | solution.py:26
  90.7 1.7 %attend.5.refs_7_ = bf16[64,1024]{1,0:T(8,128)(2,1)S(1)} custom-call(bf16[256,512]{1,0:T(8,128)(2,1)S(1)} %finish.6.refs_5_.refs_0_, bf16[256,512]{1,0:T(8,128)(2,1)S(1)} %collective-permute-done.17.refs_1_, bf16[1024,1024]{1,0:T(8,128)(2,1)S(1)} %copy-done.2, bf16[1024,1024]{1,0:T(8,128)(2,1)S(1)} %copy-done.3, ...), custom_call_target="tpu_custom_call" | custom-call | flops 1024 | bytes 1024 | tf_op jit(solution)/shard_map/attend/pallas_call | solution.py:26
  92.4 2.5 %attend_last.1 = bf16[256,1024]{1,0:T(8,128)(2,1)} custom-call(bf16[256,512]{1,0:T(8,128)(2,1)S(1)} %finish.7.refs_5_.refs_0_, bf16[256,512]{1,0:T(8,128)(2,1)S(1)} %collective-permute-done.16.refs_1_, bf16[1024,1024]{1,0:T(8,128)(2,1)S(1)} %copy-done.2, bf16[1024,1024]{1,0:T(8,128)(2,1)S(1)} %copy-done.3, bf16[64,1024]{1,0:T(8,128)(2,1)S(1)} %get-tuple-element.43.refs_4_, ...), custom_call_target="tpu_custom_call" | custom-call | flops 1024 | bytes 1024 | tf_op jit(solution)/shard_map/attend_last/pallas_call | solution.py:26
  (55 shorter events, 10.3 us)
Async XLA Ops:
  0.7 12.4 %copy-start.5 = (bf16[2048,256]{1,0:T(8,128)(2,1)S(1)}, bf16[2048,256]{1,0:T(8,128)(2,1)}, u32[]{:S(2)}) copy-start(bf16[2048,256]{1,0:T(8,128)(2,1)} %refs_1_.1) | copy-start | bytes 3145732
  42.6 8.9 %copy-start = (bf16[1024,1024]{1,0:T(8,128)(2,1)S(1)}, bf16[1024,1024]{1,0:T(8,128)(2,1)}, u32[]{:S(2)}) copy-start(bf16[1024,1024]{1,0:T(8,128)(2,1)} %refs_3_.11) | copy-start | bytes 6291460
  42.6 8.9 %copy-start.1 = (bf16[1024,1024]{1,0:T(8,128)(2,1)S(1)}, bf16[1024,1024]{1,0:T(8,128)(2,1)}, u32[]{:S(2)}) copy-start(bf16[1024,1024]{1,0:T(8,128)(2,1)} %refs_4_.7) | copy-start | bytes 6291460
  43.0 3.9 %collective-permute-start.1 = (bf16[256,256]{1,0:T(8,128)(2,1)S(1)}, bf16[256,256]{1,0:T(8,128)(2,1)S(1)}, u32[]{:S(2)}, u32[]{:S(2)}) collective-permute-start(bf16[256,256]{1,0:T(8,128)(2,1)S(1)} %order.2.refs_2_.refs_0_), channel_id=1, source_target_pairs={{0,2},{1,3},{2,0},{3,1},{4,6},{5,7},{6,4},{7,5},{8,10},{9,11},{10,... | collective-permute-start | bytes 393224 | tf_op jit(solution)/shard_map/ppermute | solution.py:39
  46.9 6.5 %copy-start.4 = (bf16[256,1024]{1,0:T(8,128)(2,1)S(1)}, bf16[256,1024]{1,0:T(8,128)(2,1)}, u32[]{:S(2)}) copy-start(bf16[256,1024]{1,0:T(8,128)(2,1)} %refs_0_.1) | copy-start | bytes 1572868
  46.9 4.5 %collective-permute-start.2 = (bf16[256,512]{1,0:T(8,128)(2,1)S(1)}, bf16[256,512]{1,0:T(8,128)(2,1)S(1)}, u32[]{:S(2)}, u32[]{:S(2)}) collective-permute-start(bf16[256,512]{1,0:T(8,128)(2,1)S(1)} %pair.2), channel_id=1, source_target_pairs={{0,1},{1,0},{2,3},{3,2},{4,5},{5,4},{6,7},{7,6},{8,9},{9,8},{10,11... | collective-permute-start | bytes 786440 | tf_op jit(solution)/shard_map/ppermute | solution.py:39
  50.2 10.7 %collective-permute-start = (bf16[768,256]{1,0:T(8,128)(2,1)S(1)}, bf16[768,256]{1,0:T(8,128)(2,1)S(1)}, u32[]{:S(2)}, u32[]{:S(2)}) collective-permute-start(bf16[768,256]{1,0:T(8,128)(2,1)S(1)} %order.3.refs_2_.refs_5_.refs_1_.refs_0_), channel_id=1, source_target_pairs={{0,2},{1,3},{2,0},{3,1},{4,6},{5,7},{6,4},{7,5},{8,10},{9,11},{10,... | collective-permute-start | bytes 1179656 | tf_op jit(solution)/shard_map/ppermute | solution.py:39
  53.0 1.7 %collective-permute-start.3 = (bf16[256,512]{1,0:T(8,128)(2,1)S(1)}, bf16[256,512]{1,0:T(8,128)(2,1)S(1)}, u32[]{:S(2)}, u32[]{:S(2)}) collective-permute-start(bf16[256,512]{1,0:T(8,128)(2,1)S(1)} %get-tuple-element.26.refs_2_), channel_id=1, source_target_pairs={{0,1},{1,0},{2,3},{3,2},{4,5},{5,4},{6,7},{7,6},{8,9},{9,8},{10,11... | collective-permute-start | bytes 786440 | tf_op jit(solution)/shard_map/ppermute | solution.py:39
  53.5 6.8 %collective-permute-start.4 = (bf16[64,1024]{1,0:T(8,128)(2,1)S(1)}, bf16[64,1024]{1,0:T(8,128)(2,1)S(1)}, u32[]{:S(2)}, u32[]{:S(2)}) collective-permute-start(bf16[64,1024]{1,0:T(8,128)(2,1)S(1)} %head.1), channel_id=1, source_target_pairs={{4,0},{8,4},{12,8},{16,12},{20,16},{24,20},{28,24},{5,1},{9,5},{13... | collective-permute-start | bytes 393224 | tf_op jit(solution)/shard_map/ppermute | solution.py:45
  60.9 2.8 %collective-permute-start.5 = (bf16[768,512]{1,0:T(8,128)(2,1)S(1)}, bf16[768,512]{1,0:T(8,128)(2,1)S(1)}, u32[]{:S(2)}, u32[]{:S(2)}) collective-permute-start(bf16[768,512]{1,0:T(8,128)(2,1)S(1)} %pair.3.refs_5_), channel_id=1, source_target_pairs={{0,1},{1,0},{2,3},{3,2},{4,5},{5,4},{6,7},{7,6},{8,9},{9,8},{10,11... | collective-permute-start | bytes 2359304 | tf_op jit(solution)/shard_map/ppermute | solution.py:39
  61.8 7.9 %collective-permute-start.8 = (bf16[256,512]{1,0:T(8,128)(2,1)S(1)}, bf16[256,512]{1,0:T(8,128)(2,1)S(1)}, u32[]{:S(2)}, u32[]{:S(2)}) collective-permute-start(bf16[256,512]{1,0:T(8,128)(2,1)S(1)} %get-tuple-element.27.refs_2_), channel_id=1, source_target_pairs={{0,2},{1,3},{2,0},{3,1},{4,6},{5,7},{6,4},{7,5},{8,10},{9,11},{10,... | collective-permute-start | bytes 786440 | tf_op jit(solution)/shard_map/ppermute | solution.py:39
  65.3 4.5 %collective-permute-start.7 = (bf16[256,512]{1,0:T(8,128)(2,1)S(1)}, bf16[256,512]{1,0:T(8,128)(2,1)S(1)}, u32[]{:S(2)}, u32[]{:S(2)}) collective-permute-start(bf16[256,512]{1,0:T(8,128)(2,1)S(1)} %get-tuple-element.28.refs_5_), channel_id=1, source_target_pairs={{0,1},{1,0},{2,3},{3,2},{4,5},{5,4},{6,7},{7,6},{8,9},{9,8},{10,11... | collective-permute-start | bytes 786440 | tf_op jit(solution)/shard_map/ppermute | solution.py:39
  67.4 3.8 %collective-permute-start.6 = (bf16[256,512]{1,0:T(8,128)(2,1)S(1)}, bf16[256,512]{1,0:T(8,128)(2,1)S(1)}, u32[]{:S(2)}, u32[]{:S(2)}) collective-permute-start(bf16[256,512]{1,0:T(8,128)(2,1)S(1)} %get-tuple-element.30.refs_4_), channel_id=1, source_target_pairs={{0,1},{1,0},{2,3},{3,2},{4,5},{5,4},{6,7},{7,6},{8,9},{9,8},{10,11... | collective-permute-start | bytes 786440 | tf_op jit(solution)/shard_map/ppermute | solution.py:39
  69.9 7.0 %collective-permute-start.10 = (bf16[256,512]{1,0:T(8,128)(2,1)S(1)}, bf16[256,512]{1,0:T(8,128)(2,1)S(1)}, u32[]{:S(2)}, u32[]{:S(2)}) collective-permute-start(bf16[256,512]{1,0:T(8,128)(2,1)S(1)} %get-tuple-element.33.refs_2_), channel_id=1, source_target_pairs={{0,2},{1,3},{2,0},{3,1},{4,6},{5,7},{6,4},{7,5},{8,10},{9,11},{10,... | collective-permute-start | bytes 786440 | tf_op jit(solution)/shard_map/ppermute | solution.py:39
  72.9 7.1 %collective-permute-start.9 = (bf16[256,512]{1,0:T(8,128)(2,1)S(1)}, bf16[256,512]{1,0:T(8,128)(2,1)S(1)}, u32[]{:S(2)}, u32[]{:S(2)}) collective-permute-start(bf16[256,512]{1,0:T(8,128)(2,1)S(1)} %get-tuple-element.36.refs_4_), channel_id=1, source_target_pairs={{0,1},{1,0},{2,3},{3,2},{4,5},{5,4},{6,7},{7,6},{8,9},{9,8},{10,11... | collective-permute-start | bytes 786440 | tf_op jit(solution)/shard_map/ppermute | solution.py:39
  74.1 7.5 %collective-permute-start.14 = (bf16[256,512]{1,0:T(8,128)(2,1)S(1)}, bf16[256,512]{1,0:T(8,128)(2,1)S(1)}, u32[]{:S(2)}, u32[]{:S(2)}) collective-permute-start(bf16[256,512]{1,0:T(8,128)(2,1)S(1)} %finish.4.refs_2_.refs_0_), channel_id=1, source_target_pairs={{0,1},{1,0},{2,3},{3,2},{4,5},{5,4},{6,7},{7,6},{8,9},{9,8},{10,11... | collective-permute-start | bytes 786440 | tf_op jit(solution)/shard_map/ppermute | solution.py:39
  74.2 7.5 %copy-start.3 = (bf16[1024,1024]{1,0:T(8,128)(2,1)S(1)}, bf16[1024,1024]{1,0:T(8,128)(2,1)}, u32[]{:S(2)}) copy-start(bf16[1024,1024]{1,0:T(8,128)(2,1)} %refs_3_.15) | copy-start | bytes 6291460
  74.3 7.4 %copy-start.2 = (bf16[1024,1024]{1,0:T(8,128)(2,1)S(1)}, bf16[1024,1024]{1,0:T(8,128)(2,1)}, u32[]{:S(2)}) copy-start(bf16[1024,1024]{1,0:T(8,128)(2,1)} %refs_2_.7) | copy-start | bytes 6291460
  74.3 12.8 %collective-permute-start.13 = (bf16[256,512]{1,0:T(8,128)(2,1)S(1)}, bf16[256,512]{1,0:T(8,128)(2,1)S(1)}, u32[]{:S(2)}, u32[]{:S(2)}) collective-permute-start(bf16[256,512]{1,0:T(8,128)(2,1)S(1)} %get-tuple-element.34.refs_5_), channel_id=1, source_target_pairs={{0,2},{1,3},{2,0},{3,1},{4,6},{5,7},{6,4},{7,5},{8,10},{9,11},{10,... | collective-permute-start | bytes 786440 | tf_op jit(solution)/shard_map/ppermute | solution.py:39
  77.0 10.8 %collective-permute-start.12 = (bf16[256,512]{1,0:T(8,128)(2,1)S(1)}, bf16[256,512]{1,0:T(8,128)(2,1)S(1)}, u32[]{:S(2)}, u32[]{:S(2)}) collective-permute-start(bf16[256,512]{1,0:T(8,128)(2,1)S(1)} %finish.5.refs_2_.refs_0_), channel_id=1, source_target_pairs={{0,1},{1,0},{2,3},{3,2},{4,5},{5,4},{6,7},{7,6},{8,9},{9,8},{10,11... | collective-permute-start | bytes 786440 | tf_op jit(solution)/shard_map/ppermute | solution.py:39
  80.1 9.5 %collective-permute-start.11 = (bf16[256,512]{1,0:T(8,128)(2,1)S(1)}, bf16[256,512]{1,0:T(8,128)(2,1)S(1)}, u32[]{:S(2)}, u32[]{:S(2)}) collective-permute-start(bf16[256,512]{1,0:T(8,128)(2,1)S(1)} %get-tuple-element.39.refs_5_), channel_id=1, source_target_pairs={{0,2},{1,3},{2,0},{3,1},{4,6},{5,7},{6,4},{7,5},{8,10},{9,11},{10,... | collective-permute-start | bytes 786440 | tf_op jit(solution)/shard_map/ppermute | solution.py:39
  83.3 6.2 %collective-permute-start.15 = (bf16[64,1024]{1,0:T(8,128)(2,1)S(1)}, bf16[64,1024]{1,0:T(8,128)(2,1)S(1)}, u32[]{:S(2)}, u32[]{:S(2)}) collective-permute-start(bf16[64,1024]{1,0:T(8,128)(2,1)S(1)} %attend.3.refs_4_.refs_8_), channel_id=1, source_target_pairs={{0,4},{4,8},{8,12},{12,16},{16,20},{20,24},{24,28},{1,5},{5,9},{9,... | collective-permute-start | bytes 393224 | tf_op jit(solution)/shard_map/ppermute | solution.py:45
  87.2 3.5 %collective-permute-start.17 = (bf16[256,512]{1,0:T(8,128)(2,1)S(1)}, bf16[256,512]{1,0:T(8,128)(2,1)S(1)}, u32[]{:S(2)}, u32[]{:S(2)}) collective-permute-start(bf16[256,512]{1,0:T(8,128)(2,1)S(1)} %finish.6.refs_5_.refs_0_), channel_id=1, source_target_pairs={{0,1},{1,0},{2,3},{3,2},{4,5},{5,4},{6,7},{7,6},{8,9},{9,8},{10,11... | collective-permute-start | bytes 786440 | tf_op jit(solution)/shard_map/ppermute | solution.py:39
  89.7 2.7 %collective-permute-start.16 = (bf16[256,512]{1,0:T(8,128)(2,1)S(1)}, bf16[256,512]{1,0:T(8,128)(2,1)S(1)}, u32[]{:S(2)}, u32[]{:S(2)}) collective-permute-start(bf16[256,512]{1,0:T(8,128)(2,1)S(1)} %finish.7.refs_5_.refs_0_), channel_id=1, source_target_pairs={{0,1},{1,0},{2,3},{3,2},{4,5},{5,4},{6,7},{7,6},{8,9},{9,8},{10,11... | collective-permute-start | bytes 786440 | tf_op jit(solution)/shard_map/ppermute | solution.py:39
  (1 other events, 0.7 us)

commit v9 on v8

--- a/solution.py
+++ b/solution.py
@@ -102,6 +102,10 @@
         ).astype(BF16)
 
 
+def mark_body(out_ref):
+    out_ref[...] = jnp.zeros_like(out_ref)
+
+
 def pair_body(left_ref, right_ref, out_ref):
     width = left_ref.shape[1]
     out_ref[:, :width] = left_ref[...]
@@ -209,6 +213,20 @@
 def attend_body(mine_ref, other_ref, w_key_ref, w_value_ref, q_ref, out_ref):
     for at, part in enumerate(attended(mine_ref, other_ref, w_key_ref, w_value_ref, q_ref)):
         out_ref[:, at * HEAD_WIDTH : (at + 1) * HEAD_WIDTH] = part.astype(BF16)
+
+
+def attend_first_body(
+    mine_ref, other_ref, w_key_ref, w_value_ref, queries_ref, next_ref, out_ref, q_ref
+):
+    edge = 16
+    for at in range(0, q_ref.shape[1], HEAD_WIDTH):
+        cols = slice(at, at + HEAD_WIDTH)
+        tall = jnp.concatenate(
+            [queries_ref[-edge:, cols].astype(F32), next_ref[:, cols].astype(F32)], axis=0
+        )
+        moved = pltpu.roll(tall, tall.shape[0] - edge + 1, 0)
+        q_ref[:, cols] = moved[: q_ref.shape[0]].astype(BF16)
+    attend_body(mine_ref, other_ref, w_key_ref, w_value_ref, q_ref, out_ref)
 
 
 def attend_last_body(
@@ -256,7 +274,7 @@
         found.reshape(seq_size, cap, width), "seq", split_axis=0, concat_axis=0, tiled=True
     ).reshape(slots, width)
     order = [groups - 1] + list(range(groups - 1))
-    plan = [order[:1], order[1:]]
+    plan = [order[:2], order[2:]]
     first, window = {}, {}
     token = slot
     pieces = []
@@ -281,7 +299,6 @@
     across(pieces[0], (token,))
     head = call(head_body, sds((GROUP, head_cols), BF16), "head", (queries,), (token,))
     next_q = shifted(head, -1)
-    local_q = jnp.concatenate([queries[GROUP - 1 :], next_q[: GROUP - 1]], axis=0)
     half = sds((per_group, 2 * width), BF16)
     whole = sds((per_group, 2 * width), F32)
     fed, summed, far, encoded = {}, {}, {}, {}
@@ -292,7 +309,11 @@
 
     def rest(_):
         nonlocal token
-        token = across(pieces[1], (token, next_q))
+        token = across(pieces[1], (token,))
+
+    def pause(_):
+        nonlocal token
+        token = call(mark_body, sds((8, LANES), F32), "mark", (), (token, pieces[1][1]))
 
     def feed(g):
         nonlocal token
@@ -323,7 +344,20 @@
 
     def attend(g):
         nonlocal token, behind, out
-        args = (*encoded[g], w_key, w_value, local_q[g * GROUP : (g + 1) * GROUP])
+        start = (g + 1) * GROUP - 1
+        args = (*encoded[g], w_key, w_value)
+        if g == order[0]:
+            window[g] = token = call(
+                attend_first_body,
+                sds((GROUP, head_cols), BF16),
+                "attend_first",
+                (*args, queries, next_q),
+                (token,),
+                scratch_shapes=[pltpu.VMEM((GROUP, head_cols), BF16)],
+            )
+            behind = shifted(token, 1)
+            return
+        args += (queries[start : start + GROUP],)
         if g == order[-1]:
             before = [window[at] for at in order[1:-1]]
             out = call(
@@ -336,14 +370,12 @@
         window[g] = token = call(
             attend_body, sds((GROUP, head_cols), BF16), "attend", args, (token,)
         )
-        if g == order[0]:
-            behind = shifted(token, 1)
 
     a, b, c, d = order
     for step, g in (
-        (feed, a), (add, a), (rest, b), (feed, b), (feed, c),
-        (finish, a), (add, b), (add, c), (feed, d),
-        (finish, b), (add, d), (attend, a),
+        (feed, a), (feed, b), (pause, c), (add, a), (rest, c), (feed, c), (add, b),
+        (finish, a), (feed, d), (add, c), (attend, a),
+        (finish, b), (add, d),
         (finish, c), (attend, b),
         (finish, d), (attend, c), (attend, d),
     ):

time: 95.4 us -> 96.6 us (1.013)
  waiting for transfers between devices: 12.8 us -> 16.9 us
  starting transfers between devices: 23 us -> 20.3 us
    ppermute x16, waiting for transfers between devices: 7.32 us -> 11.8 us  [exchange(): return lax.ppermute(x, 'tp', [(i, i ^ bit) for i in range(size)])]
    ppermute x16, starting transfers between devices: 18 us -> 14.9 us  [exchange(): return lax.ppermute(x, 'tp', [(i, i ^ bit) for i in range(size)])]
    pallas_call x23 -> x24, Pallas kernels: 19.3 us -> 19.3 us  [call(): pl.pallas_call(without_after, out_shape=outs, in_specs=in_specs + [unread...]
  transfers between devices with their start and end apart: 18 -> 18, of which waited for: 6 -> 7; matrix products, arithmetic and copies ran while one was open for 0% -> 0% of each run, Pallas kernels for 14% -> 13%
where the time goes in v9:
time: 96.6 us; the launch traced here: 96.3 us
  blocking collectives  38.6 us (40%)
  starting transfers between devices  20.3 us (21%)
  Pallas kernels  19.3 us (20%)
  waiting for transfers between devices  16.9 us (17%)
    all_to_all x1, blocking collectives, per_device(): lax.all_to_all(found.reshape(seq_size, cap, width), 'seq', split_axis=0,...  27.1 us
    pallas_call x24, Pallas kernels, call(): pl.pallas_call(without_after, out_shape=outs, in_specs=in_specs + [unread...  19.3 us
    ppermute x16, starting transfers between devices, exchange(): return lax.ppermute(x, 'tp', [(i, i ^ bit) for i in range(size)])  14.9 us
    ppermute x16, waiting for transfers between devices, exchange(): return lax.ppermute(x, 'tp', [(i, i ^ bit) for i in range(size)])  11.8 us
    all_to_all x1, blocking collectives, per_device(): lax.all_to_all(wanted, 'seq', split_axis=0, concat_axis=0, tiled=True)  11.5 us
    ppermute x2, starting transfers between devices, shifted(): return lax.ppermute(x, 'seq', pairs)  5.4 us
    ppermute x2, waiting for transfers between devices, shifted(): return lax.ppermute(x, 'seq', pairs)  5.15 us
  transfers between devices with their start and end apart: 18, of which 7 were waited for; matrix products, arithmetic and copies ran while one was open for 0% of the time, Pallas kernels for 13%

profile of v9, /device:TPU:1, one launch (start us, length us, event | category | flops | bytes accessed | tf_op | source)
XLA Modules:
  0.0 96.3 jit_solution(15192044790652730542)
XLA Ops:
  1.5 11.5 %all_to_all.14 = s32[8,1,256]{2,1,0:T(1,128)S(1)} all-to-all(s32[8,1,256]{2,1,0:T(1,128)S(1)} %copy.8), channel_id=1, replica_groups=mesh['seq'=8,'tp'=4] {'seq'}, dimensions={0} | all-to-all | bytes 16384 | tf_op jit(solution)/shard_map/all_to_all | solution.py:266
  13.1 2.4 %fetch.1 = bf16[2048,256]{1,0:T(8,128)(2,1)S(1)} custom-call(s32[1,2048]{1,0:T(1,128)S(1)} %bitcast.8, bf16[2048,256]{1,0:T(8,128)(2,1)S(1)} %copy-done.5), custom_call_target="tpu_custom_call" | custom-call | flops 1024 | bytes 1024 | tf_op jit(solution)/shard_map/fetch/pallas_call | solution.py:26
  15.5 27.1 %all_to_all.15 = bf16[8,256,256]{2,1,0:T(8,128)(2,1)S(1)} all-to-all(bf16[8,256,256]{2,1,0:T(8,128)(2,1)S(1)} %bitcast.7), channel_id=1, replica_groups=mesh['seq'=8,'tp'=4] {'seq'}, dimensions={0} | all-to-all | bytes 2097152 | tf_op jit(solution)/shard_map/all_to_all | solution.py:273
  43.3 1.3 %collective-permute-start.1 = (bf16[512,256]{1,0:T(8,128)(2,1)S(1)}, bf16[512,256]{1,0:T(8,128)(2,1)S(1)}, u32[]{:S(2)}, u32[]{:S(2)}) collective-permute-start(bf16[512,256]{1,0:T(8,128)(2,1)S(1)} %order.2.refs_2_.refs_0_), channel_id=1, source_target_pairs={{0,2},{1,3},{2,0},{3,1},{4,6},{5,7},{6,4},{7,5},{8,10},{9,11},{10,... | collective-permute-start | bytes 786440 | tf_op jit(solution)/shard_map/ppermute | solution.py:39
  45.3 3.8 %collective-permute-done.1.refs_1_ = bf16[512,256]{1,0:T(8,128)(2,1)S(1)} collective-permute-done((bf16[512,256]{1,0:T(8,128)(2,1)S(1)}, bf16[512,256]{1,0:T(8,128)(2,1)S(1)}, u32[]{:S(2)}, u32[]{:S(2)}) %collective-permute-start.1) | collective-permute-done | bytes 262176 | tf_op jit(solution)/shard_map/ppermute | solution.py:39
  49.2 3.0 %collective-permute-start.2 = (bf16[512,512]{1,0:T(8,128)(2,1)S(1)}, bf16[512,512]{1,0:T(8,128)(2,1)S(1)}, u32[]{:S(2)}, u32[]{:S(2)}) collective-permute-start(bf16[512,512]{1,0:T(8,128)(2,1)S(1)} %pair.2), channel_id=1, source_target_pairs={{0,1},{1,0},{2,3},{3,2},{4,5},{5,4},{6,7},{7,6},{8,9},{9,8},{10,11... | collective-permute-start | bytes 1572872 | tf_op jit(solution)/shard_map/ppermute | solution.py:39
  52.2 1.3 %collective-permute-start = (bf16[512,256]{1,0:T(8,128)(2,1)S(1)}, bf16[512,256]{1,0:T(8,128)(2,1)S(1)}, u32[]{:S(2)}, u32[]{:S(2)}) collective-permute-start(bf16[512,256]{1,0:T(8,128)(2,1)S(1)} %order.3.refs_2_.refs_5_.refs_0_.refs_1_), channel_id=1, source_target_pairs={{0,2},{1,3},{2,0},{3,1},{4,6},{5,7},{6,4},{7,5},{8,10},{9,11},{10,... | collective-permute-start | bytes 786440 | tf_op jit(solution)/shard_map/ppermute | solution.py:39
  53.7 1.6 %feed.4 = (f32[256,512]{1,0:T(8,128)S(1)}, bf16[256,512]{1,0:T(8,128)(2,1)S(1)}) custom-call(bf16[512,256]{1,0:T(8,128)(2,1)S(1)} %order.2.refs_2_.refs_0_, bf16[512,256]{1,0:T(8,128)(2,1)S(1)} %collective-permute-done.1.refs_1_, bf16[512,512]{1,0:T(8,128)(2,1)S(1)} %collective-permute-done.2.refs_2_, bf16[1024,1024]{1,0:T(8,128)(2,1)S(1)} %copy-done, ...), custom_call_target="tpu_custom_call" | custom-call | flops 1024 | bytes 1024 | tf_op jit(solution)/shard_map/feed/pallas_call | solution.py:26
  55.8 1.6 %feed.5 = (f32[256,512]{1,0:T(8,128)S(1)}, bf16[256,512]{1,0:T(8,128)(2,1)S(1)}) custom-call(bf16[512,256]{1,0:T(8,128)(2,1)S(1)} %order.2.refs_2_.refs_0_, bf16[512,256]{1,0:T(8,128)(2,1)S(1)} %collective-permute-done.1.refs_1_, bf16[512,512]{1,0:T(8,128)(2,1)S(1)} %collective-permute-done.2.refs_2_, bf16[1024,1024]{1,0:T(8,128)(2,1)S(1)} %copy-done, ...), custom_call_target="tpu_custom_call" | custom-call | flops 1024 | bytes 1024 | tf_op jit(solution)/shard_map/feed/pallas_call | solution.py:26
  57.4 2.7 %collective-permute-done.refs_1_ = bf16[512,256]{1,0:T(8,128)(2,1)S(1)} collective-permute-done((bf16[512,256]{1,0:T(8,128)(2,1)S(1)}, bf16[512,256]{1,0:T(8,128)(2,1)S(1)}, u32[]{:S(2)}, u32[]{:S(2)}) %collective-permute-start) | collective-permute-done | bytes 262176 | tf_op jit(solution)/shard_map/ppermute | solution.py:39
  61.2 1.2 %collective-permute-start.5 = (bf16[256,512]{1,0:T(8,128)(2,1)S(1)}, bf16[256,512]{1,0:T(8,128)(2,1)S(1)}, u32[]{:S(2)}, u32[]{:S(2)}) collective-permute-start(bf16[256,512]{1,0:T(8,128)(2,1)S(1)} %get-tuple-element.28.refs_2_), channel_id=1, source_target_pairs={{0,2},{1,3},{2,0},{3,1},{4,6},{5,7},{6,4},{7,5},{8,10},{9,11},{10,... | collective-permute-start | bytes 786440 | tf_op jit(solution)/shard_map/ppermute | solution.py:39
  62.7 1.6 %feed.6 = (f32[256,512]{1,0:T(8,128)S(1)}, bf16[256,512]{1,0:T(8,128)(2,1)S(1)}) custom-call(bf16[512,256]{1,0:T(8,128)(2,1)S(1)} %order.3.refs_2_.refs_5_.refs_0_.refs_1_, bf16[512,256]{1,0:T(8,128)(2,1)S(1)} %collective-permute-done.refs_1_, bf16[512,512]{1,0:T(8,128)(2,1)S(1)} %collective-permute-done.4.refs_2_, bf16[1024,1024]{1,0:T(8,128)(2,1)S(1)} %copy-done, ...), custom_call_target="tpu_custom_call" | custom-call | flops 1024 | bytes 1024 | tf_op jit(solution)/shard_map/feed/pallas_call | solution.py:26
  64.9 3.7 %collective-permute-done.5.refs_3_ = bf16[256,512]{1,0:T(8,128)(2,1)S(1)} collective-permute-done((bf16[256,512]{1,0:T(8,128)(2,1)S(1)}, bf16[256,512]{1,0:T(8,128)(2,1)S(1)}, u32[]{:S(2)}, u32[]{:S(2)}) %collective-permute-start.5) | collective-permute-done | bytes 262176 | tf_op jit(solution)/shard_map/ppermute | solution.py:39
  68.8 1.3 %collective-permute-start.9 = (bf16[256,512]{1,0:T(8,128)(2,1)S(1)}, bf16[256,512]{1,0:T(8,128)(2,1)S(1)}, u32[]{:S(2)}, u32[]{:S(2)}) collective-permute-start(bf16[256,512]{1,0:T(8,128)(2,1)S(1)} %finish.4.refs_5_.refs_0_), channel_id=1, source_target_pairs={{0,1},{1,0},{2,3},{3,2},{4,5},{5,4},{6,7},{7,6},{8,9},{9,8},{10,11... | collective-permute-start | bytes 786440 | tf_op jit(solution)/shard_map/ppermute | solution.py:39
  70.1 1.3 %collective-permute-start.8 = (bf16[256,512]{1,0:T(8,128)(2,1)S(1)}, bf16[256,512]{1,0:T(8,128)(2,1)S(1)}, u32[]{:S(2)}, u32[]{:S(2)}) collective-permute-start(bf16[256,512]{1,0:T(8,128)(2,1)S(1)} %get-tuple-element.32.refs_4_), channel_id=1, source_target_pairs={{0,2},{1,3},{2,0},{3,1},{4,6},{5,7},{6,4},{7,5},{8,10},{9,11},{10,... | collective-permute-start | bytes 786440 | tf_op jit(solution)/shard_map/ppermute | solution.py:39
  71.4 1.6 %feed.7 = (f32[256,512]{1,0:T(8,128)S(1)}, bf16[256,512]{1,0:T(8,128)(2,1)S(1)}) custom-call(bf16[512,256]{1,0:T(8,128)(2,1)S(1)} %order.3.refs_2_.refs_5_.refs_0_.refs_1_, bf16[512,256]{1,0:T(8,128)(2,1)S(1)} %collective-permute-done.refs_1_, bf16[512,512]{1,0:T(8,128)(2,1)S(1)} %collective-permute-done.4.refs_2_, bf16[1024,1024]{1,0:T(8,128)(2,1)S(1)} %copy-done, ...), custom_call_target="tpu_custom_call" | custom-call | flops 1024 | bytes 1024 | tf_op jit(solution)/shard_map/feed/pallas_call | solution.py:26
  73.4 1.3 %collective-permute-start.10 = (bf16[64,1024]{1,0:T(8,128)(2,1)S(1)}, bf16[64,1024]{1,0:T(8,128)(2,1)S(1)}, u32[]{:S(2)}, u32[]{:S(2)}) collective-permute-start(bf16[64,1024]{1,0:T(8,128)(2,1)S(1)} %head.1), channel_id=1, source_target_pairs={{4,0},{8,4},{12,8},{16,12},{20,16},{24,20},{28,24},{5,1},{9,5},{13... | collective-permute-start | bytes 393224 | tf_op jit(solution)/shard_map/ppermute | solution.py:45
  75.1 5.2 %collective-permute-done.10.refs_5_ = bf16[64,1024]{1,0:T(8,128)(2,1)S(1)} collective-permute-done((bf16[64,1024]{1,0:T(8,128)(2,1)S(1)}, bf16[64,1024]{1,0:T(8,128)(2,1)S(1)}, u32[]{:S(2)}, u32[]{:S(2)}) %collective-permute-start.10) | collective-permute-done | bytes 131104 | tf_op jit(solution)/shard_map/ppermute | solution.py:45
  80.2 1.7 %attend_first.1.refs_4_.refs_8_ = bf16[64,1024]{1,0:T(8,128)(2,1)S(1)} custom-call(bf16[256,512]{1,0:T(8,128)(2,1)S(1)} %finish.4.refs_5_.refs_0_, bf16[256,512]{1,0:T(8,128)(2,1)S(1)} %collective-permute-done.9.refs_1_, bf16[1024,1024]{1,0:T(8,128)(2,1)S(1)} %copy-done.2, bf16[1024,1024]{1,0:T(8,128)(2,1)S(1)} %copy-done.3, ...), custom_call_target="tpu_custom_call" | custom-call | flops 1024 | bytes 1024 | tf_op jit(solution)/shard_map/attend_first/pallas_call | solution.py:26
  82.0 1.0 %collective-permute-start.13 = (bf16[256,512]{1,0:T(8,128)(2,1)S(1)}, bf16[256,512]{1,0:T(8,128)(2,1)S(1)}, u32[]{:S(2)}, u32[]{:S(2)}) collective-permute-start(bf16[256,512]{1,0:T(8,128)(2,1)S(1)} %finish.5.refs_2_.refs_0_), channel_id=1, source_target_pairs={{0,1},{1,0},{2,3},{3,2},{4,5},{5,4},{6,7},{7,6},{8,9},{9,8},{10,11... | collective-permute-start | bytes 786440 | tf_op jit(solution)/shard_map/ppermute | solution.py:39
  83.4 4.1 %collective-permute-start.15 = (bf16[64,1024]{1,0:T(8,128)(2,1)S(1)}, bf16[64,1024]{1,0:T(8,128)(2,1)S(1)}, u32[]{:S(2)}, u32[]{:S(2)}) collective-permute-start(bf16[64,1024]{1,0:T(8,128)(2,1)S(1)} %attend_first.1.refs_4_.refs_8_), channel_id=1, source_target_pairs={{0,4},{4,8},{8,12},{12,16},{16,20},{20,24},{24,28},{1,5},{5,9},{9,... | collective-permute-start | bytes 393224 | tf_op jit(solution)/shard_map/ppermute | solution.py:45
  88.4 1.7 %attend.2.refs_4_.refs_6_ = bf16[64,1024]{1,0:T(8,128)(2,1)S(1)} custom-call(bf16[256,512]{1,0:T(8,128)(2,1)S(1)} %finish.5.refs_2_.refs_0_, bf16[256,512]{1,0:T(8,128)(2,1)S(1)} %collective-permute-done.13.refs_1_, bf16[1024,1024]{1,0:T(8,128)(2,1)S(1)} %copy-done.2, bf16[1024,1024]{1,0:T(8,128)(2,1)S(1)} %copy-done.3, ...), custom_call_target="tpu_custom_call" | custom-call | flops 1024 | bytes 1024 | tf_op jit(solution)/shard_map/attend/pallas_call | solution.py:26
  92.1 1.7 %attend.3.refs_7_ = bf16[64,1024]{1,0:T(8,128)(2,1)S(1)} custom-call(bf16[256,512]{1,0:T(8,128)(2,1)S(1)} %finish.6.refs_5_.refs_0_, bf16[256,512]{1,0:T(8,128)(2,1)S(1)} %collective-permute-done.17.refs_1_, bf16[1024,1024]{1,0:T(8,128)(2,1)S(1)} %copy-done.2, bf16[1024,1024]{1,0:T(8,128)(2,1)S(1)} %copy-done.3, ...), custom_call_target="tpu_custom_call" | custom-call | flops 1024 | bytes 1024 | tf_op jit(solution)/shard_map/attend/pallas_call | solution.py:26
  93.8 2.5 %attend_last.1 = bf16[256,1024]{1,0:T(8,128)(2,1)} custom-call(bf16[256,512]{1,0:T(8,128)(2,1)S(1)} %finish.7.refs_5_.refs_0_, bf16[256,512]{1,0:T(8,128)(2,1)S(1)} %collective-permute-done.16.refs_1_, bf16[1024,1024]{1,0:T(8,128)(2,1)S(1)} %copy-done.2, bf16[1024,1024]{1,0:T(8,128)(2,1)S(1)} %copy-done.3, bf16[64,1024]{1,0:T(8,128)(2,1)S(1)} %get-tuple-element.43.refs_4_, ...), custom_call_target="tpu_custom_call" | custom-call | flops 1024 | bytes 1024 | tf_op jit(solution)/shard_map/attend_last/pallas_call | solution.py:26
  (54 shorter events, 9.9 us)
Async XLA Ops:
  0.7 12.4 %copy-start.5 = (bf16[2048,256]{1,0:T(8,128)(2,1)S(1)}, bf16[2048,256]{1,0:T(8,128)(2,1)}, u32[]{:S(2)}) copy-start(bf16[2048,256]{1,0:T(8,128)(2,1)} %refs_1_.1) | copy-start | bytes 3145732
  42.6 11.2 %copy-start.1 = (bf16[1024,1024]{1,0:T(8,128)(2,1)S(1)}, bf16[1024,1024]{1,0:T(8,128)(2,1)}, u32[]{:S(2)}) copy-start(bf16[1024,1024]{1,0:T(8,128)(2,1)} %refs_4_.8) | copy-start | bytes 6291460
  43.3 10.4 %copy-start = (bf16[1024,1024]{1,0:T(8,128)(2,1)S(1)}, bf16[1024,1024]{1,0:T(8,128)(2,1)}, u32[]{:S(2)}) copy-start(bf16[1024,1024]{1,0:T(8,128)(2,1)} %refs_3_.11) | copy-start | bytes 6291460
  43.3 5.8 %collective-permute-start.1 = (bf16[512,256]{1,0:T(8,128)(2,1)S(1)}, bf16[512,256]{1,0:T(8,128)(2,1)S(1)}, u32[]{:S(2)}, u32[]{:S(2)}) collective-permute-start(bf16[512,256]{1,0:T(8,128)(2,1)S(1)} %order.2.refs_2_.refs_0_), channel_id=1, source_target_pairs={{0,2},{1,3},{2,0},{3,1},{4,6},{5,7},{6,4},{7,5},{8,10},{9,11},{10,... | collective-permute-start | bytes 786440 | tf_op jit(solution)/shard_map/ppermute | solution.py:39
  49.2 4.5 %collective-permute-start.2 = (bf16[512,512]{1,0:T(8,128)(2,1)S(1)}, bf16[512,512]{1,0:T(8,128)(2,1)S(1)}, u32[]{:S(2)}, u32[]{:S(2)}) collective-permute-start(bf16[512,512]{1,0:T(8,128)(2,1)S(1)} %pair.2), channel_id=1, source_target_pairs={{0,1},{1,0},{2,3},{3,2},{4,5},{5,4},{6,7},{7,6},{8,9},{9,8},{10,11... | collective-permute-start | bytes 1572872 | tf_op jit(solution)/shard_map/ppermute | solution.py:39
  52.2 7.9 %collective-permute-start = (bf16[512,256]{1,0:T(8,128)(2,1)S(1)}, bf16[512,256]{1,0:T(8,128)(2,1)S(1)}, u32[]{:S(2)}, u32[]{:S(2)}) collective-permute-start(bf16[512,256]{1,0:T(8,128)(2,1)S(1)} %order.3.refs_2_.refs_5_.refs_0_.refs_1_), channel_id=1, source_target_pairs={{0,2},{1,3},{2,0},{3,1},{4,6},{5,7},{6,4},{7,5},{8,10},{9,11},{10,... | collective-permute-start | bytes 786440 | tf_op jit(solution)/shard_map/ppermute | solution.py:39
  55.3 4.7 %collective-permute-start.3 = (bf16[256,512]{1,0:T(8,128)(2,1)S(1)}, bf16[256,512]{1,0:T(8,128)(2,1)S(1)}, u32[]{:S(2)}, u32[]{:S(2)}) collective-permute-start(bf16[256,512]{1,0:T(8,128)(2,1)S(1)} %get-tuple-element.26.refs_5_), channel_id=1, source_target_pairs={{0,1},{1,0},{2,3},{3,2},{4,5},{5,4},{6,7},{7,6},{8,9},{9,8},{10,11... | collective-permute-start | bytes 786440 | tf_op jit(solution)/shard_map/ppermute | solution.py:39
  60.2 2.5 %collective-permute-start.4 = (bf16[512,512]{1,0:T(8,128)(2,1)S(1)}, bf16[512,512]{1,0:T(8,128)(2,1)S(1)}, u32[]{:S(2)}, u32[]{:S(2)}) collective-permute-start(bf16[512,512]{1,0:T(8,128)(2,1)S(1)} %pair.3.refs_5_), channel_id=1, source_target_pairs={{0,1},{1,0},{2,3},{3,2},{4,5},{5,4},{6,7},{7,6},{8,9},{9,8},{10,11... | collective-permute-start | bytes 1572872 | tf_op jit(solution)/shard_map/ppermute | solution.py:39
  61.1 3.7 %collective-permute-start.6 = (bf16[256,512]{1,0:T(8,128)(2,1)S(1)}, bf16[256,512]{1,0:T(8,128)(2,1)S(1)}, u32[]{:S(2)}, u32[]{:S(2)}) collective-permute-start(bf16[256,512]{1,0:T(8,128)(2,1)S(1)} %get-tuple-element.27.refs_0_), channel_id=1, source_target_pairs={{0,1},{1,0},{2,3},{3,2},{4,5},{5,4},{6,7},{7,6},{8,9},{9,8},{10,11... | collective-permute-start | bytes 786440 | tf_op jit(solution)/shard_map/ppermute | solution.py:39
  61.2 7.4 %collective-permute-start.5 = (bf16[256,512]{1,0:T(8,128)(2,1)S(1)}, bf16[256,512]{1,0:T(8,128)(2,1)S(1)}, u32[]{:S(2)}, u32[]{:S(2)}) collective-permute-start(bf16[256,512]{1,0:T(8,128)(2,1)S(1)} %get-tuple-element.28.refs_2_), channel_id=1, source_target_pairs={{0,2},{1,3},{2,0},{3,1},{4,6},{5,7},{6,4},{7,5},{8,10},{9,11},{10,... | collective-permute-start | bytes 786440 | tf_op jit(solution)/shard_map/ppermute | solution.py:39
  64.3 10.4 %collective-permute-start.11 = (bf16[256,512]{1,0:T(8,128)(2,1)S(1)}, bf16[256,512]{1,0:T(8,128)(2,1)S(1)}, u32[]{:S(2)}, u32[]{:S(2)}) collective-permute-start(bf16[256,512]{1,0:T(8,128)(2,1)S(1)} %get-tuple-element.31.refs_2_), channel_id=1, source_target_pairs={{0,1},{1,0},{2,3},{3,2},{4,5},{5,4},{6,7},{7,6},{8,9},{9,8},{10,11... | collective-permute-start | bytes 786440 | tf_op jit(solution)/shard_map/ppermute | solution.py:39
  68.7 4.6 %copy-start.4 = (bf16[256,1024]{1,0:T(8,128)(2,1)S(1)}, bf16[256,1024]{1,0:T(8,128)(2,1)}, u32[]{:S(2)}) copy-start(bf16[256,1024]{1,0:T(8,128)(2,1)} %refs_4_.9) | copy-start | bytes 1572868
  68.8 11.5 %collective-permute-start.9 = (bf16[256,512]{1,0:T(8,128)(2,1)S(1)}, bf16[256,512]{1,0:T(8,128)(2,1)S(1)}, u32[]{:S(2)}, u32[]{:S(2)}) collective-permute-start(bf16[256,512]{1,0:T(8,128)(2,1)S(1)} %finish.4.refs_5_.refs_0_), channel_id=1, source_target_pairs={{0,1},{1,0},{2,3},{3,2},{4,5},{5,4},{6,7},{7,6},{8,9},{9,8},{10,11... | collective-permute-start | bytes 786440 | tf_op jit(solution)/shard_map/ppermute | solution.py:39
  70.1 11.8 %collective-permute-start.8 = (bf16[256,512]{1,0:T(8,128)(2,1)S(1)}, bf16[256,512]{1,0:T(8,128)(2,1)S(1)}, u32[]{:S(2)}, u32[]{:S(2)}) collective-permute-start(bf16[256,512]{1,0:T(8,128)(2,1)S(1)} %get-tuple-element.32.refs_4_), channel_id=1, source_target_pairs={{0,2},{1,3},{2,0},{3,1},{4,6},{5,7},{6,4},{7,5},{8,10},{9,11},{10,... | collective-permute-start | bytes 786440 | tf_op jit(solution)/shard_map/ppermute | solution.py:39
  71.4 8.9 %copy-start.2 = (bf16[1024,1024]{1,0:T(8,128)(2,1)S(1)}, bf16[1024,1024]{1,0:T(8,128)(2,1)}, u32[]{:S(2)}) copy-start(bf16[1024,1024]{1,0:T(8,128)(2,1)} %refs_2_.7) | copy-start | bytes 6291460
  71.4 8.9 %copy-start.3 = (bf16[1024,1024]{1,0:T(8,128)(2,1)S(1)}, bf16[1024,1024]{1,0:T(8,128)(2,1)}, u32[]{:S(2)}) copy-start(bf16[1024,1024]{1,0:T(8,128)(2,1)} %refs_3_.15) | copy-start | bytes 6291460
  73.0 10.1 %collective-permute-start.7 = (bf16[256,512]{1,0:T(8,128)(2,1)S(1)}, bf16[256,512]{1,0:T(8,128)(2,1)S(1)}, u32[]{:S(2)}, u32[]{:S(2)}) collective-permute-start(bf16[256,512]{1,0:T(8,128)(2,1)S(1)} %get-tuple-element.34.refs_2_), channel_id=1, source_target_pairs={{0,1},{1,0},{2,3},{3,2},{4,5},{5,4},{6,7},{7,6},{8,9},{9,8},{10,11... | collective-permute-start | bytes 786440 | tf_op jit(solution)/shard_map/ppermute | solution.py:39
  73.4 6.8 %collective-permute-start.10 = (bf16[64,1024]{1,0:T(8,128)(2,1)S(1)}, bf16[64,1024]{1,0:T(8,128)(2,1)S(1)}, u32[]{:S(2)}, u32[]{:S(2)}) collective-permute-start(bf16[64,1024]{1,0:T(8,128)(2,1)S(1)} %head.1), channel_id=1, source_target_pairs={{4,0},{8,4},{12,8},{16,12},{20,16},{24,20},{28,24},{5,1},{9,5},{13... | collective-permute-start | bytes 393224 | tf_op jit(solution)/shard_map/ppermute | solution.py:45
  74.8 12.9 %collective-permute-start.14 = (bf16[256,512]{1,0:T(8,128)(2,1)S(1)}, bf16[256,512]{1,0:T(8,128)(2,1)S(1)}, u32[]{:S(2)}, u32[]{:S(2)}) collective-permute-start(bf16[256,512]{1,0:T(8,128)(2,1)S(1)} %get-tuple-element.37.refs_6_), channel_id=1, source_target_pairs={{0,2},{1,3},{2,0},{3,1},{4,6},{5,7},{6,4},{7,5},{8,10},{9,11},{10,... | collective-permute-start | bytes 786440 | tf_op jit(solution)/shard_map/ppermute | solution.py:39
  82.0 6.4 %collective-permute-start.13 = (bf16[256,512]{1,0:T(8,128)(2,1)S(1)}, bf16[256,512]{1,0:T(8,128)(2,1)S(1)}, u32[]{:S(2)}, u32[]{:S(2)}) collective-permute-start(bf16[256,512]{1,0:T(8,128)(2,1)S(1)} %finish.5.refs_2_.refs_0_), channel_id=1, source_target_pairs={{0,1},{1,0},{2,3},{3,2},{4,5},{5,4},{6,7},{7,6},{8,9},{9,8},{10,11... | collective-permute-start | bytes 786440 | tf_op jit(solution)/shard_map/ppermute | solution.py:39
  83.2 8.0 %collective-permute-start.12 = (bf16[256,512]{1,0:T(8,128)(2,1)S(1)}, bf16[256,512]{1,0:T(8,128)(2,1)S(1)}, u32[]{:S(2)}, u32[]{:S(2)}) collective-permute-start(bf16[256,512]{1,0:T(8,128)(2,1)S(1)} %get-tuple-element.39.refs_4_), channel_id=1, source_target_pairs={{0,2},{1,3},{2,0},{3,1},{4,6},{5,7},{6,4},{7,5},{8,10},{9,11},{10,... | collective-permute-start | bytes 786440 | tf_op jit(solution)/shard_map/ppermute | solution.py:39
  83.4 6.7 %collective-permute-start.15 = (bf16[64,1024]{1,0:T(8,128)(2,1)S(1)}, bf16[64,1024]{1,0:T(8,128)(2,1)S(1)}, u32[]{:S(2)}, u32[]{:S(2)}) collective-permute-start(bf16[64,1024]{1,0:T(8,128)(2,1)S(1)} %attend_first.1.refs_4_.refs_8_), channel_id=1, source_target_pairs={{0,4},{4,8},{8,12},{12,16},{16,20},{20,24},{24,28},{1,5},{5,9},{9,... | collective-permute-start | bytes 393224 | tf_op jit(solution)/shard_map/ppermute | solution.py:45
  87.8 4.3 %collective-permute-start.17 = (bf16[256,512]{1,0:T(8,128)(2,1)S(1)}, bf16[256,512]{1,0:T(8,128)(2,1)S(1)}, u32[]{:S(2)}, u32[]{:S(2)}) collective-permute-start(bf16[256,512]{1,0:T(8,128)(2,1)S(1)} %finish.6.refs_5_.refs_0_), channel_id=1, source_target_pairs={{0,1},{1,0},{2,3},{3,2},{4,5},{5,4},{6,7},{7,6},{8,9},{9,8},{10,11... | collective-permute-start | bytes 786440 | tf_op jit(solution)/shard_map/ppermute | solution.py:39
  91.2 2.6 %collective-permute-start.16 = (bf16[256,512]{1,0:T(8,128)(2,1)S(1)}, bf16[256,512]{1,0:T(8,128)(2,1)S(1)}, u32[]{:S(2)}, u32[]{:S(2)}) collective-permute-start(bf16[256,512]{1,0:T(8,128)(2,1)S(1)} %finish.7.refs_5_.refs_0_), channel_id=1, source_target_pairs={{0,1},{1,0},{2,3},{3,2},{4,5},{5,4},{6,7},{7,6},{8,9},{9,8},{10,11... | collective-permute-start | bytes 786440 | tf_op jit(solution)/shard_map/ppermute | solution.py:39
  (1 other events, 0.7 us)

commit v10 on v9

--- a/solution.py
+++ b/solution.py
@@ -313,7 +313,7 @@
 
     def pause(_):
         nonlocal token
-        token = call(mark_body, sds((8, LANES), F32), "mark", (), (token, pieces[1][1]))
+        token = call(mark_body, sds((8, LANES), F32), "mark", (), (token, pieces[1][1], next_q))
 
     def feed(g):
         nonlocal token
@@ -368,14 +368,18 @@
             )
             return
         window[g] = token = call(
-            attend_body, sds((GROUP, head_cols), BF16), "attend", args, (token,)
+            attend_body,
+            sds((GROUP, head_cols), BF16),
+            "attend",
+            args,
+            (token,),
         )
 
     a, b, c, d = order
     for step, g in (
         (feed, a), (feed, b), (pause, c), (add, a), (rest, c), (feed, c), (add, b),
-        (finish, a), (feed, d), (add, c), (attend, a),
-        (finish, b), (add, d),
+        (finish, a), (feed, d), (add, c),
+        (finish, b), (attend, a), (add, d),
         (finish, c), (attend, b),
         (finish, d), (attend, c), (attend, d),
     ):

time: 96.6 us -> 94.5 us (0.978)
  waiting for transfers between devices: 16.9 us -> 11.5 us
  starting transfers between devices: 20.3 us -> 23.7 us
    ppermute x16, waiting for transfers between devices: 11.8 us -> 7.58 us  [exchange(): return lax.ppermute(x, 'tp', [(i, i ^ bit) for i in range(size)])]
    ppermute x16, starting transfers between devices: 14.9 us -> 18.3 us  [exchange(): return lax.ppermute(x, 'tp', [(i, i ^ bit) for i in range(size)])]
    ppermute x2, waiting for transfers between devices: 5.15 us -> 3.95 us  [shifted(): return lax.ppermute(x, 'seq', pairs)]
  transfers between devices with their start and end apart: 18 -> 18, of which waited for: 7 -> 7; matrix products, arithmetic and copies ran while one was open for 0% -> 0% of each run, Pallas kernels for 13% -> 14%
where the time goes in v10:
time: 94.5 us; the launch traced here: 94.2 us
  blocking collectives  38.6 us (41%)
  starting transfers between devices  23.7 us (25%)
  Pallas kernels  19.3 us (20%)
  waiting for transfers between devices  11.5 us (12%)
    all_to_all x1, blocking collectives, per_device(): lax.all_to_all(found.reshape(seq_size, cap, width), 'seq', split_axis=0,...  27.1 us
    pallas_call x24, Pallas kernels, call(): pl.pallas_call(without_after, out_shape=outs, in_specs=in_specs + [unread...  19.3 us
    ppermute x16, starting transfers between devices, exchange(): return lax.ppermute(x, 'tp', [(i, i ^ bit) for i in range(size)])  18.3 us
    all_to_all x1, blocking collectives, per_device(): lax.all_to_all(wanted, 'seq', split_axis=0, concat_axis=0, tiled=True)  11.5 us
    ppermute x16, waiting for transfers between devices, exchange(): return lax.ppermute(x, 'tp', [(i, i ^ bit) for i in range(size)])  7.58 us
    ppermute x2, starting transfers between devices, shifted(): return lax.ppermute(x, 'seq', pairs)  5.4 us
    ppermute x2, waiting for transfers between devices, shifted(): return lax.ppermute(x, 'seq', pairs)  3.95 us
  transfers between devices with their start and end apart: 18, of which 7 were waited for; matrix products, arithmetic and copies ran while one was open for 0% of the time, Pallas kernels for 14%

profile of v10, /device:TPU:1, one launch (start us, length us, event | category | flops | bytes accessed | tf_op | source)
XLA Modules:
  0.0 94.2 jit_solution(9119542500691318378)
XLA Ops:
  1.5 11.5 %all_to_all.14 = s32[8,1,256]{2,1,0:T(1,128)S(1)} all-to-all(s32[8,1,256]{2,1,0:T(1,128)S(1)} %copy.8), channel_id=1, replica_groups=mesh['seq'=8,'tp'=4] {'seq'}, dimensions={0} | all-to-all | bytes 16384 | tf_op jit(solution)/shard_map/all_to_all | solution.py:266
  13.1 2.4 %fetch.1 = bf16[2048,256]{1,0:T(8,128)(2,1)S(1)} custom-call(s32[1,2048]{1,0:T(1,128)S(1)} %bitcast.8, bf16[2048,256]{1,0:T(8,128)(2,1)S(1)} %copy-done.5), custom_call_target="tpu_custom_call" | custom-call | flops 1024 | bytes 1024 | tf_op jit(solution)/shard_map/fetch/pallas_call | solution.py:26
  15.5 27.1 %all_to_all.15 = bf16[8,256,256]{2,1,0:T(8,128)(2,1)S(1)} all-to-all(bf16[8,256,256]{2,1,0:T(8,128)(2,1)S(1)} %bitcast.7), channel_id=1, replica_groups=mesh['seq'=8,'tp'=4] {'seq'}, dimensions={0} | all-to-all | bytes 2097152 | tf_op jit(solution)/shard_map/all_to_all | solution.py:273
  43.3 1.3 %collective-permute-start.1 = (bf16[512,256]{1,0:T(8,128)(2,1)S(1)}, bf16[512,256]{1,0:T(8,128)(2,1)S(1)}, u32[]{:S(2)}, u32[]{:S(2)}) collective-permute-start(bf16[512,256]{1,0:T(8,128)(2,1)S(1)} %order.2.refs_2_.refs_0_), channel_id=1, source_target_pairs={{0,2},{1,3},{2,0},{3,1},{4,6},{5,7},{6,4},{7,5},{8,10},{9,11},{10,... | collective-permute-start | bytes 786440 | tf_op jit(solution)/shard_map/ppermute | solution.py:39
  45.3 3.8 %collective-permute-done.1.refs_1_ = bf16[512,256]{1,0:T(8,128)(2,1)S(1)} collective-permute-done((bf16[512,256]{1,0:T(8,128)(2,1)S(1)}, bf16[512,256]{1,0:T(8,128)(2,1)S(1)}, u32[]{:S(2)}, u32[]{:S(2)}) %collective-permute-start.1) | collective-permute-done | bytes 262176 | tf_op jit(solution)/shard_map/ppermute | solution.py:39
  49.2 3.0 %collective-permute-start.2 = (bf16[512,512]{1,0:T(8,128)(2,1)S(1)}, bf16[512,512]{1,0:T(8,128)(2,1)S(1)}, u32[]{:S(2)}, u32[]{:S(2)}) collective-permute-start(bf16[512,512]{1,0:T(8,128)(2,1)S(1)} %pair.2), channel_id=1, source_target_pairs={{0,1},{1,0},{2,3},{3,2},{4,5},{5,4},{6,7},{7,6},{8,9},{9,8},{10,11... | collective-permute-start | bytes 1572872 | tf_op jit(solution)/shard_map/ppermute | solution.py:39
  52.2 1.3 %collective-permute-start = (bf16[512,256]{1,0:T(8,128)(2,1)S(1)}, bf16[512,256]{1,0:T(8,128)(2,1)S(1)}, u32[]{:S(2)}, u32[]{:S(2)}) collective-permute-start(bf16[512,256]{1,0:T(8,128)(2,1)S(1)} %order.3.refs_2_.refs_5_.refs_1_.refs_0_), channel_id=1, source_target_pairs={{0,2},{1,3},{2,0},{3,1},{4,6},{5,7},{6,4},{7,5},{8,10},{9,11},{10,... | collective-permute-start | bytes 786440 | tf_op jit(solution)/shard_map/ppermute | solution.py:39
  53.7 1.6 %feed.4 = (f32[256,512]{1,0:T(8,128)S(1)}, bf16[256,512]{1,0:T(8,128)(2,1)S(1)}) custom-call(bf16[512,256]{1,0:T(8,128)(2,1)S(1)} %order.2.refs_2_.refs_0_, bf16[512,256]{1,0:T(8,128)(2,1)S(1)} %collective-permute-done.1.refs_1_, bf16[512,512]{1,0:T(8,128)(2,1)S(1)} %collective-permute-done.2.refs_2_, bf16[1024,1024]{1,0:T(8,128)(2,1)S(1)} %copy-done, ...), custom_call_target="tpu_custom_call" | custom-call | flops 1024 | bytes 1024 | tf_op jit(solution)/shard_map/feed/pallas_call | solution.py:26
  55.8 1.3 %collective-permute-start.4 = (bf16[64,1024]{1,0:T(8,128)(2,1)S(1)}, bf16[64,1024]{1,0:T(8,128)(2,1)S(1)}, u32[]{:S(2)}, u32[]{:S(2)}) collective-permute-start(bf16[64,1024]{1,0:T(8,128)(2,1)S(1)} %head.1), channel_id=1, source_target_pairs={{4,0},{8,4},{12,8},{16,12},{20,16},{24,20},{28,24},{5,1},{9,5},{13... | collective-permute-start | bytes 393224 | tf_op jit(solution)/shard_map/ppermute | solution.py:45
  57.1 1.6 %feed.5 = (f32[256,512]{1,0:T(8,128)S(1)}, bf16[256,512]{1,0:T(8,128)(2,1)S(1)}) custom-call(bf16[512,256]{1,0:T(8,128)(2,1)S(1)} %order.2.refs_2_.refs_0_, bf16[512,256]{1,0:T(8,128)(2,1)S(1)} %collective-permute-done.1.refs_1_, bf16[512,512]{1,0:T(8,128)(2,1)S(1)} %collective-permute-done.2.refs_2_, bf16[1024,1024]{1,0:T(8,128)(2,1)S(1)} %copy-done, ...), custom_call_target="tpu_custom_call" | custom-call | flops 1024 | bytes 1024 | tf_op jit(solution)/shard_map/feed/pallas_call | solution.py:26
  58.7 3.9 %collective-permute-done.4.refs_2_.refs_5_ = bf16[64,1024]{1,0:T(8,128)(2,1)S(1)} collective-permute-done((bf16[64,1024]{1,0:T(8,128)(2,1)S(1)}, bf16[64,1024]{1,0:T(8,128)(2,1)S(1)}, u32[]{:S(2)}, u32[]{:S(2)}) %collective-permute-start.4) | collective-permute-done | bytes 131104 | tf_op jit(solution)/shard_map/ppermute | solution.py:45
  65.4 1.6 %feed.6 = (f32[256,512]{1,0:T(8,128)S(1)}, bf16[256,512]{1,0:T(8,128)(2,1)S(1)}) custom-call(bf16[512,256]{1,0:T(8,128)(2,1)S(1)} %order.3.refs_2_.refs_5_.refs_1_.refs_0_, bf16[512,256]{1,0:T(8,128)(2,1)S(1)} %collective-permute-done.refs_1_, bf16[512,512]{1,0:T(8,128)(2,1)S(1)} %collective-permute-done.5.refs_2_, bf16[1024,1024]{1,0:T(8,128)(2,1)S(1)} %copy-done, ...), custom_call_target="tpu_custom_call" | custom-call | flops 1024 | bytes 1024 | tf_op jit(solution)/shard_map/feed/pallas_call | solution.py:26
  68.8 2.6 %collective-permute-done.6.refs_3_ = bf16[256,512]{1,0:T(8,128)(2,1)S(1)} collective-permute-done((bf16[256,512]{1,0:T(8,128)(2,1)S(1)}, bf16[256,512]{1,0:T(8,128)(2,1)S(1)}, u32[]{:S(2)}, u32[]{:S(2)}) %collective-permute-start.6) | collective-permute-done | bytes 262176 | tf_op jit(solution)/shard_map/ppermute | solution.py:39
  71.4 2.2 %collective-permute-start.9 = (bf16[256,512]{1,0:T(8,128)(2,1)S(1)}, bf16[256,512]{1,0:T(8,128)(2,1)S(1)}, u32[]{:S(2)}, u32[]{:S(2)}) collective-permute-start(bf16[256,512]{1,0:T(8,128)(2,1)S(1)} %finish.4.refs_5_.refs_0_), channel_id=1, source_target_pairs={{0,1},{1,0},{2,3},{3,2},{4,5},{5,4},{6,7},{7,6},{8,9},{9,8},{10,11... | collective-permute-start | bytes 786440 | tf_op jit(solution)/shard_map/ppermute | solution.py:39
  73.6 1.6 %feed.7 = (f32[256,512]{1,0:T(8,128)S(1)}, bf16[256,512]{1,0:T(8,128)(2,1)S(1)}) custom-call(bf16[512,256]{1,0:T(8,128)(2,1)S(1)} %order.3.refs_2_.refs_5_.refs_1_.refs_0_, bf16[512,256]{1,0:T(8,128)(2,1)S(1)} %collective-permute-done.refs_1_, bf16[512,512]{1,0:T(8,128)(2,1)S(1)} %collective-permute-done.5.refs_2_, bf16[1024,1024]{1,0:T(8,128)(2,1)S(1)} %copy-done, ...), custom_call_target="tpu_custom_call" | custom-call | flops 1024 | bytes 1024 | tf_op jit(solution)/shard_map/feed/pallas_call | solution.py:26
  75.4 1.3 %collective-permute-start.14 = (bf16[256,512]{1,0:T(8,128)(2,1)S(1)}, bf16[256,512]{1,0:T(8,128)(2,1)S(1)}, u32[]{:S(2)}, u32[]{:S(2)}) collective-permute-start(bf16[256,512]{1,0:T(8,128)(2,1)S(1)} %get-tuple-element.37.refs_4_), channel_id=1, source_target_pairs={{0,2},{1,3},{2,0},{3,1},{4,6},{5,7},{6,4},{7,5},{8,10},{9,11},{10,... | collective-permute-start | bytes 786440 | tf_op jit(solution)/shard_map/ppermute | solution.py:39
  77.1 1.3 %collective-permute-start.13 = (bf16[256,512]{1,0:T(8,128)(2,1)S(1)}, bf16[256,512]{1,0:T(8,128)(2,1)S(1)}, u32[]{:S(2)}, u32[]{:S(2)}) collective-permute-start(bf16[256,512]{1,0:T(8,128)(2,1)S(1)} %finish.5.refs_6_.refs_0_), channel_id=1, source_target_pairs={{0,1},{1,0},{2,3},{3,2},{4,5},{5,4},{6,7},{7,6},{8,9},{9,8},{10,11... | collective-permute-start | bytes 786440 | tf_op jit(solution)/shard_map/ppermute | solution.py:39
  78.4 1.7 %attend_first.1.refs_2_.refs_8_ = bf16[64,1024]{1,0:T(8,128)(2,1)S(1)} custom-call(bf16[256,512]{1,0:T(8,128)(2,1)S(1)} %finish.4.refs_5_.refs_0_, bf16[256,512]{1,0:T(8,128)(2,1)S(1)} %collective-permute-done.9.refs_1_, bf16[1024,1024]{1,0:T(8,128)(2,1)S(1)} %copy-done.2, bf16[1024,1024]{1,0:T(8,128)(2,1)S(1)} %copy-done.3, ...), custom_call_target="tpu_custom_call" | custom-call | flops 1024 | bytes 1024 | tf_op jit(solution)/shard_map/attend_first/pallas_call | solution.py:26
  80.2 1.3 %collective-permute-start.12 = (bf16[256,512]{1,0:T(8,128)(2,1)S(1)}, bf16[256,512]{1,0:T(8,128)(2,1)S(1)}, u32[]{:S(2)}, u32[]{:S(2)}) collective-permute-start(bf16[256,512]{1,0:T(8,128)(2,1)S(1)} %get-tuple-element.39.refs_4_), channel_id=1, source_target_pairs={{0,2},{1,3},{2,0},{3,1},{4,6},{5,7},{6,4},{7,5},{8,10},{9,11},{10,... | collective-permute-start | bytes 786440 | tf_op jit(solution)/shard_map/ppermute | solution.py:39
  81.5 4.1 %collective-permute-start.15 = (bf16[64,1024]{1,0:T(8,128)(2,1)S(1)}, bf16[64,1024]{1,0:T(8,128)(2,1)S(1)}, u32[]{:S(2)}, u32[]{:S(2)}) collective-permute-start(bf16[64,1024]{1,0:T(8,128)(2,1)S(1)} %attend_first.1.refs_2_.refs_8_), channel_id=1, source_target_pairs={{0,4},{4,8},{8,12},{12,16},{16,20},{20,24},{24,28},{1,5},{5,9},{9,... | collective-permute-start | bytes 393224 | tf_op jit(solution)/shard_map/ppermute | solution.py:45
  86.5 1.7 %attend.2.refs_4_.refs_6_ = bf16[64,1024]{1,0:T(8,128)(2,1)S(1)} custom-call(bf16[256,512]{1,0:T(8,128)(2,1)S(1)} %finish.5.refs_6_.refs_0_, bf16[256,512]{1,0:T(8,128)(2,1)S(1)} %collective-permute-done.13.refs_1_, bf16[1024,1024]{1,0:T(8,128)(2,1)S(1)} %copy-done.2, bf16[1024,1024]{1,0:T(8,128)(2,1)S(1)} %copy-done.3, ...), custom_call_target="tpu_custom_call" | custom-call | flops 1024 | bytes 1024 | tf_op jit(solution)/shard_map/attend/pallas_call | solution.py:26
  88.7 1.3 %collective-permute-start.16 = (bf16[256,512]{1,0:T(8,128)(2,1)S(1)}, bf16[256,512]{1,0:T(8,128)(2,1)S(1)}, u32[]{:S(2)}, u32[]{:S(2)}) collective-permute-start(bf16[256,512]{1,0:T(8,128)(2,1)S(1)} %finish.7.refs_5_.refs_0_), channel_id=1, source_target_pairs={{0,1},{1,0},{2,3},{3,2},{4,5},{5,4},{6,7},{7,6},{8,9},{9,8},{10,11... | collective-permute-start | bytes 786440 | tf_op jit(solution)/shard_map/ppermute | solution.py:39
  90.0 1.7 %attend.3.refs_7_ = bf16[64,1024]{1,0:T(8,128)(2,1)S(1)} custom-call(bf16[256,512]{1,0:T(8,128)(2,1)S(1)} %finish.6.refs_5_.refs_0_, bf16[256,512]{1,0:T(8,128)(2,1)S(1)} %collective-permute-done.17.refs_1_, bf16[1024,1024]{1,0:T(8,128)(2,1)S(1)} %copy-done.2, bf16[1024,1024]{1,0:T(8,128)(2,1)S(1)} %copy-done.3, ...), custom_call_target="tpu_custom_call" | custom-call | flops 1024 | bytes 1024 | tf_op jit(solution)/shard_map/attend/pallas_call | solution.py:26
  91.7 2.6 %attend_last.1 = bf16[256,1024]{1,0:T(8,128)(2,1)} custom-call(bf16[256,512]{1,0:T(8,128)(2,1)S(1)} %finish.7.refs_5_.refs_0_, bf16[256,512]{1,0:T(8,128)(2,1)S(1)} %collective-permute-done.16.refs_1_, bf16[1024,1024]{1,0:T(8,128)(2,1)S(1)} %copy-done.2, bf16[1024,1024]{1,0:T(8,128)(2,1)S(1)} %copy-done.3, bf16[64,1024]{1,0:T(8,128)(2,1)S(1)} %get-tuple-element.43.refs_4_, ...), custom_call_target="tpu_custom_call" | custom-call | flops 1024 | bytes 1024 | tf_op jit(solution)/shard_map/attend_last/pallas_call | solution.py:26
  (54 shorter events, 10.3 us)
Async XLA Ops:
  0.7 12.4 %copy-start.5 = (bf16[2048,256]{1,0:T(8,128)(2,1)S(1)}, bf16[2048,256]{1,0:T(8,128)(2,1)}, u32[]{:S(2)}) copy-start(bf16[2048,256]{1,0:T(8,128)(2,1)} %refs_1_.1) | copy-start | bytes 3145732
  42.6 11.2 %copy-start.1 = (bf16[1024,1024]{1,0:T(8,128)(2,1)S(1)}, bf16[1024,1024]{1,0:T(8,128)(2,1)}, u32[]{:S(2)}) copy-start(bf16[1024,1024]{1,0:T(8,128)(2,1)} %refs_4_.8) | copy-start | bytes 6291460
  43.3 10.5 %copy-start = (bf16[1024,1024]{1,0:T(8,128)(2,1)S(1)}, bf16[1024,1024]{1,0:T(8,128)(2,1)}, u32[]{:S(2)}) copy-start(bf16[1024,1024]{1,0:T(8,128)(2,1)} %refs_3_.11) | copy-start | bytes 6291460
  43.3 5.8 %collective-permute-start.1 = (bf16[512,256]{1,0:T(8,128)(2,1)S(1)}, bf16[512,256]{1,0:T(8,128)(2,1)S(1)}, u32[]{:S(2)}, u32[]{:S(2)}) collective-permute-start(bf16[512,256]{1,0:T(8,128)(2,1)S(1)} %order.2.refs_2_.refs_0_), channel_id=1, source_target_pairs={{0,2},{1,3},{2,0},{3,1},{4,6},{5,7},{6,4},{7,5},{8,10},{9,11},{10,... | collective-permute-start | bytes 786440 | tf_op jit(solution)/shard_map/ppermute | solution.py:39
  49.2 6.6 %copy-start.4 = (bf16[256,1024]{1,0:T(8,128)(2,1)S(1)}, bf16[256,1024]{1,0:T(8,128)(2,1)}, u32[]{:S(2)}) copy-start(bf16[256,1024]{1,0:T(8,128)(2,1)} %refs_4_.9) | copy-start | bytes 1572868
  49.2 4.5 %collective-permute-start.2 = (bf16[512,512]{1,0:T(8,128)(2,1)S(1)}, bf16[512,512]{1,0:T(8,128)(2,1)S(1)}, u32[]{:S(2)}, u32[]{:S(2)}) collective-permute-start(bf16[512,512]{1,0:T(8,128)(2,1)S(1)} %pair.2), channel_id=1, source_target_pairs={{0,1},{1,0},{2,3},{3,2},{4,5},{5,4},{6,7},{7,6},{8,9},{9,8},{10,11... | collective-permute-start | bytes 1572872 | tf_op jit(solution)/shard_map/ppermute | solution.py:39
  52.2 10.5 %collective-permute-start = (bf16[512,256]{1,0:T(8,128)(2,1)S(1)}, bf16[512,256]{1,0:T(8,128)(2,1)S(1)}, u32[]{:S(2)}, u32[]{:S(2)}) collective-permute-start(bf16[512,256]{1,0:T(8,128)(2,1)S(1)} %order.3.refs_2_.refs_5_.refs_1_.refs_0_), channel_id=1, source_target_pairs={{0,2},{1,3},{2,0},{3,1},{4,6},{5,7},{6,4},{7,5},{8,10},{9,11},{10,... | collective-permute-start | bytes 786440 | tf_op jit(solution)/shard_map/ppermute | solution.py:39
  55.4 7.3 %collective-permute-start.3 = (bf16[256,512]{1,0:T(8,128)(2,1)S(1)}, bf16[256,512]{1,0:T(8,128)(2,1)S(1)}, u32[]{:S(2)}, u32[]{:S(2)}) collective-permute-start(bf16[256,512]{1,0:T(8,128)(2,1)S(1)} %get-tuple-element.26.refs_5_), channel_id=1, source_target_pairs={{0,1},{1,0},{2,3},{3,2},{4,5},{5,4},{6,7},{7,6},{8,9},{9,8},{10,11... | collective-permute-start | bytes 786440 | tf_op jit(solution)/shard_map/ppermute | solution.py:39
  55.8 6.9 %collective-permute-start.4 = (bf16[64,1024]{1,0:T(8,128)(2,1)S(1)}, bf16[64,1024]{1,0:T(8,128)(2,1)S(1)}, u32[]{:S(2)}, u32[]{:S(2)}) collective-permute-start(bf16[64,1024]{1,0:T(8,128)(2,1)S(1)} %head.1), channel_id=1, source_target_pairs={{4,0},{8,4},{12,8},{16,12},{20,16},{24,20},{28,24},{5,1},{9,5},{13... | collective-permute-start | bytes 393224 | tf_op jit(solution)/shard_map/ppermute | solution.py:45
  62.8 2.6 %collective-permute-start.5 = (bf16[512,512]{1,0:T(8,128)(2,1)S(1)}, bf16[512,512]{1,0:T(8,128)(2,1)S(1)}, u32[]{:S(2)}, u32[]{:S(2)}) collective-permute-start(bf16[512,512]{1,0:T(8,128)(2,1)S(1)} %pair.3.refs_5_), channel_id=1, source_target_pairs={{0,1},{1,0},{2,3},{3,2},{4,5},{5,4},{6,7},{7,6},{8,9},{9,8},{10,11... | collective-permute-start | bytes 1572872 | tf_op jit(solution)/shard_map/ppermute | solution.py:39
  63.8 3.7 %collective-permute-start.7 = (bf16[256,512]{1,0:T(8,128)(2,1)S(1)}, bf16[256,512]{1,0:T(8,128)(2,1)S(1)}, u32[]{:S(2)}, u32[]{:S(2)}) collective-permute-start(bf16[256,512]{1,0:T(8,128)(2,1)S(1)} %get-tuple-element.27.refs_0_), channel_id=1, source_target_pairs={{0,1},{1,0},{2,3},{3,2},{4,5},{5,4},{6,7},{7,6},{8,9},{9,8},{10,11... | collective-permute-start | bytes 786440 | tf_op jit(solution)/shard_map/ppermute | solution.py:39
  63.9 7.4 %collective-permute-start.6 = (bf16[256,512]{1,0:T(8,128)(2,1)S(1)}, bf16[256,512]{1,0:T(8,128)(2,1)S(1)}, u32[]{:S(2)}, u32[]{:S(2)}) collective-permute-start(bf16[256,512]{1,0:T(8,128)(2,1)S(1)} %get-tuple-element.28.refs_2_), channel_id=1, source_target_pairs={{0,2},{1,3},{2,0},{3,1},{4,6},{5,7},{6,4},{7,5},{8,10},{9,11},{10,... | collective-permute-start | bytes 786440 | tf_op jit(solution)/shard_map/ppermute | solution.py:39
  67.0 8.4 %collective-permute-start.11 = (bf16[256,512]{1,0:T(8,128)(2,1)S(1)}, bf16[256,512]{1,0:T(8,128)(2,1)S(1)}, u32[]{:S(2)}, u32[]{:S(2)}) collective-permute-start(bf16[256,512]{1,0:T(8,128)(2,1)S(1)} %get-tuple-element.31.refs_2_), channel_id=1, source_target_pairs={{0,1},{1,0},{2,3},{3,2},{4,5},{5,4},{6,7},{7,6},{8,9},{9,8},{10,11... | collective-permute-start | bytes 786440 | tf_op jit(solution)/shard_map/ppermute | solution.py:39
  67.6 9.4 %collective-permute-start.10 = (bf16[256,512]{1,0:T(8,128)(2,1)S(1)}, bf16[256,512]{1,0:T(8,128)(2,1)S(1)}, u32[]{:S(2)}, u32[]{:S(2)}) collective-permute-start(bf16[256,512]{1,0:T(8,128)(2,1)S(1)} %get-tuple-element.32.refs_4_), channel_id=1, source_target_pairs={{0,2},{1,3},{2,0},{3,1},{4,6},{5,7},{6,4},{7,5},{8,10},{9,11},{10,... | collective-permute-start | bytes 786440 | tf_op jit(solution)/shard_map/ppermute | solution.py:39
  71.4 7.0 %collective-permute-start.9 = (bf16[256,512]{1,0:T(8,128)(2,1)S(1)}, bf16[256,512]{1,0:T(8,128)(2,1)S(1)}, u32[]{:S(2)}, u32[]{:S(2)}) collective-permute-start(bf16[256,512]{1,0:T(8,128)(2,1)S(1)} %finish.4.refs_5_.refs_0_), channel_id=1, source_target_pairs={{0,1},{1,0},{2,3},{3,2},{4,5},{5,4},{6,7},{7,6},{8,9},{9,8},{10,11... | collective-permute-start | bytes 786440 | tf_op jit(solution)/shard_map/ppermute | solution.py:39
  73.6 4.8 %copy-start.3 = (bf16[1024,1024]{1,0:T(8,128)(2,1)S(1)}, bf16[1024,1024]{1,0:T(8,128)(2,1)}, u32[]{:S(2)}) copy-start(bf16[1024,1024]{1,0:T(8,128)(2,1)} %refs_3_.15) | copy-start | bytes 6291460
  75.3 3.1 %copy-start.2 = (bf16[1024,1024]{1,0:T(8,128)(2,1)S(1)}, bf16[1024,1024]{1,0:T(8,128)(2,1)}, u32[]{:S(2)}) copy-start(bf16[1024,1024]{1,0:T(8,128)(2,1)} %refs_2_.7) | copy-start | bytes 6291460
  75.3 4.8 %collective-permute-start.8 = (bf16[256,512]{1,0:T(8,128)(2,1)S(1)}, bf16[256,512]{1,0:T(8,128)(2,1)S(1)}, u32[]{:S(2)}, u32[]{:S(2)}) collective-permute-start(bf16[256,512]{1,0:T(8,128)(2,1)S(1)} %get-tuple-element.34.refs_2_), channel_id=1, source_target_pairs={{0,1},{1,0},{2,3},{3,2},{4,5},{5,4},{6,7},{7,6},{8,9},{9,8},{10,11... | collective-permute-start | bytes 786440 | tf_op jit(solution)/shard_map/ppermute | solution.py:39
  75.4 10.3 %collective-permute-start.14 = (bf16[256,512]{1,0:T(8,128)(2,1)S(1)}, bf16[256,512]{1,0:T(8,128)(2,1)S(1)}, u32[]{:S(2)}, u32[]{:S(2)}) collective-permute-start(bf16[256,512]{1,0:T(8,128)(2,1)S(1)} %get-tuple-element.37.refs_4_), channel_id=1, source_target_pairs={{0,2},{1,3},{2,0},{3,1},{4,6},{5,7},{6,4},{7,5},{8,10},{9,11},{10,... | collective-permute-start | bytes 786440 | tf_op jit(solution)/shard_map/ppermute | solution.py:39
  77.1 9.4 %collective-permute-start.13 = (bf16[256,512]{1,0:T(8,128)(2,1)S(1)}, bf16[256,512]{1,0:T(8,128)(2,1)S(1)}, u32[]{:S(2)}, u32[]{:S(2)}) collective-permute-start(bf16[256,512]{1,0:T(8,128)(2,1)S(1)} %finish.5.refs_6_.refs_0_), channel_id=1, source_target_pairs={{0,1},{1,0},{2,3},{3,2},{4,5},{5,4},{6,7},{7,6},{8,9},{9,8},{10,11... | collective-permute-start | bytes 786440 | tf_op jit(solution)/shard_map/ppermute | solution.py:39
  80.2 8.5 %collective-permute-start.12 = (bf16[256,512]{1,0:T(8,128)(2,1)S(1)}, bf16[256,512]{1,0:T(8,128)(2,1)S(1)}, u32[]{:S(2)}, u32[]{:S(2)}) collective-permute-start(bf16[256,512]{1,0:T(8,128)(2,1)S(1)} %get-tuple-element.39.refs_4_), channel_id=1, source_target_pairs={{0,2},{1,3},{2,0},{3,1},{4,6},{5,7},{6,4},{7,5},{8,10},{9,11},{10,... | collective-permute-start | bytes 786440 | tf_op jit(solution)/shard_map/ppermute | solution.py:39
  81.5 6.7 %collective-permute-start.15 = (bf16[64,1024]{1,0:T(8,128)(2,1)S(1)}, bf16[64,1024]{1,0:T(8,128)(2,1)S(1)}, u32[]{:S(2)}, u32[]{:S(2)}) collective-permute-start(bf16[64,1024]{1,0:T(8,128)(2,1)S(1)} %attend_first.1.refs_2_.refs_8_), channel_id=1, source_target_pairs={{0,4},{4,8},{8,12},{12,16},{16,20},{20,24},{24,28},{1,5},{5,9},{9,... | collective-permute-start | bytes 393224 | tf_op jit(solution)/shard_map/ppermute | solution.py:45
  85.8 4.2 %collective-permute-start.17 = (bf16[256,512]{1,0:T(8,128)(2,1)S(1)}, bf16[256,512]{1,0:T(8,128)(2,1)S(1)}, u32[]{:S(2)}, u32[]{:S(2)}) collective-permute-start(bf16[256,512]{1,0:T(8,128)(2,1)S(1)} %finish.6.refs_5_.refs_0_), channel_id=1, source_target_pairs={{0,1},{1,0},{2,3},{3,2},{4,5},{5,4},{6,7},{7,6},{8,9},{9,8},{10,11... | collective-permute-start | bytes 786440 | tf_op jit(solution)/shard_map/ppermute | solution.py:39
  88.7 2.9 %collective-permute-start.16 = (bf16[256,512]{1,0:T(8,128)(2,1)S(1)}, bf16[256,512]{1,0:T(8,128)(2,1)S(1)}, u32[]{:S(2)}, u32[]{:S(2)}) collective-permute-start(bf16[256,512]{1,0:T(8,128)(2,1)S(1)} %finish.7.refs_5_.refs_0_), channel_id=1, source_target_pairs={{0,1},{1,0},{2,3},{3,2},{4,5},{5,4},{6,7},{7,6},{8,9},{9,8},{10,11... | collective-permute-start | bytes 786440 | tf_op jit(solution)/shard_map/ppermute | solution.py:39
  (1 other events, 0.7 us)

commit v11 on v10

--- a/solution.py
+++ b/solution.py
@@ -297,23 +297,26 @@
         return both
 
     across(pieces[0], (token,))
-    head = call(head_body, sds((GROUP, head_cols), BF16), "head", (queries,), (token,))
-    next_q = shifted(head, -1)
     half = sds((per_group, 2 * width), BF16)
     whole = sds((per_group, 2 * width), F32)
     fed, summed, far, encoded = {}, {}, {}, {}
-    behind = out = None
+    behind = out = next_q = None
 
     def emb(g):
         return pieces[0 if g in plan[0] else 1]
 
     def rest(_):
         nonlocal token
-        token = across(pieces[1], (token,))
+        token = across(pieces[1], (token, fed[order[1]][1]))
 
     def pause(_):
         nonlocal token
-        token = call(mark_body, sds((8, LANES), F32), "mark", (), (token, pieces[1][1], next_q))
+        token = call(mark_body, sds((8, LANES), F32), "mark", (), (token, pieces[1][1]))
+
+    def ask(_):
+        nonlocal next_q
+        head = call(head_body, sds((GROUP, head_cols), BF16), "head", (queries,), (token,))
+        next_q = shifted(head, -1)
 
     def feed(g):
         nonlocal token
@@ -338,7 +341,7 @@
             half,
             "finish",
             (*emb(g)[:2], summed[g], far[g]),
-            (token, behind) if g == order[-1] else (token,),
+            (token, *{order[0]: (next_q,), order[-1]: (behind,)}.get(g, ())),
         )
         encoded[g] = token, exchange(token, 1)
 
@@ -377,7 +380,7 @@
 
     a, b, c, d = order
     for step, g in (
-        (feed, a), (feed, b), (pause, c), (add, a), (rest, c), (feed, c), (add, b),
+        (feed, a), (feed, b), (pause, c), (add, a), (ask, a), (rest, c), (feed, c), (add, b),
         (finish, a), (feed, d), (add, c),
         (finish, b), (attend, a), (add, d),
         (finish, c), (attend, b),

time: 94.5 us -> 91.7 us (0.970)
  starting transfers between devices: 23.7 us -> 20.1 us
    ppermute x16, starting transfers between devices: 18.3 us -> 15.6 us  [exchange(): return lax.ppermute(x, 'tp', [(i, i ^ bit) for i in range(size)])]
    ppermute x16, waiting for transfers between devices: 7.58 us -> 9.03 us  [exchange(): return lax.ppermute(x, 'tp', [(i, i ^ bit) for i in range(size)])]
    ppermute x2, waiting for transfers between devices: 3.95 us -> 2.93 us  [shifted(): return lax.ppermute(x, 'seq', pairs)]
  transfers between devices with their start and end apart: 18 -> 18, of which waited for: 7 -> 6; matrix products, arithmetic and copies ran while one was open for 0% -> 0% of each run, Pallas kernels for 14% -> 14%
where the time goes in v11:
time: 91.7 us; the launch traced here: 91.1 us
  blocking collectives  38.6 us (42%)
  starting transfers between devices  20.1 us (22%)
  Pallas kernels  19.3 us (21%)
  waiting for transfers between devices  12 us (13%)
    all_to_all x1, blocking collectives, per_device(): lax.all_to_all(found.reshape(seq_size, cap, width), 'seq', split_axis=0,...  27.1 us
    pallas_call x24, Pallas kernels, call(): pl.pallas_call(without_after, out_shape=outs, in_specs=in_specs + [unread...  19.3 us
    ppermute x16, starting transfers between devices, exchange(): return lax.ppermute(x, 'tp', [(i, i ^ bit) for i in range(size)])  15.6 us
    all_to_all x1, blocking collectives, per_device(): lax.all_to_all(wanted, 'seq', split_axis=0, concat_axis=0, tiled=True)  11.5 us
    ppermute x16, waiting for transfers between devices, exchange(): return lax.ppermute(x, 'tp', [(i, i ^ bit) for i in range(size)])  9.03 us
    ppermute x2, starting transfers between devices, shifted(): return lax.ppermute(x, 'seq', pairs)  4.5 us
    ppermute x2, waiting for transfers between devices, shifted(): return lax.ppermute(x, 'seq', pairs)  2.93 us
  transfers between devices with their start and end apart: 18, of which 6 were waited for; matrix products, arithmetic and copies ran while one was open for 0% of the time, Pallas kernels for 14%

profile of v11, /device:TPU:1, one launch (start us, length us, event | category | flops | bytes accessed | tf_op | source)
XLA Modules:
  0.0 91.1 jit_solution(13123855620456454298)
XLA Ops:
  1.5 11.5 %all_to_all.14 = s32[8,1,256]{2,1,0:T(1,128)S(1)} all-to-all(s32[8,1,256]{2,1,0:T(1,128)S(1)} %copy.8), channel_id=1, replica_groups=mesh['seq'=8,'tp'=4] {'seq'}, dimensions={0} | all-to-all | bytes 16384 | tf_op jit(solution)/shard_map/all_to_all | solution.py:266
  13.1 2.4 %fetch.1 = bf16[2048,256]{1,0:T(8,128)(2,1)S(1)} custom-call(s32[1,2048]{1,0:T(1,128)S(1)} %bitcast.8, bf16[2048,256]{1,0:T(8,128)(2,1)S(1)} %copy-done.5), custom_call_target="tpu_custom_call" | custom-call | flops 1024 | bytes 1024 | tf_op jit(solution)/shard_map/fetch/pallas_call | solution.py:26
  15.5 27.1 %all_to_all.15 = bf16[8,256,256]{2,1,0:T(8,128)(2,1)S(1)} all-to-all(bf16[8,256,256]{2,1,0:T(8,128)(2,1)S(1)} %bitcast.7), channel_id=1, replica_groups=mesh['seq'=8,'tp'=4] {'seq'}, dimensions={0} | all-to-all | bytes 2097152 | tf_op jit(solution)/shard_map/all_to_all | solution.py:273
  43.3 1.3 %collective-permute-start.1 = (bf16[512,256]{1,0:T(8,128)(2,1)S(1)}, bf16[512,256]{1,0:T(8,128)(2,1)S(1)}, u32[]{:S(2)}, u32[]{:S(2)}) collective-permute-start(bf16[512,256]{1,0:T(8,128)(2,1)S(1)} %order.2.refs_2_.refs_0_), channel_id=1, source_target_pairs={{0,2},{1,3},{2,0},{3,1},{4,6},{5,7},{6,4},{7,5},{8,10},{9,11},{10,... | collective-permute-start | bytes 786440 | tf_op jit(solution)/shard_map/ppermute | solution.py:39
  45.3 3.8 %collective-permute-done.1.refs_1_ = bf16[512,256]{1,0:T(8,128)(2,1)S(1)} collective-permute-done((bf16[512,256]{1,0:T(8,128)(2,1)S(1)}, bf16[512,256]{1,0:T(8,128)(2,1)S(1)}, u32[]{:S(2)}, u32[]{:S(2)}) %collective-permute-start.1) | collective-permute-done | bytes 262176 | tf_op jit(solution)/shard_map/ppermute | solution.py:39
  49.2 3.0 %collective-permute-start.2 = (bf16[512,512]{1,0:T(8,128)(2,1)S(1)}, bf16[512,512]{1,0:T(8,128)(2,1)S(1)}, u32[]{:S(2)}, u32[]{:S(2)}) collective-permute-start(bf16[512,512]{1,0:T(8,128)(2,1)S(1)} %pair.2), channel_id=1, source_target_pairs={{0,1},{1,0},{2,3},{3,2},{4,5},{5,4},{6,7},{7,6},{8,9},{9,8},{10,11... | collective-permute-start | bytes 1572872 | tf_op jit(solution)/shard_map/ppermute | solution.py:39
  52.2 1.3 %collective-permute-start = (bf16[512,256]{1,0:T(8,128)(2,1)S(1)}, bf16[512,256]{1,0:T(8,128)(2,1)S(1)}, u32[]{:S(2)}, u32[]{:S(2)}) collective-permute-start(bf16[512,256]{1,0:T(8,128)(2,1)S(1)} %order.3.refs_2_.refs_5_.refs_0_), channel_id=1, source_target_pairs={{0,2},{1,3},{2,0},{3,1},{4,6},{5,7},{6,4},{7,5},{8,10},{9,11},{10,... | collective-permute-start | bytes 786440 | tf_op jit(solution)/shard_map/ppermute | solution.py:39
  53.7 1.6 %feed.4 = (f32[256,512]{1,0:T(8,128)S(1)}, bf16[256,512]{1,0:T(8,128)(2,1)S(1)}) custom-call(bf16[512,256]{1,0:T(8,128)(2,1)S(1)} %order.2.refs_2_.refs_0_, bf16[512,256]{1,0:T(8,128)(2,1)S(1)} %collective-permute-done.1.refs_1_, bf16[512,512]{1,0:T(8,128)(2,1)S(1)} %collective-permute-done.2.refs_2_, bf16[1024,1024]{1,0:T(8,128)(2,1)S(1)} %copy-done, ...), custom_call_target="tpu_custom_call" | custom-call | flops 1024 | bytes 1024 | tf_op jit(solution)/shard_map/feed/pallas_call | solution.py:26
  55.8 1.6 %feed.5 = (f32[256,512]{1,0:T(8,128)S(1)}, bf16[256,512]{1,0:T(8,128)(2,1)S(1)}) custom-call(bf16[512,256]{1,0:T(8,128)(2,1)S(1)} %order.2.refs_2_.refs_0_, bf16[512,256]{1,0:T(8,128)(2,1)S(1)} %collective-permute-done.1.refs_1_, bf16[512,512]{1,0:T(8,128)(2,1)S(1)} %collective-permute-done.2.refs_2_, bf16[1024,1024]{1,0:T(8,128)(2,1)S(1)} %copy-done, ...), custom_call_target="tpu_custom_call" | custom-call | flops 1024 | bytes 1024 | tf_op jit(solution)/shard_map/feed/pallas_call | solution.py:26
  57.6 2.5 %collective-permute-done.refs_1_ = bf16[512,256]{1,0:T(8,128)(2,1)S(1)} collective-permute-done((bf16[512,256]{1,0:T(8,128)(2,1)S(1)}, bf16[512,256]{1,0:T(8,128)(2,1)S(1)}, u32[]{:S(2)}, u32[]{:S(2)}) %collective-permute-start) | collective-permute-done | bytes 262176 | tf_op jit(solution)/shard_map/ppermute | solution.py:39
  61.1 1.3 %collective-permute-start.6 = (bf16[256,512]{1,0:T(8,128)(2,1)S(1)}, bf16[256,512]{1,0:T(8,128)(2,1)S(1)}, u32[]{:S(2)}, u32[]{:S(2)}) collective-permute-start(bf16[256,512]{1,0:T(8,128)(2,1)S(1)} %get-tuple-element.28.refs_2_.refs_1_), channel_id=1, source_target_pairs={{0,2},{1,3},{2,0},{3,1},{4,6},{5,7},{6,4},{7,5},{8,10},{9,11},{10,... | collective-permute-start | bytes 786440 | tf_op jit(solution)/shard_map/ppermute | solution.py:39
  62.4 1.3 %collective-permute-start.7 = (bf16[64,1024]{1,0:T(8,128)(2,1)S(1)}, bf16[64,1024]{1,0:T(8,128)(2,1)S(1)}, u32[]{:S(2)}, u32[]{:S(2)}) collective-permute-start(bf16[64,1024]{1,0:T(8,128)(2,1)S(1)} %head.1), channel_id=1, source_target_pairs={{4,0},{8,4},{12,8},{16,12},{20,16},{24,20},{28,24},{5,1},{9,5},{13... | collective-permute-start | bytes 393224 | tf_op jit(solution)/shard_map/ppermute | solution.py:45
  63.7 1.6 %feed.6 = (f32[256,512]{1,0:T(8,128)S(1)}, bf16[256,512]{1,0:T(8,128)(2,1)S(1)}) custom-call(bf16[512,256]{1,0:T(8,128)(2,1)S(1)} %order.3.refs_2_.refs_5_.refs_0_, bf16[512,256]{1,0:T(8,128)(2,1)S(1)} %collective-permute-done.refs_1_, bf16[512,512]{1,0:T(8,128)(2,1)S(1)} %collective-permute-done.5.refs_2_, bf16[1024,1024]{1,0:T(8,128)(2,1)S(1)} %copy-done, ...), custom_call_target="tpu_custom_call" | custom-call | flops 1024 | bytes 1024 | tf_op jit(solution)/shard_map/feed/pallas_call | solution.py:26
  66.1 2.9 %collective-permute-done.7.refs_5_ = bf16[64,1024]{1,0:T(8,128)(2,1)S(1)} collective-permute-done((bf16[64,1024]{1,0:T(8,128)(2,1)S(1)}, bf16[64,1024]{1,0:T(8,128)(2,1)S(1)}, u32[]{:S(2)}, u32[]{:S(2)}) %collective-permute-start.7) | collective-permute-done | bytes 131104 | tf_op jit(solution)/shard_map/ppermute | solution.py:45
  69.1 1.3 %collective-permute-start.9 = (bf16[256,512]{1,0:T(8,128)(2,1)S(1)}, bf16[256,512]{1,0:T(8,128)(2,1)S(1)}, u32[]{:S(2)}, u32[]{:S(2)}) collective-permute-start(bf16[256,512]{1,0:T(8,128)(2,1)S(1)} %finish.4.refs_5_.refs_0_), channel_id=1, source_target_pairs={{0,1},{1,0},{2,3},{3,2},{4,5},{5,4},{6,7},{7,6},{8,9},{9,8},{10,11... | collective-permute-start | bytes 786440 | tf_op jit(solution)/shard_map/ppermute | solution.py:39
  70.5 1.6 %feed.7 = (f32[256,512]{1,0:T(8,128)S(1)}, bf16[256,512]{1,0:T(8,128)(2,1)S(1)}) custom-call(bf16[512,256]{1,0:T(8,128)(2,1)S(1)} %order.3.refs_2_.refs_5_.refs_0_, bf16[512,256]{1,0:T(8,128)(2,1)S(1)} %collective-permute-done.refs_1_, bf16[512,512]{1,0:T(8,128)(2,1)S(1)} %collective-permute-done.5.refs_2_, bf16[1024,1024]{1,0:T(8,128)(2,1)S(1)} %copy-done, ...), custom_call_target="tpu_custom_call" | custom-call | flops 1024 | bytes 1024 | tf_op jit(solution)/shard_map/feed/pallas_call | solution.py:26
  72.3 1.3 %collective-permute-start.14 = (bf16[256,512]{1,0:T(8,128)(2,1)S(1)}, bf16[256,512]{1,0:T(8,128)(2,1)S(1)}, u32[]{:S(2)}, u32[]{:S(2)}) collective-permute-start(bf16[256,512]{1,0:T(8,128)(2,1)S(1)} %get-tuple-element.37.refs_4_), channel_id=1, source_target_pairs={{0,2},{1,3},{2,0},{3,1},{4,6},{5,7},{6,4},{7,5},{8,10},{9,11},{10,... | collective-permute-start | bytes 786440 | tf_op jit(solution)/shard_map/ppermute | solution.py:39
  75.7 1.7 %attend_first.1.refs_2_.refs_8_ = bf16[64,1024]{1,0:T(8,128)(2,1)S(1)} custom-call(bf16[256,512]{1,0:T(8,128)(2,1)S(1)} %finish.4.refs_5_.refs_0_, bf16[256,512]{1,0:T(8,128)(2,1)S(1)} %collective-permute-done.9.refs_1_, bf16[1024,1024]{1,0:T(8,128)(2,1)S(1)} %copy-done.2, bf16[1024,1024]{1,0:T(8,128)(2,1)S(1)} %copy-done.3, ...), custom_call_target="tpu_custom_call" | custom-call | flops 1024 | bytes 1024 | tf_op jit(solution)/shard_map/attend_first/pallas_call | solution.py:26
  77.5 1.3 %collective-permute-start.12 = (bf16[256,512]{1,0:T(8,128)(2,1)S(1)}, bf16[256,512]{1,0:T(8,128)(2,1)S(1)}, u32[]{:S(2)}, u32[]{:S(2)}) collective-permute-start(bf16[256,512]{1,0:T(8,128)(2,1)S(1)} %get-tuple-element.39.refs_4_), channel_id=1, source_target_pairs={{0,2},{1,3},{2,0},{3,1},{4,6},{5,7},{6,4},{7,5},{8,10},{9,11},{10,... | collective-permute-start | bytes 786440 | tf_op jit(solution)/shard_map/ppermute | solution.py:39
  78.8 3.2 %collective-permute-start.15 = (bf16[64,1024]{1,0:T(8,128)(2,1)S(1)}, bf16[64,1024]{1,0:T(8,128)(2,1)S(1)}, u32[]{:S(2)}, u32[]{:S(2)}) collective-permute-start(bf16[64,1024]{1,0:T(8,128)(2,1)S(1)} %attend_first.1.refs_2_.refs_8_), channel_id=1, source_target_pairs={{0,4},{4,8},{8,12},{12,16},{16,20},{20,24},{24,28},{1,5},{5,9},{9,... | collective-permute-start | bytes 393224 | tf_op jit(solution)/shard_map/ppermute | solution.py:45
  82.8 1.7 %attend.2.refs_4_.refs_6_ = bf16[64,1024]{1,0:T(8,128)(2,1)S(1)} custom-call(bf16[256,512]{1,0:T(8,128)(2,1)S(1)} %finish.5.refs_6_.refs_0_, bf16[256,512]{1,0:T(8,128)(2,1)S(1)} %collective-permute-done.13.refs_1_, bf16[1024,1024]{1,0:T(8,128)(2,1)S(1)} %copy-done.2, bf16[1024,1024]{1,0:T(8,128)(2,1)S(1)} %copy-done.3, ...), custom_call_target="tpu_custom_call" | custom-call | flops 1024 | bytes 1024 | tf_op jit(solution)/shard_map/attend/pallas_call | solution.py:26
  84.5 1.4 %collective-permute-done.12.refs_3_ = bf16[256,512]{1,0:T(8,128)(2,1)S(1)} collective-permute-done((bf16[256,512]{1,0:T(8,128)(2,1)S(1)}, bf16[256,512]{1,0:T(8,128)(2,1)S(1)}, u32[]{:S(2)}, u32[]{:S(2)}) %collective-permute-start.12) | collective-permute-done | bytes 262176 | tf_op jit(solution)/shard_map/ppermute | solution.py:39
  86.9 1.7 %attend.3.refs_7_ = bf16[64,1024]{1,0:T(8,128)(2,1)S(1)} custom-call(bf16[256,512]{1,0:T(8,128)(2,1)S(1)} %finish.6.refs_5_.refs_0_, bf16[256,512]{1,0:T(8,128)(2,1)S(1)} %collective-permute-done.17.refs_1_, bf16[1024,1024]{1,0:T(8,128)(2,1)S(1)} %copy-done.2, bf16[1024,1024]{1,0:T(8,128)(2,1)S(1)} %copy-done.3, ...), custom_call_target="tpu_custom_call" | custom-call | flops 1024 | bytes 1024 | tf_op jit(solution)/shard_map/attend/pallas_call | solution.py:26
  88.6 2.5 %attend_last.1 = bf16[256,1024]{1,0:T(8,128)(2,1)} custom-call(bf16[256,512]{1,0:T(8,128)(2,1)S(1)} %finish.7.refs_5_.refs_0_, bf16[256,512]{1,0:T(8,128)(2,1)S(1)} %collective-permute-done.16.refs_1_, bf16[1024,1024]{1,0:T(8,128)(2,1)S(1)} %copy-done.2, bf16[1024,1024]{1,0:T(8,128)(2,1)S(1)} %copy-done.3, bf16[64,1024]{1,0:T(8,128)(2,1)S(1)} %get-tuple-element.43.refs_4_, ...), custom_call_target="tpu_custom_call" | custom-call | flops 1024 | bytes 1024 | tf_op jit(solution)/shard_map/attend_last/pallas_call | solution.py:26
  (54 shorter events, 10.0 us)
Async XLA Ops:
  0.7 12.4 %copy-start.5 = (bf16[2048,256]{1,0:T(8,128)(2,1)S(1)}, bf16[2048,256]{1,0:T(8,128)(2,1)}, u32[]{:S(2)}) copy-start(bf16[2048,256]{1,0:T(8,128)(2,1)} %refs_1_.1) | copy-start | bytes 3145732
  42.6 11.2 %copy-start.1 = (bf16[1024,1024]{1,0:T(8,128)(2,1)S(1)}, bf16[1024,1024]{1,0:T(8,128)(2,1)}, u32[]{:S(2)}) copy-start(bf16[1024,1024]{1,0:T(8,128)(2,1)} %refs_4_.8) | copy-start | bytes 6291460
  43.3 10.4 %copy-start = (bf16[1024,1024]{1,0:T(8,128)(2,1)S(1)}, bf16[1024,1024]{1,0:T(8,128)(2,1)}, u32[]{:S(2)}) copy-start(bf16[1024,1024]{1,0:T(8,128)(2,1)} %refs_3_.11) | copy-start | bytes 6291460
  43.3 5.8 %collective-permute-start.1 = (bf16[512,256]{1,0:T(8,128)(2,1)S(1)}, bf16[512,256]{1,0:T(8,128)(2,1)S(1)}, u32[]{:S(2)}, u32[]{:S(2)}) collective-permute-start(bf16[512,256]{1,0:T(8,128)(2,1)S(1)} %order.2.refs_2_.refs_0_), channel_id=1, source_target_pairs={{0,2},{1,3},{2,0},{3,1},{4,6},{5,7},{6,4},{7,5},{8,10},{9,11},{10,... | collective-permute-start | bytes 786440 | tf_op jit(solution)/shard_map/ppermute | solution.py:39
  49.2 4.5 %collective-permute-start.2 = (bf16[512,512]{1,0:T(8,128)(2,1)S(1)}, bf16[512,512]{1,0:T(8,128)(2,1)S(1)}, u32[]{:S(2)}, u32[]{:S(2)}) collective-permute-start(bf16[512,512]{1,0:T(8,128)(2,1)S(1)} %pair.2), channel_id=1, source_target_pairs={{0,1},{1,0},{2,3},{3,2},{4,5},{5,4},{6,7},{7,6},{8,9},{9,8},{10,11... | collective-permute-start | bytes 1572872 | tf_op jit(solution)/shard_map/ppermute | solution.py:39
  52.2 7.9 %collective-permute-start = (bf16[512,256]{1,0:T(8,128)(2,1)S(1)}, bf16[512,256]{1,0:T(8,128)(2,1)S(1)}, u32[]{:S(2)}, u32[]{:S(2)}) collective-permute-start(bf16[512,256]{1,0:T(8,128)(2,1)S(1)} %order.3.refs_2_.refs_5_.refs_0_), channel_id=1, source_target_pairs={{0,2},{1,3},{2,0},{3,1},{4,6},{5,7},{6,4},{7,5},{8,10},{9,11},{10,... | collective-permute-start | bytes 786440 | tf_op jit(solution)/shard_map/ppermute | solution.py:39
  55.3 4.7 %collective-permute-start.3 = (bf16[256,512]{1,0:T(8,128)(2,1)S(1)}, bf16[256,512]{1,0:T(8,128)(2,1)S(1)}, u32[]{:S(2)}, u32[]{:S(2)}) collective-permute-start(bf16[256,512]{1,0:T(8,128)(2,1)S(1)} %get-tuple-element.26.refs_5_), channel_id=1, source_target_pairs={{0,1},{1,0},{2,3},{3,2},{4,5},{5,4},{6,7},{7,6},{8,9},{9,8},{10,11... | collective-permute-start | bytes 786440 | tf_op jit(solution)/shard_map/ppermute | solution.py:39
  57.4 5.0 %copy-start.4 = (bf16[256,1024]{1,0:T(8,128)(2,1)S(1)}, bf16[256,1024]{1,0:T(8,128)(2,1)}, u32[]{:S(2)}) copy-start(bf16[256,1024]{1,0:T(8,128)(2,1)} %refs_4_.9) | copy-start | bytes 1572868
  57.4 2.8 %collective-permute-start.4 = (bf16[256,512]{1,0:T(8,128)(2,1)S(1)}, bf16[256,512]{1,0:T(8,128)(2,1)S(1)}, u32[]{:S(2)}, u32[]{:S(2)}) collective-permute-start(bf16[256,512]{1,0:T(8,128)(2,1)S(1)} %get-tuple-element.27.refs_0_), channel_id=1, source_target_pairs={{0,1},{1,0},{2,3},{3,2},{4,5},{5,4},{6,7},{7,6},{8,9},{9,8},{10,11... | collective-permute-start | bytes 786440 | tf_op jit(solution)/shard_map/ppermute | solution.py:39
  60.2 3.5 %collective-permute-start.5 = (bf16[512,512]{1,0:T(8,128)(2,1)S(1)}, bf16[512,512]{1,0:T(8,128)(2,1)S(1)}, u32[]{:S(2)}, u32[]{:S(2)}) collective-permute-start(bf16[512,512]{1,0:T(8,128)(2,1)S(1)} %pair.3.refs_5_), channel_id=1, source_target_pairs={{0,1},{1,0},{2,3},{3,2},{4,5},{5,4},{6,7},{7,6},{8,9},{9,8},{10,11... | collective-permute-start | bytes 1572872 | tf_op jit(solution)/shard_map/ppermute | solution.py:39
  61.1 7.9 %collective-permute-start.6 = (bf16[256,512]{1,0:T(8,128)(2,1)S(1)}, bf16[256,512]{1,0:T(8,128)(2,1)S(1)}, u32[]{:S(2)}, u32[]{:S(2)}) collective-permute-start(bf16[256,512]{1,0:T(8,128)(2,1)S(1)} %get-tuple-element.28.refs_2_.refs_1_), channel_id=1, source_target_pairs={{0,2},{1,3},{2,0},{3,1},{4,6},{5,7},{6,4},{7,5},{8,10},{9,11},{10,... | collective-permute-start | bytes 786440 | tf_op jit(solution)/shard_map/ppermute | solution.py:39
  62.4 6.6 %collective-permute-start.7 = (bf16[64,1024]{1,0:T(8,128)(2,1)S(1)}, bf16[64,1024]{1,0:T(8,128)(2,1)S(1)}, u32[]{:S(2)}, u32[]{:S(2)}) collective-permute-start(bf16[64,1024]{1,0:T(8,128)(2,1)S(1)} %head.1), channel_id=1, source_target_pairs={{4,0},{8,4},{12,8},{16,12},{20,16},{24,20},{28,24},{5,1},{9,5},{13... | collective-permute-start | bytes 393224 | tf_op jit(solution)/shard_map/ppermute | solution.py:45
  65.3 6.9 %collective-permute-start.11 = (bf16[256,512]{1,0:T(8,128)(2,1)S(1)}, bf16[256,512]{1,0:T(8,128)(2,1)S(1)}, u32[]{:S(2)}, u32[]{:S(2)}) collective-permute-start(bf16[256,512]{1,0:T(8,128)(2,1)S(1)} %get-tuple-element.31.refs_2_), channel_id=1, source_target_pairs={{0,1},{1,0},{2,3},{3,2},{4,5},{5,4},{6,7},{7,6},{8,9},{9,8},{10,11... | collective-permute-start | bytes 786440 | tf_op jit(solution)/shard_map/ppermute | solution.py:39
  65.8 8.8 %collective-permute-start.10 = (bf16[256,512]{1,0:T(8,128)(2,1)S(1)}, bf16[256,512]{1,0:T(8,128)(2,1)S(1)}, u32[]{:S(2)}, u32[]{:S(2)}) collective-permute-start(bf16[256,512]{1,0:T(8,128)(2,1)S(1)} %get-tuple-element.32.refs_4_), channel_id=1, source_target_pairs={{0,2},{1,3},{2,0},{3,1},{4,6},{5,7},{6,4},{7,5},{8,10},{9,11},{10,... | collective-permute-start | bytes 786440 | tf_op jit(solution)/shard_map/ppermute | solution.py:39
  69.1 6.5 %collective-permute-start.9 = (bf16[256,512]{1,0:T(8,128)(2,1)S(1)}, bf16[256,512]{1,0:T(8,128)(2,1)S(1)}, u32[]{:S(2)}, u32[]{:S(2)}) collective-permute-start(bf16[256,512]{1,0:T(8,128)(2,1)S(1)} %finish.4.refs_5_.refs_0_), channel_id=1, source_target_pairs={{0,1},{1,0},{2,3},{3,2},{4,5},{5,4},{6,7},{7,6},{8,9},{9,8},{10,11... | collective-permute-start | bytes 786440 | tf_op jit(solution)/shard_map/ppermute | solution.py:39
  70.5 5.2 %copy-start.3 = (bf16[1024,1024]{1,0:T(8,128)(2,1)S(1)}, bf16[1024,1024]{1,0:T(8,128)(2,1)}, u32[]{:S(2)}) copy-start(bf16[1024,1024]{1,0:T(8,128)(2,1)} %refs_3_.15) | copy-start | bytes 6291460
  72.1 3.6 %copy-start.2 = (bf16[1024,1024]{1,0:T(8,128)(2,1)S(1)}, bf16[1024,1024]{1,0:T(8,128)(2,1)}, u32[]{:S(2)}) copy-start(bf16[1024,1024]{1,0:T(8,128)(2,1)} %refs_2_.7) | copy-start | bytes 6291460
  72.1 5.3 %collective-permute-start.8 = (bf16[256,512]{1,0:T(8,128)(2,1)S(1)}, bf16[256,512]{1,0:T(8,128)(2,1)S(1)}, u32[]{:S(2)}, u32[]{:S(2)}) collective-permute-start(bf16[256,512]{1,0:T(8,128)(2,1)S(1)} %get-tuple-element.34.refs_2_), channel_id=1, source_target_pairs={{0,1},{1,0},{2,3},{3,2},{4,5},{5,4},{6,7},{7,6},{8,9},{9,8},{10,11... | collective-permute-start | bytes 786440 | tf_op jit(solution)/shard_map/ppermute | solution.py:39
  72.3 9.8 %collective-permute-start.14 = (bf16[256,512]{1,0:T(8,128)(2,1)S(1)}, bf16[256,512]{1,0:T(8,128)(2,1)S(1)}, u32[]{:S(2)}, u32[]{:S(2)}) collective-permute-start(bf16[256,512]{1,0:T(8,128)(2,1)S(1)} %get-tuple-element.37.refs_4_), channel_id=1, source_target_pairs={{0,2},{1,3},{2,0},{3,1},{4,6},{5,7},{6,4},{7,5},{8,10},{9,11},{10,... | collective-permute-start | bytes 786440 | tf_op jit(solution)/shard_map/ppermute | solution.py:39
  74.7 8.1 %collective-permute-start.13 = (bf16[256,512]{1,0:T(8,128)(2,1)S(1)}, bf16[256,512]{1,0:T(8,128)(2,1)S(1)}, u32[]{:S(2)}, u32[]{:S(2)}) collective-permute-start(bf16[256,512]{1,0:T(8,128)(2,1)S(1)} %finish.5.refs_6_.refs_0_), channel_id=1, source_target_pairs={{0,1},{1,0},{2,3},{3,2},{4,5},{5,4},{6,7},{7,6},{8,9},{9,8},{10,11... | collective-permute-start | bytes 786440 | tf_op jit(solution)/shard_map/ppermute | solution.py:39
  77.5 8.5 %collective-permute-start.12 = (bf16[256,512]{1,0:T(8,128)(2,1)S(1)}, bf16[256,512]{1,0:T(8,128)(2,1)S(1)}, u32[]{:S(2)}, u32[]{:S(2)}) collective-permute-start(bf16[256,512]{1,0:T(8,128)(2,1)S(1)} %get-tuple-element.39.refs_4_), channel_id=1, source_target_pairs={{0,2},{1,3},{2,0},{3,1},{4,6},{5,7},{6,4},{7,5},{8,10},{9,11},{10,... | collective-permute-start | bytes 786440 | tf_op jit(solution)/shard_map/ppermute | solution.py:39
  78.8 5.8 %collective-permute-start.15 = (bf16[64,1024]{1,0:T(8,128)(2,1)S(1)}, bf16[64,1024]{1,0:T(8,128)(2,1)S(1)}, u32[]{:S(2)}, u32[]{:S(2)}) collective-permute-start(bf16[64,1024]{1,0:T(8,128)(2,1)S(1)} %attend_first.1.refs_2_.refs_8_), channel_id=1, source_target_pairs={{0,4},{4,8},{8,12},{12,16},{16,20},{20,24},{24,28},{1,5},{5,9},{9,... | collective-permute-start | bytes 393224 | tf_op jit(solution)/shard_map/ppermute | solution.py:45
  82.2 4.7 %collective-permute-start.17 = (bf16[256,512]{1,0:T(8,128)(2,1)S(1)}, bf16[256,512]{1,0:T(8,128)(2,1)S(1)}, u32[]{:S(2)}, u32[]{:S(2)}) collective-permute-start(bf16[256,512]{1,0:T(8,128)(2,1)S(1)} %finish.6.refs_5_.refs_0_), channel_id=1, source_target_pairs={{0,1},{1,0},{2,3},{3,2},{4,5},{5,4},{6,7},{7,6},{8,9},{9,8},{10,11... | collective-permute-start | bytes 786440 | tf_op jit(solution)/shard_map/ppermute | solution.py:39
  86.0 2.6 %collective-permute-start.16 = (bf16[256,512]{1,0:T(8,128)(2,1)S(1)}, bf16[256,512]{1,0:T(8,128)(2,1)S(1)}, u32[]{:S(2)}, u32[]{:S(2)}) collective-permute-start(bf16[256,512]{1,0:T(8,128)(2,1)S(1)} %finish.7.refs_5_.refs_0_), channel_id=1, source_target_pairs={{0,1},{1,0},{2,3},{3,2},{4,5},{5,4},{6,7},{7,6},{8,9},{9,8},{10,11... | collective-permute-start | bytes 786440 | tf_op jit(solution)/shard_map/ppermute | solution.py:39
  (1 other events, 0.7 us)

commit v12 on v11

--- a/solution.py
+++ b/solution.py
@@ -51,9 +51,11 @@
 
 def one_hot(column, width):
     lane = lax.broadcasted_iota(jnp.int32, column.shape, 1)
+    inside = jnp.where(lax.rem(column, jnp.int32(LANES)) == lane, 1.0, 0.0).astype(BF16)
+    block = lax.div(column, jnp.int32(LANES)).astype(F32).astype(BF16)
+    nothing = jnp.zeros_like(inside)
     return jnp.concatenate(
-        [jnp.where(column == lane + at, 1.0, 0.0).astype(BF16) for at in range(0, width, LANES)],
-        axis=1,
+        [jnp.where(block == BF16(at), inside, nothing) for at in range(width // LANES)], axis=1
     )
 
 
@@ -112,18 +114,24 @@
     out_ref[:, width:] = right_ref[...]
 
 
+def split_body(joint_ref, *out_refs):
+    count = out_refs[0].shape[0]
+    for at, out_ref in enumerate(out_refs):
+        out_ref[...] = joint_ref[at * count : (at + 1) * count, :]
+
+
 def head_body(queries_ref, out_ref):
     out_ref[...] = queries_ref[: out_ref.shape[0], :]
 
 
-def order_body(groups, slot_ref, rows_ref, out_ref):
+def order_body(groups, slot_ref, rows_ref, joint_ref, *out_refs):
     rows = rows_ref[...]
-    count = out_ref.shape[0] // len(groups)
-    for at, g in enumerate(groups):
+    for at, (g, out_ref) in enumerate(zip(groups, out_refs)):
+        count = out_ref.shape[0]
         picked = one_hot(slot_ref[g * count : (g + 1) * count, :], rows.shape[0])
-        out_ref[at * count : (at + 1) * count, :] = jnp.dot(
-            picked, rows, preferred_element_type=F32
-        ).astype(BF16)
+        own = jnp.dot(picked, rows, preferred_element_type=F32).astype(BF16)
+        out_ref[...] = own
+        joint_ref[at * count : (at + 1) * count, :] = own
 
 
 def block_rows(ref, index, width):
@@ -134,12 +142,17 @@
     return ref[:, pl.ds(pl.multiple_of(index * width, width), width)]
 
 
-def feed_body(first, e0_ref, e2_ref, other_ref, w_in_ref, w_out_ref, keep_ref, send_ref):
+def feed_body(first, e0_ref, e2_ref, *refs):
+    other_refs, (w_in_ref, w_out_ref, keep_ref, send_ref) = refs[:-4], refs[-4:]
     me = lax.axis_index("tp")
     width = e0_ref.shape[1]
     index = [me, me ^ 2, me ^ 1, me ^ 3]
     here = slice(first, first + keep_ref.shape[0])
-    parts = [e0_ref[here, :], e2_ref[here, :], other_ref[here, :width], other_ref[here, width:]]
+    parts = [e0_ref[here, :], e2_ref[here, :]]
+    if len(other_refs) == 1:
+        parts += [other_refs[0][here, :width], other_refs[0][here, width:]]
+    else:
+        parts += [ref[...] for ref in other_refs]
     parts = [part.astype(F32) for part in parts]
     square = sum(jnp.sum(part * part, axis=1, keepdims=True) for part in parts)
     scale = lax.rsqrt(square / (4 * width) + 1e-06)
@@ -275,39 +288,45 @@
     ).reshape(slots, width)
     order = [groups - 1] + list(range(groups - 1))
     plan = [order[:2], order[2:]]
-    first, window = {}, {}
+    first, window, other = {}, {}, {}
     token = slot
     pieces = []
+    single = sds((per_group, width), BF16)
     for part in plan:
-        e0 = token = call(
+        e0, *own = call(
             functools.partial(order_body, part),
-            sds((len(part) * per_group, width), BF16),
+            (sds((len(part) * per_group, width), BF16), *[single] * len(part)),
             "order",
             (slot, answered),
             (token,),
         )
-        pieces.append([e0, exchange(e0, 2), None])
+        token = e0
+        pieces.append((e0, exchange(e0, 2)))
         for at, g in enumerate(part):
             first[g] = at * per_group
-
-    def across(piece, after=()):
-        count = piece[0].shape[0]
-        both = call(pair_body, sds((count, 2 * width), BF16), "pair", piece[:2], after)
-        piece[2] = exchange(both, 1)
-        return both
-
-    across(pieces[0], (token,))
+            other[g] = [exchange(own[at], 1)] if part == plan[1] else []
+
+    both = call(
+        pair_body, sds((len(plan[0]) * per_group, 2 * width), BF16), "pair", pieces[0], (token,)
+    )
+    both = exchange(both, 1)
+    for g in plan[0]:
+        other[g] = [both]
     half = sds((per_group, 2 * width), BF16)
     whole = sds((per_group, 2 * width), F32)
     fed, summed, far, encoded = {}, {}, {}, {}
     behind = out = next_q = None
 
     def emb(g):
-        return pieces[0 if g in plan[0] else 1]
+        return *pieces[0 if g in plan[0] else 1], *other[g]
 
     def rest(_):
         nonlocal token
-        token = across(pieces[1], (token, fed[order[1]][1]))
+        after = token, fed[order[1]][1]
+        far_own = call(split_body, (single,) * len(plan[1]), "split", pieces[1][1:], after)
+        for g, own in zip(plan[1], far_own):
+            other[g].append(exchange(own, 1))
+        token = far_own[0]
 
     def pause(_):
         nonlocal token

time: 91.7 us -> 95.7 us (1.044)
  starting transfers between devices: 20.1 us -> 23.8 us
    ppermute x16 -> x19, starting transfers between devices: 15.6 us -> 18.4 us  [exchange(): return lax.ppermute(x, 'tp', [(i, i ^ bit) for i in range(size)])]
    ppermute x16 -> x19, waiting for transfers between devices: 9.03 us -> 9.01 us  [exchange(): return lax.ppermute(x, 'tp', [(i, i ^ bit) for i in range(size)])]
  transfers between devices with their start and end apart: 18 -> 21, of which waited for: 6 -> 7; matrix products, arithmetic and copies ran while one was open for 0% -> 0% of each run, Pallas kernels for 14% -> 13%
where the time goes in v12:
time: 95.7 us; the launch traced here: 95.5 us
  blocking collectives  38.6 us (40%)
  starting transfers between devices  23.8 us (25%)
  Pallas kernels  20.1 us (21%)
  waiting for transfers between devices  11.8 us (12%)
    all_to_all x1, blocking collectives, per_device(): lax.all_to_all(found.reshape(seq_size, cap, width), 'seq', split_axis=0,...  27.1 us
    pallas_call x24, Pallas kernels, call(): pl.pallas_call(without_after, out_shape=outs, in_specs=in_specs + [unread...  20.1 us
    ppermute x19, starting transfers between devices, exchange(): return lax.ppermute(x, 'tp', [(i, i ^ bit) for i in range(size)])  18.4 us
    all_to_all x1, blocking collectives, per_device(): lax.all_to_all(wanted, 'seq', split_axis=0, concat_axis=0, tiled=True)  11.5 us
    ppermute x19, waiting for transfers between devices, exchange(): return lax.ppermute(x, 'tp', [(i, i ^ bit) for i in range(size)])  9.01 us
    ppermute x2, starting transfers between devices, shifted(): return lax.ppermute(x, 'seq', pairs)  5.41 us
    ppermute x2, waiting for transfers between devices, shifted(): return lax.ppermute(x, 'seq', pairs)  2.77 us
  transfers between devices with their start and end apart: 21, of which 7 were waited for; matrix products, arithmetic and copies ran while one was open for 0% of the time, Pallas kernels for 13%

profile of v12, /device:TPU:1, one launch (start us, length us, event | category | flops | bytes accessed | tf_op | source)
XLA Modules:
  0.0 95.5 jit_solution(11934871213000786974)
XLA Ops:
  1.5 11.5 %all_to_all.14 = s32[8,1,256]{2,1,0:T(1,128)S(1)} all-to-all(s32[8,1,256]{2,1,0:T(1,128)S(1)} %copy.8), channel_id=1, replica_groups=mesh['seq'=8,'tp'=4] {'seq'}, dimensions={0} | all-to-all | bytes 16384 | tf_op jit(solution)/shard_map/all_to_all | solution.py:279
  13.1 2.4 %fetch.1 = bf16[2048,256]{1,0:T(8,128)(2,1)S(1)} custom-call(s32[1,2048]{1,0:T(1,128)S(1)} %bitcast.8, bf16[2048,256]{1,0:T(8,128)(2,1)S(1)} %copy-done.5), custom_call_target="tpu_custom_call" | custom-call | flops 1024 | bytes 1024 | tf_op jit(solution)/shard_map/fetch/pallas_call | solution.py:26
  15.5 27.1 %all_to_all.15 = bf16[8,256,256]{2,1,0:T(8,128)(2,1)S(1)} all-to-all(bf16[8,256,256]{2,1,0:T(8,128)(2,1)S(1)} %bitcast.7), channel_id=1, replica_groups=mesh['seq'=8,'tp'=4] {'seq'}, dimensions={0} | all-to-all | bytes 2097152 | tf_op jit(solution)/shard_map/all_to_all | solution.py:286
  42.6 1.4 %order.2 = (bf16[512,256]{1,0:T(8,128)(2,1)S(1)}, bf16[256,256]{1,0:T(8,128)(2,1)}, bf16[256,256]{1,0:T(8,128)(2,1)}) custom-call(s32[1024,128]{1,0:T(8,128)S(1)} %get-tuple-element.29.refs_0_.refs_2_, bf16[2048,256]{1,0:T(8,128)(2,1)S(1)} %bitcast.5, s32[1024,128]{1,0:T(8,128)S(1)} %get-tuple-element.29.refs_0_.refs_2_), custom_call_target="tpu_custom_call" | custom-call | flops 1024 | bytes 1024 | tf_op jit(solution)/shard_map/order/pallas_call | solution.py:26
  46.1 3.8 %collective-permute-done.2.refs_1_ = bf16[512,256]{1,0:T(8,128)(2,1)S(1)} collective-permute-done((bf16[512,256]{1,0:T(8,128)(2,1)S(1)}, bf16[512,256]{1,0:T(8,128)(2,1)S(1)}, u32[]{:S(2)}, u32[]{:S(2)}) %collective-permute-start.2) | collective-permute-done | bytes 262176 | tf_op jit(solution)/shard_map/ppermute | solution.py:39
  49.9 3.0 %collective-permute-start.3 = (bf16[512,512]{1,0:T(8,128)(2,1)S(1)}, bf16[512,512]{1,0:T(8,128)(2,1)S(1)}, u32[]{:S(2)}, u32[]{:S(2)}) collective-permute-start(bf16[512,512]{1,0:T(8,128)(2,1)S(1)} %pair.1), channel_id=1, source_target_pairs={{0,1},{1,0},{2,3},{3,2},{4,5},{5,4},{6,7},{7,6},{8,9},{9,8},{10,11... | collective-permute-start | bytes 1572872 | tf_op jit(solution)/shard_map/ppermute | solution.py:39
  52.9 1.3 %collective-permute-start = (bf16[512,256]{1,0:T(8,128)(2,1)S(1)}, bf16[512,256]{1,0:T(8,128)(2,1)S(1)}, u32[]{:S(2)}, u32[]{:S(2)}) collective-permute-start(bf16[512,256]{1,0:T(8,128)(2,1)S(1)} %get-tuple-element.32.refs_2_.refs_5_.refs_0_), channel_id=1, source_target_pairs={{0,2},{1,3},{2,0},{3,1},{4,6},{5,7},{6,4},{7,5},{8,10},{9,11},{10,... | collective-permute-start | bytes 786440 | tf_op jit(solution)/shard_map/ppermute | solution.py:39
  54.4 1.6 %feed.4 = (f32[256,512]{1,0:T(8,128)S(1)}, bf16[256,512]{1,0:T(8,128)(2,1)S(1)}) custom-call(bf16[512,256]{1,0:T(8,128)(2,1)S(1)} %get-tuple-element.31.refs_2_.refs_0_, bf16[512,256]{1,0:T(8,128)(2,1)S(1)} %collective-permute-done.2.refs_1_, bf16[512,512]{1,0:T(8,128)(2,1)S(1)} %collective-permute-done.3.refs_2_, bf16[1024,1024]{1,0:T(8,128)(2,1)S(1)} %copy-done, ...), custom_call_target="tpu_custom_call" | custom-call | flops 1024 | bytes 1024 | tf_op jit(solution)/shard_map/feed/pallas_call | solution.py:26
  56.5 1.6 %feed.5 = (f32[256,512]{1,0:T(8,128)S(1)}, bf16[256,512]{1,0:T(8,128)(2,1)S(1)}) custom-call(bf16[512,256]{1,0:T(8,128)(2,1)S(1)} %get-tuple-element.31.refs_2_.refs_0_, bf16[512,256]{1,0:T(8,128)(2,1)S(1)} %collective-permute-done.2.refs_1_, bf16[512,512]{1,0:T(8,128)(2,1)S(1)} %collective-permute-done.3.refs_2_, bf16[1024,1024]{1,0:T(8,128)(2,1)S(1)} %copy-done, ...), custom_call_target="tpu_custom_call" | custom-call | flops 1024 | bytes 1024 | tf_op jit(solution)/shard_map/feed/pallas_call | solution.py:26
  58.3 2.5 %collective-permute-done.refs_1_.refs_0_ = bf16[512,256]{1,0:T(8,128)(2,1)S(1)} collective-permute-done((bf16[512,256]{1,0:T(8,128)(2,1)S(1)}, bf16[512,256]{1,0:T(8,128)(2,1)S(1)}, u32[]{:S(2)}, u32[]{:S(2)}) %collective-permute-start) | collective-permute-done | bytes 262176 | tf_op jit(solution)/shard_map/ppermute | solution.py:39
  60.9 1.3 %collective-permute-start.7 = (bf16[256,512]{1,0:T(8,128)(2,1)S(1)}, bf16[256,512]{1,0:T(8,128)(2,1)S(1)}, u32[]{:S(2)}, u32[]{:S(2)}) collective-permute-start(bf16[256,512]{1,0:T(8,128)(2,1)S(1)} %get-tuple-element.37.refs_1_), channel_id=1, source_target_pairs={{0,2},{1,3},{2,0},{3,1},{4,6},{5,7},{6,4},{7,5},{8,10},{9,11},{10,... | collective-permute-start | bytes 786440 | tf_op jit(solution)/shard_map/ppermute | solution.py:39
  63.4 1.5 %collective-permute-start.10 = (bf16[64,1024]{1,0:T(8,128)(2,1)S(1)}, bf16[64,1024]{1,0:T(8,128)(2,1)S(1)}, u32[]{:S(2)}, u32[]{:S(2)}) collective-permute-start(bf16[64,1024]{1,0:T(8,128)(2,1)S(1)} %head.1), channel_id=1, source_target_pairs={{4,0},{8,4},{12,8},{16,12},{20,16},{24,20},{28,24},{5,1},{9,5},{13... | collective-permute-start | bytes 393224 | tf_op jit(solution)/shard_map/ppermute | solution.py:45
  65.6 1.6 %feed.6 = (f32[256,512]{1,0:T(8,128)S(1)}, bf16[256,512]{1,0:T(8,128)(2,1)S(1)}) custom-call(bf16[512,256]{1,0:T(8,128)(2,1)S(1)} %get-tuple-element.32.refs_2_.refs_5_.refs_0_, bf16[512,256]{1,0:T(8,128)(2,1)S(1)} %collective-permute-done.refs_1_.refs_0_, bf16[256,256]{1,0:T(8,128)(2,1)S(1)} %collective-permute-done.8.refs_2_, ...), custom_call_target="tpu_custom_call" | custom-call | flops 1024 | bytes 1024 | tf_op jit(solution)/shard_map/feed/pallas_call | solution.py:26
  67.7 2.2 %collective-permute-done.10.refs_5_ = bf16[64,1024]{1,0:T(8,128)(2,1)S(1)} collective-permute-done((bf16[64,1024]{1,0:T(8,128)(2,1)S(1)}, bf16[64,1024]{1,0:T(8,128)(2,1)S(1)}, u32[]{:S(2)}, u32[]{:S(2)}) %collective-permute-start.10) | collective-permute-done | bytes 131104 | tf_op jit(solution)/shard_map/ppermute | solution.py:45
  70.2 1.7 %collective-permute-start.12 = (bf16[256,512]{1,0:T(8,128)(2,1)S(1)}, bf16[256,512]{1,0:T(8,128)(2,1)S(1)}, u32[]{:S(2)}, u32[]{:S(2)}) collective-permute-start(bf16[256,512]{1,0:T(8,128)(2,1)S(1)} %finish.4.refs_6_.refs_0_), channel_id=1, source_target_pairs={{0,1},{1,0},{2,3},{3,2},{4,5},{5,4},{6,7},{7,6},{8,9},{9,8},{10,11... | collective-permute-start | bytes 786440 | tf_op jit(solution)/shard_map/ppermute | solution.py:39
  71.9 1.6 %feed.7 = (f32[256,512]{1,0:T(8,128)S(1)}, bf16[256,512]{1,0:T(8,128)(2,1)S(1)}) custom-call(bf16[512,256]{1,0:T(8,128)(2,1)S(1)} %get-tuple-element.32.refs_2_.refs_5_.refs_0_, bf16[512,256]{1,0:T(8,128)(2,1)S(1)} %collective-permute-done.refs_1_.refs_0_, bf16[256,256]{1,0:T(8,128)(2,1)S(1)} %collective-permute-done.1.refs_2_, ...), custom_call_target="tpu_custom_call" | custom-call | flops 1024 | bytes 1024 | tf_op jit(solution)/shard_map/feed/pallas_call | solution.py:26
  73.7 1.3 %collective-permute-start.17 = (bf16[256,512]{1,0:T(8,128)(2,1)S(1)}, bf16[256,512]{1,0:T(8,128)(2,1)S(1)}, u32[]{:S(2)}, u32[]{:S(2)}) collective-permute-start(bf16[256,512]{1,0:T(8,128)(2,1)S(1)} %get-tuple-element.49.refs_4_), channel_id=1, source_target_pairs={{0,2},{1,3},{2,0},{3,1},{4,6},{5,7},{6,4},{7,5},{8,10},{9,11},{10,... | collective-permute-start | bytes 786440 | tf_op jit(solution)/shard_map/ppermute | solution.py:39
  75.0 1.4 %collective-permute-done.13.refs_3_ = bf16[256,512]{1,0:T(8,128)(2,1)S(1)} collective-permute-done((bf16[256,512]{1,0:T(8,128)(2,1)S(1)}, bf16[256,512]{1,0:T(8,128)(2,1)S(1)}, u32[]{:S(2)}, u32[]{:S(2)}) %collective-permute-start.13) | collective-permute-done | bytes 262176 | tf_op jit(solution)/shard_map/ppermute | solution.py:39
  76.5 4.0 %collective-permute-start.16 = (bf16[256,512]{1,0:T(8,128)(2,1)S(1)}, bf16[256,512]{1,0:T(8,128)(2,1)S(1)}, u32[]{:S(2)}, u32[]{:S(2)}) collective-permute-start(bf16[256,512]{1,0:T(8,128)(2,1)S(1)} %finish.5.refs_6_.refs_0_), channel_id=1, source_target_pairs={{0,1},{1,0},{2,3},{3,2},{4,5},{5,4},{6,7},{7,6},{8,9},{9,8},{10,11... | collective-permute-start | bytes 786440 | tf_op jit(solution)/shard_map/ppermute | solution.py:39
  80.5 1.7 %attend_first.1.refs_2_.refs_8_ = bf16[64,1024]{1,0:T(8,128)(2,1)S(1)} custom-call(bf16[256,512]{1,0:T(8,128)(2,1)S(1)} %finish.4.refs_6_.refs_0_, bf16[256,512]{1,0:T(8,128)(2,1)S(1)} %collective-permute-done.12.refs_1_, bf16[1024,1024]{1,0:T(8,128)(2,1)S(1)} %copy-done.2, bf16[1024,1024]{1,0:T(8,128)(2,1)S(1)} %copy-done.3, ...), custom_call_target="tpu_custom_call" | custom-call | flops 1024 | bytes 1024 | tf_op jit(solution)/shard_map/attend_first/pallas_call | solution.py:26
  82.3 3.9 %collective-permute-start.18 = (bf16[64,1024]{1,0:T(8,128)(2,1)S(1)}, bf16[64,1024]{1,0:T(8,128)(2,1)S(1)}, u32[]{:S(2)}, u32[]{:S(2)}) collective-permute-start(bf16[64,1024]{1,0:T(8,128)(2,1)S(1)} %attend_first.1.refs_2_.refs_8_), channel_id=1, source_target_pairs={{0,4},{4,8},{8,12},{12,16},{16,20},{20,24},{24,28},{1,5},{5,9},{9,... | collective-permute-start | bytes 393224 | tf_op jit(solution)/shard_map/ppermute | solution.py:45
  86.9 1.7 %attend.2.refs_4_.refs_6_ = bf16[64,1024]{1,0:T(8,128)(2,1)S(1)} custom-call(bf16[256,512]{1,0:T(8,128)(2,1)S(1)} %finish.5.refs_6_.refs_0_, bf16[256,512]{1,0:T(8,128)(2,1)S(1)} %collective-permute-done.16.refs_1_, bf16[1024,1024]{1,0:T(8,128)(2,1)S(1)} %copy-done.2, bf16[1024,1024]{1,0:T(8,128)(2,1)S(1)} %copy-done.3, ...), custom_call_target="tpu_custom_call" | custom-call | flops 1024 | bytes 1024 | tf_op jit(solution)/shard_map/attend/pallas_call | solution.py:26
  91.2 1.7 %attend.3.refs_7_ = bf16[64,1024]{1,0:T(8,128)(2,1)S(1)} custom-call(bf16[256,512]{1,0:T(8,128)(2,1)S(1)} %finish.6.refs_5_.refs_0_, bf16[256,512]{1,0:T(8,128)(2,1)S(1)} %collective-permute-done.20.refs_1_, bf16[1024,1024]{1,0:T(8,128)(2,1)S(1)} %copy-done.2, bf16[1024,1024]{1,0:T(8,128)(2,1)S(1)} %copy-done.3, ...), custom_call_target="tpu_custom_call" | custom-call | flops 1024 | bytes 1024 | tf_op jit(solution)/shard_map/attend/pallas_call | solution.py:26
  92.9 2.5 %attend_last.1 = bf16[256,1024]{1,0:T(8,128)(2,1)} custom-call(bf16[256,512]{1,0:T(8,128)(2,1)S(1)} %finish.7.refs_5_.refs_0_, bf16[256,512]{1,0:T(8,128)(2,1)S(1)} %collective-permute-done.19.refs_1_, bf16[1024,1024]{1,0:T(8,128)(2,1)S(1)} %copy-done.2, bf16[1024,1024]{1,0:T(8,128)(2,1)S(1)} %copy-done.3, bf16[64,1024]{1,0:T(8,128)(2,1)S(1)} %get-tuple-element.55.refs_4_, ...), custom_call_target="tpu_custom_call" | custom-call | flops 1024 | bytes 1024 | tf_op jit(solution)/shard_map/attend_last/pallas_call | solution.py:26
  (60 shorter events, 10.9 us)
Async XLA Ops:
  0.7 12.4 %copy-start.5 = (bf16[2048,256]{1,0:T(8,128)(2,1)S(1)}, bf16[2048,256]{1,0:T(8,128)(2,1)}, u32[]{:S(2)}) copy-start(bf16[2048,256]{1,0:T(8,128)(2,1)} %refs_1_.1) | copy-start | bytes 3145732
  42.6 11.8 %copy-start.1 = (bf16[1024,1024]{1,0:T(8,128)(2,1)S(1)}, bf16[1024,1024]{1,0:T(8,128)(2,1)}, u32[]{:S(2)}) copy-start(bf16[1024,1024]{1,0:T(8,128)(2,1)} %refs_5_.3) | copy-start | bytes 6291460
  44.1 10.4 %copy-start = (bf16[1024,1024]{1,0:T(8,128)(2,1)S(1)}, bf16[1024,1024]{1,0:T(8,128)(2,1)}, u32[]{:S(2)}) copy-start(bf16[1024,1024]{1,0:T(8,128)(2,1)} %refs_4_.8) | copy-start | bytes 6291460
  44.1 5.8 %collective-permute-start.2 = (bf16[512,256]{1,0:T(8,128)(2,1)S(1)}, bf16[512,256]{1,0:T(8,128)(2,1)S(1)}, u32[]{:S(2)}, u32[]{:S(2)}) collective-permute-start(bf16[512,256]{1,0:T(8,128)(2,1)S(1)} %get-tuple-element.31.refs_2_.refs_0_), channel_id=1, source_target_pairs={{0,2},{1,3},{2,0},{3,1},{4,6},{5,7},{6,4},{7,5},{8,10},{9,11},{10,... | collective-permute-start | bytes 786440 | tf_op jit(solution)/shard_map/ppermute | solution.py:39
  49.9 4.5 %collective-permute-start.3 = (bf16[512,512]{1,0:T(8,128)(2,1)S(1)}, bf16[512,512]{1,0:T(8,128)(2,1)S(1)}, u32[]{:S(2)}, u32[]{:S(2)}) collective-permute-start(bf16[512,512]{1,0:T(8,128)(2,1)S(1)} %pair.1), channel_id=1, source_target_pairs={{0,1},{1,0},{2,3},{3,2},{4,5},{5,4},{6,7},{7,6},{8,9},{9,8},{10,11... | collective-permute-start | bytes 1572872 | tf_op jit(solution)/shard_map/ppermute | solution.py:39
  52.9 7.9 %collective-permute-start = (bf16[512,256]{1,0:T(8,128)(2,1)S(1)}, bf16[512,256]{1,0:T(8,128)(2,1)S(1)}, u32[]{:S(2)}, u32[]{:S(2)}) collective-permute-start(bf16[512,256]{1,0:T(8,128)(2,1)S(1)} %get-tuple-element.32.refs_2_.refs_5_.refs_0_), channel_id=1, source_target_pairs={{0,2},{1,3},{2,0},{3,1},{4,6},{5,7},{6,4},{7,5},{8,10},{9,11},{10,... | collective-permute-start | bytes 786440 | tf_op jit(solution)/shard_map/ppermute | solution.py:39
  56.0 4.7 %collective-permute-start.4 = (bf16[256,512]{1,0:T(8,128)(2,1)S(1)}, bf16[256,512]{1,0:T(8,128)(2,1)S(1)}, u32[]{:S(2)}, u32[]{:S(2)}) collective-permute-start(bf16[256,512]{1,0:T(8,128)(2,1)S(1)} %get-tuple-element.35.refs_5_), channel_id=1, source_target_pairs={{0,1},{1,0},{2,3},{3,2},{4,5},{5,4},{6,7},{7,6},{8,9},{9,8},{10,11... | collective-permute-start | bytes 786440 | tf_op jit(solution)/shard_map/ppermute | solution.py:39
  58.1 5.2 %collective-permute-start.5 = (bf16[256,512]{1,0:T(8,128)(2,1)S(1)}, bf16[256,512]{1,0:T(8,128)(2,1)S(1)}, u32[]{:S(2)}, u32[]{:S(2)}) collective-permute-start(bf16[256,512]{1,0:T(8,128)(2,1)S(1)} %get-tuple-element.36.refs_0_), channel_id=1, source_target_pairs={{0,1},{1,0},{2,3},{3,2},{4,5},{5,4},{6,7},{7,6},{8,9},{9,8},{10,11... | collective-permute-start | bytes 786440 | tf_op jit(solution)/shard_map/ppermute | solution.py:39
  60.9 9.3 %collective-permute-start.7 = (bf16[256,512]{1,0:T(8,128)(2,1)S(1)}, bf16[256,512]{1,0:T(8,128)(2,1)S(1)}, u32[]{:S(2)}, u32[]{:S(2)}) collective-permute-start(bf16[256,512]{1,0:T(8,128)(2,1)S(1)} %get-tuple-element.37.refs_1_), channel_id=1, source_target_pairs={{0,2},{1,3},{2,0},{3,1},{4,6},{5,7},{6,4},{7,5},{8,10},{9,11},{10,... | collective-permute-start | bytes 786440 | tf_op jit(solution)/shard_map/ppermute | solution.py:39
  62.2 3.3 %collective-permute-start.8 = (bf16[256,256]{1,0:T(8,128)(2,1)S(1)}, bf16[256,256]{1,0:T(8,128)(2,1)S(1)}, u32[]{:S(2)}, u32[]{:S(2)}) collective-permute-start(bf16[256,256]{1,0:T(8,128)(2,1)S(1)} %get-tuple-element.41), channel_id=1, source_target_pairs={{0,1},{1,0},{2,3},{3,2},{4,5},{5,4},{6,7},{7,6},{8,9},{9,8},{10,11... | collective-permute-start | bytes 393224 | tf_op jit(solution)/shard_map/ppermute | solution.py:39
  63.3 2.2 %collective-permute-start.9 = (bf16[256,256]{1,0:T(8,128)(2,1)S(1)}, bf16[256,256]{1,0:T(8,128)(2,1)S(1)}, u32[]{:S(2)}, u32[]{:S(2)}) collective-permute-start(bf16[256,256]{1,0:T(8,128)(2,1)S(1)} %get-tuple-element.42.refs_6_), channel_id=1, source_target_pairs={{0,1},{1,0},{2,3},{3,2},{4,5},{5,4},{6,7},{7,6},{8,9},{9,8},{10,11... | collective-permute-start | bytes 393224 | tf_op jit(solution)/shard_map/ppermute | solution.py:39
  63.4 6.5 %collective-permute-start.10 = (bf16[64,1024]{1,0:T(8,128)(2,1)S(1)}, bf16[64,1024]{1,0:T(8,128)(2,1)S(1)}, u32[]{:S(2)}, u32[]{:S(2)}) collective-permute-start(bf16[64,1024]{1,0:T(8,128)(2,1)S(1)} %head.1), channel_id=1, source_target_pairs={{4,0},{8,4},{12,8},{16,12},{20,16},{24,20},{28,24},{5,1},{9,5},{13... | collective-permute-start | bytes 393224 | tf_op jit(solution)/shard_map/ppermute | solution.py:45
  64.9 7.0 %collective-permute-start.1 = (bf16[256,256]{1,0:T(8,128)(2,1)S(1)}, bf16[256,256]{1,0:T(8,128)(2,1)S(1)}, u32[]{:S(2)}, u32[]{:S(2)}) collective-permute-start(bf16[256,256]{1,0:T(8,128)(2,1)S(1)} %get-tuple-element.33), channel_id=1, source_target_pairs={{0,1},{1,0},{2,3},{3,2},{4,5},{5,4},{6,7},{7,6},{8,9},{9,8},{10,11... | collective-permute-start | bytes 393224 | tf_op jit(solution)/shard_map/ppermute | solution.py:39
  65.5 6.4 %collective-permute-start.6 = (bf16[256,256]{1,0:T(8,128)(2,1)S(1)}, bf16[256,256]{1,0:T(8,128)(2,1)S(1)}, u32[]{:S(2)}, u32[]{:S(2)}) collective-permute-start(bf16[256,256]{1,0:T(8,128)(2,1)S(1)} %get-tuple-element.38), channel_id=1, source_target_pairs={{0,1},{1,0},{2,3},{3,2},{4,5},{5,4},{6,7},{7,6},{8,9},{9,8},{10,11... | collective-permute-start | bytes 393224 | tf_op jit(solution)/shard_map/ppermute | solution.py:39
  67.2 6.5 %collective-permute-start.14 = (bf16[256,512]{1,0:T(8,128)(2,1)S(1)}, bf16[256,512]{1,0:T(8,128)(2,1)S(1)}, u32[]{:S(2)}, u32[]{:S(2)}) collective-permute-start(bf16[256,512]{1,0:T(8,128)(2,1)S(1)} %get-tuple-element.43.refs_2_), channel_id=1, source_target_pairs={{0,1},{1,0},{2,3},{3,2},{4,5},{5,4},{6,7},{7,6},{8,9},{9,8},{10,11... | collective-permute-start | bytes 786440 | tf_op jit(solution)/shard_map/ppermute | solution.py:39
  69.9 6.5 %collective-permute-start.13 = (bf16[256,512]{1,0:T(8,128)(2,1)S(1)}, bf16[256,512]{1,0:T(8,128)(2,1)S(1)}, u32[]{:S(2)}, u32[]{:S(2)}) collective-permute-start(bf16[256,512]{1,0:T(8,128)(2,1)S(1)} %get-tuple-element.44.refs_4_), channel_id=1, source_target_pairs={{0,2},{1,3},{2,0},{3,1},{4,6},{5,7},{6,4},{7,5},{8,10},{9,11},{10,... | collective-permute-start | bytes 786440 | tf_op jit(solution)/shard_map/ppermute | solution.py:39
  70.2 10.2 %collective-permute-start.12 = (bf16[256,512]{1,0:T(8,128)(2,1)S(1)}, bf16[256,512]{1,0:T(8,128)(2,1)S(1)}, u32[]{:S(2)}, u32[]{:S(2)}) collective-permute-start(bf16[256,512]{1,0:T(8,128)(2,1)S(1)} %finish.4.refs_6_.refs_0_), channel_id=1, source_target_pairs={{0,1},{1,0},{2,3},{3,2},{4,5},{5,4},{6,7},{7,6},{8,9},{9,8},{10,11... | collective-permute-start | bytes 786440 | tf_op jit(solution)/shard_map/ppermute | solution.py:39
  73.5 8.6 %collective-permute-start.11 = (bf16[256,512]{1,0:T(8,128)(2,1)S(1)}, bf16[256,512]{1,0:T(8,128)(2,1)S(1)}, u32[]{:S(2)}, u32[]{:S(2)}) collective-permute-start(bf16[256,512]{1,0:T(8,128)(2,1)S(1)} %get-tuple-element.46.refs_2_), channel_id=1, source_target_pairs={{0,1},{1,0},{2,3},{3,2},{4,5},{5,4},{6,7},{7,6},{8,9},{9,8},{10,11... | collective-permute-start | bytes 786440 | tf_op jit(solution)/shard_map/ppermute | solution.py:39
  73.7 12.7 %collective-permute-start.17 = (bf16[256,512]{1,0:T(8,128)(2,1)S(1)}, bf16[256,512]{1,0:T(8,128)(2,1)S(1)}, u32[]{:S(2)}, u32[]{:S(2)}) collective-permute-start(bf16[256,512]{1,0:T(8,128)(2,1)S(1)} %get-tuple-element.49.refs_4_), channel_id=1, source_target_pairs={{0,2},{1,3},{2,0},{3,1},{4,6},{5,7},{6,4},{7,5},{8,10},{9,11},{10,... | collective-permute-start | bytes 786440 | tf_op jit(solution)/shard_map/ppermute | solution.py:39
  76.5 10.4 %collective-permute-start.16 = (bf16[256,512]{1,0:T(8,128)(2,1)S(1)}, bf16[256,512]{1,0:T(8,128)(2,1)S(1)}, u32[]{:S(2)}, u32[]{:S(2)}) collective-permute-start(bf16[256,512]{1,0:T(8,128)(2,1)S(1)} %finish.5.refs_6_.refs_0_), channel_id=1, source_target_pairs={{0,1},{1,0},{2,3},{3,2},{4,5},{5,4},{6,7},{7,6},{8,9},{9,8},{10,11... | collective-permute-start | bytes 786440 | tf_op jit(solution)/shard_map/ppermute | solution.py:39
  82.3 8.0 %collective-permute-start.15 = (bf16[256,512]{1,0:T(8,128)(2,1)S(1)}, bf16[256,512]{1,0:T(8,128)(2,1)S(1)}, u32[]{:S(2)}, u32[]{:S(2)}) collective-permute-start(bf16[256,512]{1,0:T(8,128)(2,1)S(1)} %get-tuple-element.51.refs_4_), channel_id=1, source_target_pairs={{0,2},{1,3},{2,0},{3,1},{4,6},{5,7},{6,4},{7,5},{8,10},{9,11},{10,... | collective-permute-start | bytes 786440 | tf_op jit(solution)/shard_map/ppermute | solution.py:39
  82.3 6.8 %collective-permute-start.18 = (bf16[64,1024]{1,0:T(8,128)(2,1)S(1)}, bf16[64,1024]{1,0:T(8,128)(2,1)S(1)}, u32[]{:S(2)}, u32[]{:S(2)}) collective-permute-start(bf16[64,1024]{1,0:T(8,128)(2,1)S(1)} %attend_first.1.refs_2_.refs_8_), channel_id=1, source_target_pairs={{0,4},{4,8},{8,12},{12,16},{16,20},{20,24},{24,28},{1,5},{5,9},{9,... | collective-permute-start | bytes 393224 | tf_op jit(solution)/shard_map/ppermute | solution.py:45
  86.5 4.7 %collective-permute-start.20 = (bf16[256,512]{1,0:T(8,128)(2,1)S(1)}, bf16[256,512]{1,0:T(8,128)(2,1)S(1)}, u32[]{:S(2)}, u32[]{:S(2)}) collective-permute-start(bf16[256,512]{1,0:T(8,128)(2,1)S(1)} %finish.6.refs_5_.refs_0_), channel_id=1, source_target_pairs={{0,1},{1,0},{2,3},{3,2},{4,5},{5,4},{6,7},{7,6},{8,9},{9,8},{10,11... | collective-permute-start | bytes 786440 | tf_op jit(solution)/shard_map/ppermute | solution.py:39
  90.3 2.6 %collective-permute-start.19 = (bf16[256,512]{1,0:T(8,128)(2,1)S(1)}, bf16[256,512]{1,0:T(8,128)(2,1)S(1)}, u32[]{:S(2)}, u32[]{:S(2)}) collective-permute-start(bf16[256,512]{1,0:T(8,128)(2,1)S(1)} %finish.7.refs_5_.refs_0_), channel_id=1, source_target_pairs={{0,1},{1,0},{2,3},{3,2},{4,5},{5,4},{6,7},{7,6},{8,9},{9,8},{10,11... | collective-permute-start | bytes 786440 | tf_op jit(solution)/shard_map/ppermute | solution.py:39
  (4 other events, 21.5 us)

commit v13 on v11

--- a/solution.py
+++ b/solution.py
@@ -102,6 +102,14 @@
         ).astype(BF16)
 
 
+def deal_body(left_ref, right_ref, left_out, right_out, both_out):
+    count, width = left_out.shape
+    left_out[...] = left_ref[:count, :]
+    right_out[...] = right_ref[:count, :]
+    both_out[:, :width] = left_ref[count:, :]
+    both_out[:, width:] = right_ref[count:, :]
+
+
 def mark_body(out_ref):
     out_ref[...] = jnp.zeros_like(out_ref)
 
@@ -134,12 +142,18 @@
     return ref[:, pl.ds(pl.multiple_of(index * width, width), width)]
 
 
-def feed_body(first, e0_ref, e2_ref, other_ref, w_in_ref, w_out_ref, keep_ref, send_ref):
+def feed_body(first, e0_ref, e2_ref, *refs):
+    other_refs, (w_in_ref, w_out_ref, keep_ref, send_ref) = refs[:-4], refs[-4:]
     me = lax.axis_index("tp")
     width = e0_ref.shape[1]
     index = [me, me ^ 2, me ^ 1, me ^ 3]
     here = slice(first, first + keep_ref.shape[0])
-    parts = [e0_ref[here, :], e2_ref[here, :], other_ref[here, :width], other_ref[here, width:]]
+    parts = [e0_ref[here, :], e2_ref[here, :]]
+    if len(other_refs) == 1:
+        there = here if other_refs[0].shape[0] == e0_ref.shape[0] else slice(None)
+        parts += [other_refs[0][there, :width], other_refs[0][there, width:]]
+    else:
+        parts += [ref[...] for ref in other_refs]
     parts = [part.astype(F32) for part in parts]
     square = sum(jnp.sum(part * part, axis=1, keepdims=True) for part in parts)
     scale = lax.rsqrt(square / (4 * width) + 1e-06)
@@ -302,12 +316,23 @@
     fed, summed, far, encoded = {}, {}, {}, {}
     behind = out = next_q = None
 
+    other = {g: (pieces[0][2],) for g in plan[0]}
+
     def emb(g):
-        return pieces[0 if g in plan[0] else 1]
+        return *pieces[0 if g in plan[0] else 1][:2], *other[g]
 
     def rest(_):
         nonlocal token
-        token = across(pieces[1], (token, fed[order[1]][1]))
+        single, double = sds((per_group, width), BF16), sds((per_group, 2 * width), BF16)
+        token, far_own, both = call(
+            deal_body,
+            (single, single, double),
+            "deal",
+            pieces[1][:2],
+            (token, fed[order[1]][1]),
+        )
+        other[order[2]] = exchange(token, 1), exchange(far_own, 1)
+        other[order[3]] = (exchange(both, 1),)
 
     def pause(_):
         nonlocal token
@@ -340,7 +365,7 @@
             functools.partial(finish_body, first[g]),
             half,
             "finish",
-            (*emb(g)[:2], summed[g], far[g]),
+            (*pieces[0 if g in plan[0] else 1][:2], summed[g], far[g]),
             (token, *{order[0]: (next_q,), order[-1]: (behind,)}.get(g, ())),
         )
         encoded[g] = token, exchange(token, 1)
@@ -380,7 +405,7 @@
 
     a, b, c, d = order
     for step, g in (
-        (feed, a), (feed, b), (pause, c), (add, a), (ask, a), (rest, c), (feed, c), (add, b),
+        (feed, a), (feed, b), (add, a), (pause, c), (ask, a), (rest, c), (feed, c), (add, b),
         (finish, a), (feed, d), (add, c),
         (finish, b), (attend, a), (add, d),
         (finish, c), (attend, b),

time: 91.7 us -> 95.9 us (1.046); the launches traced: 91.1 us -> 94.3 us
  starting transfers between devices: 20.1 us -> 22.7 us
    ppermute x16 -> x18, starting transfers between devices: 15.6 us -> 16.9 us  [exchange(): return lax.ppermute(x, 'tp', [(i, i ^ bit) for i in range(size)])]
    ppermute x2, starting transfers between devices: 4.5 us -> 5.73 us  [shifted(): return lax.ppermute(x, 'seq', pairs)]
    ppermute x16 -> x18, waiting for transfers between devices: 9.03 us -> 10 us  [exchange(): return lax.ppermute(x, 'tp', [(i, i ^ bit) for i in range(size)])]
  transfers between devices with their start and end apart: 18 -> 20, of which waited for: 6 -> 5; matrix products, arithmetic and copies ran while one was open for 0% -> 0% of each run, Pallas kernels for 14% -> 12%
where the time goes in v13:
time: 95.9 us; the launch traced here: 94.3 us
  blocking collectives  38.6 us (40%)
  starting transfers between devices  22.7 us (24%)
  Pallas kernels  19.3 us (20%)
  waiting for transfers between devices  12.5 us (13%)
    all_to_all x1, blocking collectives, per_device(): lax.all_to_all(found.reshape(seq_size, cap, width), 'seq', split_axis=0,...  27.1 us
    pallas_call x24, Pallas kernels, call(): pl.pallas_call(without_after, out_shape=outs, in_specs=in_specs + [unread...  19.3 us
    ppermute x18, starting transfers between devices, exchange(): return lax.ppermute(x, 'tp', [(i, i ^ bit) for i in range(size)])  16.9 us
    all_to_all x1, blocking collectives, per_device(): lax.all_to_all(wanted, 'seq', split_axis=0, concat_axis=0, tiled=True)  11.5 us
    ppermute x18, waiting for transfers between devices, exchange(): return lax.ppermute(x, 'tp', [(i, i ^ bit) for i in range(size)])  10 us
    ppermute x2, starting transfers between devices, shifted(): return lax.ppermute(x, 'seq', pairs)  5.73 us
    ppermute x2, waiting for transfers between devices, shifted(): return lax.ppermute(x, 'seq', pairs)  2.5 us
  transfers between devices with their start and end apart: 20, of which 5 were waited for; matrix products, arithmetic and copies ran while one was open for 0% of the time, Pallas kernels for 12%

profile of v13, /device:TPU:1, one launch (start us, length us, event | category | flops | bytes accessed | tf_op | source)
XLA Modules:
  0.0 94.3 jit_solution(3586765972977485466)
XLA Ops:
  1.5 11.5 %all_to_all.14 = s32[8,1,256]{2,1,0:T(1,128)S(1)} all-to-all(s32[8,1,256]{2,1,0:T(1,128)S(1)} %copy.8), channel_id=1, replica_groups=mesh['seq'=8,'tp'=4] {'seq'}, dimensions={0} | all-to-all | bytes 16384 | tf_op jit(solution)/shard_map/all_to_all | solution.py:280
  13.1 2.4 %fetch.1 = bf16[2048,256]{1,0:T(8,128)(2,1)S(1)} custom-call(s32[1,2048]{1,0:T(1,128)S(1)} %bitcast.8, bf16[2048,256]{1,0:T(8,128)(2,1)S(1)} %copy-done.5), custom_call_target="tpu_custom_call" | custom-call | flops 1024 | bytes 1024 | tf_op jit(solution)/shard_map/fetch/pallas_call | solution.py:26
  15.5 27.1 %all_to_all.15 = bf16[8,256,256]{2,1,0:T(8,128)(2,1)S(1)} all-to-all(bf16[8,256,256]{2,1,0:T(8,128)(2,1)S(1)} %bitcast.7), channel_id=1, replica_groups=mesh['seq'=8,'tp'=4] {'seq'}, dimensions={0} | all-to-all | bytes 2097152 | tf_op jit(solution)/shard_map/all_to_all | solution.py:287
  43.3 1.3 %collective-permute-start.1 = (bf16[512,256]{1,0:T(8,128)(2,1)S(1)}, bf16[512,256]{1,0:T(8,128)(2,1)S(1)}, u32[]{:S(2)}, u32[]{:S(2)}) collective-permute-start(bf16[512,256]{1,0:T(8,128)(2,1)S(1)} %order.2.refs_2_.refs_0_), channel_id=1, source_target_pairs={{0,2},{1,3},{2,0},{3,1},{4,6},{5,7},{6,4},{7,5},{8,10},{9,11},{10,... | collective-permute-start | bytes 786440 | tf_op jit(solution)/shard_map/ppermute | solution.py:39
  45.3 3.8 %collective-permute-done.1.refs_1_ = bf16[512,256]{1,0:T(8,128)(2,1)S(1)} collective-permute-done((bf16[512,256]{1,0:T(8,128)(2,1)S(1)}, bf16[512,256]{1,0:T(8,128)(2,1)S(1)}, u32[]{:S(2)}, u32[]{:S(2)}) %collective-permute-start.1) | collective-permute-done | bytes 262176 | tf_op jit(solution)/shard_map/ppermute | solution.py:39
  49.2 3.0 %collective-permute-start.2 = (bf16[512,512]{1,0:T(8,128)(2,1)S(1)}, bf16[512,512]{1,0:T(8,128)(2,1)S(1)}, u32[]{:S(2)}, u32[]{:S(2)}) collective-permute-start(bf16[512,512]{1,0:T(8,128)(2,1)S(1)} %pair.1), channel_id=1, source_target_pairs={{0,1},{1,0},{2,3},{3,2},{4,5},{5,4},{6,7},{7,6},{8,9},{9,8},{10,11... | collective-permute-start | bytes 1572872 | tf_op jit(solution)/shard_map/ppermute | solution.py:39
  52.2 1.5 %collective-permute-done.2.refs_2_ = bf16[512,512]{1,0:T(8,128)(2,1)S(1)} collective-permute-done((bf16[512,512]{1,0:T(8,128)(2,1)S(1)}, bf16[512,512]{1,0:T(8,128)(2,1)S(1)}, u32[]{:S(2)}, u32[]{:S(2)}) %collective-permute-start.2) | collective-permute-done | bytes 524320 | tf_op jit(solution)/shard_map/ppermute | solution.py:39
  53.7 1.6 %feed.4 = (f32[256,512]{1,0:T(8,128)S(1)}, bf16[256,512]{1,0:T(8,128)(2,1)S(1)}) custom-call(bf16[512,256]{1,0:T(8,128)(2,1)S(1)} %order.2.refs_2_.refs_0_, bf16[512,256]{1,0:T(8,128)(2,1)S(1)} %collective-permute-done.1.refs_1_, bf16[512,512]{1,0:T(8,128)(2,1)S(1)} %collective-permute-done.2.refs_2_, bf16[1024,1024]{1,0:T(8,128)(2,1)S(1)} %copy-done, ...), custom_call_target="tpu_custom_call" | custom-call | flops 1024 | bytes 1024 | tf_op jit(solution)/shard_map/feed/pallas_call | solution.py:26
  57.0 1.6 %feed.5 = (f32[256,512]{1,0:T(8,128)S(1)}, bf16[256,512]{1,0:T(8,128)(2,1)S(1)}) custom-call(bf16[512,256]{1,0:T(8,128)(2,1)S(1)} %order.2.refs_2_.refs_0_, bf16[512,256]{1,0:T(8,128)(2,1)S(1)} %collective-permute-done.1.refs_1_, bf16[512,512]{1,0:T(8,128)(2,1)S(1)} %collective-permute-done.2.refs_2_, bf16[1024,1024]{1,0:T(8,128)(2,1)S(1)} %copy-done, ...), custom_call_target="tpu_custom_call" | custom-call | flops 1024 | bytes 1024 | tf_op jit(solution)/shard_map/feed/pallas_call | solution.py:26
  59.5 4.0 %collective-permute-done.refs_1_ = bf16[512,256]{1,0:T(8,128)(2,1)S(1)} collective-permute-done((bf16[512,256]{1,0:T(8,128)(2,1)S(1)}, bf16[512,256]{1,0:T(8,128)(2,1)S(1)}, u32[]{:S(2)}, u32[]{:S(2)}) %collective-permute-start) | collective-permute-done | bytes 262176 | tf_op jit(solution)/shard_map/ppermute | solution.py:39
  63.6 1.6 %collective-permute-start.5 = (bf16[256,512]{1,0:T(8,128)(2,1)S(1)}, bf16[256,512]{1,0:T(8,128)(2,1)S(1)}, u32[]{:S(2)}, u32[]{:S(2)}) collective-permute-start(bf16[256,512]{1,0:T(8,128)(2,1)S(1)} %get-tuple-element.32), channel_id=1, source_target_pairs={{0,1},{1,0},{2,3},{3,2},{4,5},{5,4},{6,7},{7,6},{8,9},{9,8},{10,11... | collective-permute-start | bytes 786440 | tf_op jit(solution)/shard_map/ppermute | solution.py:39
  65.7 1.3 %collective-permute-start.9 = (bf16[64,1024]{1,0:T(8,128)(2,1)S(1)}, bf16[64,1024]{1,0:T(8,128)(2,1)S(1)}, u32[]{:S(2)}, u32[]{:S(2)}) collective-permute-start(bf16[64,1024]{1,0:T(8,128)(2,1)S(1)} %head.1), channel_id=1, source_target_pairs={{4,0},{8,4},{12,8},{16,12},{20,16},{24,20},{28,24},{5,1},{9,5},{13... | collective-permute-start | bytes 393224 | tf_op jit(solution)/shard_map/ppermute | solution.py:45
  67.0 1.6 %feed.6 = (f32[256,512]{1,0:T(8,128)S(1)}, bf16[256,512]{1,0:T(8,128)(2,1)S(1)}) custom-call(bf16[512,256]{1,0:T(8,128)(2,1)S(1)} %order.3.refs_2_.refs_5_.refs_0_, bf16[512,256]{1,0:T(8,128)(2,1)S(1)} %collective-permute-done.refs_1_, bf16[256,256]{1,0:T(8,128)(2,1)S(1)} %collective-permute-done.7.refs_2_, ...), custom_call_target="tpu_custom_call" | custom-call | flops 1024 | bytes 1024 | tf_op jit(solution)/shard_map/feed/pallas_call | solution.py:26
  68.8 1.3 %collective-permute-start.12 = (bf16[256,512]{1,0:T(8,128)(2,1)S(1)}, bf16[256,512]{1,0:T(8,128)(2,1)S(1)}, u32[]{:S(2)}, u32[]{:S(2)}) collective-permute-start(bf16[256,512]{1,0:T(8,128)(2,1)S(1)} %get-tuple-element.38.refs_4_), channel_id=1, source_target_pairs={{0,2},{1,3},{2,0},{3,1},{4,6},{5,7},{6,4},{7,5},{8,10},{9,11},{10,... | collective-permute-start | bytes 786440 | tf_op jit(solution)/shard_map/ppermute | solution.py:39
  70.2 2.5 %collective-permute-done.9.refs_5_ = bf16[64,1024]{1,0:T(8,128)(2,1)S(1)} collective-permute-done((bf16[64,1024]{1,0:T(8,128)(2,1)S(1)}, bf16[64,1024]{1,0:T(8,128)(2,1)S(1)}, u32[]{:S(2)}, u32[]{:S(2)}) %collective-permute-start.9) | collective-permute-done | bytes 131104 | tf_op jit(solution)/shard_map/ppermute | solution.py:45
  73.7 1.6 %feed.7 = (f32[256,512]{1,0:T(8,128)S(1)}, bf16[256,512]{1,0:T(8,128)(2,1)S(1)}) custom-call(bf16[512,256]{1,0:T(8,128)(2,1)S(1)} %order.3.refs_2_.refs_5_.refs_0_, bf16[512,256]{1,0:T(8,128)(2,1)S(1)} %collective-permute-done.refs_1_, bf16[256,512]{1,0:T(8,128)(2,1)S(1)} %collective-permute-done.5.refs_2_, bf16[1024,1024]{1,0:T(8,128)(2,1)S(1)} %copy-done, ...), custom_call_target="tpu_custom_call" | custom-call | flops 1024 | bytes 1024 | tf_op jit(solution)/shard_map/feed/pallas_call | solution.py:26
  75.5 1.3 %collective-permute-start.16 = (bf16[256,512]{1,0:T(8,128)(2,1)S(1)}, bf16[256,512]{1,0:T(8,128)(2,1)S(1)}, u32[]{:S(2)}, u32[]{:S(2)}) collective-permute-start(bf16[256,512]{1,0:T(8,128)(2,1)S(1)} %get-tuple-element.43.refs_4_), channel_id=1, source_target_pairs={{0,2},{1,3},{2,0},{3,1},{4,6},{5,7},{6,4},{7,5},{8,10},{9,11},{10,... | collective-permute-start | bytes 786440 | tf_op jit(solution)/shard_map/ppermute | solution.py:39
  77.8 1.7 %attend_first.1.refs_2_.refs_8_ = bf16[64,1024]{1,0:T(8,128)(2,1)S(1)} custom-call(bf16[256,512]{1,0:T(8,128)(2,1)S(1)} %finish.4.refs_5_.refs_0_, bf16[256,512]{1,0:T(8,128)(2,1)S(1)} %collective-permute-done.11.refs_1_, bf16[1024,1024]{1,0:T(8,128)(2,1)S(1)} %copy-done.2, bf16[1024,1024]{1,0:T(8,128)(2,1)S(1)} %copy-done.3, ...), custom_call_target="tpu_custom_call" | custom-call | flops 1024 | bytes 1024 | tf_op jit(solution)/shard_map/attend_first/pallas_call | solution.py:26
  79.6 1.3 %collective-permute-start.14 = (bf16[256,512]{1,0:T(8,128)(2,1)S(1)}, bf16[256,512]{1,0:T(8,128)(2,1)S(1)}, u32[]{:S(2)}, u32[]{:S(2)}) collective-permute-start(bf16[256,512]{1,0:T(8,128)(2,1)S(1)} %get-tuple-element.45.refs_4_), channel_id=1, source_target_pairs={{0,2},{1,3},{2,0},{3,1},{4,6},{5,7},{6,4},{7,5},{8,10},{9,11},{10,... | collective-permute-start | bytes 786440 | tf_op jit(solution)/shard_map/ppermute | solution.py:39
  80.9 4.4 %collective-permute-start.17 = (bf16[64,1024]{1,0:T(8,128)(2,1)S(1)}, bf16[64,1024]{1,0:T(8,128)(2,1)S(1)}, u32[]{:S(2)}, u32[]{:S(2)}) collective-permute-start(bf16[64,1024]{1,0:T(8,128)(2,1)S(1)} %attend_first.1.refs_2_.refs_8_), channel_id=1, source_target_pairs={{0,4},{4,8},{8,12},{12,16},{16,20},{20,24},{24,28},{1,5},{5,9},{9,... | collective-permute-start | bytes 393224 | tf_op jit(solution)/shard_map/ppermute | solution.py:45
  86.2 1.7 %attend.2.refs_4_.refs_6_ = bf16[64,1024]{1,0:T(8,128)(2,1)S(1)} custom-call(bf16[256,512]{1,0:T(8,128)(2,1)S(1)} %finish.5.refs_6_.refs_0_, bf16[256,512]{1,0:T(8,128)(2,1)S(1)} %collective-permute-done.15.refs_1_, bf16[1024,1024]{1,0:T(8,128)(2,1)S(1)} %copy-done.2, bf16[1024,1024]{1,0:T(8,128)(2,1)S(1)} %copy-done.3, ...), custom_call_target="tpu_custom_call" | custom-call | flops 1024 | bytes 1024 | tf_op jit(solution)/shard_map/attend/pallas_call | solution.py:26
  88.6 1.4 %collective-permute-start.18 = (bf16[256,512]{1,0:T(8,128)(2,1)S(1)}, bf16[256,512]{1,0:T(8,128)(2,1)S(1)}, u32[]{:S(2)}, u32[]{:S(2)}) collective-permute-start(bf16[256,512]{1,0:T(8,128)(2,1)S(1)} %finish.7.refs_5_.refs_0_), channel_id=1, source_target_pairs={{0,1},{1,0},{2,3},{3,2},{4,5},{5,4},{6,7},{7,6},{8,9},{9,8},{10,11... | collective-permute-start | bytes 786440 | tf_op jit(solution)/shard_map/ppermute | solution.py:39
  90.0 1.7 %attend.3.refs_7_ = bf16[64,1024]{1,0:T(8,128)(2,1)S(1)} custom-call(bf16[256,512]{1,0:T(8,128)(2,1)S(1)} %finish.6.refs_5_.refs_0_, bf16[256,512]{1,0:T(8,128)(2,1)S(1)} %collective-permute-done.19.refs_1_, bf16[1024,1024]{1,0:T(8,128)(2,1)S(1)} %copy-done.2, bf16[1024,1024]{1,0:T(8,128)(2,1)S(1)} %copy-done.3, ...), custom_call_target="tpu_custom_call" | custom-call | flops 1024 | bytes 1024 | tf_op jit(solution)/shard_map/attend/pallas_call | solution.py:26
  91.7 2.6 %attend_last.1 = bf16[256,1024]{1,0:T(8,128)(2,1)} custom-call(bf16[256,512]{1,0:T(8,128)(2,1)S(1)} %finish.7.refs_5_.refs_0_, bf16[256,512]{1,0:T(8,128)(2,1)S(1)} %collective-permute-done.18.refs_1_, bf16[1024,1024]{1,0:T(8,128)(2,1)S(1)} %copy-done.2, bf16[1024,1024]{1,0:T(8,128)(2,1)S(1)} %copy-done.3, bf16[64,1024]{1,0:T(8,128)(2,1)S(1)} %get-tuple-element.49.refs_4_, ...), custom_call_target="tpu_custom_call" | custom-call | flops 1024 | bytes 1024 | tf_op jit(solution)/shard_map/attend_last/pallas_call | solution.py:26
  (58 shorter events, 10.2 us)
Async XLA Ops:
  0.7 12.4 %copy-start.5 = (bf16[2048,256]{1,0:T(8,128)(2,1)S(1)}, bf16[2048,256]{1,0:T(8,128)(2,1)}, u32[]{:S(2)}) copy-start(bf16[2048,256]{1,0:T(8,128)(2,1)} %refs_1_.1) | copy-start | bytes 3145732
  42.6 11.2 %copy-start.1 = (bf16[1024,1024]{1,0:T(8,128)(2,1)S(1)}, bf16[1024,1024]{1,0:T(8,128)(2,1)}, u32[]{:S(2)}) copy-start(bf16[1024,1024]{1,0:T(8,128)(2,1)} %refs_4_.8) | copy-start | bytes 6291460
  43.3 10.4 %copy-start = (bf16[1024,1024]{1,0:T(8,128)(2,1)S(1)}, bf16[1024,1024]{1,0:T(8,128)(2,1)}, u32[]{:S(2)}) copy-start(bf16[1024,1024]{1,0:T(8,128)(2,1)} %refs_3_.9) | copy-start | bytes 6291460
  43.3 5.8 %collective-permute-start.1 = (bf16[512,256]{1,0:T(8,128)(2,1)S(1)}, bf16[512,256]{1,0:T(8,128)(2,1)S(1)}, u32[]{:S(2)}, u32[]{:S(2)}) collective-permute-start(bf16[512,256]{1,0:T(8,128)(2,1)S(1)} %order.2.refs_2_.refs_0_), channel_id=1, source_target_pairs={{0,2},{1,3},{2,0},{3,1},{4,6},{5,7},{6,4},{7,5},{8,10},{9,11},{10,... | collective-permute-start | bytes 786440 | tf_op jit(solution)/shard_map/ppermute | solution.py:39
  49.2 4.5 %collective-permute-start.2 = (bf16[512,512]{1,0:T(8,128)(2,1)S(1)}, bf16[512,512]{1,0:T(8,128)(2,1)S(1)}, u32[]{:S(2)}, u32[]{:S(2)}) collective-permute-start(bf16[512,512]{1,0:T(8,128)(2,1)S(1)} %pair.1), channel_id=1, source_target_pairs={{0,1},{1,0},{2,3},{3,2},{4,5},{5,4},{6,7},{7,6},{8,9},{9,8},{10,11... | collective-permute-start | bytes 1572872 | tf_op jit(solution)/shard_map/ppermute | solution.py:39
  55.3 3.8 %collective-permute-start.3 = (bf16[256,512]{1,0:T(8,128)(2,1)S(1)}, bf16[256,512]{1,0:T(8,128)(2,1)S(1)}, u32[]{:S(2)}, u32[]{:S(2)}) collective-permute-start(bf16[256,512]{1,0:T(8,128)(2,1)S(1)} %get-tuple-element.29.refs_5_), channel_id=1, source_target_pairs={{0,1},{1,0},{2,3},{3,2},{4,5},{5,4},{6,7},{7,6},{8,9},{9,8},{10,11... | collective-permute-start | bytes 786440 | tf_op jit(solution)/shard_map/ppermute | solution.py:39
  55.8 7.8 %collective-permute-start = (bf16[512,256]{1,0:T(8,128)(2,1)S(1)}, bf16[512,256]{1,0:T(8,128)(2,1)S(1)}, u32[]{:S(2)}, u32[]{:S(2)}) collective-permute-start(bf16[512,256]{1,0:T(8,128)(2,1)S(1)} %order.3.refs_2_.refs_5_.refs_0_), channel_id=1, source_target_pairs={{0,2},{1,3},{2,0},{3,1},{4,6},{5,7},{6,4},{7,5},{8,10},{9,11},{10,... | collective-permute-start | bytes 786440 | tf_op jit(solution)/shard_map/ppermute | solution.py:39
  58.6 7.1 %copy-start.4 = (bf16[256,1024]{1,0:T(8,128)(2,1)S(1)}, bf16[256,1024]{1,0:T(8,128)(2,1)}, u32[]{:S(2)}) copy-start(bf16[256,1024]{1,0:T(8,128)(2,1)} %refs_4_.9) | copy-start | bytes 1572868
  58.6 4.9 %collective-permute-start.4 = (bf16[256,512]{1,0:T(8,128)(2,1)S(1)}, bf16[256,512]{1,0:T(8,128)(2,1)S(1)}, u32[]{:S(2)}, u32[]{:S(2)}) collective-permute-start(bf16[256,512]{1,0:T(8,128)(2,1)S(1)} %get-tuple-element.30.refs_2_), channel_id=1, source_target_pairs={{0,1},{1,0},{2,3},{3,2},{4,5},{5,4},{6,7},{7,6},{8,9},{9,8},{10,11... | collective-permute-start | bytes 786440 | tf_op jit(solution)/shard_map/ppermute | solution.py:39
  59.2 13.4 %collective-permute-start.6 = (bf16[256,512]{1,0:T(8,128)(2,1)S(1)}, bf16[256,512]{1,0:T(8,128)(2,1)S(1)}, u32[]{:S(2)}, u32[]{:S(2)}) collective-permute-start(bf16[256,512]{1,0:T(8,128)(2,1)S(1)} %get-tuple-element.31.refs_0_), channel_id=1, source_target_pairs={{0,2},{1,3},{2,0},{3,1},{4,6},{5,7},{6,4},{7,5},{8,10},{9,11},{10,... | collective-permute-start | bytes 786440 | tf_op jit(solution)/shard_map/ppermute | solution.py:39
  63.6 10.1 %collective-permute-start.5 = (bf16[256,512]{1,0:T(8,128)(2,1)S(1)}, bf16[256,512]{1,0:T(8,128)(2,1)S(1)}, u32[]{:S(2)}, u32[]{:S(2)}) collective-permute-start(bf16[256,512]{1,0:T(8,128)(2,1)S(1)} %get-tuple-element.32), channel_id=1, source_target_pairs={{0,1},{1,0},{2,3},{3,2},{4,5},{5,4},{6,7},{7,6},{8,9},{9,8},{10,11... | collective-permute-start | bytes 786440 | tf_op jit(solution)/shard_map/ppermute | solution.py:39
  65.2 1.8 %collective-permute-start.7 = (bf16[256,256]{1,0:T(8,128)(2,1)S(1)}, bf16[256,256]{1,0:T(8,128)(2,1)S(1)}, u32[]{:S(2)}, u32[]{:S(2)}) collective-permute-start(bf16[256,256]{1,0:T(8,128)(2,1)S(1)} %get-tuple-element.35.refs_6_), channel_id=1, source_target_pairs={{0,1},{1,0},{2,3},{3,2},{4,5},{5,4},{6,7},{7,6},{8,9},{9,8},{10,11... | collective-permute-start | bytes 393224 | tf_op jit(solution)/shard_map/ppermute | solution.py:39
  65.2 1.8 %collective-permute-start.8 = (bf16[256,256]{1,0:T(8,128)(2,1)S(1)}, bf16[256,256]{1,0:T(8,128)(2,1)S(1)}, u32[]{:S(2)}, u32[]{:S(2)}) collective-permute-start(bf16[256,256]{1,0:T(8,128)(2,1)S(1)} %get-tuple-element.36), channel_id=1, source_target_pairs={{0,1},{1,0},{2,3},{3,2},{4,5},{5,4},{6,7},{7,6},{8,9},{9,8},{10,11... | collective-permute-start | bytes 393224 | tf_op jit(solution)/shard_map/ppermute | solution.py:39
  65.7 7.0 %collective-permute-start.9 = (bf16[64,1024]{1,0:T(8,128)(2,1)S(1)}, bf16[64,1024]{1,0:T(8,128)(2,1)S(1)}, u32[]{:S(2)}, u32[]{:S(2)}) collective-permute-start(bf16[64,1024]{1,0:T(8,128)(2,1)S(1)} %head.1), channel_id=1, source_target_pairs={{4,0},{8,4},{12,8},{16,12},{20,16},{24,20},{28,24},{5,1},{9,5},{13... | collective-permute-start | bytes 393224 | tf_op jit(solution)/shard_map/ppermute | solution.py:45
  68.6 6.8 %collective-permute-start.13 = (bf16[256,512]{1,0:T(8,128)(2,1)S(1)}, bf16[256,512]{1,0:T(8,128)(2,1)S(1)}, u32[]{:S(2)}, u32[]{:S(2)}) collective-permute-start(bf16[256,512]{1,0:T(8,128)(2,1)S(1)} %get-tuple-element.37.refs_2_), channel_id=1, source_target_pairs={{0,1},{1,0},{2,3},{3,2},{4,5},{5,4},{6,7},{7,6},{8,9},{9,8},{10,11... | collective-permute-start | bytes 786440 | tf_op jit(solution)/shard_map/ppermute | solution.py:39
  68.8 7.9 %collective-permute-start.12 = (bf16[256,512]{1,0:T(8,128)(2,1)S(1)}, bf16[256,512]{1,0:T(8,128)(2,1)S(1)}, u32[]{:S(2)}, u32[]{:S(2)}) collective-permute-start(bf16[256,512]{1,0:T(8,128)(2,1)S(1)} %get-tuple-element.38.refs_4_), channel_id=1, source_target_pairs={{0,2},{1,3},{2,0},{3,1},{4,6},{5,7},{6,4},{7,5},{8,10},{9,11},{10,... | collective-permute-start | bytes 786440 | tf_op jit(solution)/shard_map/ppermute | solution.py:39
  72.8 5.0 %collective-permute-start.11 = (bf16[256,512]{1,0:T(8,128)(2,1)S(1)}, bf16[256,512]{1,0:T(8,128)(2,1)S(1)}, u32[]{:S(2)}, u32[]{:S(2)}) collective-permute-start(bf16[256,512]{1,0:T(8,128)(2,1)S(1)} %finish.4.refs_5_.refs_0_), channel_id=1, source_target_pairs={{0,1},{1,0},{2,3},{3,2},{4,5},{5,4},{6,7},{7,6},{8,9},{9,8},{10,11... | collective-permute-start | bytes 786440 | tf_op jit(solution)/shard_map/ppermute | solution.py:39
  75.3 4.2 %collective-permute-start.10 = (bf16[256,512]{1,0:T(8,128)(2,1)S(1)}, bf16[256,512]{1,0:T(8,128)(2,1)S(1)}, u32[]{:S(2)}, u32[]{:S(2)}) collective-permute-start(bf16[256,512]{1,0:T(8,128)(2,1)S(1)} %get-tuple-element.40.refs_2_), channel_id=1, source_target_pairs={{0,1},{1,0},{2,3},{3,2},{4,5},{5,4},{6,7},{7,6},{8,9},{9,8},{10,11... | collective-permute-start | bytes 786440 | tf_op jit(solution)/shard_map/ppermute | solution.py:39
  75.5 10.0 %collective-permute-start.16 = (bf16[256,512]{1,0:T(8,128)(2,1)S(1)}, bf16[256,512]{1,0:T(8,128)(2,1)S(1)}, u32[]{:S(2)}, u32[]{:S(2)}) collective-permute-start(bf16[256,512]{1,0:T(8,128)(2,1)S(1)} %get-tuple-element.43.refs_4_), channel_id=1, source_target_pairs={{0,2},{1,3},{2,0},{3,1},{4,6},{5,7},{6,4},{7,5},{8,10},{9,11},{10,... | collective-permute-start | bytes 786440 | tf_op jit(solution)/shard_map/ppermute | solution.py:39
  76.9 9.3 %collective-permute-start.15 = (bf16[256,512]{1,0:T(8,128)(2,1)S(1)}, bf16[256,512]{1,0:T(8,128)(2,1)S(1)}, u32[]{:S(2)}, u32[]{:S(2)}) collective-permute-start(bf16[256,512]{1,0:T(8,128)(2,1)S(1)} %finish.5.refs_6_.refs_0_), channel_id=1, source_target_pairs={{0,1},{1,0},{2,3},{3,2},{4,5},{5,4},{6,7},{7,6},{8,9},{9,8},{10,11... | collective-permute-start | bytes 786440 | tf_op jit(solution)/shard_map/ppermute | solution.py:39
  79.6 9.0 %collective-permute-start.14 = (bf16[256,512]{1,0:T(8,128)(2,1)S(1)}, bf16[256,512]{1,0:T(8,128)(2,1)S(1)}, u32[]{:S(2)}, u32[]{:S(2)}) collective-permute-start(bf16[256,512]{1,0:T(8,128)(2,1)S(1)} %get-tuple-element.45.refs_4_), channel_id=1, source_target_pairs={{0,2},{1,3},{2,0},{3,1},{4,6},{5,7},{6,4},{7,5},{8,10},{9,11},{10,... | collective-permute-start | bytes 786440 | tf_op jit(solution)/shard_map/ppermute | solution.py:39
  80.9 7.0 %collective-permute-start.17 = (bf16[64,1024]{1,0:T(8,128)(2,1)S(1)}, bf16[64,1024]{1,0:T(8,128)(2,1)S(1)}, u32[]{:S(2)}, u32[]{:S(2)}) collective-permute-start(bf16[64,1024]{1,0:T(8,128)(2,1)S(1)} %attend_first.1.refs_2_.refs_8_), channel_id=1, source_target_pairs={{0,4},{4,8},{8,12},{12,16},{16,20},{20,24},{24,28},{1,5},{5,9},{9,... | collective-permute-start | bytes 393224 | tf_op jit(solution)/shard_map/ppermute | solution.py:45
  85.6 4.5 %collective-permute-start.19 = (bf16[256,512]{1,0:T(8,128)(2,1)S(1)}, bf16[256,512]{1,0:T(8,128)(2,1)S(1)}, u32[]{:S(2)}, u32[]{:S(2)}) collective-permute-start(bf16[256,512]{1,0:T(8,128)(2,1)S(1)} %finish.6.refs_5_.refs_0_), channel_id=1, source_target_pairs={{0,1},{1,0},{2,3},{3,2},{4,5},{5,4},{6,7},{7,6},{8,9},{9,8},{10,11... | collective-permute-start | bytes 786440 | tf_op jit(solution)/shard_map/ppermute | solution.py:39
  88.6 3.1 %collective-permute-start.18 = (bf16[256,512]{1,0:T(8,128)(2,1)S(1)}, bf16[256,512]{1,0:T(8,128)(2,1)S(1)}, u32[]{:S(2)}, u32[]{:S(2)}) collective-permute-start(bf16[256,512]{1,0:T(8,128)(2,1)S(1)} %finish.7.refs_5_.refs_0_), channel_id=1, source_target_pairs={{0,1},{1,0},{2,3},{3,2},{4,5},{5,4},{6,7},{7,6},{8,9},{9,8},{10,11... | collective-permute-start | bytes 786440 | tf_op jit(solution)/shard_map/ppermute | solution.py:39
  (3 other events, 7.3 us)

commit v14 on v11

--- a/solution.py
+++ b/solution.py
@@ -232,7 +232,8 @@
 def attend_last_body(
     mine_ref, other_ref, w_key_ref, w_value_ref, q_ref, behind_ref, *refs
 ):
-    before, last_ref, out_ref = refs[:-2], refs[-2], refs[-1]
+    before, (last_ref, out_hbm, out_ref, sems) = refs[:-4], refs[-4:]
+    copies = []
     parts = attended(mine_ref, other_ref, w_key_ref, w_value_ref, q_ref)
     for at, part in enumerate(parts):
         cols = slice(at * HEAD_WIDTH, (at + 1) * HEAD_WIDTH)
@@ -243,6 +244,11 @@
         tall = jnp.concatenate(stack, axis=0)
         moved = pltpu.roll(tall, tall.shape[0] - 1, 0)
         out_ref[:, cols] = moved[: out_ref.shape[0]].astype(BF16)
+        copy = pltpu.make_async_copy(out_ref.at[:, cols], out_hbm.at[:, cols], sems.at[at])
+        copy.start()
+        copies.append(copy)
+    for copy in copies:
+        copy.wait()
 
 
 def per_device(queries, vocab_rows, neighbour_ids, w_in, w_out, w_key, w_value):
@@ -368,6 +374,11 @@
                 sds((tok, head_cols), BF16),
                 "attend_last",
                 (*args, behind, *before, window[order[0]]),
+                out_specs=pl.BlockSpec(memory_space=pl.ANY),
+                scratch_shapes=[
+                    pltpu.VMEM((tok, head_cols), BF16),
+                    pltpu.SemaphoreType.DMA((head_cols // HEAD_WIDTH,)),
+                ],
             )
             return
         window[g] = token = call(

time: 91.7 us -> 91.8 us (level)
  no operation moved by 1% of the time
where the time goes in v14:
time: 91.8 us; the launch traced here: 91.2 us
  blocking collectives  38.6 us (42%)
  starting transfers between devices  20.1 us (22%)
  Pallas kernels  19.3 us (21%)
  waiting for transfers between devices  12 us (13%)
    all_to_all x1, blocking collectives, per_device(): lax.all_to_all(found.reshape(seq_size, cap, width), 'seq', split_axis=0,...  27.1 us
    pallas_call x24, Pallas kernels, call(): pl.pallas_call(without_after, out_shape=outs, in_specs=in_specs + [unread...  19.3 us
    ppermute x16, starting transfers between devices, exchange(): return lax.ppermute(x, 'tp', [(i, i ^ bit) for i in range(size)])  15.6 us
    all_to_all x1, blocking collectives, per_device(): lax.all_to_all(wanted, 'seq', split_axis=0, concat_axis=0, tiled=True)  11.5 us
    ppermute x16, waiting for transfers between devices, exchange(): return lax.ppermute(x, 'tp', [(i, i ^ bit) for i in range(size)])  9.03 us
    ppermute x2, starting transfers between devices, shifted(): return lax.ppermute(x, 'seq', pairs)  4.5 us
    ppermute x2, waiting for transfers between devices, shifted(): return lax.ppermute(x, 'seq', pairs)  2.93 us
  transfers between devices with their start and end apart: 18, of which 6 were waited for; matrix products, arithmetic and copies ran while one was open for 0% of the time, Pallas kernels for 14%

profile of v14, /device:TPU:1, one launch (start us, length us, event | category | flops | bytes accessed | tf_op | source)
XLA Modules:
  0.0 91.2 jit_solution(4823164609345299266)
XLA Ops:
  1.5 11.5 %all_to_all.14 = s32[8,1,256]{2,1,0:T(1,128)S(1)} all-to-all(s32[8,1,256]{2,1,0:T(1,128)S(1)} %copy.8), channel_id=1, replica_groups=mesh['seq'=8,'tp'=4] {'seq'}, dimensions={0} | all-to-all | bytes 16384 | tf_op jit(solution)/shard_map/all_to_all | solution.py:272
  13.1 2.4 %fetch.1 = bf16[2048,256]{1,0:T(8,128)(2,1)S(1)} custom-call(s32[1,2048]{1,0:T(1,128)S(1)} %bitcast.8, bf16[2048,256]{1,0:T(8,128)(2,1)S(1)} %copy-done.5), custom_call_target="tpu_custom_call" | custom-call | flops 1024 | bytes 1024 | tf_op jit(solution)/shard_map/fetch/pallas_call | solution.py:26
  15.5 27.1 %all_to_all.15 = bf16[8,256,256]{2,1,0:T(8,128)(2,1)S(1)} all-to-all(bf16[8,256,256]{2,1,0:T(8,128)(2,1)S(1)} %bitcast.7), channel_id=1, replica_groups=mesh['seq'=8,'tp'=4] {'seq'}, dimensions={0} | all-to-all | bytes 2097152 | tf_op jit(solution)/shard_map/all_to_all | solution.py:279
  43.3 1.3 %collective-permute-start.1 = (bf16[512,256]{1,0:T(8,128)(2,1)S(1)}, bf16[512,256]{1,0:T(8,128)(2,1)S(1)}, u32[]{:S(2)}, u32[]{:S(2)}) collective-permute-start(bf16[512,256]{1,0:T(8,128)(2,1)S(1)} %order.2.refs_2_.refs_0_), channel_id=1, source_target_pairs={{0,2},{1,3},{2,0},{3,1},{4,6},{5,7},{6,4},{7,5},{8,10},{9,11},{10,... | collective-permute-start | bytes 786440 | tf_op jit(solution)/shard_map/ppermute | solution.py:39
  45.3 3.8 %collective-permute-done.1.refs_1_ = bf16[512,256]{1,0:T(8,128)(2,1)S(1)} collective-permute-done((bf16[512,256]{1,0:T(8,128)(2,1)S(1)}, bf16[512,256]{1,0:T(8,128)(2,1)S(1)}, u32[]{:S(2)}, u32[]{:S(2)}) %collective-permute-start.1) | collective-permute-done | bytes 262176 | tf_op jit(solution)/shard_map/ppermute | solution.py:39
  49.2 3.0 %collective-permute-start.2 = (bf16[512,512]{1,0:T(8,128)(2,1)S(1)}, bf16[512,512]{1,0:T(8,128)(2,1)S(1)}, u32[]{:S(2)}, u32[]{:S(2)}) collective-permute-start(bf16[512,512]{1,0:T(8,128)(2,1)S(1)} %pair.2), channel_id=1, source_target_pairs={{0,1},{1,0},{2,3},{3,2},{4,5},{5,4},{6,7},{7,6},{8,9},{9,8},{10,11... | collective-permute-start | bytes 1572872 | tf_op jit(solution)/shard_map/ppermute | solution.py:39
  52.2 1.3 %collective-permute-start = (bf16[512,256]{1,0:T(8,128)(2,1)S(1)}, bf16[512,256]{1,0:T(8,128)(2,1)S(1)}, u32[]{:S(2)}, u32[]{:S(2)}) collective-permute-start(bf16[512,256]{1,0:T(8,128)(2,1)S(1)} %order.3.refs_2_.refs_5_.refs_0_), channel_id=1, source_target_pairs={{0,2},{1,3},{2,0},{3,1},{4,6},{5,7},{6,4},{7,5},{8,10},{9,11},{10,... | collective-permute-start | bytes 786440 | tf_op jit(solution)/shard_map/ppermute | solution.py:39
  53.7 1.6 %feed.4 = (f32[256,512]{1,0:T(8,128)S(1)}, bf16[256,512]{1,0:T(8,128)(2,1)S(1)}) custom-call(bf16[512,256]{1,0:T(8,128)(2,1)S(1)} %order.2.refs_2_.refs_0_, bf16[512,256]{1,0:T(8,128)(2,1)S(1)} %collective-permute-done.1.refs_1_, bf16[512,512]{1,0:T(8,128)(2,1)S(1)} %collective-permute-done.2.refs_2_, bf16[1024,1024]{1,0:T(8,128)(2,1)S(1)} %copy-done, ...), custom_call_target="tpu_custom_call" | custom-call | flops 1024 | bytes 1024 | tf_op jit(solution)/shard_map/feed/pallas_call | solution.py:26
  55.8 1.6 %feed.5 = (f32[256,512]{1,0:T(8,128)S(1)}, bf16[256,512]{1,0:T(8,128)(2,1)S(1)}) custom-call(bf16[512,256]{1,0:T(8,128)(2,1)S(1)} %order.2.refs_2_.refs_0_, bf16[512,256]{1,0:T(8,128)(2,1)S(1)} %collective-permute-done.1.refs_1_, bf16[512,512]{1,0:T(8,128)(2,1)S(1)} %collective-permute-done.2.refs_2_, bf16[1024,1024]{1,0:T(8,128)(2,1)S(1)} %copy-done, ...), custom_call_target="tpu_custom_call" | custom-call | flops 1024 | bytes 1024 | tf_op jit(solution)/shard_map/feed/pallas_call | solution.py:26
  57.6 2.5 %collective-permute-done.refs_1_ = bf16[512,256]{1,0:T(8,128)(2,1)S(1)} collective-permute-done((bf16[512,256]{1,0:T(8,128)(2,1)S(1)}, bf16[512,256]{1,0:T(8,128)(2,1)S(1)}, u32[]{:S(2)}, u32[]{:S(2)}) %collective-permute-start) | collective-permute-done | bytes 262176 | tf_op jit(solution)/shard_map/ppermute | solution.py:39
  61.1 1.3 %collective-permute-start.6 = (bf16[256,512]{1,0:T(8,128)(2,1)S(1)}, bf16[256,512]{1,0:T(8,128)(2,1)S(1)}, u32[]{:S(2)}, u32[]{:S(2)}) collective-permute-start(bf16[256,512]{1,0:T(8,128)(2,1)S(1)} %get-tuple-element.28.refs_2_.refs_1_), channel_id=1, source_target_pairs={{0,2},{1,3},{2,0},{3,1},{4,6},{5,7},{6,4},{7,5},{8,10},{9,11},{10,... | collective-permute-start | bytes 786440 | tf_op jit(solution)/shard_map/ppermute | solution.py:39
  62.4 1.3 %collective-permute-start.7 = (bf16[64,1024]{1,0:T(8,128)(2,1)S(1)}, bf16[64,1024]{1,0:T(8,128)(2,1)S(1)}, u32[]{:S(2)}, u32[]{:S(2)}) collective-permute-start(bf16[64,1024]{1,0:T(8,128)(2,1)S(1)} %head.1), channel_id=1, source_target_pairs={{4,0},{8,4},{12,8},{16,12},{20,16},{24,20},{28,24},{5,1},{9,5},{13... | collective-permute-start | bytes 393224 | tf_op jit(solution)/shard_map/ppermute | solution.py:45
  63.7 1.6 %feed.6 = (f32[256,512]{1,0:T(8,128)S(1)}, bf16[256,512]{1,0:T(8,128)(2,1)S(1)}) custom-call(bf16[512,256]{1,0:T(8,128)(2,1)S(1)} %order.3.refs_2_.refs_5_.refs_0_, bf16[512,256]{1,0:T(8,128)(2,1)S(1)} %collective-permute-done.refs_1_, bf16[512,512]{1,0:T(8,128)(2,1)S(1)} %collective-permute-done.5.refs_2_, bf16[1024,1024]{1,0:T(8,128)(2,1)S(1)} %copy-done, ...), custom_call_target="tpu_custom_call" | custom-call | flops 1024 | bytes 1024 | tf_op jit(solution)/shard_map/feed/pallas_call | solution.py:26
  66.1 2.9 %collective-permute-done.7.refs_5_ = bf16[64,1024]{1,0:T(8,128)(2,1)S(1)} collective-permute-done((bf16[64,1024]{1,0:T(8,128)(2,1)S(1)}, bf16[64,1024]{1,0:T(8,128)(2,1)S(1)}, u32[]{:S(2)}, u32[]{:S(2)}) %collective-permute-start.7) | collective-permute-done | bytes 131104 | tf_op jit(solution)/shard_map/ppermute | solution.py:45
  69.1 1.3 %collective-permute-start.9 = (bf16[256,512]{1,0:T(8,128)(2,1)S(1)}, bf16[256,512]{1,0:T(8,128)(2,1)S(1)}, u32[]{:S(2)}, u32[]{:S(2)}) collective-permute-start(bf16[256,512]{1,0:T(8,128)(2,1)S(1)} %finish.4.refs_5_.refs_0_), channel_id=1, source_target_pairs={{0,1},{1,0},{2,3},{3,2},{4,5},{5,4},{6,7},{7,6},{8,9},{9,8},{10,11... | collective-permute-start | bytes 786440 | tf_op jit(solution)/shard_map/ppermute | solution.py:39
  70.5 1.6 %feed.7 = (f32[256,512]{1,0:T(8,128)S(1)}, bf16[256,512]{1,0:T(8,128)(2,1)S(1)}) custom-call(bf16[512,256]{1,0:T(8,128)(2,1)S(1)} %order.3.refs_2_.refs_5_.refs_0_, bf16[512,256]{1,0:T(8,128)(2,1)S(1)} %collective-permute-done.refs_1_, bf16[512,512]{1,0:T(8,128)(2,1)S(1)} %collective-permute-done.5.refs_2_, bf16[1024,1024]{1,0:T(8,128)(2,1)S(1)} %copy-done, ...), custom_call_target="tpu_custom_call" | custom-call | flops 1024 | bytes 1024 | tf_op jit(solution)/shard_map/feed/pallas_call | solution.py:26
  72.3 1.3 %collective-permute-start.14 = (bf16[256,512]{1,0:T(8,128)(2,1)S(1)}, bf16[256,512]{1,0:T(8,128)(2,1)S(1)}, u32[]{:S(2)}, u32[]{:S(2)}) collective-permute-start(bf16[256,512]{1,0:T(8,128)(2,1)S(1)} %get-tuple-element.37.refs_4_), channel_id=1, source_target_pairs={{0,2},{1,3},{2,0},{3,1},{4,6},{5,7},{6,4},{7,5},{8,10},{9,11},{10,... | collective-permute-start | bytes 786440 | tf_op jit(solution)/shard_map/ppermute | solution.py:39
  75.7 1.7 %attend_first.1.refs_2_.refs_8_ = bf16[64,1024]{1,0:T(8,128)(2,1)S(1)} custom-call(bf16[256,512]{1,0:T(8,128)(2,1)S(1)} %finish.4.refs_5_.refs_0_, bf16[256,512]{1,0:T(8,128)(2,1)S(1)} %collective-permute-done.9.refs_1_, bf16[1024,1024]{1,0:T(8,128)(2,1)S(1)} %copy-done.2, bf16[1024,1024]{1,0:T(8,128)(2,1)S(1)} %copy-done.3, ...), custom_call_target="tpu_custom_call" | custom-call | flops 1024 | bytes 1024 | tf_op jit(solution)/shard_map/attend_first/pallas_call | solution.py:26
  77.5 1.3 %collective-permute-start.12 = (bf16[256,512]{1,0:T(8,128)(2,1)S(1)}, bf16[256,512]{1,0:T(8,128)(2,1)S(1)}, u32[]{:S(2)}, u32[]{:S(2)}) collective-permute-start(bf16[256,512]{1,0:T(8,128)(2,1)S(1)} %get-tuple-element.39.refs_4_), channel_id=1, source_target_pairs={{0,2},{1,3},{2,0},{3,1},{4,6},{5,7},{6,4},{7,5},{8,10},{9,11},{10,... | collective-permute-start | bytes 786440 | tf_op jit(solution)/shard_map/ppermute | solution.py:39
  78.8 3.2 %collective-permute-start.15 = (bf16[64,1024]{1,0:T(8,128)(2,1)S(1)}, bf16[64,1024]{1,0:T(8,128)(2,1)S(1)}, u32[]{:S(2)}, u32[]{:S(2)}) collective-permute-start(bf16[64,1024]{1,0:T(8,128)(2,1)S(1)} %attend_first.1.refs_2_.refs_8_), channel_id=1, source_target_pairs={{0,4},{4,8},{8,12},{12,16},{16,20},{20,24},{24,28},{1,5},{5,9},{9,... | collective-permute-start | bytes 393224 | tf_op jit(solution)/shard_map/ppermute | solution.py:45
  82.8 1.7 %attend.2.refs_4_.refs_6_ = bf16[64,1024]{1,0:T(8,128)(2,1)S(1)} custom-call(bf16[256,512]{1,0:T(8,128)(2,1)S(1)} %finish.5.refs_6_.refs_0_, bf16[256,512]{1,0:T(8,128)(2,1)S(1)} %collective-permute-done.13.refs_1_, bf16[1024,1024]{1,0:T(8,128)(2,1)S(1)} %copy-done.2, bf16[1024,1024]{1,0:T(8,128)(2,1)S(1)} %copy-done.3, ...), custom_call_target="tpu_custom_call" | custom-call | flops 1024 | bytes 1024 | tf_op jit(solution)/shard_map/attend/pallas_call | solution.py:26
  84.5 1.4 %collective-permute-done.12.refs_3_ = bf16[256,512]{1,0:T(8,128)(2,1)S(1)} collective-permute-done((bf16[256,512]{1,0:T(8,128)(2,1)S(1)}, bf16[256,512]{1,0:T(8,128)(2,1)S(1)}, u32[]{:S(2)}, u32[]{:S(2)}) %collective-permute-start.12) | collective-permute-done | bytes 262176 | tf_op jit(solution)/shard_map/ppermute | solution.py:39
  86.9 1.7 %attend.3.refs_7_ = bf16[64,1024]{1,0:T(8,128)(2,1)S(1)} custom-call(bf16[256,512]{1,0:T(8,128)(2,1)S(1)} %finish.6.refs_5_.refs_0_, bf16[256,512]{1,0:T(8,128)(2,1)S(1)} %collective-permute-done.17.refs_1_, bf16[1024,1024]{1,0:T(8,128)(2,1)S(1)} %copy-done.2, bf16[1024,1024]{1,0:T(8,128)(2,1)S(1)} %copy-done.3, ...), custom_call_target="tpu_custom_call" | custom-call | flops 1024 | bytes 1024 | tf_op jit(solution)/shard_map/attend/pallas_call | solution.py:26
  88.6 2.5 %attend_last.1 = bf16[256,1024]{1,0:T(8,128)(2,1)} custom-call(bf16[256,512]{1,0:T(8,128)(2,1)S(1)} %finish.7.refs_5_.refs_0_, bf16[256,512]{1,0:T(8,128)(2,1)S(1)} %collective-permute-done.16.refs_1_, bf16[1024,1024]{1,0:T(8,128)(2,1)S(1)} %copy-done.2, bf16[1024,1024]{1,0:T(8,128)(2,1)S(1)} %copy-done.3, bf16[64,1024]{1,0:T(8,128)(2,1)S(1)} %get-tuple-element.43.refs_4_, ...), custom_call_target="tpu_custom_call" | custom-call | flops 1024 | bytes 1024 | tf_op jit(solution)/shard_map/attend_last/pallas_call | solution.py:26
  (54 shorter events, 10.0 us)
Async XLA Ops:
  0.7 12.4 %copy-start.5 = (bf16[2048,256]{1,0:T(8,128)(2,1)S(1)}, bf16[2048,256]{1,0:T(8,128)(2,1)}, u32[]{:S(2)}) copy-start(bf16[2048,256]{1,0:T(8,128)(2,1)} %refs_1_.1) | copy-start | bytes 3145732
  42.6 11.2 %copy-start.1 = (bf16[1024,1024]{1,0:T(8,128)(2,1)S(1)}, bf16[1024,1024]{1,0:T(8,128)(2,1)}, u32[]{:S(2)}) copy-start(bf16[1024,1024]{1,0:T(8,128)(2,1)} %refs_4_.8) | copy-start | bytes 6291460
  43.3 10.4 %copy-start = (bf16[1024,1024]{1,0:T(8,128)(2,1)S(1)}, bf16[1024,1024]{1,0:T(8,128)(2,1)}, u32[]{:S(2)}) copy-start(bf16[1024,1024]{1,0:T(8,128)(2,1)} %refs_3_.11) | copy-start | bytes 6291460
  43.3 5.8 %collective-permute-start.1 = (bf16[512,256]{1,0:T(8,128)(2,1)S(1)}, bf16[512,256]{1,0:T(8,128)(2,1)S(1)}, u32[]{:S(2)}, u32[]{:S(2)}) collective-permute-start(bf16[512,256]{1,0:T(8,128)(2,1)S(1)} %order.2.refs_2_.refs_0_), channel_id=1, source_target_pairs={{0,2},{1,3},{2,0},{3,1},{4,6},{5,7},{6,4},{7,5},{8,10},{9,11},{10,... | collective-permute-start | bytes 786440 | tf_op jit(solution)/shard_map/ppermute | solution.py:39
  49.2 4.5 %collective-permute-start.2 = (bf16[512,512]{1,0:T(8,128)(2,1)S(1)}, bf16[512,512]{1,0:T(8,128)(2,1)S(1)}, u32[]{:S(2)}, u32[]{:S(2)}) collective-permute-start(bf16[512,512]{1,0:T(8,128)(2,1)S(1)} %pair.2), channel_id=1, source_target_pairs={{0,1},{1,0},{2,3},{3,2},{4,5},{5,4},{6,7},{7,6},{8,9},{9,8},{10,11... | collective-permute-start | bytes 1572872 | tf_op jit(solution)/shard_map/ppermute | solution.py:39
  52.2 7.9 %collective-permute-start = (bf16[512,256]{1,0:T(8,128)(2,1)S(1)}, bf16[512,256]{1,0:T(8,128)(2,1)S(1)}, u32[]{:S(2)}, u32[]{:S(2)}) collective-permute-start(bf16[512,256]{1,0:T(8,128)(2,1)S(1)} %order.3.refs_2_.refs_5_.refs_0_), channel_id=1, source_target_pairs={{0,2},{1,3},{2,0},{3,1},{4,6},{5,7},{6,4},{7,5},{8,10},{9,11},{10,... | collective-permute-start | bytes 786440 | tf_op jit(solution)/shard_map/ppermute | solution.py:39
  55.3 4.7 %collective-permute-start.3 = (bf16[256,512]{1,0:T(8,128)(2,1)S(1)}, bf16[256,512]{1,0:T(8,128)(2,1)S(1)}, u32[]{:S(2)}, u32[]{:S(2)}) collective-permute-start(bf16[256,512]{1,0:T(8,128)(2,1)S(1)} %get-tuple-element.26.refs_5_), channel_id=1, source_target_pairs={{0,1},{1,0},{2,3},{3,2},{4,5},{5,4},{6,7},{7,6},{8,9},{9,8},{10,11... | collective-permute-start | bytes 786440 | tf_op jit(solution)/shard_map/ppermute | solution.py:39
  57.4 5.0 %copy-start.4 = (bf16[256,1024]{1,0:T(8,128)(2,1)S(1)}, bf16[256,1024]{1,0:T(8,128)(2,1)}, u32[]{:S(2)}) copy-start(bf16[256,1024]{1,0:T(8,128)(2,1)} %refs_4_.9) | copy-start | bytes 1572868
  57.4 2.8 %collective-permute-start.4 = (bf16[256,512]{1,0:T(8,128)(2,1)S(1)}, bf16[256,512]{1,0:T(8,128)(2,1)S(1)}, u32[]{:S(2)}, u32[]{:S(2)}) collective-permute-start(bf16[256,512]{1,0:T(8,128)(2,1)S(1)} %get-tuple-element.27.refs_0_), channel_id=1, source_target_pairs={{0,1},{1,0},{2,3},{3,2},{4,5},{5,4},{6,7},{7,6},{8,9},{9,8},{10,11... | collective-permute-start | bytes 786440 | tf_op jit(solution)/shard_map/ppermute | solution.py:39
  60.2 3.5 %collective-permute-start.5 = (bf16[512,512]{1,0:T(8,128)(2,1)S(1)}, bf16[512,512]{1,0:T(8,128)(2,1)S(1)}, u32[]{:S(2)}, u32[]{:S(2)}) collective-permute-start(bf16[512,512]{1,0:T(8,128)(2,1)S(1)} %pair.3.refs_5_), channel_id=1, source_target_pairs={{0,1},{1,0},{2,3},{3,2},{4,5},{5,4},{6,7},{7,6},{8,9},{9,8},{10,11... | collective-permute-start | bytes 1572872 | tf_op jit(solution)/shard_map/ppermute | solution.py:39
  61.1 7.9 %collective-permute-start.6 = (bf16[256,512]{1,0:T(8,128)(2,1)S(1)}, bf16[256,512]{1,0:T(8,128)(2,1)S(1)}, u32[]{:S(2)}, u32[]{:S(2)}) collective-permute-start(bf16[256,512]{1,0:T(8,128)(2,1)S(1)} %get-tuple-element.28.refs_2_.refs_1_), channel_id=1, source_target_pairs={{0,2},{1,3},{2,0},{3,1},{4,6},{5,7},{6,4},{7,5},{8,10},{9,11},{10,... | collective-permute-start | bytes 786440 | tf_op jit(solution)/shard_map/ppermute | solution.py:39
  62.4 6.6 %collective-permute-start.7 = (bf16[64,1024]{1,0:T(8,128)(2,1)S(1)}, bf16[64,1024]{1,0:T(8,128)(2,1)S(1)}, u32[]{:S(2)}, u32[]{:S(2)}) collective-permute-start(bf16[64,1024]{1,0:T(8,128)(2,1)S(1)} %head.1), channel_id=1, source_target_pairs={{4,0},{8,4},{12,8},{16,12},{20,16},{24,20},{28,24},{5,1},{9,5},{13... | collective-permute-start | bytes 393224 | tf_op jit(solution)/shard_map/ppermute | solution.py:45
  65.3 6.9 %collective-permute-start.11 = (bf16[256,512]{1,0:T(8,128)(2,1)S(1)}, bf16[256,512]{1,0:T(8,128)(2,1)S(1)}, u32[]{:S(2)}, u32[]{:S(2)}) collective-permute-start(bf16[256,512]{1,0:T(8,128)(2,1)S(1)} %get-tuple-element.31.refs_2_), channel_id=1, source_target_pairs={{0,1},{1,0},{2,3},{3,2},{4,5},{5,4},{6,7},{7,6},{8,9},{9,8},{10,11... | collective-permute-start | bytes 786440 | tf_op jit(solution)/shard_map/ppermute | solution.py:39
  65.8 8.8 %collective-permute-start.10 = (bf16[256,512]{1,0:T(8,128)(2,1)S(1)}, bf16[256,512]{1,0:T(8,128)(2,1)S(1)}, u32[]{:S(2)}, u32[]{:S(2)}) collective-permute-start(bf16[256,512]{1,0:T(8,128)(2,1)S(1)} %get-tuple-element.32.refs_4_), channel_id=1, source_target_pairs={{0,2},{1,3},{2,0},{3,1},{4,6},{5,7},{6,4},{7,5},{8,10},{9,11},{10,... | collective-permute-start | bytes 786440 | tf_op jit(solution)/shard_map/ppermute | solution.py:39
  69.1 6.5 %collective-permute-start.9 = (bf16[256,512]{1,0:T(8,128)(2,1)S(1)}, bf16[256,512]{1,0:T(8,128)(2,1)S(1)}, u32[]{:S(2)}, u32[]{:S(2)}) collective-permute-start(bf16[256,512]{1,0:T(8,128)(2,1)S(1)} %finish.4.refs_5_.refs_0_), channel_id=1, source_target_pairs={{0,1},{1,0},{2,3},{3,2},{4,5},{5,4},{6,7},{7,6},{8,9},{9,8},{10,11... | collective-permute-start | bytes 786440 | tf_op jit(solution)/shard_map/ppermute | solution.py:39
  70.5 5.2 %copy-start.3 = (bf16[1024,1024]{1,0:T(8,128)(2,1)S(1)}, bf16[1024,1024]{1,0:T(8,128)(2,1)}, u32[]{:S(2)}) copy-start(bf16[1024,1024]{1,0:T(8,128)(2,1)} %refs_3_.15) | copy-start | bytes 6291460
  72.1 3.6 %copy-start.2 = (bf16[1024,1024]{1,0:T(8,128)(2,1)S(1)}, bf16[1024,1024]{1,0:T(8,128)(2,1)}, u32[]{:S(2)}) copy-start(bf16[1024,1024]{1,0:T(8,128)(2,1)} %refs_2_.7) | copy-start | bytes 6291460
  72.1 5.3 %collective-permute-start.8 = (bf16[256,512]{1,0:T(8,128)(2,1)S(1)}, bf16[256,512]{1,0:T(8,128)(2,1)S(1)}, u32[]{:S(2)}, u32[]{:S(2)}) collective-permute-start(bf16[256,512]{1,0:T(8,128)(2,1)S(1)} %get-tuple-element.34.refs_2_), channel_id=1, source_target_pairs={{0,1},{1,0},{2,3},{3,2},{4,5},{5,4},{6,7},{7,6},{8,9},{9,8},{10,11... | collective-permute-start | bytes 786440 | tf_op jit(solution)/shard_map/ppermute | solution.py:39
  72.3 9.8 %collective-permute-start.14 = (bf16[256,512]{1,0:T(8,128)(2,1)S(1)}, bf16[256,512]{1,0:T(8,128)(2,1)S(1)}, u32[]{:S(2)}, u32[]{:S(2)}) collective-permute-start(bf16[256,512]{1,0:T(8,128)(2,1)S(1)} %get-tuple-element.37.refs_4_), channel_id=1, source_target_pairs={{0,2},{1,3},{2,0},{3,1},{4,6},{5,7},{6,4},{7,5},{8,10},{9,11},{10,... | collective-permute-start | bytes 786440 | tf_op jit(solution)/shard_map/ppermute | solution.py:39
  74.7 8.1 %collective-permute-start.13 = (bf16[256,512]{1,0:T(8,128)(2,1)S(1)}, bf16[256,512]{1,0:T(8,128)(2,1)S(1)}, u32[]{:S(2)}, u32[]{:S(2)}) collective-permute-start(bf16[256,512]{1,0:T(8,128)(2,1)S(1)} %finish.5.refs_6_.refs_0_), channel_id=1, source_target_pairs={{0,1},{1,0},{2,3},{3,2},{4,5},{5,4},{6,7},{7,6},{8,9},{9,8},{10,11... | collective-permute-start | bytes 786440 | tf_op jit(solution)/shard_map/ppermute | solution.py:39
  77.5 8.5 %collective-permute-start.12 = (bf16[256,512]{1,0:T(8,128)(2,1)S(1)}, bf16[256,512]{1,0:T(8,128)(2,1)S(1)}, u32[]{:S(2)}, u32[]{:S(2)}) collective-permute-start(bf16[256,512]{1,0:T(8,128)(2,1)S(1)} %get-tuple-element.39.refs_4_), channel_id=1, source_target_pairs={{0,2},{1,3},{2,0},{3,1},{4,6},{5,7},{6,4},{7,5},{8,10},{9,11},{10,... | collective-permute-start | bytes 786440 | tf_op jit(solution)/shard_map/ppermute | solution.py:39
  78.8 5.8 %collective-permute-start.15 = (bf16[64,1024]{1,0:T(8,128)(2,1)S(1)}, bf16[64,1024]{1,0:T(8,128)(2,1)S(1)}, u32[]{:S(2)}, u32[]{:S(2)}) collective-permute-start(bf16[64,1024]{1,0:T(8,128)(2,1)S(1)} %attend_first.1.refs_2_.refs_8_), channel_id=1, source_target_pairs={{0,4},{4,8},{8,12},{12,16},{16,20},{20,24},{24,28},{1,5},{5,9},{9,... | collective-permute-start | bytes 393224 | tf_op jit(solution)/shard_map/ppermute | solution.py:45
  82.2 4.7 %collective-permute-start.17 = (bf16[256,512]{1,0:T(8,128)(2,1)S(1)}, bf16[256,512]{1,0:T(8,128)(2,1)S(1)}, u32[]{:S(2)}, u32[]{:S(2)}) collective-permute-start(bf16[256,512]{1,0:T(8,128)(2,1)S(1)} %finish.6.refs_5_.refs_0_), channel_id=1, source_target_pairs={{0,1},{1,0},{2,3},{3,2},{4,5},{5,4},{6,7},{7,6},{8,9},{9,8},{10,11... | collective-permute-start | bytes 786440 | tf_op jit(solution)/shard_map/ppermute | solution.py:39
  86.0 2.6 %collective-permute-start.16 = (bf16[256,512]{1,0:T(8,128)(2,1)S(1)}, bf16[256,512]{1,0:T(8,128)(2,1)S(1)}, u32[]{:S(2)}, u32[]{:S(2)}) collective-permute-start(bf16[256,512]{1,0:T(8,128)(2,1)S(1)} %finish.7.refs_5_.refs_0_), channel_id=1, source_target_pairs={{0,1},{1,0},{2,3},{3,2},{4,5},{5,4},{6,7},{7,6},{8,9},{9,8},{10,11... | collective-permute-start | bytes 786440 | tf_op jit(solution)/shard_map/ppermute | solution.py:39
  (1 other events, 0.7 us)
